TPU v7x, 32 devices: a whole 2x2x4 slice. The times are simulated.
32 devices in a mesh: groups: 2 (over x), store: 16 (over z, y, core).
Axes of the slice: x: 2, y: 2, z: 4, core: 2. Of those that a mesh axis runs over, the one named last changes fastest.
Arguments:
- tokens: bfloat16 [24576, 8192], P(('groups', 'store')), parts along dimension 0, may hold values from -400 to 400
- input_norm_gain: bfloat16 [8192], replicated, may hold values from 0.5 to 1.5
- value_matrix: bfloat16 [8192, 1024], P('store'), may hold values from -0.0625 to 0.0625
- adapter_down_factors: bfloat16 [8192, 16, 64], P('store'), may hold values from -0.0625 to 0.0625
- adapter_up_factors: bfloat16 [16, 64, 1024], P(None, None, 'store'), may hold values from -0.75 to 0.75
- document_lengths: int32 [32, 4], P(('groups', 'store')), parts along dimension 0, may hold values from 1 to 384, 768 in all within a row
- document_tenant: int32 [32, 4], P(('groups', 'store')), parts along dimension 0, may hold values from 0 to 15
- tenant_adapter_slot: int32 [16], replicated, may hold values from 0 to 15, each once
Outputs:
- values_out: bfloat16 [24576, 1024], P(('groups', 'store')), parts along dimension 0
There are 2 independent parts, one for each index of `groups`. A program takes and returns all parts, laid end to end along the dimension named above; an argument that names none is the same for every part. Nothing has to cross between parts.
Inputs may be any that keep to these rules, and one draw needn't show every extreme that they name: `document_lengths`: each row sums to 768. `tenant_adapter_slot`: A permutation of the slots.
All inputs are finite; a program needn't handle non-finite values.
Results may differ from a plain program's by a relative error of at most 0.0056.
Values may be sent and summed in bfloat16 or wider, within the bound.
No kernel may reach another device: no remote copies, remote signals or barrier semaphores. Data moves between devices by JAX's collectives and lax.ppermute only.
A program may use at most 128 MiB of HBM per device.

v0:
```python
import jax
import jax.numpy as jnp
from jax import lax
from jax.sharding import PartitionSpec as P

adapter_scale = 2.0


def token_slots(lengths, tenants, tenant_adapter_slot, row_count):
    ends = jnp.cumsum(lengths)
    position = jnp.arange(row_count, dtype=jnp.int32)
    doc_index = jnp.sum((position[:, None] >= ends[None, :]).astype(jnp.int32), axis=1)
    doc_pick = (
        doc_index[:, None] == jnp.arange(lengths.shape[0], dtype=jnp.int32)[None, :]
    ).astype(jnp.int32)
    tenant = jnp.sum(doc_pick * tenants[None, :], axis=1)
    tenant_pick = (
        tenant[:, None] == jnp.arange(tenant_adapter_slot.shape[0], dtype=jnp.int32)[None, :]
    ).astype(jnp.int32)
    return jnp.sum(tenant_pick * tenant_adapter_slot[None, :], axis=1)


def pick_rank(rank_total_rows, slots, count_of_adapters, rank_span_width):
    select = (slots[:, None] == jnp.arange(count_of_adapters, dtype=jnp.int32)[None, :]).astype(
        jnp.float32
    )
    shaped = rank_total_rows.reshape(slots.shape[0], count_of_adapters, rank_span_width)
    return jnp.sum(shaped * select[:, :, None], axis=1)


def per_device(
    tokens,
    input_norm_gain,
    value_matrix,
    adapter_down_factors,
    adapter_up_factors,
    document_lengths,
    document_tenant,
    tenant_adapter_slot,
):
    row_count = tokens.shape[0]
    count_of_adapters = adapter_down_factors.shape[1]
    rank_span_width = adapter_down_factors.shape[2]
    flat_width = count_of_adapters * rank_span_width
    wide = tokens.astype(jnp.float32)
    meansq = jnp.mean(wide * wide, axis=1, keepdims=True)
    normed_input = (wide * lax.rsqrt(meansq + 1e-05) * input_norm_gain.astype(jnp.float32)).astype(
        jnp.bfloat16
    )
    slots = token_slots(document_lengths[0], document_tenant[0], tenant_adapter_slot, row_count)
    columns = normed_input
    base_output = jnp.dot(
        columns,
        lax.all_gather(value_matrix, "store", axis=0, tiled=True),
        preferred_element_type=jnp.float32,
    )
    document_piece = lax.all_gather(adapter_down_factors, "store", axis=0, tiled=True)
    columns = normed_input
    rank_total_rows = jnp.dot(
        columns,
        document_piece.reshape(document_piece.shape[0], flat_width),
        preferred_element_type=jnp.float32,
    )
    mid_sum = pick_rank(rank_total_rows, slots, count_of_adapters, rank_span_width)
    mid = mid_sum.astype(jnp.bfloat16)
    select = (slots[:, None] == jnp.arange(count_of_adapters, dtype=jnp.int32)[None, :]).astype(
        jnp.bfloat16
    )
    expanded_rows = (mid[:, None, :] * select[:, :, None]).reshape(row_count, flat_width)
    document_piece = lax.all_gather(adapter_up_factors, "store", axis=2, tiled=True)
    adapter_update = jnp.dot(
        expanded_rows,
        document_piece.reshape(flat_width, document_piece.shape[2]),
        preferred_element_type=jnp.float32,
    )
    return (base_output + adapter_scale * adapter_update).astype(jnp.bfloat16)


def solution(mesh):
    in_specs = (
        P(("groups", "store"), None),
        P(),
        P("store", None),
        P("store", None, None),
        P(None, None, "store"),
        P(("groups", "store"), None),
        P(("groups", "store"), None),
        P(),
    )
    out_specs = P(("groups", "store"), None)
    return jax.shard_map(
        per_device, mesh=mesh, in_specs=in_specs, out_specs=out_specs, check_vma=False
    )
```

profile of v0, /device:TPU:9, one launch (start us, length us, event | category | flops | bytes accessed | tf_op | source)
XLA Modules:
  0.0 345.4 jit_solution(4552228435148138985)
XLA Ops:
  6.5 0.0 all-gather.6.cloned.1.call-start
  6.5 0.7 all-gather.6.cloned.1.call-update
  7.3 0.0 all-gather.8.cloned.1.call-start
  7.3 1.9 copy.13
  9.2 0.0 all-gather.8.cloned.1.call-update
  9.2 0.0 all-gather.4.cloned.1.call-start
  9.3 0.7 all-gather.4.cloned.1.call-update
  9.9 0.7 convert_element_type.39
  10.7 0.8 reduce-window.8
  11.5 0.1 convert_reduce_fusion
  11.6 0.7 select_reduce_fusion.1
  12.3 0.7 select_reduce_fusion
  13.1 7.1 %fusion = f32[768]{0:T(1024)S(1)} fusion(bf16[768,8192]{1,0:T(8,128)(2,1)} %param.8), kind=kLoop, calls=%fused_computation.2 | loop fusion | flops 18873600 | bytes 12585984 | tf_op jit(solution)/shard_map/reduce_sum | solution.py:46
  20.2 119.5 %all-gather.6.cloned.1.call-done = bf16[8192,16,64]{0,2,1:T(8,128)(2,1)} async-done(((bf16[512,16,64]{0,2,1:T(8,128)(2,1)}), bf16[8192,16,64]{0,2,1:T(8,128)(2,1)}) %all-gather.6.cloned.1.call-update) | async-done | bytes 16777232 | tf_op jit(solution)/shard_map/all_gather | solution.py:57
  139.7 18.6 %multiply_reduce_fusion = bf16[768,64]{0,1:T(8,128)(2,1)S(1)} fusion(bf16[8192,16,64]{0,2,1:T(8,128)(2,1)} %all-gather.6.cloned.1.call-done, f32[8192]{0:T(1024)S(1)} %convert_element_type.39, f32[768]{0:T(1024)S(1)} %add_rsqrt_fusion, bf16[768,8192]{1,0:T(8,128)(2,1)} %param.8, f32[768,16]{0,1:T(8,128)S(1)} %get-tuple-element.5), kind=kOutput, calls=%fused_computation.14 | convolution fusion | flops 12911591424 | bytes 29543424 | tf_op jit(solution)/shard_map/dot_general | solution.py:59
  158.2 34.4 %all-gather.8.cloned.1.call-done = bf16[16,64,1024]{1,0,2:T(8,128)(2,1)} async-done(((bf16[16,64,64]{1,0,2:T(8,128)(2,1)}), bf16[16,64,1024]{1,0,2:T(8,128)(2,1)}) %all-gather.8.cloned.1.call-update) | async-done | bytes 2097168 | tf_op jit(solution)/shard_map/all_gather | solution.py:70
  192.6 5.5 %fusion.6 = f32[768,1024,1]{1,0,2:T(8,128)S(1)} fusion(bf16[16,64,1024]{1,0,2:T(8,128)(2,1)} %all-gather.8.cloned.1.call-done, bf16[768,16]{0,1:T(8,128)(2,1)S(1)} %get-tuple-element.6, bf16[768,64]{0,1:T(8,128)(2,1)S(1)} %multiply_reduce_fusion), kind=kOutput, calls=%fused_computation.8 | convolution fusion | flops 1611399168 | bytes 5365760 | tf_op jit(solution)/shard_map/dot_general | solution.py:71
  198.1 120.3 %all-gather.4.cloned.1.call-done = bf16[8192,1024]{1,0:T(8,128)(2,1)} async-done(((bf16[512,1024]{1,0:T(8,128)(2,1)}), bf16[8192,1024]{1,0:T(8,128)(2,1)}) %all-gather.4.cloned.1.call-update) | async-done | bytes 16777232 | tf_op jit(solution)/shard_map/all_gather | solution.py:54
  318.4 20.6 %fusion.12 = bf16[768,1024]{1,0:T(8,128)(2,1)} fusion(f32[768,1024,1]{1,0,2:T(8,128)S(1)} %fusion.6, bf16[8192,1024]{1,0:T(8,128)(2,1)} %all-gather.4.cloned.1.call-done, bf16[768,8192]{1,0:T(8,128)(2,1)} %param.8, f32[8192]{0:T(1024)S(1)} %convert_element_type.39, f32[768]{0:T(1024)S(1)} %add_rsqrt_fusion), kind=kOutput, calls=%fused_computation.13 | convolution fusion | flops 12912427008 | bytes 34114560 | tf_op jit(solution)/shard_map/dot_general | solution.py:52
  (2 shorter events, 0.0 us)
Async XLA Ops:
  6.5 133.1 %all-gather.6.cloned.1.call-start = ((), (), s32[]{:S(2)}) async-start(), calls=%async_computation.1 | async-start | bytes 17825792 | tf_op jit(solution)/shard_map/all_gather | solution.py:57
  7.3 185.4 %all-gather.8.cloned.1.call-start = ((), (), s32[]{:S(2)}) async-start(), calls=%async_computation.2 | async-start | bytes 4456448 | tf_op jit(solution)/shard_map/all_gather | solution.py:70
  9.2 309.1 %all-gather.4.cloned.1.call-start = ((), (), s32[]{:S(2)}) async-start(), calls=%async_computation | async-start | bytes 17825792 | tf_op jit(solution)/shard_map/all_gather | solution.py:54
Sparse Core Ops, SparseCore 0:
  9.5 130.0 all-gather.5
  141.8 50.7 all-gather.7
  194.8 123.5 all-gather.3
where the time goes:
time: 349 us; the launch traced here: 345 us
  waiting for transfers between devices  276 us (79%)
  matrix products  44.6 us (13%)
  between operations  13.1 us (4%)
  other arithmetic  10.2 us (3%)
    all_gather x1, waiting for transfers between devices, per_device(): lax.all_gather(value_matrix, 'store', axis=0, tiled=True)  120 us
    all_gather x1, waiting for transfers between devices, per_device(): lax.all_gather(adapter_down_factors, 'store', axis=0, tiled=True)  119 us
    all_gather x1, waiting for transfers between devices, per_device(): lax.all_gather(adapter_up_factors, 'store', axis=2, tiled=True)  34.4 us
    dot_general x1, matrix products, per_device(): jnp.dot(columns, lax.all_gather(value_matrix, 'store', axis=0, tiled=True...  20.6 us
    dot_general x1, matrix products, per_device(): jnp.dot(columns, document_piece.reshape(document_piece.shape[0], flat_wid...  18.6 us
    reduce_sum x1, other arithmetic, per_device(): meansq = jnp.mean(wide * wide, axis=1, keepdims=True)  7.1 us
  transfers between devices with their start and end apart: 3, of which 3 were waited for; matrix products, arithmetic and copies ran while one was open for 10% of the time, Pallas kernels for 0%

commit v1 on v0

v1 whole, which is shorter than its diff:
```python
import functools

import jax
import jax.numpy as jnp
from jax import lax
from jax.experimental import pallas as pl
from jax.experimental.pallas import tpu as pltpu
from jax.sharding import PartitionSpec as P

adapter_scale = 2.0
cores, rows_y, lane = 2, 2, 128
nt = (((1,), (1,)), ((), ()))


def token_slots(lengths, tenants, tenant_adapter_slot, row_count):
    ends = jnp.cumsum(lengths)
    position = jnp.arange(row_count, dtype=jnp.int32)
    doc_index = jnp.sum((position[:, None] >= ends[None, :]).astype(jnp.int32), axis=1)
    doc_pick = (
        doc_index[:, None] == jnp.arange(lengths.shape[0], dtype=jnp.int32)[None, :]
    ).astype(jnp.int32)
    tenant = jnp.sum(doc_pick * tenants[None, :], axis=1)
    tenant_pick = (
        tenant[:, None] == jnp.arange(tenant_adapter_slot.shape[0], dtype=jnp.int32)[None, :]
    ).astype(jnp.int32)
    return jnp.sum(tenant_pick * tenant_adapter_slot[None, :], axis=1)


def pick_rank(rank_total_rows, slots, count_of_adapters, rank_span_width):
    select = (slots[:, None] == jnp.arange(count_of_adapters, dtype=jnp.int32)[None, :]).astype(
        jnp.float32
    )
    shaped = rank_total_rows.reshape(slots.shape[0], count_of_adapters, rank_span_width)
    return jnp.sum(shaped * select[:, :, None], axis=1)


def plain(
    tokens,
    input_norm_gain,
    value_matrix,
    adapter_down_factors,
    adapter_up_factors,
    document_lengths,
    document_tenant,
    tenant_adapter_slot,
):
    row_count = tokens.shape[0]
    count_of_adapters = adapter_down_factors.shape[1]
    rank_span_width = adapter_down_factors.shape[2]
    flat_width = count_of_adapters * rank_span_width
    wide = tokens.astype(jnp.float32)
    meansq = jnp.mean(wide * wide, axis=1, keepdims=True)
    normed = (wide * lax.rsqrt(meansq + 1e-05) * input_norm_gain.astype(jnp.float32)).astype(
        jnp.bfloat16
    )
    slots = token_slots(document_lengths[0], document_tenant[0], tenant_adapter_slot, row_count)
    base_output = jnp.dot(
        normed,
        lax.all_gather(value_matrix, "store", axis=0, tiled=True),
        preferred_element_type=jnp.float32,
    )
    down = lax.all_gather(adapter_down_factors, "store", axis=0, tiled=True)
    rank_total_rows = jnp.dot(
        normed, down.reshape(down.shape[0], flat_width), preferred_element_type=jnp.float32
    )
    mid = pick_rank(rank_total_rows, slots, count_of_adapters, rank_span_width)
    mid = mid.astype(jnp.bfloat16)
    select = (slots[:, None] == jnp.arange(count_of_adapters, dtype=jnp.int32)[None, :]).astype(
        jnp.bfloat16
    )
    expanded_rows = (mid[:, None, :] * select[:, :, None]).reshape(row_count, flat_width)
    up = lax.all_gather(adapter_up_factors, "store", axis=2, tiled=True)
    adapter_update = jnp.dot(
        expanded_rows, up.reshape(flat_width, up.shape[2]), preferred_element_type=jnp.float32
    )
    return (base_output + adapter_scale * adapter_update).astype(jnp.bfloat16)


def norm_kernel(source_ref, tokens_ref, gain_ref, own_ref, other_ref):
    width = tokens_ref.shape[1]
    half = width // 2
    total = jnp.zeros((tokens_ref.shape[0], lane), jnp.float32)
    for i in range(width // lane):
        part = tokens_ref[:, i * lane : (i + 1) * lane].astype(jnp.float32)
        total += part * part
    scale = lax.rsqrt(jnp.sum(total, axis=1, keepdims=True) / width + 1e-05)
    for out_ref, first in ((own_ref, 0), (other_ref, half // lane)):
        for i in range(half // lane):
            start = pl.multiple_of(source_ref[first + i], lane)
            part = tokens_ref[:, pl.ds(start, lane)].astype(jnp.float32)
            gain = gain_ref[:, pl.ds(start, lane)].astype(jnp.float32)
            out_ref[:, i * lane : (i + 1) * lane] = (part * scale * gain).astype(jnp.bfloat16)


def norm_in_order(tokens, gain, source):
    rows, width = tokens.shape
    block = 64
    half = jax.ShapeDtypeStruct((rows, width // 2), jnp.bfloat16)
    return pl.pallas_call(
        norm_kernel,
        out_shape=(half, half),
        grid_spec=pltpu.PrefetchScalarGridSpec(
            num_scalar_prefetch=1,
            grid=(rows // block,),
            in_specs=[
                pl.BlockSpec((block, width), lambda i, *_: (i, 0)),
                pl.BlockSpec((1, width), lambda i, *_: (0, 0)),
            ],
            out_specs=[pl.BlockSpec((block, width // 2), lambda i, *_: (i, 0))] * 2,
        ),
        compiler_params=pltpu.CompilerParams(vmem_limit_bytes=16 << 20),
        cost_estimate=pl.CostEstimate(
            flops=6 * rows * width, bytes_accessed=4 * rows * width, transcendentals=rows
        ),
    )(source, tokens, gain.reshape(1, width))


def fixed(array):
    return pl.BlockSpec(array.shape, lambda i, *_: (0,) * array.ndim, pipeline_mode=pl.Buffered(1))


def tiled(array, tile):
    return pl.BlockSpec((tile,) + array.shape[1:], lambda i, *_: (i, 0))


def mid_kernel(docs, rank, pieces, ends_ref, slots_ref, *refs):
    token_refs, down_refs, out_refs = refs[:2], refs[2:-2], refs[-2:]
    tile = token_refs[0].shape[0]
    shard = sum(down_refs[i].shape[1] for i in pieces[0])
    row = pl.program_id(0) * tile + lax.broadcasted_iota(jnp.int32, (tile, rank), 0)
    for side in range(2):
        acc = jnp.zeros((tile, docs * rank), jnp.float32)
        for at, parts in enumerate(pieces):
            slabs = []
            for doc in range(docs):
                start = pl.multiple_of(slots_ref[side, doc] * rank, rank)
                slabs.append(
                    jnp.concatenate([down_refs[i][pl.ds(start, rank), :] for i in parts], 1)
                )
            acc += lax.dot_general(
                token_refs[side][:, at * shard : (at + 1) * shard],
                jnp.concatenate(slabs, 0),
                nt,
                preferred_element_type=jnp.float32,
            )
        mid = jnp.zeros((tile, rank), jnp.float32)
        for doc in range(docs):
            low = 0 if doc == 0 else ends_ref[side, doc - 1]
            inside = (row >= low) & (row < ends_ref[side, doc])
            mid = jnp.where(inside, acc[:, doc * rank : (doc + 1) * rank], mid)
        out_refs[side][...] = mid


def mid_partials(own, other, pieces, ends, slots, rank):
    rows = own.shape[0]
    tile = 256 if rows % 256 == 0 else rows
    arrays, places = [], []
    for parts in pieces:
        places.append(tuple(range(len(arrays), len(arrays) + len(parts))))
        arrays += parts
    docs = slots.shape[1]
    out = jax.ShapeDtypeStruct((rows, rank), jnp.float32)
    return pl.pallas_call(
        functools.partial(mid_kernel, docs, rank, tuple(places)),
        out_shape=(out, out),
        grid_spec=pltpu.PrefetchScalarGridSpec(
            num_scalar_prefetch=2,
            grid=(rows // tile,),
            in_specs=[tiled(own, tile), tiled(other, tile)] + [fixed(a) for a in arrays],
            out_specs=[pl.BlockSpec((tile, rank), lambda i, *_: (i, 0))] * 2,
        ),
        compiler_params=pltpu.CompilerParams(vmem_limit_bytes=32 << 20),
        cost_estimate=pl.CostEstimate(
            flops=4 * rows * own.shape[1] * docs * rank,
            bytes_accessed=4 * own.size + sum(2 * a.size for a in arrays),
            transcendentals=0,
        ),
    )(ends, slots, own, other, *arrays)


def shard_rows(refs, parts, cols):
    return jnp.concatenate([refs[i][a:b, cols] for i, a, b in parts], 0)


def part_kernel(pieces, columns, *refs):
    token_refs, value_refs, out_refs = refs[:2], refs[2:-2], refs[-2:]
    for n in range(0, out_refs[0].shape[1], columns):
        cols = slice(n, n + columns)
        acc = [None, None]
        for at, parts in pieces:
            rhs = shard_rows(value_refs, parts, cols)
            for side in range(2):
                term = jnp.dot(
                    token_refs[side][:, at : at + rhs.shape[0]],
                    rhs,
                    preferred_element_type=jnp.float32,
                )
                acc[side] = term if acc[side] is None else acc[side] + term
        for side in range(2):
            out_refs[side][:, cols] = acc[side]


def value_partials(own, other, arrays, pieces, width):
    rows = own.shape[0]
    tile = 256 if rows % 256 == 0 else rows
    out = jax.ShapeDtypeStruct((rows, width), jnp.float32)
    depth = sum(b - a for _, parts in pieces for _, a, b in parts)
    return pl.pallas_call(
        functools.partial(part_kernel, pieces, 256),
        out_shape=(out, out),
        grid=(rows // tile,),
        in_specs=[tiled(own, tile), tiled(other, tile)] + [fixed(a) for a in arrays],
        out_specs=[tiled(out, tile)] * 2,
        compiler_params=pltpu.CompilerParams(vmem_limit_bytes=40 << 20),
        cost_estimate=pl.CostEstimate(
            flops=4 * rows * depth * width,
            bytes_accessed=4 * own.size + 8 * out.size + sum(2 * a.size for a in arrays),
            transcendentals=0,
        ),
    )(own, other, *arrays)


def last_kernel(pieces, columns, spans, slots_ref, ends_ref, *refs):
    token_refs, sum_refs, mid_refs, up_ref = refs[:2], refs[2:4], refs[4:6], refs[6]
    value_refs, out_ref = refs[7:-1], refs[-1]
    docs = slots_ref.shape[0]
    tile, rank = mid_refs[0].shape
    row = pl.program_id(0) * tile + lax.broadcasted_iota(jnp.int32, (tile, rank), 0)
    mid = (mid_refs[0][...] + mid_refs[1][...]).astype(jnp.bfloat16)
    nothing = jnp.zeros_like(mid)
    spread = []
    for doc in range(docs):
        low = 0 if doc == 0 else ends_ref[doc - 1]
        spread.append(jnp.where((row >= low) & (row < ends_ref[doc]), mid, nothing))
    spread = jnp.concatenate(spread, 1)
    for n in range(0, out_ref.shape[1], columns):
        cols = slice(n, n + columns)
        up = [
            up_ref[pl.ds(pl.multiple_of(slots_ref[doc] * rank, rank), rank), cols]
            for doc in range(docs)
        ]
        acc = adapter_scale * jnp.dot(
            spread, jnp.concatenate(up, 0), preferred_element_type=jnp.float32
        )
        acc += sum_refs[0][:, cols] + sum_refs[1][:, cols]
        for side, at, parts in pieces:
            rhs = shard_rows(value_refs, parts, cols)
            acc += jnp.dot(
                token_refs[side][:, at - spans[side] : at - spans[side] + rhs.shape[0]],
                rhs,
                preferred_element_type=jnp.float32,
            )
        out_ref[:, cols] = acc.astype(out_ref.dtype)


def last_values(own, other, sums, mids, up, slots, ends, arrays, pieces):
    rows, width = sums[0].shape
    tile = 256 if rows % 256 == 0 else rows
    depth = sum(b - a for _, _, parts in pieces for _, a, b in parts)
    return pl.pallas_call(
        functools.partial(last_kernel, pieces, 256, (0, 0)),
        out_shape=jax.ShapeDtypeStruct((rows, width), jnp.bfloat16),
        grid_spec=pltpu.PrefetchScalarGridSpec(
            num_scalar_prefetch=2,
            grid=(rows // tile,),
            in_specs=[tiled(a, tile) for a in (own, other, *sums, *mids)]
            + [fixed(a) for a in (up, *arrays)],
            out_specs=pl.BlockSpec((tile, width), lambda i, *_: (i, 0)),
        ),
        compiler_params=pltpu.CompilerParams(vmem_limit_bytes=40 << 20),
        cost_estimate=pl.CostEstimate(
            flops=2 * rows * depth * width,
            bytes_accessed=4 * own.size + 10 * rows * width + sum(2 * a.size for a in arrays),
            transcendentals=0,
        ),
    )(slots, ends, own, other, *sums, *mids, up, *arrays)


def after(value, *earlier):
    return lax.optimization_barrier((value, *earlier))[0]


def make(groups, store):
    depth = store // (rows_y * cores)

    def index(z, y, c):
        return (z * rows_y + y) * cores + c

    def pairs(move):
        return [
            (index(z, y, c), index(*move(z, y, c)))
            for z in range(depth)
            for y in range(rows_y)
            for c in range(cores)
        ]

    def along_z(value, k):
        return lax.ppermute(value, "store", pairs(lambda z, y, c: ((z + k) % depth, y, c)))

    def along_y(value):
        return lax.ppermute(value, "store", pairs(lambda z, y, c: (z, 1 - y, c)))

    def across(value):
        return lax.ppermute(value, "store", pairs(lambda z, y, c: (z, y, 1 - c)))

    def along_x(value):
        return lax.ppermute(value, "groups", [(g, g ^ 1) for g in range(groups)])

    class Line:
        def __init__(self, send):
            self.send, self.sent = send, []

        def __call__(self, value, *args):
            if len(self.sent) >= 2:
                value = after(value, self.sent[-2])
            self.sent.append(self.send(value, *args))
            return self.sent[-1]

    def per_device(
        tokens,
        input_norm_gain,
        value_matrix,
        adapter_down_factors,
        adapter_up_factors,
        document_lengths,
        document_tenant,
        tenant_adapter_slot,
    ):
        shard, adapters, rank = adapter_down_factors.shape
        flat = adapters * rank
        width = value_matrix.shape[1]
        quarter, half = shard // 4, shard // 2
        me = lax.axis_index("store")
        side = lax.axis_index("groups") % 2
        mz, my, mc = me // (rows_y * cores), (me // cores) % rows_y, me % cores

        down = adapter_down_factors.reshape(shard, flat).T
        take = lax.dynamic_slice_in_dim
        d_have = {(0, 0): take(down, side * half, half, 1)}
        d_miss = {(0, 0): take(down, half - side * half, half, 1)}
        v_have = {
            (0, 0): jnp.concatenate(
                [
                    take(value_matrix, side * half, half, 0),
                    take(value_matrix, 3 * quarter - side * half, quarter, 0),
                ],
                0,
            )
        }
        v_miss = {(0, 0): (take(value_matrix, half - side * half, quarter, 0), 0)}
        up = adapter_up_factors.reshape(flat, -1).T
        up_all = lax.all_gather(up, "store", axis=0, tiled=True).T

        source = []
        for lane_at in (mc, 1 - mc):
            for dy in range(rows_y):
                for k in range(depth):
                    s = index((mz - k) % depth, my ^ dy, lane_at)
                    for c in range(shard // lane):
                        piece = c * lane + jnp.where(c * lane < half, 1, -1) * side * half
                        source.append(s * shard + piece)
        ks = []
        for k in range(1, depth // 2 + 1):
            ks += [k, depth - k] if k != depth - k else [k]
        last = ks[-1]
        z, y, x = Line(along_z), Line(along_y), Line(along_x)

        def x_values(names):
            got = x(jnp.concatenate([v_have[name][:quarter] for name in names], 0))
            for i, name in enumerate(names):
                v_miss[name] = (got, i * quarter)

        d_have[1, 0] = y(d_have[0, 0])
        for k in ks:
            d_have[0, k] = z(d_have[0, 0], k)
        v_have[1, 0] = y(v_have[0, 0])
        for k in ks:
            v_have[0, k] = z(v_have[0, 0], k)
        d_miss[1, 0] = x(d_have[1, 0])
        own, other = norm_in_order(
            after(tokens, d_have[1, 0]), input_norm_gain, jnp.stack(source).astype(jnp.int32))
        for k in ks:
            d_have[1, k] = y(d_have[0, k])
        for k in ks:
            d_miss[0, k] = x(d_have[0, k])
            d_miss[1, k] = x(d_have[1, k])
        for k in ks:
            v_have[1, k] = y(v_have[0, k])
        early = [k for k in ks if k != last]
        x_values([(1, 0)] + [(0, k) for k in early])
        x_values([(1, k) for k in early])
        x_values([(0, last)])
        x_values([(1, last)])

        partner = across(other)

        ends = jnp.cumsum(document_lengths, axis=1).astype(jnp.int32)
        slots = jnp.sum(
            (document_tenant[0][:, None] == jnp.arange(adapters, dtype=jnp.int32)[None, :])
            * tenant_adapter_slot[None, :],
            axis=1,
        ).astype(jnp.int32)[None, :]
        near = jnp.concatenate([ends, slots], 0)
        far = across(near)
        ends_both = jnp.concatenate([ends, far[:1]], 0)
        slots_both = jnp.concatenate([slots, far[1:]], 0)

        names = [(dy, k) for dy in range(rows_y) for k in range(depth)]
        mid_own, mid_far = mid_partials(
            after(own, up_all), partner, [[d_have[n], d_miss[n]] for n in names], ends_both, slots_both, rank
        )
        mids = (mid_own, across(mid_far))

        def lay(names, have, miss):
            arrays, pieces = [], []

            def place(array):
                for i, known in enumerate(arrays):
                    if known is array:
                        return i
                arrays.append(array)
                return len(arrays) - 1

            for name in names:
                h = place(have[name])
                m, row = miss[name]
                m = place(m)
                pieces.append(
                    (
                        (name[0] * depth + name[1]) * shard,
                        ((h, 0, half), (m, row, row + quarter), (h, half, half + quarter)),
                    )
                )
            return arrays, pieces

        arrays, pieces = lay([n for n in names if n[1] != last], v_have, v_miss)
        arrays[0] = after(arrays[0], v_have[0, last])
        sum_own, sum_far = value_partials(own, partner, arrays, tuple(pieces), width)
        sums = (sum_own, across(sum_far))

        final = [(dy, last) for dy in range(rows_y)]
        arrays, pieces = lay(final, v_have, v_miss)
        far_have = {n: across(v_have[n]) for n in final}
        far_miss = {n: (across(v_miss[n][0]), v_miss[n][1]) for n in final}
        far_arrays, far_pieces = lay(final, far_have, far_miss)
        pieces = [(0, at, parts) for at, parts in pieces] + [
            (1, at, tuple((i + len(arrays), a, b) for i, a, b in parts))
            for at, parts in far_pieces
        ]
        return last_values(
            own, other, sums, mids, up_all, slots[0], ends[0], arrays + far_arrays, tuple(pieces)
        )

    return per_device


def solution(mesh):
    in_specs = (
        P(("groups", "store"), None),
        P(),
        P("store", None),
        P("store", None, None),
        P(None, None, "store"),
        P(("groups", "store"), None),
        P(("groups", "store"), None),
        P(),
    )
    out_specs = P(("groups", "store"), None)
    groups, store = mesh.shape["groups"], mesh.shape["store"]

    def run(*args):
        shard = args[2].shape[0]
        cut = shard % (4 * lane) == 0 and store % (rows_y * cores) == 0 and groups % 2 == 0
        return (make(groups, store) if cut else plain)(*args)

    return jax.shard_map(
        run, mesh=mesh, in_specs=in_specs, out_specs=out_specs, check_vma=False
    )
```

time: 349 us -> 287 us (0.82)
  waiting for transfers between devices: 276 us -> 134 us
  local copies, waits for them, and re-layouts: 1.88 us -> 54.7 us
  matrix products: 44.6 us -> 0 us
  Pallas kernels: 0 us -> 42 us
  starting transfers between devices: 0.08 us -> 36.5 us
  other arithmetic: 10.2 us -> 2.3 us
    all_gather x3 -> x1, waiting for transfers between devices: 274 us -> 0.01 us  [per_device(): up_all = lax.all_gather(up, 'store', axis=0, tiled=True).T]
    ppermute x0 -> x33, waiting for transfers between devices: none -> 134 us  [the longest x6 82.1 us: along_z(): lax.ppermute(value, 'store', pairs(lambda z, y, c: ((z + k) % depth, y, c)))]
    dot_general x3 -> x0, matrix products: 44.6 us -> none  [the longest x1 20.6 us: per_device(): jnp.dot(columns, lax.all_gather(value_matrix, 'store', axis=0, tiled=True...]
    unnamed x1 -> x100, local copies, waits for them, and re-layouts: 1.88 us -> 45.4 us
    pallas_call x0 -> x4, Pallas kernels: none -> 42 us  [the longest x1 13.8 us: value_partials(): pl.pallas_call(functools.partial(part_kernel, pieces, 256), out_shape=(ou...]
    ppermute x0 -> x33, starting transfers between devices: none -> 36.5 us  [the longest x11 12.8 us: along_x(): return lax.ppermute(value, 'groups', [(g, g ^ 1) for g in range(groups)])]
    reduce_sum x4 -> x1, other arithmetic: 8.65 us -> 0.18 us  [per_device(): jnp.sum((document_tenant[0][:, None] == jnp.arange(adapters, dtype=jnp.in...]
  transfers between devices with their start and end apart: 3 -> 34, of which waited for: 3 -> 14; matrix products, arithmetic and copies ran while one was open for 10% -> 4% of each run, Pallas kernels for 0% -> 7%
where the time goes in v1:
time: 287 us; the launch traced here: 284 us
  waiting for transfers between devices  134 us (47%)
  local copies, waits for them, and re-layouts  54.7 us (19%)
  Pallas kernels  42 us (15%)
  starting transfers between devices  36.5 us (13%)
  between operations  13.6 us (5%)
    ppermute x6, waiting for transfers between devices, along_z(): lax.ppermute(value, 'store', pairs(lambda z, y, c: ((z + k) % depth, y, c)))  82.1 us
    unnamed x100, local copies, waits for them, and re-layouts  45.4 us
    ppermute x8, waiting for transfers between devices, along_y(): return lax.ppermute(value, 'store', pairs(lambda z, y, c: (z, 1 - y, c)))  35.3 us
    ppermute x11, waiting for transfers between devices, along_x(): return lax.ppermute(value, 'groups', [(g, g ^ 1) for g in range(groups)])  15.4 us
    pallas_call x1, Pallas kernels, value_partials(): pl.pallas_call(functools.partial(part_kernel, pieces, 256), out_shape=(ou...  13.8 us
    ppermute x11, starting transfers between devices, along_x(): return lax.ppermute(value, 'groups', [(g, g ^ 1) for g in range(groups)])  12.8 us
    pallas_call x1, Pallas kernels, last_values(): pl.pallas_call(functools.partial(last_kernel, pieces, 256, (0, 0)), out_s...  11.8 us
    pallas_call x1, Pallas kernels, norm_in_order(): pl.pallas_call(norm_kernel, out_shape=(half, half), grid_spec=pltpu.Prefe...  9.3 us
  transfers between devices with their start and end apart: 34, of which 14 were waited for; matrix products, arithmetic and copies ran while one was open for 4% of the time, Pallas kernels for 7%

profile of v1, /device:TPU:9, one launch (start us, length us, event | category | flops | bytes accessed | tf_op | source)
XLA Modules:
  0.0 283.5 jit_solution(13947065832901247731)
XLA Ops:
  7.8 1.3 collective-permute-start
  9.3 11.4 %collective-permute-done.refs_10_ = bf16[1024,256]{1,0:T(8,128)(2,1)S(1)} collective-permute-done((bf16[1024,256]{1,0:T(8,128)(2,1)S(1)}, bf16[1024,256]{1,0:T(8,128)(2,1)S(1)}, u32[]{:S(2)}, u32[]{:S(2)}) %collective-permute-start) | collective-permute-done | bytes 524320 | tf_op jit(solution)/shard_map/ppermute | solution.py:301
  20.7 4.6 %copy-done.2 = bf16[768,8192]{1,0:T(8,128)(2,1)S(1)} copy-done((bf16[768,8192]{1,0:T(8,128)(2,1)S(1)}, bf16[768,8192]{1,0:T(8,128)(2,1)}, u32[]{:S(2)}) %copy-start.2) | copy-done | bytes 12582936
  25.3 9.3 %shard_map.82 = (bf16[768,4096]{1,0:T(8,128)(2,1)S(1)}, bf16[768,4096]{1,0:T(8,128)(2,1)}) custom-call(s32[64]{0:T(128)S(1)} %stack.259.source_ref, bf16[768,8192]{1,0:T(8,128)(2,1)S(1)} %copy-done.2, bf16[1,8192]{1,0:T(2,128)(2,1)S(1)} %reshape.12.gain_ref), custom_call_target="tpu_custom_call" | custom-call | flops 37748736 | bytes 25165824 | tf_op jit(solution)/shard_map/pallas_call | solution.py:99
  34.6 2.7 copy-done
  37.3 1.5 collective-permute-start.1
  42.3 1.3 collective-permute-start.5
  43.8 8.6 %collective-permute-done.6.refs_4_ = bf16[1024,256]{1,0:T(8,128)(2,1)S(1)} collective-permute-done((bf16[1024,256]{1,0:T(8,128)(2,1)S(1)}, bf16[1024,256]{1,0:T(8,128)(2,1)S(1)}, u32[]{:S(2)}, u32[]{:S(2)}) %collective-permute-start.6) | collective-permute-done | bytes 524320 | tf_op jit(solution)/shard_map/ppermute | solution.py:298
  54.8 9.9 %collective-permute-done.2.refs_8_ = bf16[1024,256]{1,0:T(8,128)(2,1)S(1)} collective-permute-done((bf16[1024,256]{1,0:T(8,128)(2,1)S(1)}, bf16[1024,256]{1,0:T(8,128)(2,1)S(1)}, u32[]{:S(2)}, u32[]{:S(2)}) %collective-permute-start.2) | collective-permute-done | bytes 524320 | tf_op jit(solution)/shard_map/ppermute | solution.py:298
  67.0 5.5 %collective-permute-done.15.refs_12_ = bf16[1024,256]{1,0:T(8,128)(2,1)S(1)} collective-permute-done((bf16[1024,256]{1,0:T(8,128)(2,1)S(1)}, bf16[1024,256]{1,0:T(8,128)(2,1)S(1)}, u32[]{:S(2)}, u32[]{:S(2)}) %collective-permute-start.15) | collective-permute-done | bytes 524320 | tf_op jit(solution)/shard_map/ppermute | solution.py:301
  76.6 11.9 %collective-permute-done.7.refs_6_ = bf16[1024,256]{1,0:T(8,128)(2,1)S(1)} collective-permute-done((bf16[1024,256]{1,0:T(8,128)(2,1)S(1)}, bf16[1024,256]{1,0:T(8,128)(2,1)S(1)}, u32[]{:S(2)}, u32[]{:S(2)}) %collective-permute-start.7) | collective-permute-done | bytes 524320 | tf_op jit(solution)/shard_map/ppermute | solution.py:298
  88.5 1.5 collective-permute-start.3
  90.8 1.9 collective-permute-start.8
  96.8 12.6 %collective-permute-done.3.refs_4_ = bf16[384,1024]{1,0:T(8,128)(2,1)S(1)} collective-permute-done((bf16[384,1024]{1,0:T(8,128)(2,1)S(1)}, bf16[384,1024]{1,0:T(8,128)(2,1)S(1)}, u32[]{:S(2)}, u32[]{:S(2)}) %collective-permute-start.3) | collective-permute-done | bytes 786464 | tf_op jit(solution)/shard_map/ppermute | solution.py:298
  112.6 13.9 %collective-permute-done.8.refs_6_ = bf16[384,1024]{1,0:T(8,128)(2,1)S(1)} collective-permute-done((bf16[384,1024]{1,0:T(8,128)(2,1)S(1)}, bf16[384,1024]{1,0:T(8,128)(2,1)S(1)}, u32[]{:S(2)}, u32[]{:S(2)}) %collective-permute-start.8) | collective-permute-done | bytes 786464 | tf_op jit(solution)/shard_map/ppermute | solution.py:298
  126.5 1.5 collective-permute-start.17
  136.4 4.2 %collective-permute-done.11.refs_7_ = bf16[1024,256]{1,0:T(8,128)(2,1)S(1)} collective-permute-done((bf16[1024,256]{1,0:T(8,128)(2,1)S(1)}, bf16[1024,256]{1,0:T(8,128)(2,1)S(1)}, u32[]{:S(2)}, u32[]{:S(2)}) %collective-permute-start.11) | collective-permute-done | bytes 524320 | tf_op jit(solution)/shard_map/ppermute | solution.py:307
  140.6 1.9 collective-permute-start.4
  143.8 2.4 collective-permute-done.17.refs_10_
  147.2 4.8 %collective-permute-done.21.refs_15_ = bf16[1024,256]{1,0:T(8,128)(2,1)S(1)} collective-permute-done((bf16[1024,256]{1,0:T(8,128)(2,1)S(1)}, bf16[1024,256]{1,0:T(8,128)(2,1)S(1)}, u32[]{:S(2)}, u32[]{:S(2)}) %collective-permute-start.21) | collective-permute-done | bytes 524320 | tf_op jit(solution)/shard_map/ppermute | solution.py:307
  154.8 25.2 %collective-permute-done.4.refs_7_ = bf16[384,1024]{1,0:T(8,128)(2,1)} collective-permute-done((bf16[384,1024]{1,0:T(8,128)(2,1)S(1)}, bf16[384,1024]{1,0:T(8,128)(2,1)}, u32[]{:S(2)}, u32[]{:S(2)}) %collective-permute-start.4) | collective-permute-done | bytes 786464 | tf_op jit(solution)/shard_map/ppermute | solution.py:298
  187.6 13.8 %shard_map.83 = (f32[768,1024]{1,0:T(8,128)S(1)}, f32[768,1024]{1,0:T(8,128)}) custom-call(bf16[768,4096]{1,0:T(8,128)(2,1)} %copy-done, bf16[768,4096]{1,0:T(8,128)(2,1)} %collective-permute-done.1.refs_1_, bf16[384,1024]{1,0:T(8,128)(2,1)S(1)} %pad_maximum_fusion.refs_2_, bf16[128,1024]{1,0:T(8,128)(2,1)S(1)} %get-tuple-element.63.refs_3_, ...), custom_call_target="tpu_custom_call" | custom-call | flops 9663676416 | bytes 25165824 | tf_op jit(solution)/shard_map/pallas_call | solution.py:208
  201.4 1.7 copy-done.3
  203.0 2.5 collective-permute-start.23
  207.4 1.6 collective-permute-start.26
  209.1 15.9 %collective-permute-done.27.refs_9_ = bf16[384,1024]{1,0:T(8,128)(2,1)} collective-permute-done((bf16[384,1024]{1,0:T(8,128)(2,1)}, bf16[384,1024]{1,0:T(8,128)(2,1)}, u32[]{:S(2)}, u32[]{:S(2)}) %collective-permute-start.27) | collective-permute-done | bytes 786464 | tf_op jit(solution)/shard_map/ppermute | solution.py:301
  228.5 6.3 %collective-permute-done.28.refs_10_ = bf16[128,1024]{1,0:T(8,128)(2,1)} collective-permute-done((bf16[128,1024]{1,0:T(8,128)(2,1)S(1)}, bf16[128,1024]{1,0:T(8,128)(2,1)}, u32[]{:S(2)}, u32[]{:S(2)}) %collective-permute-start.28) | collective-permute-done | bytes 262176 | tf_op jit(solution)/shard_map/ppermute | solution.py:307
  235.6 2.9 %copy.12 = bf16[1024,1024]{0,1:T(8,128)(2,1)S(1)} copy(bf16[1024,1024]{1,0:T(8,128)(2,1)} %all-gather.2.cloned.1.call-done) | data formatting | bytes 4194304 | tf_op jit(solution)/shard_map/all_gather | solution.py:352
  238.5 2.8 copy-done.1
  255.9 7.2 %shard_map.84 = (f32[768,64]{1,0:T(8,128)S(1)}, f32[768,64]{1,0:T(8,128)S(1)}) custom-call(s32[2,4]{1,0:T(2,128)S(1)} %get-tuple-element.67.ends_ref, s32[2,4]{1,0:T(2,128)S(1)} %get-tuple-element.68.slots_ref, bf16[768,4096]{1,0:T(8,128)(2,1)S(1)} %copy-done.1, bf16[768,4096]{1,0:T(8,128)(2,1)} %collective-permute-done.1.refs_1_, ...), custom_call_target="tpu_custom_call" | custom-call | flops 3221225472 | bytes 20971520 | tf_op jit(solution)/shard_map/pallas_call | solution.py:163
  263.2 1.7 collective-permute-done.25.refs_5_
  264.9 11.8 %shard_map.85 = bf16[768,1024]{1,0:T(8,128)(2,1)} custom-call(s32[4]{0:T(128)S(1)} %select_reduce_fusion.slots_ref, s32[4]{0:T(128)S(1)} %bitcast.78, bf16[768,4096]{1,0:T(8,128)(2,1)} %copy-done, bf16[768,4096]{1,0:T(8,128)(2,1)} %get-tuple-element.35.refs_1_, f32[768,1024]{1,0:T(8,128)S(1)} %copy-done.4, f32[768,1024]{1,0:T(8,128)} %collective-permute-done.23.refs_3_, ...), custom_call_target="tpu_custom_call" | custom-call | flops 3221225472 | bytes 24641536 | tf_op jit(solution)/shard_map/pallas_call | solution.py:260
  (163 shorter events, 63.8 us)
Async XLA Ops:
  6.5 229.1 %all-gather.2.cloned.1.call-start = ((), (), s32[]{:S(2)}) async-start(), calls=%async_computation | async-start | bytes 2228224 | tf_op jit(solution)/shard_map/all_gather | solution.py:352
  7.8 12.9 %collective-permute-start = (bf16[1024,256]{1,0:T(8,128)(2,1)S(1)}, bf16[1024,256]{1,0:T(8,128)(2,1)S(1)}, u32[]{:S(2)}, u32[]{:S(2)}) collective-permute-start(bf16[1024,256]{1,0:T(8,128)(2,1)S(1)} %get-tuple-element.39.refs_2_), channel_id=1, source_target_pairs={{0,2},{1,3},{2,0},{3,1},{4,6},{5,7},{6,4},{7,5},{8,10},{9,11},{10,... | collective-permute-start | bytes 1572872 | tf_op jit(solution)/shard_map/ppermute | solution.py:301
  37.3 143.6 %collective-permute-start.1 = (bf16[768,4096]{1,0:T(8,128)(2,1)}, bf16[768,4096]{1,0:T(8,128)(2,1)}, u32[]{:S(2)}, u32[]{:S(2)}) collective-permute-start(bf16[768,4096]{1,0:T(8,128)(2,1)} %get-tuple-element.35.refs_1_), channel_id=1, source_target_pairs={{0,1},{1,0},{2,3},{3,2},{4,5},{5,4},{6,7},{7,6},{8,9},{9,8},{10,11... | collective-permute-start | bytes 18874376 | tf_op jit(solution)/shard_map/ppermute | solution.py:304
  38.8 13.6 %collective-permute-start.6 = (bf16[1024,256]{1,0:T(8,128)(2,1)S(1)}, bf16[1024,256]{1,0:T(8,128)(2,1)S(1)}, u32[]{:S(2)}, u32[]{:S(2)}) collective-permute-start(bf16[1024,256]{1,0:T(8,128)(2,1)S(1)} %get-tuple-element.39.refs_2_), channel_id=1, source_target_pairs={{0,4},{1,5},{2,6},{3,7},{4,8},{5,9},{6,10},{7,11},{8,12},{9,13},{1... | collective-permute-start | bytes 1572872 | tf_op jit(solution)/shard_map/ppermute | solution.py:298
  42.3 23.4 %collective-permute-start.5 = (bf16[384,1024]{1,0:T(8,128)(2,1)S(1)}, bf16[384,1024]{1,0:T(8,128)(2,1)S(1)}, u32[]{:S(2)}, u32[]{:S(2)}) collective-permute-start(bf16[384,1024]{1,0:T(8,128)(2,1)S(1)} %pad_maximum_fusion.refs_2_), channel_id=1, source_target_pairs={{0,2},{1,3},{2,0},{3,1},{4,6},{5,7},{6,4},{7,5},{8,10},{9,11},{10,... | collective-permute-start | bytes 2359304 | tf_op jit(solution)/shard_map/ppermute | solution.py:301
  43.6 21.1 %collective-permute-start.2 = (bf16[1024,256]{1,0:T(8,128)(2,1)S(1)}, bf16[1024,256]{1,0:T(8,128)(2,1)S(1)}, u32[]{:S(2)}, u32[]{:S(2)}) collective-permute-start(bf16[1024,256]{1,0:T(8,128)(2,1)S(1)} %get-tuple-element.39.refs_2_), channel_id=1, source_target_pairs={{0,12},{1,13},{2,14},{3,15},{4,0},{5,1},{6,2},{7,3},{8,4},{9,5},{1... | collective-permute-start | bytes 1572872 | tf_op jit(solution)/shard_map/ppermute | solution.py:298
  52.4 20.1 %collective-permute-start.15 = (bf16[1024,256]{1,0:T(8,128)(2,1)S(1)}, bf16[1024,256]{1,0:T(8,128)(2,1)S(1)}, u32[]{:S(2)}, u32[]{:S(2)}) collective-permute-start(bf16[1024,256]{1,0:T(8,128)(2,1)S(1)} %collective-permute-done.6.refs_4_), channel_id=1, source_target_pairs={{0,2},{1,3},{2,0},{3,1},{4,6},{5,7},{6,4},{7,5},{8,10},{9,11},{10,... | collective-permute-start | bytes 1572872 | tf_op jit(solution)/shard_map/ppermute | solution.py:301
  53.6 20.1 %collective-permute-start.18 = (bf16[1024,256]{1,0:T(8,128)(2,1)S(1)}, bf16[1024,256]{1,0:T(8,128)(2,1)S(1)}, u32[]{:S(2)}, u32[]{:S(2)}) collective-permute-start(bf16[1024,256]{1,0:T(8,128)(2,1)S(1)} %collective-permute-done.refs_10_), channel_id=1, source_target_pairs={{0,16},{16,0},{1,17},{17,1},{2,18},{18,2},{3,19},{19,3},{4,20},{20... | collective-permute-start | bytes 1572872 | tf_op jit(solution)/shard_map/ppermute | solution.py:307
  64.8 23.7 %collective-permute-start.7 = (bf16[1024,256]{1,0:T(8,128)(2,1)S(1)}, bf16[1024,256]{1,0:T(8,128)(2,1)S(1)}, u32[]{:S(2)}, u32[]{:S(2)}) collective-permute-start(bf16[1024,256]{1,0:T(8,128)(2,1)S(1)} %get-tuple-element.39.refs_2_), channel_id=1, source_target_pairs={{0,8},{1,9},{2,10},{3,11},{4,12},{5,13},{6,14},{7,15},{8,0},{9,1},... | collective-permute-start | bytes 1572872 | tf_op jit(solution)/shard_map/ppermute | solution.py:298
  65.7 24.3 %collective-permute-start.9 = (bf16[1024,256]{1,0:T(8,128)(2,1)S(1)}, bf16[1024,256]{1,0:T(8,128)(2,1)S(1)}, u32[]{:S(2)}, u32[]{:S(2)}) collective-permute-start(bf16[1024,256]{1,0:T(8,128)(2,1)S(1)} %collective-permute-done.6.refs_4_), channel_id=1, source_target_pairs={{0,16},{16,0},{1,17},{17,1},{2,18},{18,2},{3,19},{19,3},{4,20},{20... | collective-permute-start | bytes 1572872 | tf_op jit(solution)/shard_map/ppermute | solution.py:307
  72.5 20.2 %collective-permute-start.13 = (bf16[1024,256]{1,0:T(8,128)(2,1)S(1)}, bf16[1024,256]{1,0:T(8,128)(2,1)S(1)}, u32[]{:S(2)}, u32[]{:S(2)}) collective-permute-start(bf16[1024,256]{1,0:T(8,128)(2,1)S(1)} %collective-permute-done.2.refs_8_), channel_id=1, source_target_pairs={{0,2},{1,3},{2,0},{3,1},{4,6},{5,7},{6,4},{7,5},{8,10},{9,11},{10,... | collective-permute-start | bytes 1572872 | tf_op jit(solution)/shard_map/ppermute | solution.py:301
  74.6 19.4 %collective-permute-start.19 = (bf16[1024,256]{1,0:T(8,128)(2,1)S(1)}, bf16[1024,256]{1,0:T(8,128)(2,1)S(1)}, u32[]{:S(2)}, u32[]{:S(2)}) collective-permute-start(bf16[1024,256]{1,0:T(8,128)(2,1)S(1)} %collective-permute-done.15.refs_12_), channel_id=1, source_target_pairs={{0,16},{16,0},{1,17},{17,1},{2,18},{18,2},{3,19},{19,3},{4,20},{20... | collective-permute-start | bytes 1572872 | tf_op jit(solution)/shard_map/ppermute | solution.py:307
  88.5 20.9 %collective-permute-start.3 = (bf16[384,1024]{1,0:T(8,128)(2,1)S(1)}, bf16[384,1024]{1,0:T(8,128)(2,1)S(1)}, u32[]{:S(2)}, u32[]{:S(2)}) collective-permute-start(bf16[384,1024]{1,0:T(8,128)(2,1)S(1)} %pad_maximum_fusion.refs_2_), channel_id=1, source_target_pairs={{0,4},{1,5},{2,6},{3,7},{4,8},{5,9},{6,10},{7,11},{8,12},{9,13},{1... | collective-permute-start | bytes 2359304 | tf_op jit(solution)/shard_map/ppermute | solution.py:298
  90.8 35.7 %collective-permute-start.8 = (bf16[384,1024]{1,0:T(8,128)(2,1)S(1)}, bf16[384,1024]{1,0:T(8,128)(2,1)S(1)}, u32[]{:S(2)}, u32[]{:S(2)}) collective-permute-start(bf16[384,1024]{1,0:T(8,128)(2,1)S(1)} %pad_maximum_fusion.refs_2_), channel_id=1, source_target_pairs={{0,12},{1,13},{2,14},{3,15},{4,0},{5,1},{6,2},{7,3},{8,4},{9,5},{1... | collective-permute-start | bytes 2359304 | tf_op jit(solution)/shard_map/ppermute | solution.py:298
  92.7 18.7 %collective-permute-start.16 = (bf16[1024,256]{1,0:T(8,128)(2,1)S(1)}, bf16[1024,256]{1,0:T(8,128)(2,1)S(1)}, u32[]{:S(2)}, u32[]{:S(2)}) collective-permute-start(bf16[1024,256]{1,0:T(8,128)(2,1)S(1)} %collective-permute-done.7.refs_6_), channel_id=1, source_target_pairs={{0,2},{1,3},{2,0},{3,1},{4,6},{5,7},{6,4},{7,5},{8,10},{9,11},{10,... | collective-permute-start | bytes 1572872 | tf_op jit(solution)/shard_map/ppermute | solution.py:301
  94.8 33.2 %collective-permute-start.10 = (bf16[1024,256]{1,0:T(8,128)(2,1)S(1)}, bf16[1024,256]{1,0:T(8,128)(2,1)S(1)}, u32[]{:S(2)}, u32[]{:S(2)}) collective-permute-start(bf16[1024,256]{1,0:T(8,128)(2,1)S(1)} %collective-permute-done.2.refs_8_), channel_id=1, source_target_pairs={{0,16},{16,0},{1,17},{17,1},{2,18},{18,2},{3,19},{19,3},{4,20},{20... | collective-permute-start | bytes 1572872 | tf_op jit(solution)/shard_map/ppermute | solution.py:307
  109.4 21.5 %collective-permute-start.20 = (bf16[1024,256]{1,0:T(8,128)(2,1)S(1)}, bf16[1024,256]{1,0:T(8,128)(2,1)S(1)}, u32[]{:S(2)}, u32[]{:S(2)}) collective-permute-start(bf16[1024,256]{1,0:T(8,128)(2,1)S(1)} %collective-permute-done.13.refs_16_), channel_id=1, source_target_pairs={{0,16},{16,0},{1,17},{17,1},{2,18},{18,2},{3,19},{19,3},{4,20},{20... | collective-permute-start | bytes 1572872 | tf_op jit(solution)/shard_map/ppermute | solution.py:307
  111.4 31.1 %collective-permute-start.14 = (bf16[384,1024]{1,0:T(8,128)(2,1)S(1)}, bf16[384,1024]{1,0:T(8,128)(2,1)S(1)}, u32[]{:S(2)}, u32[]{:S(2)}) collective-permute-start(bf16[384,1024]{1,0:T(8,128)(2,1)S(1)} %collective-permute-done.3.refs_4_), channel_id=1, source_target_pairs={{0,2},{1,3},{2,0},{3,1},{4,6},{5,7},{6,4},{7,5},{8,10},{9,11},{10,... | collective-permute-start | bytes 2359304 | tf_op jit(solution)/shard_map/ppermute | solution.py:301
  126.5 19.7 %collective-permute-start.17 = (bf16[384,1024]{1,0:T(8,128)(2,1)S(1)}, bf16[384,1024]{1,0:T(8,128)(2,1)S(1)}, u32[]{:S(2)}, u32[]{:S(2)}) collective-permute-start(bf16[384,1024]{1,0:T(8,128)(2,1)S(1)} %collective-permute-done.8.refs_6_), channel_id=1, source_target_pairs={{0,2},{1,3},{2,0},{3,1},{4,6},{5,7},{6,4},{7,5},{8,10},{9,11},{10,... | collective-permute-start | bytes 2359304 | tf_op jit(solution)/shard_map/ppermute | solution.py:301
  128.8 11.8 %collective-permute-start.11 = (bf16[1024,256]{1,0:T(8,128)(2,1)S(1)}, bf16[1024,256]{1,0:T(8,128)(2,1)S(1)}, u32[]{:S(2)}, u32[]{:S(2)}) collective-permute-start(bf16[1024,256]{1,0:T(8,128)(2,1)S(1)} %collective-permute-done.7.refs_6_), channel_id=1, source_target_pairs={{0,16},{16,0},{1,17},{17,1},{2,18},{18,2},{3,19},{19,3},{4,20},{20... | collective-permute-start | bytes 1572872 | tf_op jit(solution)/shard_map/ppermute | solution.py:307
  131.7 20.3 %collective-permute-start.21 = (bf16[1024,256]{1,0:T(8,128)(2,1)S(1)}, bf16[1024,256]{1,0:T(8,128)(2,1)S(1)}, u32[]{:S(2)}, u32[]{:S(2)}) collective-permute-start(bf16[1024,256]{1,0:T(8,128)(2,1)S(1)} %collective-permute-done.16.refs_14_), channel_id=1, source_target_pairs={{0,16},{16,0},{1,17},{17,1},{2,18},{18,2},{3,19},{19,3},{4,20},{20... | collective-permute-start | bytes 1572872 | tf_op jit(solution)/shard_map/ppermute | solution.py:307
  140.6 39.4 %collective-permute-start.4 = (bf16[384,1024]{1,0:T(8,128)(2,1)S(1)}, bf16[384,1024]{1,0:T(8,128)(2,1)}, u32[]{:S(2)}, u32[]{:S(2)}) collective-permute-start(bf16[384,1024]{1,0:T(8,128)(2,1)S(1)} %pad_maximum_fusion.refs_2_), channel_id=1, source_target_pairs={{0,8},{1,9},{2,10},{3,11},{4,12},{5,13},{6,14},{7,15},{8,0},{9,1},... | collective-permute-start | bytes 2359304 | tf_op jit(solution)/shard_map/ppermute | solution.py:298
  142.5 37.5 %collective-permute-start.12 = (bf16[384,1024]{1,0:T(8,128)(2,1)}, bf16[384,1024]{1,0:T(8,128)(2,1)}, u32[]{:S(2)}, u32[]{:S(2)}) collective-permute-start(bf16[384,1024]{1,0:T(8,128)(2,1)} %pad_maximum_fusion.1), channel_id=1, source_target_pairs={{0,16},{16,0},{1,17},{17,1},{2,18},{18,2},{3,19},{19,3},{4,20},{20... | collective-permute-start | bytes 2359304 | tf_op jit(solution)/shard_map/ppermute | solution.py:307
  152.8 27.3 %collective-permute-start.22 = (bf16[256,1024]{1,0:T(8,128)(2,1)}, bf16[256,1024]{1,0:T(8,128)(2,1)S(1)}, u32[]{:S(2)}, u32[]{:S(2)}) collective-permute-start(bf16[256,1024]{1,0:T(8,128)(2,1)} %pad_maximum_fusion.2), channel_id=1, source_target_pairs={{0,16},{16,0},{1,17},{17,1},{2,18},{18,2},{3,19},{19,3},{4,20},{20... | collective-permute-start | bytes 1572872 | tf_op jit(solution)/shard_map/ppermute | solution.py:307
  203.0 61.9 %collective-permute-start.23 = (f32[768,1024]{1,0:T(8,128)}, f32[768,1024]{1,0:T(8,128)}, u32[]{:S(2)}, u32[]{:S(2)}) collective-permute-start(f32[768,1024]{1,0:T(8,128)} %get-tuple-element.54), channel_id=1, source_target_pairs={{0,1},{1,0},{2,3},{3,2},{4,5},{5,4},{6,7},{7,6},{8,9},{9,8},{10,11... | collective-permute-start | bytes 9437192 | tf_op jit(solution)/shard_map/ppermute | solution.py:304
  205.5 19.5 %collective-permute-start.27 = (bf16[384,1024]{1,0:T(8,128)(2,1)}, bf16[384,1024]{1,0:T(8,128)(2,1)}, u32[]{:S(2)}, u32[]{:S(2)}) collective-permute-start(bf16[384,1024]{1,0:T(8,128)(2,1)} %collective-permute-done.4.refs_7_), channel_id=1, source_target_pairs={{0,2},{1,3},{2,0},{3,1},{4,6},{5,7},{6,4},{7,5},{8,10},{9,11},{10,... | collective-permute-start | bytes 2359304 | tf_op jit(solution)/shard_map/ppermute | solution.py:301
  205.5 57.6 %collective-permute-start.29 = (bf16[384,1024]{1,0:T(8,128)(2,1)}, bf16[384,1024]{1,0:T(8,128)(2,1)}, u32[]{:S(2)}, u32[]{:S(2)}) collective-permute-start(bf16[384,1024]{1,0:T(8,128)(2,1)} %collective-permute-done.4.refs_7_), channel_id=1, source_target_pairs={{0,1},{1,0},{2,3},{3,2},{4,5},{5,4},{6,7},{7,6},{8,9},{9,8},{10,11... | collective-permute-start | bytes 2359304 | tf_op jit(solution)/shard_map/ppermute | solution.py:304
  206.1 20.7 %collective-permute-start.24 = (s32[2,4]{1,0:T(2,128)S(1)}, s32[2,4]{1,0:T(2,128)S(1)}, u32[]{:S(2)}, u32[]{:S(2)}) collective-permute-start(s32[2,4]{1,0:T(2,128)S(1)} %pad_add_fusion), channel_id=1, source_target_pairs={{0,1},{1,0},{2,3},{3,2},{4,5},{5,4},{6,7},{7,6},{8,9},{9,8},{10,11... | collective-permute-start | bytes 104 | tf_op jit(solution)/shard_map/ppermute | solution.py:304
  207.4 20.6 %collective-permute-start.26 = (bf16[128,1024]{1,0:T(8,128)(2,1)S(1)}, bf16[128,1024]{1,0:T(8,128)(2,1)S(1)}, u32[]{:S(2)}, u32[]{:S(2)}) collective-permute-start(bf16[128,1024]{1,0:T(8,128)(2,1)S(1)} %slice.41), channel_id=1, source_target_pairs={{0,16},{16,0},{1,17},{17,1},{2,18},{18,2},{3,19},{19,3},{4,20},{20... | collective-permute-start | bytes 786440 | tf_op jit(solution)/shard_map/ppermute | solution.py:307
  225.9 37.2 %collective-permute-start.31 = (bf16[384,1024]{1,0:T(8,128)(2,1)}, bf16[384,1024]{1,0:T(8,128)(2,1)}, u32[]{:S(2)}, u32[]{:S(2)}) collective-permute-start(bf16[384,1024]{1,0:T(8,128)(2,1)} %collective-permute-done.27.refs_9_), channel_id=1, source_target_pairs={{0,1},{1,0},{2,3},{3,2},{4,5},{5,4},{6,7},{7,6},{8,9},{9,8},{10,11... | collective-permute-start | bytes 2359304 | tf_op jit(solution)/shard_map/ppermute | solution.py:304
  228.0 35.1 %collective-permute-start.30 = (bf16[128,1024]{1,0:T(8,128)(2,1)S(1)}, bf16[128,1024]{1,0:T(8,128)(2,1)}, u32[]{:S(2)}, u32[]{:S(2)}) collective-permute-start(bf16[128,1024]{1,0:T(8,128)(2,1)S(1)} %collective-permute-done.26.refs_8_), channel_id=1, source_target_pairs={{0,1},{1,0},{2,3},{3,2},{4,5},{5,4},{6,7},{7,6},{8,9},{9,8},{10,11... | collective-permute-start | bytes 786440 | tf_op jit(solution)/shard_map/ppermute | solution.py:304
  234.8 28.4 %collective-permute-start.32 = (bf16[128,1024]{1,0:T(8,128)(2,1)}, bf16[128,1024]{1,0:T(8,128)(2,1)}, u32[]{:S(2)}, u32[]{:S(2)}) collective-permute-start(bf16[128,1024]{1,0:T(8,128)(2,1)} %collective-permute-done.28.refs_10_), channel_id=1, source_target_pairs={{0,1},{1,0},{2,3},{3,2},{4,5},{5,4},{6,7},{7,6},{8,9},{9,8},{10,11... | collective-permute-start | bytes 786440 | tf_op jit(solution)/shard_map/ppermute | solution.py:304
  (52 other events, 293.8 us)
Sparse Core Ops, SparseCore 0:
  154.9 47.7 all-gather.1

commit v2 on v0

v2 whole, which is shorter than its diff:
```python
import functools

import jax
import jax.numpy as jnp
from jax import lax
from jax.experimental import pallas as pl
from jax.experimental.pallas import tpu as pltpu
from jax.sharding import PartitionSpec as P

adapter_scale = 2.0
cores, rows_y, lane = 2, 2, 128
nt = (((1,), (1,)), ((), ()))
vmem = 58 << 20


def token_slots(lengths, tenants, tenant_adapter_slot, row_count):
    ends = jnp.cumsum(lengths)
    position = jnp.arange(row_count, dtype=jnp.int32)
    doc_index = jnp.sum((position[:, None] >= ends[None, :]).astype(jnp.int32), axis=1)
    doc_pick = (
        doc_index[:, None] == jnp.arange(lengths.shape[0], dtype=jnp.int32)[None, :]
    ).astype(jnp.int32)
    tenant = jnp.sum(doc_pick * tenants[None, :], axis=1)
    tenant_pick = (
        tenant[:, None] == jnp.arange(tenant_adapter_slot.shape[0], dtype=jnp.int32)[None, :]
    ).astype(jnp.int32)
    return jnp.sum(tenant_pick * tenant_adapter_slot[None, :], axis=1)


def pick_rank(rank_total_rows, slots, count_of_adapters, rank_span_width):
    select = (slots[:, None] == jnp.arange(count_of_adapters, dtype=jnp.int32)[None, :]).astype(
        jnp.float32
    )
    shaped = rank_total_rows.reshape(slots.shape[0], count_of_adapters, rank_span_width)
    return jnp.sum(shaped * select[:, :, None], axis=1)


def plain(
    tokens,
    input_norm_gain,
    value_matrix,
    adapter_down_factors,
    adapter_up_factors,
    document_lengths,
    document_tenant,
    tenant_adapter_slot,
):
    row_count = tokens.shape[0]
    count_of_adapters = adapter_down_factors.shape[1]
    rank_span_width = adapter_down_factors.shape[2]
    flat_width = count_of_adapters * rank_span_width
    wide = tokens.astype(jnp.float32)
    meansq = jnp.mean(wide * wide, axis=1, keepdims=True)
    normed = (wide * lax.rsqrt(meansq + 1e-05) * input_norm_gain.astype(jnp.float32)).astype(
        jnp.bfloat16
    )
    slots = token_slots(document_lengths[0], document_tenant[0], tenant_adapter_slot, row_count)
    base_output = jnp.dot(
        normed,
        lax.all_gather(value_matrix, "store", axis=0, tiled=True),
        preferred_element_type=jnp.float32,
    )
    down = lax.all_gather(adapter_down_factors, "store", axis=0, tiled=True)
    rank_total_rows = jnp.dot(
        normed, down.reshape(down.shape[0], flat_width), preferred_element_type=jnp.float32
    )
    mid = pick_rank(rank_total_rows, slots, count_of_adapters, rank_span_width)
    mid = mid.astype(jnp.bfloat16)
    select = (slots[:, None] == jnp.arange(count_of_adapters, dtype=jnp.int32)[None, :]).astype(
        jnp.bfloat16
    )
    expanded_rows = (mid[:, None, :] * select[:, :, None]).reshape(row_count, flat_width)
    up = lax.all_gather(adapter_up_factors, "store", axis=2, tiled=True)
    adapter_update = jnp.dot(
        expanded_rows, up.reshape(flat_width, up.shape[2]), preferred_element_type=jnp.float32
    )
    return (base_output + adapter_scale * adapter_update).astype(jnp.bfloat16)


def norm_kernel(source_ref, tokens_ref, gain_ref, *out_refs):
    width = tokens_ref.shape[1]
    total = jnp.zeros((tokens_ref.shape[0], lane), jnp.float32)
    for i in range(width // lane):
        part = tokens_ref[:, i * lane : (i + 1) * lane].astype(jnp.float32)
        total += part * part
    scale = lax.rsqrt(jnp.sum(total, axis=1, keepdims=True) / width + 1e-05)
    first = 0
    for out_ref in out_refs:
        for i in range(out_ref.shape[1] // lane):
            start = pl.multiple_of(source_ref[first + i], lane)
            part = tokens_ref[:, pl.ds(start, lane)].astype(jnp.float32)
            gain = gain_ref[:, pl.ds(start, lane)].astype(jnp.float32)
            out_ref[:, i * lane : (i + 1) * lane] = (part * scale * gain).astype(jnp.bfloat16)
        first += out_ref.shape[1] // lane


def norm_in_order(tokens, gain, source, widths):
    rows, width = tokens.shape
    block = 64
    return pl.pallas_call(
        norm_kernel,
        out_shape=[jax.ShapeDtypeStruct((rows, w), jnp.bfloat16) for w in widths],
        grid_spec=pltpu.PrefetchScalarGridSpec(
            num_scalar_prefetch=1,
            grid=(rows // block,),
            in_specs=[
                pl.BlockSpec((block, width), lambda i, *_: (i, 0)),
                pl.BlockSpec((1, width), lambda i, *_: (0, 0)),
            ],
            out_specs=[pl.BlockSpec((block, w), lambda i, *_: (i, 0)) for w in widths],
        ),
        compiler_params=pltpu.CompilerParams(vmem_limit_bytes=vmem),
        cost_estimate=pl.CostEstimate(
            flops=6 * rows * width, bytes_accessed=4 * rows * width, transcendentals=rows
        ),
    )(source, tokens, gain.reshape(1, width))


def far_memory():
    return pl.BlockSpec(memory_space=pltpu.HBM)


def held(arrays):
    return [pltpu.VMEM(a.shape, a.dtype) for a in arrays] + [
        pltpu.SemaphoreType.DMA((len(arrays),))
    ]


def load(array_refs, held_refs):
    *held_refs, sem = held_refs
    copies = [
        pltpu.make_async_copy(a, h, sem.at[i])
        for i, (a, h) in enumerate(zip(array_refs, held_refs))
    ]

    @pl.when(pl.program_id(0) == 0)
    def _():
        for copy in copies:
            copy.start()
        for copy in copies:
            copy.wait()

    return held_refs


def tiled(array, tile, block=None):
    if block is None:
        return pl.BlockSpec((tile,) + array.shape[1:], lambda i, *_: (i, 0))
    at, width = block
    return pl.BlockSpec((tile, width), lambda i, *_: (i, at))


def pick_kernel(rank, slots_ref, *refs):
    piece_refs, out_ref, sem = refs[:-2], refs[-2], refs[-1]
    count = slots_ref.shape[0] * slots_ref.shape[1]
    docs = slots_ref.shape[1]
    copies = []
    for j, piece in enumerate(piece_refs):
        for i in range(count):
            start = pl.multiple_of(slots_ref[i // docs, i % docs] * rank, rank)
            copies.append(
                pltpu.make_async_copy(
                    piece.at[pl.ds(start, rank), :],
                    out_ref.at[pl.ds((j * count + i) * rank, rank), :],
                    sem.at[j * count + i],
                )
            )
    for copy in copies:
        copy.start()
    for copy in copies:
        copy.wait()


def pick_adapters(pieces, slots, rank):
    count = slots.shape[0] * slots.shape[1] * len(pieces)
    columns = pieces[0].shape[1]
    return pl.pallas_call(
        functools.partial(pick_kernel, rank),
        out_shape=jax.ShapeDtypeStruct((count * rank, columns), jnp.bfloat16),
        grid_spec=pltpu.PrefetchScalarGridSpec(
            num_scalar_prefetch=1,
            in_specs=[far_memory()] * len(pieces),
            out_specs=far_memory(),
            scratch_shapes=[pltpu.SemaphoreType.DMA((count,))],
        ),
        compiler_params=pltpu.CompilerParams(vmem_limit_bytes=vmem),
        cost_estimate=pl.CostEstimate(
            flops=0, bytes_accessed=4 * count * rank * columns, transcendentals=0
        ),
    )(slots, *pieces)


def slab(rank, slot, have, miss, at):
    start = pl.multiple_of(slot * rank, rank)
    miss_ref, first = miss
    at = first + at * rank
    return jnp.concatenate([have[pl.ds(start, rank), :], miss_ref[at : at + rank, :]], 1)


def by_document(acc, ends, tile, rank):
    row = pl.program_id(0) * tile + lax.broadcasted_iota(jnp.int32, (tile, rank), 0)
    mid = jnp.zeros((tile, rank), jnp.float32)
    low = 0
    for doc, end in enumerate(ends):
        mid = jnp.where((row >= low) & (row < end), acc[:, doc * rank : (doc + 1) * rank], mid)
        low = end
    return mid


def mid_kernel(rank, plan, blocks, arrays, ends_ref, slots_ref, *refs):
    block_refs, array_refs = refs[:blocks], refs[blocks : blocks + arrays]
    out_refs = refs[blocks + arrays : blocks + arrays + 2]
    refs = list(block_refs) + load(array_refs, refs[blocks + arrays + 2 :])
    docs = slots_ref.shape[1]
    tile = out_refs[0].shape[0]
    for side in range(2):
        acc = None
        for block, column, have, rest, row in plan[side]:
            rhs = jnp.concatenate(
                [
                    slab(rank, slots_ref[side, d], refs[have], (refs[rest], row), side * docs + d)
                    for d in range(docs)
                ],
                0,
            )
            term = lax.dot_general(
                refs[block][:, column : column + rhs.shape[1]],
                rhs,
                nt,
                preferred_element_type=jnp.float32,
            )
            acc = term if acc is None else acc + term
        ends = [ends_ref[side, d] for d in range(docs)]
        out_refs[side][...] = by_document(acc, ends, tile, rank)


def mid_partials(blocks, arrays, plan, ends, slots, rank):
    rows = blocks[0].shape[0]
    tile = 256 if rows % 256 == 0 else rows
    out = jax.ShapeDtypeStruct((rows, rank), jnp.float32)
    return pl.pallas_call(
        functools.partial(mid_kernel, rank, plan, len(blocks), len(arrays)),
        out_shape=(out, out),
        grid_spec=pltpu.PrefetchScalarGridSpec(
            num_scalar_prefetch=2,
            grid=(rows // tile,),
            in_specs=[tiled(b, tile) for b in blocks] + [far_memory()] * len(arrays),
            out_specs=[pl.BlockSpec((tile, rank), lambda i, *_: (i, 0))] * 2,
            scratch_shapes=held(arrays),
        ),
        compiler_params=pltpu.CompilerParams(vmem_limit_bytes=vmem),
        cost_estimate=pl.CostEstimate(
            flops=2 * sum(b.size for b in blocks) * slots.shape[1] * rank,
            bytes_accessed=2 * sum(a.size for a in (*blocks, *arrays)),
            transcendentals=0,
        ),
    )(ends, slots, *blocks, *arrays)


def value_kernel(plan, columns, blocks, arrays, has_sum, *refs):
    block_refs, sum_refs = refs[:blocks], refs[blocks : blocks + has_sum]
    refs = refs[blocks + has_sum :]
    array_refs, out_ref = refs[:arrays], refs[arrays]
    refs = list(block_refs) + load(array_refs, refs[arrays + 1 :])
    for n in range(0, out_ref.shape[1], columns):
        cols = slice(n, n + columns)
        acc = sum_refs[0][:, cols] if has_sum else None
        for block, at, parts in plan:
            rhs = jnp.concatenate([refs[i][a:b, cols] for i, a, b in parts], 0)
            term = jnp.dot(
                refs[block][:, at : at + rhs.shape[0]], rhs, preferred_element_type=jnp.float32
            )
            acc = term if acc is None else acc + term
        out_ref[:, cols] = acc


def value_sums(blocks, arrays, plan, width, start=None):
    rows = blocks[0].shape[0]
    tile = 256 if rows % 256 == 0 else rows
    out = jax.ShapeDtypeStruct((rows, width), jnp.float32)
    extra = [] if start is None else [start]
    size = sum(b.size for b in blocks)
    return pl.pallas_call(
        functools.partial(value_kernel, plan, 256, len(blocks), len(arrays), len(extra)),
        out_shape=out,
        grid=(rows // tile,),
        in_specs=[tiled(b, tile) for b in (*blocks, *extra)] + [far_memory()] * len(arrays),
        out_specs=tiled(out, tile),
        scratch_shapes=held(arrays),
        compiler_params=pltpu.CompilerParams(vmem_limit_bytes=vmem),
        cost_estimate=pl.CostEstimate(
            flops=2 * size * width,
            bytes_accessed=2 * size + 4 * out.size + sum(2 * a.size for a in arrays),
            transcendentals=0,
        ),
    )(*blocks, *extra, *arrays)


def last_kernel(rank, plan, blocks, arrays, slots_ref, ends_ref, *refs):
    sum_ref, mid_refs, refs = refs[0], refs[1:3], refs[3:]
    block_refs, array_refs, out_ref = refs[:blocks], refs[blocks:-arrays - 2], refs[-arrays - 2]
    *refs, up_ref = load(array_refs, refs[-arrays - 1 :])
    refs = list(block_refs) + refs
    docs = slots_ref.shape[0]
    tile = out_ref.shape[0]
    acc = None
    for block, have, rest, row, first in plan:
        rhs = jnp.concatenate(
            [
                slab(rank, slots_ref[d], refs[have], (refs[rest], row), first + d)
                for d in range(docs)
            ],
            0,
        )
        term = lax.dot_general(refs[block][...], rhs, nt, preferred_element_type=jnp.float32)
        acc = term if acc is None else acc + term
    ends = [ends_ref[d] for d in range(docs)]
    mid = by_document(acc, ends, tile, rank) + mid_refs[0][...] + mid_refs[1][...]
    row = pl.program_id(0) * tile + lax.broadcasted_iota(jnp.int32, (tile, rank), 0)
    spread, low = [], 0
    for end in ends:
        spread.append(jnp.where((row >= low) & (row < end), mid, 0.0).astype(jnp.bfloat16))
        low = end
    spread = jnp.concatenate(spread, 1)
    columns = 256
    for n in range(0, out_ref.shape[1], columns):
        cols = slice(n, n + columns)
        up = [
            up_ref[pl.ds(pl.multiple_of(slots_ref[d] * rank, rank), rank), cols]
            for d in range(docs)
        ]
        delta = jnp.dot(spread, jnp.concatenate(up, 0), preferred_element_type=jnp.float32)
        out_ref[:, cols] = (sum_ref[:, cols] + adapter_scale * delta).astype(out_ref.dtype)


def last_values(base, mids, up, blocks, arrays, plan, slots, ends):
    rows, width = base.shape
    rank = mids[0].shape[1]
    tile = 256 if rows % 256 == 0 else rows
    return pl.pallas_call(
        functools.partial(last_kernel, rank, plan, len(blocks), len(arrays) + 1),
        out_shape=jax.ShapeDtypeStruct((rows, width), jnp.bfloat16),
        grid_spec=pltpu.PrefetchScalarGridSpec(
            num_scalar_prefetch=2,
            grid=(rows // tile,),
            in_specs=[tiled(a, tile) for a in (base, *mids)]
            + [tiled(b, tile, (at, w)) for b, at, w in blocks]
            + [far_memory()] * (len(arrays) + 1),
            out_specs=pl.BlockSpec((tile, width), lambda i, *_: (i, 0)),
            scratch_shapes=held([*arrays, up]),
        ),
        compiler_params=pltpu.CompilerParams(vmem_limit_bytes=vmem),
        cost_estimate=pl.CostEstimate(
            flops=2 * rows * width * 256,
            bytes_accessed=8 * rows * width + sum(2 * a.size for a in arrays),
            transcendentals=0,
        ),
    )(slots, ends, base, *mids, *[b for b, _, _ in blocks], *arrays, up)


def after(value, *earlier):
    return lax.optimization_barrier((value, *earlier))[0]


def make(groups, store):
    depth = store // (rows_y * cores)

    def index(z, y, c):
        return (z * rows_y + y) * cores + c

    def pairs(move):
        return [
            (index(z, y, c), index(*move(z, y, c)))
            for z in range(depth)
            for y in range(rows_y)
            for c in range(cores)
        ]

    def along_z(value, k):
        return lax.ppermute(value, "store", pairs(lambda z, y, c: ((z + k) % depth, y, c)))

    def along_y(value):
        return lax.ppermute(value, "store", pairs(lambda z, y, c: (z, 1 - y, c)))

    def across(value):
        return lax.ppermute(value, "store", pairs(lambda z, y, c: (z, y, 1 - c)))

    def along_x(value):
        return lax.ppermute(value, "groups", [(g, g ^ 1) for g in range(groups)])

    class Line:
        def __init__(self, send):
            self.send, self.sent = send, []

        def __call__(self, value, *args):
            if len(self.sent) >= 2:
                value = after(value, self.sent[-2])
            self.sent.append(self.send(value, *args))
            return self.sent[-1]

    def per_device(
        tokens,
        input_norm_gain,
        value_matrix,
        adapter_down_factors,
        adapter_up_factors,
        document_lengths,
        document_tenant,
        tenant_adapter_slot,
    ):
        shard, adapters, rank = adapter_down_factors.shape
        flat = adapters * rank
        width = value_matrix.shape[1]
        half, part = shard // 2, 3 * shard // 8
        me = lax.axis_index("store")
        side = lax.axis_index("groups") % 2
        mz, my, mc = me // (rows_y * cores), (me // cores) % rows_y, me % cores
        take = lax.dynamic_slice_in_dim

        down = adapter_down_factors.reshape(shard, flat).T
        v_have = {
            (0, 0): jnp.concatenate(
                [
                    take(value_matrix, side * half, half, 0),
                    take(value_matrix, half + part - side * half, half - part, 0),
                ],
                0,
            )
        }
        v_miss = {(0, 0): (take(value_matrix, half - side * half, part, 0), 0)}
        d_have = {(0, 0): take(down, side * half, half, 1)}
        d_rest = take(down, half - side * half, half, 1)
        up = adapter_up_factors.reshape(flat, -1).T
        up_all = lax.all_gather(up, "store", axis=0, tiled=True).T

        ends = jnp.cumsum(document_lengths, axis=1).astype(jnp.int32)
        slots = jnp.sum(
            (document_tenant[0][:, None] == jnp.arange(adapters, dtype=jnp.int32)[None, :])
            * tenant_adapter_slot[None, :],
            axis=1,
        ).astype(jnp.int32)[None, :]
        near = jnp.concatenate([ends, slots], 0)
        far = across(near)
        ends_both = jnp.concatenate([ends, far[:1]], 0)
        slots_both = jnp.concatenate([slots, far[1:]], 0)
        slots_there = along_x(slots_both)
        d_miss = {(0, 0): (pick_adapters([d_rest], slots_both, rank), 0)}
        chosen = slots_both.size * rank

        ks = []
        for k in range(1, depth // 2 + 1):
            ks += [k, depth - k] if k != depth - k else [k]
        last = ks[-1]
        early = [k for k in ks if k != last]
        z, y, x = Line(along_z), Line(along_y), Line(along_x)

        def x_values(names, *earlier):
            got = x(after(jnp.concatenate([v_have[name][:part] for name in names], 0), *earlier))
            for i, name in enumerate(names):
                v_miss[name] = (got, i * part)

        def x_down(names):
            got = x(pick_adapters([d_have[name] for name in names], slots_there, rank))
            for i, name in enumerate(names):
                d_miss[name] = (got, i * chosen)

        for k in ks:
            v_have[0, k] = z(v_have[0, 0], k)
        for k in ks:
            d_have[0, k] = z(d_have[0, 0], k)
        v_have[1, 0] = y(v_have[0, 0])
        d_have[1, 0] = y(d_have[0, 0])
        x_values([(1, 0)])
        for k in early:
            v_have[1, k] = y(v_have[0, k])
        x_values([(0, k) for k in early])
        x_values([(1, k) for k in early])
        v_have[1, last] = y(v_have[0, last])
        x_values([(0, last)])
        x_values([(1, last)], *[d_have[0, k] for k in early])
        x_down([(1, 0)])
        for k in early:
            d_have[1, k] = y(d_have[0, k])
        x_down([(0, k) for k in early])
        x_down([(1, k) for k in early])
        d_have[1, last] = y(d_have[0, last])
        x_down([(0, last)])
        x_down([(1, last)])

        source = []
        for lane_at in (mc, 1 - mc):
            for dy in range(rows_y):
                for k in range(depth):
                    s = index((mz - k) % depth, my ^ dy, lane_at)
                    for c in range(shard // lane):
                        piece = c * lane + jnp.where(c * lane < half, 1, -1) * side * half
                        source.append(s * shard + piece)
        span = rows_y * depth * shard
        chunk = span // 4
        ready = [v_have[0, k] for k in early] + [v_miss[1, 0][0], d_miss[1, 0][0], up_all]
        own, *other = norm_in_order(
            after(tokens, *ready),
            input_norm_gain,
            jnp.stack(source).astype(jnp.int32),
            [span] + [chunk] * 4,
        )
        partner = [across(o) for o in other]

        names = [(dy, k) for dy in range(rows_y) for k in range(depth)]

        def column(name):
            return (name[0] * depth + name[1]) * shard

        def lay(blocks):
            arrays = []

            def place(array):
                for i, known in enumerate(arrays):
                    if known is array:
                        return blocks + i
                arrays.append(array)
                return blocks + len(arrays) - 1

            return arrays, place

        def values(blocks, start=None):
            arrays, place = lay(len(blocks))
            width_of = blocks[0].shape[1]
            plan = []
            for name in names:
                h = place(v_have[name])
                m, row = v_miss[name]
                m = place(m)
                parts = ((h, 0, half), (m, row, row + part), (h, half, shard - part))
                plan.append((column(name) // width_of, column(name) % width_of, parts))
            return value_sums(blocks, arrays, tuple(plan), width, start)

        ready = [d_have[1, k] for k in early] + [d_have[0, last]]
        partner[0] = after(partner[0], *ready)
        base = values([own], across(values(partner)))

        arrays, place = lay(5)
        plan = ([], [])
        for name in names:
            if name[1] != last:
                miss, row = d_miss[name]
                entry = (place(d_have[name]), place(miss), row)
                at = column(name)
                plan[0].append((0, at, *entry))
                plan[1].append((1 + at // chunk, at % chunk, *entry))
        mid_own, mid_far = mid_partials(
            [own, *partner], arrays, tuple(map(tuple, plan)), ends_both, slots_both, rank
        )
        mids = (mid_own, across(mid_far))

        final = [(dy, last) for dy in range(rows_y)]
        blocks, pieces = [], []
        for name in final:
            blocks.append((own, column(name) // shard, shard))
            pieces.append((d_have[name], *d_miss[name], 0))
        for name in final:
            at = column(name)
            blocks.append((other[at // chunk], at % chunk // shard, shard))
            miss, row = d_miss[name]
            pieces.append((across(d_have[name]), across(miss), row, slots.shape[1]))
        arrays, place = lay(len(blocks))
        plan = [
            (i, place(have), place(miss), row, first)
            for i, (have, miss, row, first) in enumerate(pieces)
        ]
        return last_values(base, mids, up_all, blocks, arrays, tuple(plan), slots[0], ends[0])

    return per_device


def solution(mesh):
    in_specs = (
        P(("groups", "store"), None),
        P(),
        P("store", None),
        P("store", None, None),
        P(None, None, "store"),
        P(("groups", "store"), None),
        P(("groups", "store"), None),
        P(),
    )
    out_specs = P(("groups", "store"), None)
    groups, store = mesh.shape["groups"], mesh.shape["store"]

    def run(*args):
        shard = args[2].shape[0]
        cut = shard % (4 * lane) == 0 and store > 4 and store % (rows_y * cores) == 0 and groups % 2 == 0
        return (make(groups, store) if cut else plain)(*args)

    return jax.shard_map(
        run, mesh=mesh, in_specs=in_specs, out_specs=out_specs, check_vma=False
    )
```

time: 349 us -> 321 us (0.920)
  waiting for transfers between devices: 276 us -> 100 us
  Pallas kernels: 0 us -> 139 us
  matrix products: 44.6 us -> 0 us
  starting transfers between devices: 0.08 us -> 44.3 us
  local copies, waits for them, and re-layouts: 1.88 us -> 18.4 us
  other arithmetic: 10.2 us -> 3.74 us
    all_gather x3 -> x1, waiting for transfers between devices: 274 us -> 0.01 us  [per_device(): up_all = lax.all_gather(up, 'store', axis=0, tiled=True).T]
    pallas_call x0 -> x11, Pallas kernels: none -> 139 us  [the longest x6 74.8 us: pick_adapters(): pl.pallas_call(functools.partial(pick_kernel, rank), out_shape=jax.ShapeD...]
    ppermute x0 -> x36, waiting for transfers between devices: none -> 100 us  [the longest x6 55.1 us: along_z(): lax.ppermute(value, 'store', pairs(lambda z, y, c: ((z + k) % depth, y, c)))]
    dot_general x3 -> x0, matrix products: 44.6 us -> none  [the longest x1 20.6 us: per_device(): jnp.dot(columns, lax.all_gather(value_matrix, 'store', axis=0, tiled=True...]
    ppermute x0 -> x36, starting transfers between devices: none -> 44.3 us  [the longest x6 16.5 us: along_z(): lax.ppermute(value, 'store', pairs(lambda z, y, c: ((z + k) % depth, y, c)))]
    reduce_sum x4 -> x1, other arithmetic: 8.65 us -> 0.18 us  [per_device(): jnp.sum((document_tenant[0][:, None] == jnp.arange(adapters, dtype=jnp.in...]
    slice x0 -> x8, local copies, waits for them, and re-layouts: none -> 6.18 us  [the longest x7 6.17 us: x_values(): v_have[name][:part]]
    all_gather x0 -> x1, local copies, waits for them, and re-layouts: none -> 3.93 us  [per_device(): up_all = lax.all_gather(up, 'store', axis=0, tiled=True).T]
  transfers between devices with their start and end apart: 3 -> 37, of which waited for: 3 -> 9; matrix products, arithmetic and copies ran while one was open for 10% -> 5% of each run, Pallas kernels for 0% -> 36%
where the time goes in v2:
time: 321 us; the launch traced here: 319 us
  Pallas kernels  139 us (43%)
  waiting for transfers between devices  100 us (31%)
  starting transfers between devices  44.3 us (14%)
  local copies, waits for them, and re-layouts  18.4 us (6%)
  between operations  13.9 us (4%)
  other arithmetic  3.74 us (1%)
    pallas_call x6, Pallas kernels, pick_adapters(): pl.pallas_call(functools.partial(pick_kernel, rank), out_shape=jax.ShapeD...  74.8 us
    ppermute x6, waiting for transfers between devices, along_z(): lax.ppermute(value, 'store', pairs(lambda z, y, c: ((z + k) % depth, y, c)))  55.1 us
    ppermute x8, waiting for transfers between devices, along_y(): return lax.ppermute(value, 'store', pairs(lambda z, y, c: (z, 1 - y, c)))  28.4 us
    pallas_call x2, Pallas kernels, value_sums(): pl.pallas_call(functools.partial(value_kernel, plan, 256, len(blocks), le...  26.8 us
    ppermute x6, starting transfers between devices, along_z(): lax.ppermute(value, 'store', pairs(lambda z, y, c: ((z + k) % depth, y, c)))  16.5 us
    ppermute x11, waiting for transfers between devices, along_x(): return lax.ppermute(value, 'groups', [(g, g ^ 1) for g in range(groups)])  16.4 us
    pallas_call x1, Pallas kernels, norm_in_order(): pl.pallas_call(norm_kernel, out_shape=[jax.ShapeDtypeStruct((rows, w), jn...  15.6 us
    pallas_call x1, Pallas kernels, mid_partials(): pl.pallas_call(functools.partial(mid_kernel, rank, plan, len(blocks), len...  11.3 us
  transfers between devices with their start and end apart: 37, of which 9 were waited for; matrix products, arithmetic and copies ran while one was open for 5% of the time, Pallas kernels for 36%

profile of v2, /device:TPU:9, one launch (start us, length us, event | category | flops | bytes accessed | tf_op | source)
XLA Modules:
  0.0 319.2 jit_solution(8818767202138016493)
XLA Ops:
  6.5 1.8 copy.13
  12.1 14.6 %collective-permute-done.refs_6_.refs_4_ = bf16[320,1024]{1,0:T(8,128)(2,1)S(1)} collective-permute-done((bf16[320,1024]{1,0:T(8,128)(2,1)}, bf16[320,1024]{1,0:T(8,128)(2,1)S(1)}, u32[]{:S(2)}, u32[]{:S(2)}) %collective-permute-start) | collective-permute-done | bytes 655392 | tf_op jit(solution)/shard_map/ppermute | solution.py:380
  26.7 18.7 %collective-permute-done.1.refs_10_.refs_8_ = bf16[320,1024]{1,0:T(8,128)(2,1)} collective-permute-done((bf16[320,1024]{1,0:T(8,128)(2,1)}, bf16[320,1024]{1,0:T(8,128)(2,1)}, u32[]{:S(2)}, u32[]{:S(2)}) %collective-permute-start.1) | collective-permute-done | bytes 655392 | tf_op jit(solution)/shard_map/ppermute | solution.py:380
  51.2 17.6 %collective-permute-done.6.refs_0_.refs_10_ = bf16[1024,256]{1,0:T(8,128)(2,1)S(1)} collective-permute-done((bf16[1024,256]{1,0:T(8,128)(2,1)S(1)}, bf16[1024,256]{1,0:T(8,128)(2,1)S(1)}, u32[]{:S(2)}, u32[]{:S(2)}) %collective-permute-start.6) | collective-permute-done | bytes 524320 | tf_op jit(solution)/shard_map/ppermute | solution.py:383
  69.6 17.0 %collective-permute-done.7.refs_8_.refs_6_ = bf16[320,1024]{1,0:T(8,128)(2,1)} collective-permute-done((bf16[320,1024]{1,0:T(8,128)(2,1)}, bf16[320,1024]{1,0:T(8,128)(2,1)}, u32[]{:S(2)}, u32[]{:S(2)}) %collective-permute-start.7) | collective-permute-done | bytes 655392 | tf_op jit(solution)/shard_map/ppermute | solution.py:380
  87.7 1.5 collective-permute-start.9
  91.7 1.4 collective-permute-start.17
  93.1 4.7 %collective-permute-done.12.refs_0_.refs_7_ = bf16[1024,256]{1,0:T(8,128)(2,1)S(1)} collective-permute-done((bf16[1024,256]{1,0:T(8,128)(2,1)S(1)}, bf16[1024,256]{1,0:T(8,128)(2,1)S(1)}, u32[]{:S(2)}, u32[]{:S(2)}) %collective-permute-start.12) | collective-permute-done | bytes 524320 | tf_op jit(solution)/shard_map/ppermute | solution.py:380
  97.8 1.4 collective-permute-start.5
  99.2 6.6 %collective-permute-done.5.slots_ref = s32[2,4]{1,0:T(2,128)S(1)} collective-permute-done((s32[2,4]{1,0:T(2,128)S(1)}, s32[2,4]{1,0:T(2,128)S(1)}, u32[]{:S(2)}, u32[]{:S(2)}) %collective-permute-start.5) | collective-permute-done | bytes 64 | tf_op jit(solution)/shard_map/ppermute | solution.py:389
  105.8 14.8 %collective-permute-start.15 = (bf16[1024,256]{1,0:T(8,128)(2,1)S(1)}, bf16[1024,256]{1,0:T(8,128)(2,1)}, u32[]{:S(2)}, u32[]{:S(2)}) collective-permute-start(bf16[1024,256]{1,0:T(8,128)(2,1)S(1)} %get-tuple-element.46.refs_5_), channel_id=1, source_target_pairs={{0,12},{1,13},{2,14},{3,15},{4,0},{5,1},{6,2},{7,3},{8,4},{9,5},{1... | collective-permute-start | bytes 1572872 | tf_op jit(solution)/shard_map/ppermute | solution.py:380
  121.7 9.8 %shard_map.82 = bf16[512,256]{1,0:T(8,128)(2,1)} custom-call(s32[2,4]{1,0:T(2,128)} %copy-done.23, bf16[1024,256]{1,0:T(8,128)(2,1)} %copy-done.2), custom_call_target="tpu_custom_call" | custom-call | bytes 524288 | tf_op jit(solution)/shard_map/pallas_call | solution.py:177
  134.8 2.7 collective-permute-done.10.refs_11_
  138.9 3.9 %copy.12 = bf16[1024,1024]{0,1:T(8,128)(2,1)} copy(bf16[1024,1024]{1,0:T(8,128)(2,1)} %all-gather.2.cloned.1.call-done) | data formatting | bytes 4194304 | tf_op jit(solution)/shard_map/all_gather | solution.py:434
  142.8 15.6 %shard_map.83 = (bf16[768,4096]{1,0:T(8,128)(2,1)}, bf16[768,1024]{1,0:T(8,128)(2,1)}, bf16[768,1024]{1,0:T(8,128)(2,1)}, bf16[768,1024]{1,0:T(8,128)(2,1)}, bf16[768,1024]{1,0:T(8,128)(2,1)}) custom-call(s32[64]{0:T(128)} %stack.259.source_ref, bf16[768,8192]{1,0:T(8,128)(2,1)} %tokens_ref, bf16[1,8192]{1,0:T(2,128)(2,1)} %reshape.13.gain_ref), custom_call_target="tpu_custom_call" | custom-call | flops 37748736 | bytes 25165824 | tf_op jit(solution)/shard_map/pallas_call | solution.py:100
  158.4 3.4 %collective-permute-start.11 = (bf16[768,1024]{1,0:T(8,128)(2,1)}, bf16[768,1024]{1,0:T(8,128)(2,1)S(1)}, u32[]{:S(2)}, u32[]{:S(2)}) collective-permute-start(bf16[768,1024]{1,0:T(8,128)(2,1)} %get-tuple-element.38), channel_id=1, source_target_pairs={{0,1},{1,0},{2,3},{3,2},{4,5},{5,4},{6,7},{7,6},{8,9},{9,8},{10,11... | collective-permute-start | bytes 4718600 | tf_op jit(solution)/shard_map/ppermute | solution.py:386
  162.5 1.4 collective-permute-start.18
  164.9 10.8 %collective-permute-done.18.refs_1_.refs_14_ = bf16[1024,256]{1,0:T(8,128)(2,1)S(1)} collective-permute-done((bf16[1024,256]{1,0:T(8,128)(2,1)}, bf16[1024,256]{1,0:T(8,128)(2,1)S(1)}, u32[]{:S(2)}, u32[]{:S(2)}) %collective-permute-start.18) | collective-permute-done | bytes 524320 | tf_op jit(solution)/shard_map/ppermute | solution.py:383
  175.7 1.4 collective-permute-start.24
  177.9 7.1 %collective-permute-done.24.refs_16_.refs_14_ = bf16[192,1024]{1,0:T(8,128)(2,1)S(1)} collective-permute-done((bf16[192,1024]{1,0:T(8,128)(2,1)S(1)}, bf16[192,1024]{1,0:T(8,128)(2,1)S(1)}, u32[]{:S(2)}, u32[]{:S(2)}) %collective-permute-start.24) | collective-permute-done | bytes 393248 | tf_op jit(solution)/shard_map/ppermute | solution.py:389
  186.4 13.2 %shard_map.84 = f32[768,1024]{1,0:T(8,128)} custom-call(bf16[768,1024]{1,0:T(8,128)(2,1)} %copy-done.9, bf16[768,1024]{1,0:T(8,128)(2,1)} %copy-done.10, bf16[768,1024]{1,0:T(8,128)(2,1)} %collective-permute-done.21.refs_2_.refs_3_, bf16[768,1024]{1,0:T(8,128)(2,1)} %collective-permute-done.22.refs_3_.refs_4_, ...), custom_call_target="tpu_custom_call" | custom-call | flops 6442450944 | bytes 17825792 | tf_op jit(solution)/shard_map/pallas_call | solution.py:283
  199.6 2.3 collective-permute-start.25
  201.9 1.5 collective-permute-start.30
  203.3 17.8 %shard_map.87 = bf16[1024,256]{1,0:T(8,128)(2,1)} custom-call(s32[2,4]{1,0:T(2,128)} %copy-done.23, bf16[1024,256]{1,0:T(8,128)(2,1)} %copy-done.7, bf16[1024,256]{1,0:T(8,128)(2,1)} %collective-permute-done.15.refs_1_.refs_9_), custom_call_target="tpu_custom_call" | custom-call | bytes 1048576 | tf_op jit(solution)/shard_map/pallas_call | solution.py:177
  221.5 17.8 %shard_map.88 = bf16[1024,256]{1,0:T(8,128)(2,1)} custom-call(s32[2,4]{1,0:T(2,128)} %copy-done.23, bf16[1024,256]{1,0:T(8,128)(2,1)} %collective-permute-done.14.refs_0_.refs_12_, bf16[1024,256]{1,0:T(8,128)(2,1)} %copy-done.8), custom_call_target="tpu_custom_call" | custom-call | bytes 1048576 | tf_op jit(solution)/shard_map/pallas_call | solution.py:177
  240.6 9.8 %shard_map.90 = bf16[512,256]{1,0:T(8,128)(2,1)} custom-call(s32[2,4]{1,0:T(2,128)} %copy-done.23, bf16[1024,256]{1,0:T(8,128)(2,1)} %copy-done.3), custom_call_target="tpu_custom_call" | custom-call | bytes 524288 | tf_op jit(solution)/shard_map/pallas_call | solution.py:177
  251.2 9.8 %shard_map.91 = bf16[512,256]{1,0:T(8,128)(2,1)} custom-call(s32[2,4]{1,0:T(2,128)} %copy-done.23, bf16[1024,256]{1,0:T(8,128)(2,1)} %copy-done.5), custom_call_target="tpu_custom_call" | custom-call | bytes 524288 | tf_op jit(solution)/shard_map/pallas_call | solution.py:177
  262.6 9.8 %shard_map.86.refs_6_ = bf16[512,256]{1,0:T(8,128)(2,1)} custom-call(s32[2,4]{1,0:T(2,128)} %copy-done.25, bf16[1024,256]{1,0:T(8,128)(2,1)} %get-tuple-element.61.refs_0_), custom_call_target="tpu_custom_call" | custom-call | bytes 524288 | tf_op jit(solution)/shard_map/pallas_call | solution.py:177
  273.0 1.5 collective-permute-start.32
  275.7 11.3 %shard_map.89 = (f32[768,64]{1,0:T(8,128)}, f32[768,64]{1,0:T(8,128)}) custom-call(s32[2,4]{1,0:T(2,128)} %pad_add_fusion.ends_ref, s32[2,4]{1,0:T(2,128)} %copy-done.25, bf16[768,4096]{1,0:T(8,128)(2,1)} %get-tuple-element.37.refs_0_.refs_3_.refs_4_, bf16[768,1024]{1,0:T(8,128)(2,1)} %copy-done.9, bf16[768,1024]{1,0:T(8,128)(2,1)} %copy-done.10, ...), custom_call_target="tpu_custom_call" | custom-call | flops 3221225472 | bytes 17301504 | tf_op jit(solution)/shard_map/pallas_call | solution.py:241
  287.0 13.6 %shard_map.85.refs_0_ = f32[768,1024]{1,0:T(8,128)} custom-call(bf16[768,4096]{1,0:T(8,128)(2,1)} %get-tuple-element.37.refs_0_.refs_3_.refs_4_, f32[768,1024]{1,0:T(8,128)} %collective-permute-done.25.refs_1_, bf16[320,1024]{1,0:T(8,128)(2,1)} %pad_maximum_fusion.2.refs_4_.refs_2_, bf16[192,1024]{1,0:T(8,128)(2,1)} %constant_dynamic-slice_fusion.refs_5_.refs_3_, ...), custom_call_target="tpu_custom_call" | custom-call | flops 6442450944 | bytes 17825792 | tf_op jit(solution)/shard_map/pallas_call | solution.py:283
  302.0 10.3 %shard_map.92 = bf16[768,1024]{1,0:T(8,128)(2,1)} custom-call(s32[4]{0:T(128)} %copy-done.27, s32[4]{0:T(128)} %bitcast.79, f32[768,1024]{1,0:T(8,128)} %shard_map.85.refs_0_, f32[768,64]{1,0:T(8,128)} %get-tuple-element.56.refs_1_, f32[768,64]{1,0:T(8,128)} %copy-done.16, bf16[768,4096]{1,0:T(8,128)(2,1)} %get-tuple-element.37.refs_0_.refs_3_.refs_4_, ...), custom_call_target="tpu_custom_call" | custom-call | flops 402653184 | bytes 9437184 | tf_op jit(solution)/shard_map/pallas_call | solution.py:340
  (146 shorter events, 30.3 us)
Async XLA Ops:
  6.5 132.3 %all-gather.2.cloned.1.call-start = ((), (), s32[]{:S(2)}) async-start(), calls=%async_computation | async-start | bytes 2228224 | tf_op jit(solution)/shard_map/all_gather | solution.py:434
  9.4 17.3 %collective-permute-start = (bf16[320,1024]{1,0:T(8,128)(2,1)}, bf16[320,1024]{1,0:T(8,128)(2,1)S(1)}, u32[]{:S(2)}, u32[]{:S(2)}) collective-permute-start(bf16[320,1024]{1,0:T(8,128)(2,1)} %pad_maximum_fusion.2.refs_4_.refs_2_), channel_id=1, source_target_pairs={{0,4},{1,5},{2,6},{3,7},{4,8},{5,9},{6,10},{7,11},{8,12},{9,13},{1... | collective-permute-start | bytes 1966088 | tf_op jit(solution)/shard_map/ppermute | solution.py:380
  10.7 34.8 %collective-permute-start.1 = (bf16[320,1024]{1,0:T(8,128)(2,1)}, bf16[320,1024]{1,0:T(8,128)(2,1)}, u32[]{:S(2)}, u32[]{:S(2)}) collective-permute-start(bf16[320,1024]{1,0:T(8,128)(2,1)} %pad_maximum_fusion.2.refs_4_.refs_2_), channel_id=1, source_target_pairs={{0,12},{1,13},{2,14},{3,15},{4,0},{5,1},{6,2},{7,3},{8,4},{9,5},{1... | collective-permute-start | bytes 1966088 | tf_op jit(solution)/shard_map/ppermute | solution.py:380
  10.8 40.1 %collective-permute-start.2 = (bf16[320,1024]{1,0:T(8,128)(2,1)}, bf16[320,1024]{1,0:T(8,128)(2,1)}, u32[]{:S(2)}, u32[]{:S(2)}) collective-permute-start(bf16[320,1024]{1,0:T(8,128)(2,1)} %pad_maximum_fusion.2.refs_4_.refs_2_), channel_id=1, source_target_pairs={{0,2},{1,3},{2,0},{3,1},{4,6},{5,7},{6,4},{7,5},{8,10},{9,11},{10,... | collective-permute-start | bytes 1966088 | tf_op jit(solution)/shard_map/ppermute | solution.py:383
  47.4 40.2 %collective-permute-start.8 = (bf16[384,1024]{1,0:T(8,128)(2,1)}, bf16[384,1024]{1,0:T(8,128)(2,1)}, u32[]{:S(2)}, u32[]{:S(2)}) collective-permute-start(bf16[384,1024]{1,0:T(8,128)(2,1)} %pad_maximum_fusion), channel_id=1, source_target_pairs={{0,16},{16,0},{1,17},{17,1},{2,18},{18,2},{3,19},{19,3},{4,20},{20... | collective-permute-start | bytes 2359304 | tf_op jit(solution)/shard_map/ppermute | solution.py:389
  49.6 19.2 %collective-permute-start.6 = (bf16[1024,256]{1,0:T(8,128)(2,1)S(1)}, bf16[1024,256]{1,0:T(8,128)(2,1)S(1)}, u32[]{:S(2)}, u32[]{:S(2)}) collective-permute-start(bf16[1024,256]{1,0:T(8,128)(2,1)S(1)} %get-tuple-element.46.refs_5_), channel_id=1, source_target_pairs={{0,2},{1,3},{2,0},{3,1},{4,6},{5,7},{6,4},{7,5},{8,10},{9,11},{10,... | collective-permute-start | bytes 1572872 | tf_op jit(solution)/shard_map/ppermute | solution.py:383
  50.8 35.8 %collective-permute-start.7 = (bf16[320,1024]{1,0:T(8,128)(2,1)}, bf16[320,1024]{1,0:T(8,128)(2,1)}, u32[]{:S(2)}, u32[]{:S(2)}) collective-permute-start(bf16[320,1024]{1,0:T(8,128)(2,1)} %pad_maximum_fusion.2.refs_4_.refs_2_), channel_id=1, source_target_pairs={{0,8},{1,9},{2,10},{3,11},{4,12},{5,13},{6,14},{7,15},{8,0},{9,1},... | collective-permute-start | bytes 1966088 | tf_op jit(solution)/shard_map/ppermute | solution.py:380
  51.0 40.5 %collective-permute-start.16 = (bf16[320,1024]{1,0:T(8,128)(2,1)}, bf16[320,1024]{1,0:T(8,128)(2,1)}, u32[]{:S(2)}, u32[]{:S(2)}) collective-permute-start(bf16[320,1024]{1,0:T(8,128)(2,1)} %copy-done.22), channel_id=1, source_target_pairs={{0,2},{1,3},{2,0},{3,1},{4,6},{5,7},{6,4},{7,5},{8,10},{9,11},{10,... | collective-permute-start | bytes 1966088 | tf_op jit(solution)/shard_map/ppermute | solution.py:383
  68.8 30.4 %collective-permute-start.13 = (bf16[320,1024]{1,0:T(8,128)(2,1)}, bf16[320,1024]{1,0:T(8,128)(2,1)}, u32[]{:S(2)}, u32[]{:S(2)}) collective-permute-start(bf16[320,1024]{1,0:T(8,128)(2,1)} %collective-permute-done.1.refs_10_.refs_8_), channel_id=1, source_target_pairs={{0,2},{1,3},{2,0},{3,1},{4,6},{5,7},{6,4},{7,5},{8,10},{9,11},{10,... | collective-permute-start | bytes 1966088 | tf_op jit(solution)/shard_map/ppermute | solution.py:383
  69.4 28.4 %collective-permute-start.12 = (bf16[1024,256]{1,0:T(8,128)(2,1)S(1)}, bf16[1024,256]{1,0:T(8,128)(2,1)S(1)}, u32[]{:S(2)}, u32[]{:S(2)}) collective-permute-start(bf16[1024,256]{1,0:T(8,128)(2,1)S(1)} %get-tuple-element.46.refs_5_), channel_id=1, source_target_pairs={{0,4},{1,5},{2,6},{3,7},{4,8},{5,9},{6,10},{7,11},{8,12},{9,13},{1... | collective-permute-start | bytes 1572872 | tf_op jit(solution)/shard_map/ppermute | solution.py:380
  87.7 32.9 %collective-permute-start.9 = (bf16[192,1024]{1,0:T(8,128)(2,1)S(1)}, bf16[192,1024]{1,0:T(8,128)(2,1)S(1)}, u32[]{:S(2)}, u32[]{:S(2)}) collective-permute-start(bf16[192,1024]{1,0:T(8,128)(2,1)S(1)} %slice.37), channel_id=1, source_target_pairs={{0,16},{16,0},{1,17},{17,1},{2,18},{18,2},{3,19},{19,3},{4,20},{20... | collective-permute-start | bytes 1179656 | tf_op jit(solution)/shard_map/ppermute | solution.py:389
  91.5 40.0 %collective-permute-start.3 = (bf16[192,1024]{1,0:T(8,128)(2,1)S(1)}, bf16[192,1024]{1,0:T(8,128)(2,1)S(1)}, u32[]{:S(2)}, u32[]{:S(2)}) collective-permute-start(bf16[192,1024]{1,0:T(8,128)(2,1)S(1)} %slice.36), channel_id=1, source_target_pairs={{0,16},{16,0},{1,17},{17,1},{2,18},{18,2},{3,19},{19,3},{4,20},{20... | collective-permute-start | bytes 1179656 | tf_op jit(solution)/shard_map/ppermute | solution.py:389
  91.7 70.7 %collective-permute-start.17 = (bf16[320,1024]{1,0:T(8,128)(2,1)}, bf16[320,1024]{1,0:T(8,128)(2,1)}, u32[]{:S(2)}, u32[]{:S(2)}) collective-permute-start(bf16[320,1024]{1,0:T(8,128)(2,1)} %collective-permute-done.7.refs_8_.refs_6_), channel_id=1, source_target_pairs={{0,2},{1,3},{2,0},{3,1},{4,6},{5,7},{6,4},{7,5},{8,10},{9,11},{10,... | collective-permute-start | bytes 1966088 | tf_op jit(solution)/shard_map/ppermute | solution.py:383
  99.2 59.2 %collective-permute-start.19 = (bf16[1024,256]{1,0:T(8,128)(2,1)S(1)}, bf16[1024,256]{1,0:T(8,128)(2,1)S(1)}, u32[]{:S(2)}, u32[]{:S(2)}) collective-permute-start(bf16[1024,256]{1,0:T(8,128)(2,1)S(1)} %get-tuple-element.46.refs_5_), channel_id=1, source_target_pairs={{0,8},{1,9},{2,10},{3,11},{4,12},{5,13},{6,14},{7,15},{8,0},{9,1},... | collective-permute-start | bytes 1572872 | tf_op jit(solution)/shard_map/ppermute | solution.py:380
  105.8 56.1 %collective-permute-start.15 = (bf16[1024,256]{1,0:T(8,128)(2,1)S(1)}, bf16[1024,256]{1,0:T(8,128)(2,1)}, u32[]{:S(2)}, u32[]{:S(2)}) collective-permute-start(bf16[1024,256]{1,0:T(8,128)(2,1)S(1)} %get-tuple-element.46.refs_5_), channel_id=1, source_target_pairs={{0,12},{1,13},{2,14},{3,15},{4,0},{5,1},{6,2},{7,3},{8,4},{9,5},{1... | collective-permute-start | bytes 1572872 | tf_op jit(solution)/shard_map/ppermute | solution.py:380
  120.6 41.3 %collective-permute-start.14 = (bf16[1024,256]{1,0:T(8,128)(2,1)S(1)}, bf16[1024,256]{1,0:T(8,128)(2,1)}, u32[]{:S(2)}, u32[]{:S(2)}) collective-permute-start(bf16[1024,256]{1,0:T(8,128)(2,1)S(1)} %collective-permute-done.12.refs_0_.refs_7_), channel_id=1, source_target_pairs={{0,2},{1,3},{2,0},{3,1},{4,6},{5,7},{6,4},{7,5},{8,10},{9,11},{10,... | collective-permute-start | bytes 1572872 | tf_op jit(solution)/shard_map/ppermute | solution.py:383
  137.4 25.0 %collective-permute-start.23 = (bf16[384,1024]{1,0:T(8,128)(2,1)}, bf16[384,1024]{1,0:T(8,128)(2,1)}, u32[]{:S(2)}, u32[]{:S(2)}) collective-permute-start(bf16[384,1024]{1,0:T(8,128)(2,1)} %pad_maximum_fusion.1), channel_id=1, source_target_pairs={{0,16},{16,0},{1,17},{17,1},{2,18},{18,2},{3,19},{19,3},{4,20},{20... | collective-permute-start | bytes 2359304 | tf_op jit(solution)/shard_map/ppermute | solution.py:389
  158.4 19.5 %collective-permute-start.11 = (bf16[768,1024]{1,0:T(8,128)(2,1)}, bf16[768,1024]{1,0:T(8,128)(2,1)S(1)}, u32[]{:S(2)}, u32[]{:S(2)}) collective-permute-start(bf16[768,1024]{1,0:T(8,128)(2,1)} %get-tuple-element.38), channel_id=1, source_target_pairs={{0,1},{1,0},{2,3},{3,2},{4,5},{5,4},{6,7},{7,6},{8,9},{9,8},{10,11... | collective-permute-start | bytes 4718600 | tf_op jit(solution)/shard_map/ppermute | solution.py:386
  161.9 23.2 %collective-permute-start.20 = (bf16[768,1024]{1,0:T(8,128)(2,1)}, bf16[768,1024]{1,0:T(8,128)(2,1)S(1)}, u32[]{:S(2)}, u32[]{:S(2)}) collective-permute-start(bf16[768,1024]{1,0:T(8,128)(2,1)} %get-tuple-element.48.refs_5_), channel_id=1, source_target_pairs={{0,1},{1,0},{2,3},{3,2},{4,5},{5,4},{6,7},{7,6},{8,9},{9,8},{10,11... | collective-permute-start | bytes 4718600 | tf_op jit(solution)/shard_map/ppermute | solution.py:386
  161.9 23.2 %collective-permute-start.21 = (bf16[768,1024]{1,0:T(8,128)(2,1)}, bf16[768,1024]{1,0:T(8,128)(2,1)}, u32[]{:S(2)}, u32[]{:S(2)}) collective-permute-start(bf16[768,1024]{1,0:T(8,128)(2,1)} %get-tuple-element.49), channel_id=1, source_target_pairs={{0,1},{1,0},{2,3},{3,2},{4,5},{5,4},{6,7},{7,6},{8,9},{9,8},{10,11... | collective-permute-start | bytes 4718600 | tf_op jit(solution)/shard_map/ppermute | solution.py:386
  162.4 22.7 %collective-permute-start.22 = (bf16[768,1024]{1,0:T(8,128)(2,1)}, bf16[768,1024]{1,0:T(8,128)(2,1)}, u32[]{:S(2)}, u32[]{:S(2)}) collective-permute-start(bf16[768,1024]{1,0:T(8,128)(2,1)} %get-tuple-element.50.refs_6_), channel_id=1, source_target_pairs={{0,1},{1,0},{2,3},{3,2},{4,5},{5,4},{6,7},{7,6},{8,9},{9,8},{10,11... | collective-permute-start | bytes 4718600 | tf_op jit(solution)/shard_map/ppermute | solution.py:386
  199.6 87.3 %collective-permute-start.25 = (f32[768,1024]{1,0:T(8,128)}, f32[768,1024]{1,0:T(8,128)}, u32[]{:S(2)}, u32[]{:S(2)}) collective-permute-start(f32[768,1024]{1,0:T(8,128)} %shard_map.84), channel_id=1, source_target_pairs={{0,1},{1,0},{2,3},{3,2},{4,5},{5,4},{6,7},{7,6},{8,9},{9,8},{10,11... | collective-permute-start | bytes 9437192 | tf_op jit(solution)/shard_map/ppermute | solution.py:386
  201.9 48.5 %collective-permute-start.30 = (bf16[1024,256]{1,0:T(8,128)(2,1)S(1)}, bf16[1024,256]{1,0:T(8,128)(2,1)S(1)}, u32[]{:S(2)}, u32[]{:S(2)}) collective-permute-start(bf16[1024,256]{1,0:T(8,128)(2,1)S(1)} %collective-permute-done.19.refs_0_.refs_7_), channel_id=1, source_target_pairs={{0,2},{1,3},{2,0},{3,1},{4,6},{5,7},{6,4},{7,5},{8,10},{9,11},{10,... | collective-permute-start | bytes 1572872 | tf_op jit(solution)/shard_map/ppermute | solution.py:383
  221.2 39.9 %collective-permute-start.26 = (bf16[1024,256]{1,0:T(8,128)(2,1)}, bf16[1024,256]{1,0:T(8,128)(2,1)S(1)}, u32[]{:S(2)}, u32[]{:S(2)}) collective-permute-start(bf16[1024,256]{1,0:T(8,128)(2,1)} %shard_map.87), channel_id=1, source_target_pairs={{0,16},{16,0},{1,17},{17,1},{2,18},{18,2},{3,19},{19,3},{4,20},{20... | collective-permute-start | bytes 1572872 | tf_op jit(solution)/shard_map/ppermute | solution.py:389
  239.4 22.0 %collective-permute-start.27 = (bf16[1024,256]{1,0:T(8,128)(2,1)}, bf16[1024,256]{1,0:T(8,128)(2,1)S(1)}, u32[]{:S(2)}, u32[]{:S(2)}) collective-permute-start(bf16[1024,256]{1,0:T(8,128)(2,1)} %shard_map.88), channel_id=1, source_target_pairs={{0,16},{16,0},{1,17},{17,1},{2,18},{18,2},{3,19},{19,3},{4,20},{20... | collective-permute-start | bytes 1572872 | tf_op jit(solution)/shard_map/ppermute | solution.py:389
  261.0 13.4 %collective-permute-start.29 = (bf16[512,256]{1,0:T(8,128)(2,1)}, bf16[512,256]{1,0:T(8,128)(2,1)S(1)}, u32[]{:S(2)}, u32[]{:S(2)}) collective-permute-start(bf16[512,256]{1,0:T(8,128)(2,1)} %shard_map.90), channel_id=1, source_target_pairs={{0,16},{16,0},{1,17},{17,1},{2,18},{18,2},{3,19},{19,3},{4,20},{20... | collective-permute-start | bytes 786440 | tf_op jit(solution)/shard_map/ppermute | solution.py:389
  261.4 13.6 %collective-permute-start.31 = (bf16[512,256]{1,0:T(8,128)(2,1)}, bf16[512,256]{1,0:T(8,128)(2,1)S(1)}, u32[]{:S(2)}, u32[]{:S(2)}) collective-permute-start(bf16[512,256]{1,0:T(8,128)(2,1)} %shard_map.91), channel_id=1, source_target_pairs={{0,16},{16,0},{1,17},{17,1},{2,18},{18,2},{3,19},{19,3},{4,20},{20... | collective-permute-start | bytes 786440 | tf_op jit(solution)/shard_map/ppermute | solution.py:389
  273.0 27.7 %collective-permute-start.32 = (bf16[1024,256]{1,0:T(8,128)(2,1)S(1)}, bf16[1024,256]{1,0:T(8,128)(2,1)S(1)}, u32[]{:S(2)}, u32[]{:S(2)}) collective-permute-start(bf16[1024,256]{1,0:T(8,128)(2,1)S(1)} %copy-done.4), channel_id=1, source_target_pairs={{0,1},{1,0},{2,3},{3,2},{4,5},{5,4},{6,7},{7,6},{8,9},{9,8},{10,11... | collective-permute-start | bytes 1572872 | tf_op jit(solution)/shard_map/ppermute | solution.py:386
  274.5 26.2 %collective-permute-start.34 = (bf16[1024,256]{1,0:T(8,128)(2,1)}, bf16[1024,256]{1,0:T(8,128)(2,1)S(1)}, u32[]{:S(2)}, u32[]{:S(2)}) collective-permute-start(bf16[1024,256]{1,0:T(8,128)(2,1)} %copy-done.5), channel_id=1, source_target_pairs={{0,1},{1,0},{2,3},{3,2},{4,5},{5,4},{6,7},{7,6},{8,9},{9,8},{10,11... | collective-permute-start | bytes 1572872 | tf_op jit(solution)/shard_map/ppermute | solution.py:386
  274.5 26.2 %collective-permute-start.33 = (bf16[512,256]{1,0:T(8,128)(2,1)S(1)}, bf16[512,256]{1,0:T(8,128)(2,1)S(1)}, u32[]{:S(2)}, u32[]{:S(2)}) collective-permute-start(bf16[512,256]{1,0:T(8,128)(2,1)S(1)} %collective-permute-done.29.refs_8_), channel_id=1, source_target_pairs={{0,1},{1,0},{2,3},{3,2},{4,5},{5,4},{6,7},{7,6},{8,9},{9,8},{10,11... | collective-permute-start | bytes 786440 | tf_op jit(solution)/shard_map/ppermute | solution.py:386
  275.0 25.8 %collective-permute-start.35 = (bf16[512,256]{1,0:T(8,128)(2,1)S(1)}, bf16[512,256]{1,0:T(8,128)(2,1)S(1)}, u32[]{:S(2)}, u32[]{:S(2)}) collective-permute-start(bf16[512,256]{1,0:T(8,128)(2,1)S(1)} %collective-permute-done.31.refs_10_), channel_id=1, source_target_pairs={{0,1},{1,0},{2,3},{3,2},{4,5},{5,4},{6,7},{7,6},{8,9},{9,8},{10,11... | collective-permute-start | bytes 786440 | tf_op jit(solution)/shard_map/ppermute | solution.py:386
  287.0 13.8 %collective-permute-start.28 = (f32[768,64]{1,0:T(8,128)}, f32[768,64]{1,0:T(8,128)S(1)}, u32[]{:S(2)}, u32[]{:S(2)}) collective-permute-start(f32[768,64]{1,0:T(8,128)} %get-tuple-element.57), channel_id=1, source_target_pairs={{0,1},{1,0},{2,3},{3,2},{4,5},{5,4},{6,7},{7,6},{8,9},{9,8},{10,11... | collective-permute-start | bytes 589832 | tf_op jit(solution)/shard_map/ppermute | solution.py:386
  (39 other events, 895.8 us)
Sparse Core Ops, SparseCore 0:
  9.5 75.3 all-gather.1

commit v3 on v0

v3 whole, which is shorter than its diff:
```python
import functools

import jax
import jax.numpy as jnp
from jax import lax
from jax.experimental import pallas as pl
from jax.experimental.pallas import tpu as pltpu
from jax.sharding import PartitionSpec as P

adapter_scale = 2.0
cores, rows_y, lane = 2, 2, 128
nt = (((1,), (1,)), ((), ()))
vmem = 58 << 20
light = pl.CostEstimate(flops=0, bytes_accessed=0, transcendentals=0)


def token_slots(lengths, tenants, tenant_adapter_slot, row_count):
    ends = jnp.cumsum(lengths)
    position = jnp.arange(row_count, dtype=jnp.int32)
    doc_index = jnp.sum((position[:, None] >= ends[None, :]).astype(jnp.int32), axis=1)
    doc_pick = (
        doc_index[:, None] == jnp.arange(lengths.shape[0], dtype=jnp.int32)[None, :]
    ).astype(jnp.int32)
    tenant = jnp.sum(doc_pick * tenants[None, :], axis=1)
    tenant_pick = (
        tenant[:, None] == jnp.arange(tenant_adapter_slot.shape[0], dtype=jnp.int32)[None, :]
    ).astype(jnp.int32)
    return jnp.sum(tenant_pick * tenant_adapter_slot[None, :], axis=1)


def pick_rank(rank_total_rows, slots, count_of_adapters, rank_span_width):
    select = (slots[:, None] == jnp.arange(count_of_adapters, dtype=jnp.int32)[None, :]).astype(
        jnp.float32
    )
    shaped = rank_total_rows.reshape(slots.shape[0], count_of_adapters, rank_span_width)
    return jnp.sum(shaped * select[:, :, None], axis=1)


def plain(
    tokens,
    input_norm_gain,
    value_matrix,
    adapter_down_factors,
    adapter_up_factors,
    document_lengths,
    document_tenant,
    tenant_adapter_slot,
):
    row_count = tokens.shape[0]
    count_of_adapters = adapter_down_factors.shape[1]
    rank_span_width = adapter_down_factors.shape[2]
    flat_width = count_of_adapters * rank_span_width
    wide = tokens.astype(jnp.float32)
    meansq = jnp.mean(wide * wide, axis=1, keepdims=True)
    normed = (wide * lax.rsqrt(meansq + 1e-05) * input_norm_gain.astype(jnp.float32)).astype(
        jnp.bfloat16
    )
    slots = token_slots(document_lengths[0], document_tenant[0], tenant_adapter_slot, row_count)
    base_output = jnp.dot(
        normed,
        lax.all_gather(value_matrix, "store", axis=0, tiled=True),
        preferred_element_type=jnp.float32,
    )
    down = lax.all_gather(adapter_down_factors, "store", axis=0, tiled=True)
    rank_total_rows = jnp.dot(
        normed, down.reshape(down.shape[0], flat_width), preferred_element_type=jnp.float32
    )
    mid = pick_rank(rank_total_rows, slots, count_of_adapters, rank_span_width)
    mid = mid.astype(jnp.bfloat16)
    select = (slots[:, None] == jnp.arange(count_of_adapters, dtype=jnp.int32)[None, :]).astype(
        jnp.bfloat16
    )
    expanded_rows = (mid[:, None, :] * select[:, :, None]).reshape(row_count, flat_width)
    up = lax.all_gather(adapter_up_factors, "store", axis=2, tiled=True)
    adapter_update = jnp.dot(
        expanded_rows, up.reshape(flat_width, up.shape[2]), preferred_element_type=jnp.float32
    )
    return (base_output + adapter_scale * adapter_update).astype(jnp.bfloat16)


def norm_kernel(source_ref, tokens_ref, gain_ref, *out_refs):
    width = tokens_ref.shape[1]
    total = jnp.zeros((tokens_ref.shape[0], lane), jnp.float32)
    for i in range(width // lane):
        part = tokens_ref[:, i * lane : (i + 1) * lane].astype(jnp.float32)
        total += part * part
    scale = lax.rsqrt(jnp.sum(total, axis=1, keepdims=True) / width + 1e-05)
    first = 0
    for out_ref in out_refs:
        for i in range(out_ref.shape[1] // lane):
            start = pl.multiple_of(source_ref[first + i], lane)
            part = tokens_ref[:, pl.ds(start, lane)].astype(jnp.float32)
            gain = gain_ref[:, pl.ds(start, lane)].astype(jnp.float32)
            out_ref[:, i * lane : (i + 1) * lane] = (part * scale * gain).astype(jnp.bfloat16)
        first += out_ref.shape[1] // lane


def norm_in_order(tokens, gain, source, widths):
    rows, width = tokens.shape
    block = 64
    return pl.pallas_call(
        norm_kernel,
        out_shape=[jax.ShapeDtypeStruct((rows, w), jnp.bfloat16) for w in widths],
        grid_spec=pltpu.PrefetchScalarGridSpec(
            num_scalar_prefetch=1,
            grid=(rows // block,),
            in_specs=[
                pl.BlockSpec((block, width), lambda i, *_: (i, 0)),
                pl.BlockSpec((1, width), lambda i, *_: (0, 0)),
            ],
            out_specs=[pl.BlockSpec((block, w), lambda i, *_: (i, 0)) for w in widths],
        ),
        compiler_params=pltpu.CompilerParams(vmem_limit_bytes=vmem),
        cost_estimate=light,
    )(source, tokens, gain.reshape(1, width))


def far_memory():
    return pl.BlockSpec(memory_space=pltpu.HBM)


def tiled(array, tile):
    return pl.BlockSpec((tile,) + array.shape[1:], lambda i, *_: (i, 0))


def rows_tile(rows):
    return 256 if rows % 256 == 0 else rows


def pick_kernel(rank, slots_ref, *refs):
    piece_refs, out_ref = refs[:-1], refs[-1]
    sides, docs = slots_ref.shape
    at = 0
    for piece in piece_refs:
        for i in range(sides * docs):
            start = pl.multiple_of(slots_ref[i // docs, i % docs] * rank, rank)
            out_ref[at : at + rank, :] = piece[pl.ds(start, rank), :]
            at += rank


def pick_adapters(pieces, slots, rank):
    count = slots.shape[0] * slots.shape[1] * len(pieces)
    columns = pieces[0].shape[1]
    whole = [pl.BlockSpec(p.shape, lambda i, *_: (0, 0)) for p in pieces]
    return pl.pallas_call(
        functools.partial(pick_kernel, rank),
        out_shape=jax.ShapeDtypeStruct((count * rank, columns), jnp.bfloat16),
        grid_spec=pltpu.PrefetchScalarGridSpec(
            num_scalar_prefetch=1,
            grid=(1,),
            in_specs=whole,
            out_specs=pl.BlockSpec((count * rank, columns), lambda i, *_: (0, 0)),
        ),
        compiler_params=pltpu.CompilerParams(vmem_limit_bytes=12 << 20),
        cost_estimate=light,
    )(slots, *pieces)


def value_kernel(plan, columns, has_sum, arrays, *refs):
    own_ref, far_ref, refs = refs[0], refs[1], refs[2:]
    sum_refs, refs = refs[:has_sum], refs[has_sum:]
    array_refs, out_refs, held_ref, sem = refs[:arrays], refs[arrays:-2], refs[-2], refs[-1]

    @pl.when(pl.program_id(0) == 0)
    def _():
        copies = [
            pltpu.make_async_copy(
                array_refs[i].at[a:b, :], held_ref.at[row : row + b - a, :], sem.at[j]
            )
            for j, (i, a, b, row) in enumerate(plan)
        ]
        for copy in copies:
            copy.start()
        for copy in copies:
            copy.wait()

    tile = own_ref.shape[0]
    both = jnp.concatenate([own_ref[...], far_ref[...]], 0)
    for n in range(0, held_ref.shape[1], columns):
        cols = slice(n, n + columns)
        acc = jnp.dot(both, held_ref[:, cols], preferred_element_type=jnp.float32)
        for side in range(2):
            term = acc[side * tile : (side + 1) * tile]
            if has_sum:
                term += sum_refs[side][:, cols]
            out_refs[side][:, cols] = term


def value_sums(own, far, arrays, plan, width, sums=()):
    rows, depth = own.shape
    tile = rows_tile(rows)
    out = jax.ShapeDtypeStruct((rows, width), jnp.float32)
    return pl.pallas_call(
        functools.partial(value_kernel, plan, 256, len(sums), len(arrays)),
        out_shape=(out, out),
        grid=(rows // tile,),
        in_specs=[tiled(b, tile) for b in (own, far, *sums)] + [far_memory()] * len(arrays),
        out_specs=[tiled(out, tile)] * 2,
        scratch_shapes=[
            pltpu.VMEM((depth, width), jnp.bfloat16),
            pltpu.SemaphoreType.DMA((len(plan),)),
        ],
        compiler_params=pltpu.CompilerParams(vmem_limit_bytes=vmem),
        cost_estimate=light,
    )(own, far, *sums, *arrays)


def load_all(array_refs, held_refs, sem, first=0):
    copies = [
        pltpu.make_async_copy(a, h, sem.at[first + i])
        for i, (a, h) in enumerate(zip(array_refs, held_refs))
    ]
    for copy in copies:
        copy.start()
    return copies


def lay_slabs(rank, parts, slots, first, held_refs, rhs_ref):
    for at, have, miss, row in parts:
        for d, slot in enumerate(slots):
            rows = slice(d * rank, (d + 1) * rank)
            start = pl.multiple_of(slot * rank, rank)
            half = held_refs[have].shape[1]
            rhs_ref[rows, at : at + half] = held_refs[have][pl.ds(start, rank), :]
            low = row + (first + d) * rank
            rhs_ref[rows, at + half : at + 2 * half] = held_refs[miss][low : low + rank, :]


def by_document(acc, ends, tile, rank):
    row = pl.program_id(0) * tile + lax.broadcasted_iota(jnp.int32, (tile, rank), 0)
    mid = jnp.zeros((tile, rank), jnp.float32)
    low = 0
    for doc, end in enumerate(ends):
        mid = jnp.where((row >= low) & (row < end), acc[:, doc * rank : (doc + 1) * rank], mid)
        low = end
    return mid


def mid_kernel(rank, parts, arrays, ends_ref, slots_ref, *refs):
    token_refs, array_refs, out_refs = refs[:2], refs[2 : 2 + arrays], refs[2 + arrays : 4 + arrays]
    held_refs, rhs_refs, sem = refs[4 + arrays : -3], refs[-3:-1], refs[-1]
    docs = slots_ref.shape[1]
    tile = out_refs[0].shape[0]

    @pl.when(pl.program_id(0) == 0)
    def _():
        for copy in load_all(array_refs, held_refs, sem):
            copy.wait()
        for side in range(2):
            slots = [slots_ref[side, d] for d in range(docs)]
            lay_slabs(rank, parts, slots, side * docs, held_refs, rhs_refs[side])

    for side in range(2):
        acc = lax.dot_general(
            token_refs[side][...], rhs_refs[side][...], nt, preferred_element_type=jnp.float32
        )
        ends = [ends_ref[side, d] for d in range(docs)]
        out_refs[side][...] = by_document(acc, ends, tile, rank)


def mid_partials(own, far, arrays, parts, ends, slots, rank):
    rows, depth = own.shape
    tile = rows_tile(rows)
    docs = slots.shape[1]
    out = jax.ShapeDtypeStruct((rows, rank), jnp.float32)
    return pl.pallas_call(
        functools.partial(mid_kernel, rank, parts, len(arrays)),
        out_shape=(out, out),
        grid_spec=pltpu.PrefetchScalarGridSpec(
            num_scalar_prefetch=2,
            grid=(rows // tile,),
            in_specs=[tiled(own, tile), tiled(far, tile)] + [far_memory()] * len(arrays),
            out_specs=[pl.BlockSpec((tile, rank), lambda i, *_: (i, 0))] * 2,
            scratch_shapes=[pltpu.VMEM(a.shape, a.dtype) for a in arrays]
            + [pltpu.VMEM((docs * rank, depth), jnp.bfloat16)] * 2
            + [pltpu.SemaphoreType.DMA((len(arrays),))],
        ),
        compiler_params=pltpu.CompilerParams(vmem_limit_bytes=vmem),
        cost_estimate=light,
    )(ends, slots, own, far, *arrays)


def last_kernel(rank, parts, arrays, slots_ref, ends_ref, at_ref, *refs):
    sum_refs, mid_refs, token_refs, refs = refs[:2], refs[2:4], refs[4:6], refs[6:]
    up_refs, array_refs, out_ref = refs[:2], refs[2 : 2 + arrays], refs[2 + arrays]
    held_refs, rhs_refs, up_ref, sem = refs[3 + arrays : -4], refs[-4:-2], refs[-2], refs[-1]
    docs = slots_ref.shape[0]
    tile, width = out_ref.shape
    ends = [ends_ref[d] for d in range(docs)]

    @pl.when(pl.program_id(0) == 0)
    def _():
        copies = load_all(array_refs, held_refs, sem)
        count = at_ref.shape[1]
        span = up_refs[0].shape[0] // count
        for i in range(2):
            for j in range(count):
                start = pl.multiple_of(at_ref[i, j], span)
                copies.append(
                    pltpu.make_async_copy(
                        up_refs[i].at[pl.ds(j * span, span), :],
                        up_ref.at[pl.ds(start, span), :],
                        sem.at[arrays + i * count + j],
                    )
                )
                copies[-1].start()
        for copy in copies:
            copy.wait()
        slots = [slots_ref[d] for d in range(docs)]
        for i, (first, part) in enumerate(parts):
            lay_slabs(rank, part, slots, first, held_refs, rhs_refs[i])

    acc = lax.dot_general(
        token_refs[0][...], rhs_refs[0][...], nt, preferred_element_type=jnp.float32
    )
    acc += lax.dot_general(
        token_refs[1][...], rhs_refs[1][...], nt, preferred_element_type=jnp.float32
    )
    mid = by_document(acc, ends, tile, rank) + mid_refs[0][...] + mid_refs[1][...]
    flat = up_ref.shape[1]
    row = pl.program_id(0) * tile + lax.broadcasted_iota(jnp.int32, (tile, flat), 0)
    slot, low = jnp.zeros((tile, flat), jnp.int32), 0
    for d, end in enumerate(ends):
        slot = jnp.where((row >= low) & (row < end), slots_ref[d], slot)
        low = end
    adapter = lax.broadcasted_iota(jnp.int32, (tile, flat), 1) // rank
    spread = jnp.where(slot == adapter, jnp.concatenate([mid] * (flat // rank), 1), 0.0)
    spread = spread.astype(jnp.bfloat16)
    columns = 256
    for n in range(0, width, columns):
        cols = slice(n, n + columns)
        delta = lax.dot_general(spread, up_ref[cols, :], nt, preferred_element_type=jnp.float32)
        base = sum_refs[0][:, cols] + sum_refs[1][:, cols]
        out_ref[:, cols] = (base + adapter_scale * delta).astype(out_ref.dtype)


def last_values(sums, mids, tokens, ups, up_at, arrays, parts, slots, ends):
    rows, width = sums[0].shape
    rank = mids[0].shape[1]
    flat = ups[0].shape[1]
    tile = rows_tile(rows)
    docs = slots.shape[0]
    return pl.pallas_call(
        functools.partial(last_kernel, rank, parts, len(arrays)),
        out_shape=jax.ShapeDtypeStruct((rows, width), jnp.bfloat16),
        grid_spec=pltpu.PrefetchScalarGridSpec(
            num_scalar_prefetch=3,
            grid=(rows // tile,),
            in_specs=[tiled(a, tile) for a in (*sums, *mids, *tokens)]
            + [far_memory()] * (2 + len(arrays)),
            out_specs=pl.BlockSpec((tile, width), lambda i, *_: (i, 0)),
            scratch_shapes=[pltpu.VMEM(a.shape, a.dtype) for a in arrays]
            + [pltpu.VMEM((docs * rank, tokens[0].shape[1]), jnp.bfloat16)] * 2
            + [pltpu.VMEM((width, flat), jnp.bfloat16)]
            + [pltpu.SemaphoreType.DMA((len(arrays) + up_at.size,))],
        ),
        compiler_params=pltpu.CompilerParams(vmem_limit_bytes=vmem),
        cost_estimate=light,
    )(slots, ends, up_at, *sums, *mids, *tokens, *ups, *arrays)


def after(value, *earlier):
    return lax.optimization_barrier((value, *earlier))[0]


def make(groups, store):
    depth = store // (rows_y * cores)

    def index(z, y, c):
        return (z * rows_y + y) * cores + c

    def pairs(move):
        return [
            (index(z, y, c), index(*move(z, y, c)))
            for z in range(depth)
            for y in range(rows_y)
            for c in range(cores)
        ]

    def along_z(value, k):
        return lax.ppermute(value, "store", pairs(lambda z, y, c: ((z + k) % depth, y, c)))

    def along_y(value):
        return lax.ppermute(value, "store", pairs(lambda z, y, c: (z, 1 - y, c)))

    def across(value):
        return lax.ppermute(value, "store", pairs(lambda z, y, c: (z, y, 1 - c)))

    def along_x(value):
        return lax.ppermute(value, "groups", [(g, g ^ 1) for g in range(groups)])

    class Line:
        def __init__(self, send):
            self.send, self.sent = send, []

        def __call__(self, value, *args):
            if len(self.sent) >= 2:
                value = after(value, self.sent[-2])
            self.sent.append(self.send(value, *args))
            return self.sent[-1]

    def per_device(
        tokens,
        input_norm_gain,
        value_matrix,
        adapter_down_factors,
        adapter_up_factors,
        document_lengths,
        document_tenant,
        tenant_adapter_slot,
    ):
        shard, adapters, rank = adapter_down_factors.shape
        flat = adapters * rank
        width = value_matrix.shape[1]
        half, part = shard // 2, 3 * shard // 8
        me = lax.axis_index("store")
        side = lax.axis_index("groups") % 2
        mz, my, mc = me // (rows_y * cores), (me // cores) % rows_y, me % cores
        take = lax.dynamic_slice_in_dim

        down = adapter_down_factors.reshape(shard, flat).T
        up = adapter_up_factors.reshape(flat, -1).T
        bit = up.shape[0] // 2
        cut = part + bit
        v_have = {
            (0, 0): jnp.concatenate(
                [
                    take(value_matrix, side * half, part, 0),
                    take(up, side * bit, bit, 0),
                    take(value_matrix, side * half + part, half - part, 0),
                    take(value_matrix, half + part - side * half, half - part, 0),
                ],
                0,
            )
        }
        v_miss = {
            (0, 0): (
                jnp.concatenate(
                    [
                        take(value_matrix, half - side * half, part, 0),
                        take(up, bit - side * bit, bit, 0),
                    ],
                    0,
                ),
                0,
            )
        }
        d_have = {(0, 0): take(down, side * half, half, 1)}
        d_rest = take(down, half - side * half, half, 1)

        ends = jnp.cumsum(document_lengths, axis=1).astype(jnp.int32)
        slots = jnp.sum(
            (document_tenant[0][:, None] == jnp.arange(adapters, dtype=jnp.int32)[None, :])
            * tenant_adapter_slot[None, :],
            axis=1,
        ).astype(jnp.int32)[None, :]
        near = jnp.concatenate([ends, slots], 0)
        far = across(near)
        ends_both = jnp.concatenate([ends, far[:1]], 0)
        slots_both = jnp.concatenate([slots, far[1:]], 0)
        slots_there = along_x(slots_both)
        d_miss = {(0, 0): (pick_adapters([d_rest], slots_both, rank), 0)}
        chosen = slots_both.size * rank

        ks = []
        for k in range(1, depth // 2 + 1):
            ks += [k, depth - k] if k != depth - k else [k]
        last = ks[-1]
        early = [k for k in ks if k != last]
        z, y, x = Line(along_z), Line(along_y), Line(along_x)

        def x_values(names, *earlier):
            got = x(after(jnp.concatenate([v_have[name][:cut] for name in names], 0), *earlier))
            for i, name in enumerate(names):
                v_miss[name] = (got, i * cut)

        def x_down(names):
            got = x(pick_adapters([d_have[name] for name in names], slots_there, rank))
            for i, name in enumerate(names):
                d_miss[name] = (got, i * chosen)

        names = [(k, dy) for k in [0] + ks for dy in range(rows_y)]
        source, up_at = [], []
        for lane_at in (mc, 1 - mc):
            for k, dy in names:
                s = index((mz - k) % depth, my ^ dy, lane_at)
                for c in range(shard // lane):
                    piece = c * lane + jnp.where(c * lane < half, 1, -1) * side * half
                    source.append(s * shard + piece)
                up_at += [(2 * s + side) * bit, (2 * s + 1 - side) * bit]
        up_at = jnp.stack(up_at).astype(jnp.int32).reshape(2, -1)
        bulk = (len(names) - rows_y) * shard
        rest = rows_y * shard
        own, own_rest, other, other_rest = norm_in_order(
            tokens,
            input_norm_gain,
            jnp.stack(source).astype(jnp.int32),
            [bulk, rest] * 2,
        )
        partner, partner_rest = across(other), across(other_rest)

        for k in ks:
            v_have[k, 0] = z(v_have[0, 0], k)
        for k in ks:
            d_have[k, 0] = z(d_have[0, 0], k)
        v_have[0, 1] = y(v_have[0, 0])
        d_have[0, 1] = y(d_have[0, 0])
        x_values([(0, 1)], slots_there)
        for k in early:
            v_have[k, 1] = y(after(v_have[k, 0], partner, v_miss[0, 1][0]))
        x_values([(k, 0) for k in early])
        x_values([(k, 1) for k in early])
        v_have[last, 1] = y(v_have[last, 0])
        x_values([(last, 0)])
        x_down([(0, 1)])
        for k in early:
            d_have[k, 1] = y(d_have[k, 0])
        x_values([(last, 1)])
        x_down([(k, 0) for k in early])
        x_down([(k, 1) for k in early])
        d_have[last, 1] = y(d_have[last, 0])
        x_down([(last, 0)])
        x_down([(last, 1)])

        def lay():
            arrays = []

            def place(array):
                for i, known in enumerate(arrays):
                    if known is array:
                        return i
                arrays.append(array)
                return len(arrays) - 1

            return arrays, place

        def values(names, *args):
            arrays, place = lay()
            plan = []
            for i, name in enumerate(names):
                h, (m, row) = place(v_have[name]), v_miss[name]
                m, at = place(m), i * shard
                plan += [
                    (h, 0, part, at),
                    (h, cut, cut + half - part, at + part),
                    (m, row, row + part, at + half),
                    (h, cut + half - part, cut + 2 * (half - part), at + half + part),
                ]
            return arrays, tuple(plan)

        arrays, plan = values(names[:-rows_y])
        sums = value_sums(own, partner, arrays, plan, width)
        arrays, plan = values(names[-rows_y:])
        sum_own, sum_far = value_sums(own_rest, partner_rest, arrays, plan, width, sums)
        sums = (sum_own, across(sum_far))

        up_lane = []
        for name in names:
            miss, row = v_miss[name]
            up_lane += [v_have[name][part:cut], miss[row + part : row + cut]]
        up_lane = jnp.concatenate(up_lane, 0)
        ups = (up_lane, across(up_lane))

        def slabs(place, names, have, miss):
            out = []
            for i, name in enumerate(names):
                m, row = miss[name]
                out.append((i * shard, place(have[name]), place(m), row))
            return tuple(out)

        arrays, place = lay()
        parts = slabs(place, names[:-rows_y], d_have, d_miss)
        mid_own, mid_far = mid_partials(own, partner, arrays, parts, ends_both, slots_both, rank)
        mids = (mid_own, across(mid_far))

        final = names[-rows_y:]
        arrays, place = lay()
        parts = [(0, slabs(place, final, d_have, d_miss))]
        far_have = {n: across(d_have[n]) for n in final}
        far_miss = {n: (across(d_miss[n][0]), d_miss[n][1]) for n in final}
        parts.append((slots.shape[1], slabs(place, final, far_have, far_miss)))
        return last_values(
            sums,
            mids,
            (own_rest, other_rest),
            ups,
            up_at,
            arrays,
            tuple(parts),
            slots[0],
            ends[0],
        )

    return per_device


def solution(mesh):
    in_specs = (
        P(("groups", "store"), None),
        P(),
        P("store", None),
        P("store", None, None),
        P(None, None, "store"),
        P(("groups", "store"), None),
        P(("groups", "store"), None),
        P(),
    )
    out_specs = P(("groups", "store"), None)
    groups, store = mesh.shape["groups"], mesh.shape["store"]

    def run(*args):
        shard = args[2].shape[0]
        cut = shard % (4 * lane) == 0 and args[4].shape[2] % 32 == 0 and store > 4 and store % (rows_y * cores) == 0 and groups % 2 == 0
        return (make(groups, store) if cut else plain)(*args)

    return jax.shard_map(
        run, mesh=mesh, in_specs=in_specs, out_specs=out_specs, check_vma=False
    )
```

time: 349 us -> 246 us (0.70)
  waiting for transfers between devices: 276 us -> 95.3 us
  Pallas kernels: 0 us -> 70 us
  starting transfers between devices: 0.08 us -> 47.5 us
  matrix products: 44.6 us -> 0 us
  local copies, waits for them, and re-layouts: 1.88 us -> 26.4 us
  between operations: 13.1 us -> 0.59 us
  other arithmetic: 10.2 us -> 2.88 us
    all_gather x3 -> x0, waiting for transfers between devices: 274 us -> none  [the longest x1 120 us: per_device(): lax.all_gather(value_matrix, 'store', axis=0, tiled=True)]
    ppermute x0 -> x35, waiting for transfers between devices: none -> 95.3 us  [the longest x6 50.9 us: along_z(): lax.ppermute(value, 'store', pairs(lambda z, y, c: ((z + k) % depth, y, c)))]
    pallas_call x0 -> x11, Pallas kernels: none -> 70 us  [the longest x2 27.4 us: value_sums(): pl.pallas_call(functools.partial(value_kernel, plan, 256, len(sums), len(...]
    ppermute x0 -> x35, starting transfers between devices: none -> 47.5 us  [the longest x6 17.7 us: along_z(): lax.ppermute(value, 'store', pairs(lambda z, y, c: ((z + k) % depth, y, c)))]
    dot_general x3 -> x0, matrix products: 44.6 us -> none  [the longest x1 20.6 us: per_device(): jnp.dot(columns, lax.all_gather(value_matrix, 'store', axis=0, tiled=True...]
    unnamed x1 -> x83, local copies, waits for them, and re-layouts: 1.88 us -> 13.8 us
    reduce_sum x4 -> x1, other arithmetic: 8.65 us -> 0.18 us  [per_device(): jnp.sum((document_tenant[0][:, None] == jnp.arange(adapters, dtype=jnp.in...]
    slice x0 -> x8, local copies, waits for them, and re-layouts: none -> 6.32 us  [the longest x7 6.31 us: x_values(): v_have[name][:cut]]
  transfers between devices with their start and end apart: 3 -> 35, of which waited for: 3 -> 12; matrix products, arithmetic and copies ran while one was open for 10% -> 11% of each run, Pallas kernels for 0% -> 17%
where the time goes in v3:
time: 246 us; the launch traced here: 243 us
  waiting for transfers between devices  95.3 us (39%)
  Pallas kernels  70 us (28%)
  starting transfers between devices  47.5 us (19%)
  local copies, waits for them, and re-layouts  26.4 us (11%)
  other arithmetic  2.88 us (1%)
    ppermute x6, waiting for transfers between devices, along_z(): lax.ppermute(value, 'store', pairs(lambda z, y, c: ((z + k) % depth, y, c)))  50.9 us
    pallas_call x2, Pallas kernels, value_sums(): pl.pallas_call(functools.partial(value_kernel, plan, 256, len(sums), len(...  27.4 us
    ppermute x8, waiting for transfers between devices, along_y(): return lax.ppermute(value, 'store', pairs(lambda z, y, c: (z, 1 - y, c)))  25.7 us
    ppermute x6, starting transfers between devices, along_z(): lax.ppermute(value, 'store', pairs(lambda z, y, c: ((z + k) % depth, y, c)))  17.7 us
    ppermute x11, waiting for transfers between devices, along_x(): return lax.ppermute(value, 'groups', [(g, g ^ 1) for g in range(groups)])  16.1 us
    pallas_call x1, Pallas kernels, norm_in_order(): pl.pallas_call(norm_kernel, out_shape=[jax.ShapeDtypeStruct((rows, w), jn...  15.9 us
    unnamed x83, local copies, waits for them, and re-layouts  13.8 us
    ppermute x10, starting transfers between devices, across(): return lax.ppermute(value, 'store', pairs(lambda z, y, c: (z, y, 1 - c)))  12.9 us
  transfers between devices with their start and end apart: 35, of which 12 were waited for; matrix products, arithmetic and copies ran while one was open for 11% of the time, Pallas kernels for 17%

profile of v3, /device:TPU:9, one launch (start us, length us, event | category | flops | bytes accessed | tf_op | source)
XLA Modules:
  0.0 242.7 jit_solution(8854373367460021534)
XLA Ops:
  0.0 1.3 reshape.15.gain_ref
  2.1 15.9 %shard_map.82 = (bf16[768,3072]{1,0:T(8,128)(2,1)}, bf16[768,1024]{1,0:T(8,128)(2,1)}, bf16[768,3072]{1,0:T(8,128)(2,1)}, bf16[768,1024]{1,0:T(8,128)(2,1)}) custom-call(s32[64]{0:T(128)} %stack.391.source_ref, bf16[768,8192]{1,0:T(8,128)(2,1)} %tokens_ref.1, bf16[1,8192]{1,0:T(2,128)(2,1)} %reshape.15.gain_ref), custom_call_target="tpu_custom_call" | custom-call | tf_op jit(solution)/shard_map/pallas_call | solution.py:101
  20.7 1.3 collective-permute-start.2
  22.0 1.3 collective-permute-start.6
  24.8 1.5 collective-permute-done.3
  26.2 1.3 collective-permute-start.4
  27.5 11.1 %collective-permute-done.2.refs_4_ = bf16[352,1024]{1,0:T(8,128)(2,1)S(1)} collective-permute-done((bf16[352,1024]{1,0:T(8,128)(2,1)S(1)}, bf16[352,1024]{1,0:T(8,128)(2,1)S(1)}, u32[]{:S(2)}, u32[]{:S(2)}) %collective-permute-start.2) | collective-permute-done | bytes 720928 | tf_op jit(solution)/shard_map/ppermute | solution.py:384
  38.7 1.3 collective-permute-start.5
  40.8 1.2 collective-permute-start.10
  42.1 2.3 collective-permute-start.13
  44.4 5.8 %collective-permute-done.5.refs_5_ = bf16[224,1024]{1,0:T(8,128)(2,1)S(1)} collective-permute-done((bf16[224,1024]{1,0:T(8,128)(2,1)S(1)}, bf16[224,1024]{1,0:T(8,128)(2,1)S(1)}, u32[]{:S(2)}, u32[]{:S(2)}) %collective-permute-start.5) | collective-permute-done | bytes 458784 | tf_op jit(solution)/shard_map/ppermute | solution.py:390
  50.2 1.2 collective-permute-start.9
  52.6 4.4 %collective-permute-done.7.refs_10_ = bf16[352,1024]{1,0:T(8,128)(2,1)} collective-permute-done((bf16[352,1024]{1,0:T(8,128)(2,1)S(1)}, bf16[352,1024]{1,0:T(8,128)(2,1)}, u32[]{:S(2)}, u32[]{:S(2)}) %collective-permute-start.7) | collective-permute-done | bytes 720928 | tf_op jit(solution)/shard_map/ppermute | solution.py:381
  60.4 25.3 %collective-permute-done.13.refs_4_ = bf16[352,1024]{1,0:T(8,128)(2,1)} collective-permute-done((bf16[352,1024]{1,0:T(8,128)(2,1)S(1)}, bf16[352,1024]{1,0:T(8,128)(2,1)}, u32[]{:S(2)}, u32[]{:S(2)}) %collective-permute-start.13) | collective-permute-done | bytes 720928 | tf_op jit(solution)/shard_map/ppermute | solution.py:381
  87.3 9.7 %collective-permute-done.19.refs_0_.refs_6_ = bf16[1024,256]{1,0:T(8,128)(2,1)S(1)} collective-permute-done((bf16[1024,256]{1,0:T(8,128)(2,1)}, bf16[1024,256]{1,0:T(8,128)(2,1)S(1)}, u32[]{:S(2)}, u32[]{:S(2)}) %collective-permute-start.19) | collective-permute-done | bytes 524320 | tf_op jit(solution)/shard_map/ppermute | solution.py:381
  97.1 1.2 slice.97
  98.3 1.3 collective-permute-start.14
  104.4 14.0 %collective-permute-start.20 = (bf16[1024,256]{1,0:T(8,128)(2,1)}, bf16[1024,256]{1,0:T(8,128)(2,1)S(1)}, u32[]{:S(2)}, u32[]{:S(2)}) collective-permute-start(bf16[1024,256]{1,0:T(8,128)(2,1)} %get-tuple-element.63.refs_2_), channel_id=1, source_target_pairs={{0,12},{1,13},{2,14},{3,15},{4,0},{5,1},{6,2},{7,3},{8,4},{9,5},{1... | collective-permute-start | bytes 1572872 | tf_op jit(solution)/shard_map/ppermute | solution.py:381
  119.2 1.2 collective-permute-start.16
  121.2 10.0 %collective-permute-done.27.refs_0_.refs_8_ = bf16[1024,256]{1,0:T(8,128)(2,1)S(1)} collective-permute-done((bf16[1024,256]{1,0:T(8,128)(2,1)}, bf16[1024,256]{1,0:T(8,128)(2,1)S(1)}, u32[]{:S(2)}, u32[]{:S(2)}) %collective-permute-start.27) | collective-permute-done | bytes 524320 | tf_op jit(solution)/shard_map/ppermute | solution.py:381
  133.1 1.5 collective-permute-done.20.refs_1_.refs_10_
  135.6 16.7 %shard_map.83 = (f32[768,1024]{1,0:T(8,128)}, f32[768,1024]{1,0:T(8,128)}) custom-call(bf16[768,3072]{1,0:T(8,128)(2,1)} %get-tuple-element.38.refs_0_, bf16[768,3072]{1,0:T(8,128)(2,1)} %collective-permute-done.1.refs_1_, bf16[352,1024]{1,0:T(8,128)(2,1)} %copy-done.9, bf16[224,1024]{1,0:T(8,128)(2,1)} %pad_maximum_fusion.3.refs_3_, ...), custom_call_target="tpu_custom_call" | custom-call | tf_op jit(solution)/shard_map/pallas_call | solution.py:193
  152.4 10.8 %shard_map.84 = (f32[768,1024]{1,0:T(8,128)}, f32[768,1024]{1,0:T(8,128)}) custom-call(bf16[768,1024]{1,0:T(8,128)(2,1)} %get-tuple-element.36.refs_0_.refs_4_, bf16[768,1024]{1,0:T(8,128)(2,1)} %collective-permute-done.refs_1_, f32[768,1024]{1,0:T(8,128)} %get-tuple-element.46.refs_2_, f32[768,1024]{1,0:T(8,128)} %get-tuple-element.47.refs_3_, ...), custom_call_target="tpu_custom_call" | custom-call | tf_op jit(solution)/shard_map/pallas_call | solution.py:193
  174.0 14.6 %collective-permute-done.23.refs_1_.refs_11_ = bf16[1024,256]{1,0:T(8,128)(2,1)S(1)} collective-permute-done((bf16[1024,256]{1,0:T(8,128)(2,1)S(1)}, bf16[1024,256]{1,0:T(8,128)(2,1)S(1)}, u32[]{:S(2)}, u32[]{:S(2)}) %collective-permute-start.23) | collective-permute-done | bytes 524320 | tf_op jit(solution)/shard_map/ppermute | solution.py:384
  189.3 1.3 collective-permute-start.24
  191.4 1.5 collective-permute-start.26
  194.2 7.3 %collective-permute-done.24.refs_9_ = bf16[1024,256]{1,0:T(8,128)(2,1)S(1)} collective-permute-done((bf16[1024,256]{1,0:T(8,128)(2,1)S(1)}, bf16[1024,256]{1,0:T(8,128)(2,1)S(1)}, u32[]{:S(2)}, u32[]{:S(2)}) %collective-permute-start.24) | collective-permute-done | bytes 524320 | tf_op jit(solution)/shard_map/ppermute | solution.py:390
  204.3 2.9 %collective-permute-done.28.refs_9_ = bf16[512,256]{1,0:T(8,128)(2,1)S(1)} collective-permute-done((bf16[512,256]{1,0:T(8,128)(2,1)S(1)}, bf16[512,256]{1,0:T(8,128)(2,1)S(1)}, u32[]{:S(2)}, u32[]{:S(2)}) %collective-permute-start.28) | collective-permute-done | bytes 262176 | tf_op jit(solution)/shard_map/ppermute | solution.py:390
  207.2 5.7 %collective-permute-start.32 = (bf16[512,256]{1,0:T(8,128)(2,1)S(1)}, bf16[512,256]{1,0:T(8,128)(2,1)S(1)}, u32[]{:S(2)}, u32[]{:S(2)}) collective-permute-start(bf16[512,256]{1,0:T(8,128)(2,1)S(1)} %collective-permute-done.28.refs_9_), channel_id=1, source_target_pairs={{0,1},{1,0},{2,3},{3,2},{4,5},{5,4},{6,7},{7,6},{8,9},{9,8},{10,11... | collective-permute-start | bytes 786440 | tf_op jit(solution)/shard_map/ppermute | solution.py:387
  212.9 3.0 %collective-permute-start.34 = (bf16[512,256]{1,0:T(8,128)(2,1)S(1)}, bf16[512,256]{1,0:T(8,128)(2,1)S(1)}, u32[]{:S(2)}, u32[]{:S(2)}) collective-permute-start(bf16[512,256]{1,0:T(8,128)(2,1)S(1)} %collective-permute-done.30.refs_11_), channel_id=1, source_target_pairs={{0,1},{1,0},{2,3},{3,2},{4,5},{5,4},{6,7},{7,6},{8,9},{9,8},{10,11... | collective-permute-start | bytes 786440 | tf_op jit(solution)/shard_map/ppermute | solution.py:387
  216.5 10.7 %shard_map.89 = (f32[768,64]{1,0:T(8,128)}, f32[768,64]{1,0:T(8,128)}) custom-call(s32[2,4]{1,0:T(2,128)} %pad_add_fusion.ends_ref, s32[2,4]{1,0:T(2,128)} %copy-done.8, bf16[768,3072]{1,0:T(8,128)(2,1)} %get-tuple-element.38.refs_0_, bf16[768,3072]{1,0:T(8,128)(2,1)} %collective-permute-done.1.refs_1_, bf16[1024,256]{1,0:T(8,128)(2,1)} %get-tuple-element.63.refs_2_, ...), custom_call_target="tpu_custom_call" | custom-call | tf_op jit(solution)/shard_map/pallas_call | solution.py:266
  230.2 12.6 %shard_map.92 = bf16[768,1024]{1,0:T(8,128)(2,1)} custom-call(s32[4]{0:T(128)} %copy-done.29, s32[4]{0:T(128)} %bitcast.113, s32[2,16]{1,0:T(2,128)} %reshape.14.at_ref, f32[768,1024]{1,0:T(8,128)} %get-tuple-element.52.refs_0_, f32[768,1024]{1,0:T(8,128)} %collective-permute-done.17.refs_1_, f32[768,64]{1,0:T(8,128)} %get-tuple-element.61.refs_2_, ...), custom_call_target="tpu_custom_call" | custom-call | tf_op jit(solution)/shard_map/pallas_call | solution.py:343
  (158 shorter events, 40.9 us)
Async XLA Ops:
  18.0 32.2 %collective-permute-start.1 = (bf16[768,3072]{1,0:T(8,128)(2,1)}, bf16[768,3072]{1,0:T(8,128)(2,1)}, u32[]{:S(2)}, u32[]{:S(2)}) collective-permute-start(bf16[768,3072]{1,0:T(8,128)(2,1)} %get-tuple-element.39), channel_id=1, source_target_pairs={{0,1},{1,0},{2,3},{3,2},{4,5},{5,4},{6,7},{7,6},{8,9},{9,8},{10,11... | collective-permute-start | bytes 14155784 | tf_op jit(solution)/shard_map/ppermute | solution.py:387
  20.7 17.9 %collective-permute-start.2 = (bf16[352,1024]{1,0:T(8,128)(2,1)S(1)}, bf16[352,1024]{1,0:T(8,128)(2,1)S(1)}, u32[]{:S(2)}, u32[]{:S(2)}) collective-permute-start(bf16[352,1024]{1,0:T(8,128)(2,1)S(1)} %pad_maximum_fusion.2.refs_2_), channel_id=1, source_target_pairs={{0,2},{1,3},{2,0},{3,1},{4,6},{5,7},{6,4},{7,5},{8,10},{9,11},{10,... | collective-permute-start | bytes 2162696 | tf_op jit(solution)/shard_map/ppermute | solution.py:384
  22.0 20.1 %collective-permute-start.6 = (bf16[352,1024]{1,0:T(8,128)(2,1)S(1)}, bf16[352,1024]{1,0:T(8,128)(2,1)}, u32[]{:S(2)}, u32[]{:S(2)}) collective-permute-start(bf16[352,1024]{1,0:T(8,128)(2,1)S(1)} %pad_maximum_fusion.2.refs_2_), channel_id=1, source_target_pairs={{0,4},{1,5},{2,6},{3,7},{4,8},{5,9},{6,10},{7,11},{8,12},{9,13},{1... | collective-permute-start | bytes 2162696 | tf_op jit(solution)/shard_map/ppermute | solution.py:381
  23.3 33.7 %collective-permute-start.7 = (bf16[352,1024]{1,0:T(8,128)(2,1)S(1)}, bf16[352,1024]{1,0:T(8,128)(2,1)}, u32[]{:S(2)}, u32[]{:S(2)}) collective-permute-start(bf16[352,1024]{1,0:T(8,128)(2,1)S(1)} %pad_maximum_fusion.2.refs_2_), channel_id=1, source_target_pairs={{0,12},{1,13},{2,14},{3,15},{4,0},{5,1},{6,2},{7,3},{8,4},{9,5},{1... | collective-permute-start | bytes 2162696 | tf_op jit(solution)/shard_map/ppermute | solution.py:381
  26.2 12.4 %collective-permute-start.4 = (s32[2,4]{1,0:T(2,128)S(1)}, s32[2,4]{1,0:T(2,128)S(1)}, u32[]{:S(2)}, u32[]{:S(2)}) collective-permute-start(s32[2,4]{1,0:T(2,128)S(1)} %pad_add_fusion.2.slots_ref), channel_id=1, source_target_pairs={{0,16},{16,0},{1,17},{17,1},{2,18},{18,2},{3,19},{19,3},{4,20},{20... | collective-permute-start | bytes 104 | tf_op jit(solution)/shard_map/ppermute | solution.py:390
  38.7 11.5 %collective-permute-start.5 = (bf16[224,1024]{1,0:T(8,128)(2,1)S(1)}, bf16[224,1024]{1,0:T(8,128)(2,1)S(1)}, u32[]{:S(2)}, u32[]{:S(2)}) collective-permute-start(bf16[224,1024]{1,0:T(8,128)(2,1)S(1)} %slice.92), channel_id=1, source_target_pairs={{0,16},{16,0},{1,17},{17,1},{2,18},{18,2},{3,19},{19,3},{4,20},{20... | collective-permute-start | bytes 1376264 | tf_op jit(solution)/shard_map/ppermute | solution.py:390
  40.8 19.4 %collective-permute-start.10 = (bf16[1024,256]{1,0:T(8,128)(2,1)}, bf16[1024,256]{1,0:T(8,128)(2,1)S(1)}, u32[]{:S(2)}, u32[]{:S(2)}) collective-permute-start(bf16[1024,256]{1,0:T(8,128)(2,1)} %get-tuple-element.63.refs_2_), channel_id=1, source_target_pairs={{0,2},{1,3},{2,0},{3,1},{4,6},{5,7},{6,4},{7,5},{8,10},{9,11},{10,... | collective-permute-start | bytes 1572872 | tf_op jit(solution)/shard_map/ppermute | solution.py:384
  42.1 43.7 %collective-permute-start.13 = (bf16[352,1024]{1,0:T(8,128)(2,1)S(1)}, bf16[352,1024]{1,0:T(8,128)(2,1)}, u32[]{:S(2)}, u32[]{:S(2)}) collective-permute-start(bf16[352,1024]{1,0:T(8,128)(2,1)S(1)} %pad_maximum_fusion.2.refs_2_), channel_id=1, source_target_pairs={{0,8},{1,9},{2,10},{3,11},{4,12},{5,13},{6,14},{7,15},{8,0},{9,1},... | collective-permute-start | bytes 2162696 | tf_op jit(solution)/shard_map/ppermute | solution.py:381
  50.2 35.8 %collective-permute-start.9 = (bf16[352,1024]{1,0:T(8,128)(2,1)}, bf16[352,1024]{1,0:T(8,128)(2,1)}, u32[]{:S(2)}, u32[]{:S(2)}) collective-permute-start(bf16[352,1024]{1,0:T(8,128)(2,1)} %collective-permute-done.6.refs_6_), channel_id=1, source_target_pairs={{0,2},{1,3},{2,0},{3,1},{4,6},{5,7},{6,4},{7,5},{8,10},{9,11},{10,... | collective-permute-start | bytes 2162696 | tf_op jit(solution)/shard_map/ppermute | solution.py:384
  59.0 39.3 %collective-permute-start.8 = (bf16[448,1024]{1,0:T(8,128)(2,1)}, bf16[448,1024]{1,0:T(8,128)(2,1)}, u32[]{:S(2)}, u32[]{:S(2)}) collective-permute-start(bf16[448,1024]{1,0:T(8,128)(2,1)} %pad_maximum_fusion), channel_id=1, source_target_pairs={{0,16},{16,0},{1,17},{17,1},{2,18},{18,2},{3,19},{19,3},{4,20},{20... | collective-permute-start | bytes 2752520 | tf_op jit(solution)/shard_map/ppermute | solution.py:390
  60.2 40.5 %collective-permute-start.11 = (bf16[352,1024]{1,0:T(8,128)(2,1)}, bf16[352,1024]{1,0:T(8,128)(2,1)}, u32[]{:S(2)}, u32[]{:S(2)}) collective-permute-start(bf16[352,1024]{1,0:T(8,128)(2,1)} %collective-permute-done.7.refs_10_), channel_id=1, source_target_pairs={{0,2},{1,3},{2,0},{3,1},{4,6},{5,7},{6,4},{7,5},{8,10},{9,11},{10,... | collective-permute-start | bytes 2162696 | tf_op jit(solution)/shard_map/ppermute | solution.py:384
  60.4 36.6 %collective-permute-start.19 = (bf16[1024,256]{1,0:T(8,128)(2,1)}, bf16[1024,256]{1,0:T(8,128)(2,1)S(1)}, u32[]{:S(2)}, u32[]{:S(2)}) collective-permute-start(bf16[1024,256]{1,0:T(8,128)(2,1)} %get-tuple-element.63.refs_2_), channel_id=1, source_target_pairs={{0,4},{1,5},{2,6},{3,7},{4,8},{5,9},{6,10},{7,11},{8,12},{9,13},{1... | collective-permute-start | bytes 1572872 | tf_op jit(solution)/shard_map/ppermute | solution.py:381
  85.7 66.6 %collective-permute-start = (bf16[768,1024]{1,0:T(8,128)(2,1)}, bf16[768,1024]{1,0:T(8,128)(2,1)}, u32[]{:S(2)}, u32[]{:S(2)}) collective-permute-start(bf16[768,1024]{1,0:T(8,128)(2,1)} %get-tuple-element.37.refs_5_), channel_id=1, source_target_pairs={{0,1},{1,0},{2,3},{3,2},{4,5},{5,4},{6,7},{7,6},{8,9},{9,8},{10,11... | collective-permute-start | bytes 4718600 | tf_op jit(solution)/shard_map/ppermute | solution.py:387
  86.0 18.4 %collective-permute-start.15 = (bf16[352,1024]{1,0:T(8,128)(2,1)}, bf16[352,1024]{1,0:T(8,128)(2,1)S(1)}, u32[]{:S(2)}, u32[]{:S(2)}) collective-permute-start(bf16[352,1024]{1,0:T(8,128)(2,1)} %collective-permute-done.13.refs_4_), channel_id=1, source_target_pairs={{0,2},{1,3},{2,0},{3,1},{4,6},{5,7},{6,4},{7,5},{8,10},{9,11},{10,... | collective-permute-start | bytes 2162696 | tf_op jit(solution)/shard_map/ppermute | solution.py:384
  97.1 34.1 %collective-permute-start.27 = (bf16[1024,256]{1,0:T(8,128)(2,1)}, bf16[1024,256]{1,0:T(8,128)(2,1)S(1)}, u32[]{:S(2)}, u32[]{:S(2)}) collective-permute-start(bf16[1024,256]{1,0:T(8,128)(2,1)} %get-tuple-element.63.refs_2_), channel_id=1, source_target_pairs={{0,8},{1,9},{2,10},{3,11},{4,12},{5,13},{6,14},{7,15},{8,0},{9,1},... | collective-permute-start | bytes 1572872 | tf_op jit(solution)/shard_map/ppermute | solution.py:381
  98.3 20.8 %collective-permute-start.14 = (bf16[224,1024]{1,0:T(8,128)(2,1)S(1)}, bf16[224,1024]{1,0:T(8,128)(2,1)S(1)}, u32[]{:S(2)}, u32[]{:S(2)}) collective-permute-start(bf16[224,1024]{1,0:T(8,128)(2,1)S(1)} %slice.97), channel_id=1, source_target_pairs={{0,16},{16,0},{1,17},{17,1},{2,18},{18,2},{3,19},{19,3},{4,20},{20... | collective-permute-start | bytes 1376264 | tf_op jit(solution)/shard_map/ppermute | solution.py:390
  101.8 33.8 %collective-permute-start.12 = (bf16[448,1024]{1,0:T(8,128)(2,1)S(1)}, bf16[448,1024]{1,0:T(8,128)(2,1)}, u32[]{:S(2)}, u32[]{:S(2)}) collective-permute-start(bf16[448,1024]{1,0:T(8,128)(2,1)S(1)} %pad_maximum_fusion.1), channel_id=1, source_target_pairs={{0,16},{16,0},{1,17},{17,1},{2,18},{18,2},{3,19},{19,3},{4,20},{20... | collective-permute-start | bytes 2752520 | tf_op jit(solution)/shard_map/ppermute | solution.py:390
  104.4 30.3 %collective-permute-start.20 = (bf16[1024,256]{1,0:T(8,128)(2,1)}, bf16[1024,256]{1,0:T(8,128)(2,1)S(1)}, u32[]{:S(2)}, u32[]{:S(2)}) collective-permute-start(bf16[1024,256]{1,0:T(8,128)(2,1)} %get-tuple-element.63.refs_2_), channel_id=1, source_target_pairs={{0,12},{1,13},{2,14},{3,15},{4,0},{5,1},{6,2},{7,3},{8,4},{9,5},{1... | collective-permute-start | bytes 1572872 | tf_op jit(solution)/shard_map/ppermute | solution.py:381
  119.2 33.2 %collective-permute-start.16 = (bf16[224,1024]{1,0:T(8,128)(2,1)}, bf16[224,1024]{1,0:T(8,128)(2,1)}, u32[]{:S(2)}, u32[]{:S(2)}) collective-permute-start(bf16[224,1024]{1,0:T(8,128)(2,1)} %slice.98), channel_id=1, source_target_pairs={{0,16},{16,0},{1,17},{17,1},{2,18},{18,2},{3,19},{19,3},{4,20},{20... | collective-permute-start | bytes 1376264 | tf_op jit(solution)/shard_map/ppermute | solution.py:390
  131.2 33.0 %collective-permute-start.22 = (bf16[1024,256]{1,0:T(8,128)(2,1)S(1)}, bf16[1024,256]{1,0:T(8,128)(2,1)S(1)}, u32[]{:S(2)}, u32[]{:S(2)}) collective-permute-start(bf16[1024,256]{1,0:T(8,128)(2,1)S(1)} %collective-permute-done.19.refs_0_.refs_6_), channel_id=1, source_target_pairs={{0,2},{1,3},{2,0},{3,1},{4,6},{5,7},{6,4},{7,5},{8,10},{9,11},{10,... | collective-permute-start | bytes 1572872 | tf_op jit(solution)/shard_map/ppermute | solution.py:384
  134.7 68.1 %collective-permute-start.31 = (bf16[1024,256]{1,0:T(8,128)(2,1)S(1)}, bf16[1024,256]{1,0:T(8,128)(2,1)}, u32[]{:S(2)}, u32[]{:S(2)}) collective-permute-start(bf16[1024,256]{1,0:T(8,128)(2,1)S(1)} %collective-permute-done.27.refs_0_.refs_8_), channel_id=1, source_target_pairs={{0,1},{1,0},{2,3},{3,2},{4,5},{5,4},{6,7},{7,6},{8,9},{9,8},{10,11... | collective-permute-start | bytes 1572872 | tf_op jit(solution)/shard_map/ppermute | solution.py:387
  163.1 66.2 %collective-permute-start.17 = (f32[768,1024]{1,0:T(8,128)}, f32[768,1024]{1,0:T(8,128)}, u32[]{:S(2)}, u32[]{:S(2)}) collective-permute-start(f32[768,1024]{1,0:T(8,128)} %get-tuple-element.53), channel_id=1, source_target_pairs={{0,1},{1,0},{2,3},{3,2},{4,5},{5,4},{6,7},{7,6},{8,9},{9,8},{10,11... | collective-permute-start | bytes 9437192 | tf_op jit(solution)/shard_map/ppermute | solution.py:387
  164.2 27.2 %collective-permute-start.29 = (bf16[1024,256]{1,0:T(8,128)(2,1)S(1)}, bf16[1024,256]{1,0:T(8,128)(2,1)S(1)}, u32[]{:S(2)}, u32[]{:S(2)}) collective-permute-start(bf16[1024,256]{1,0:T(8,128)(2,1)S(1)} %collective-permute-done.27.refs_0_.refs_8_), channel_id=1, source_target_pairs={{0,2},{1,3},{2,0},{3,1},{4,6},{5,7},{6,4},{7,5},{8,10},{9,11},{10,... | collective-permute-start | bytes 1572872 | tf_op jit(solution)/shard_map/ppermute | solution.py:384
  164.6 24.0 %collective-permute-start.23 = (bf16[1024,256]{1,0:T(8,128)(2,1)S(1)}, bf16[1024,256]{1,0:T(8,128)(2,1)S(1)}, u32[]{:S(2)}, u32[]{:S(2)}) collective-permute-start(bf16[1024,256]{1,0:T(8,128)(2,1)S(1)} %collective-permute-done.20.refs_1_.refs_10_), channel_id=1, source_target_pairs={{0,2},{1,3},{2,0},{3,1},{4,6},{5,7},{6,4},{7,5},{8,10},{9,11},{10,... | collective-permute-start | bytes 1572872 | tf_op jit(solution)/shard_map/ppermute | solution.py:384
  165.7 8.0 %collective-permute-start.18 = (bf16[512,256]{1,0:T(8,128)(2,1)S(1)}, bf16[512,256]{1,0:T(8,128)(2,1)S(1)}, u32[]{:S(2)}, u32[]{:S(2)}) collective-permute-start(bf16[512,256]{1,0:T(8,128)(2,1)S(1)} %shard_map.86), channel_id=1, source_target_pairs={{0,16},{16,0},{1,17},{17,1},{2,18},{18,2},{3,19},{19,3},{4,20},{20... | collective-permute-start | bytes 786440 | tf_op jit(solution)/shard_map/ppermute | solution.py:390
  173.7 19.2 %collective-permute-start.21 = (bf16[1024,256]{1,0:T(8,128)(2,1)S(1)}, bf16[1024,256]{1,0:T(8,128)(2,1)S(1)}, u32[]{:S(2)}, u32[]{:S(2)}) collective-permute-start(bf16[1024,256]{1,0:T(8,128)(2,1)S(1)} %shard_map.87), channel_id=1, source_target_pairs={{0,16},{16,0},{1,17},{17,1},{2,18},{18,2},{3,19},{19,3},{4,20},{20... | collective-permute-start | bytes 1572872 | tf_op jit(solution)/shard_map/ppermute | solution.py:390
  189.3 12.3 %collective-permute-start.24 = (bf16[1024,256]{1,0:T(8,128)(2,1)S(1)}, bf16[1024,256]{1,0:T(8,128)(2,1)S(1)}, u32[]{:S(2)}, u32[]{:S(2)}) collective-permute-start(bf16[1024,256]{1,0:T(8,128)(2,1)S(1)} %shard_map.88), channel_id=1, source_target_pairs={{0,16},{16,0},{1,17},{17,1},{2,18},{18,2},{3,19},{19,3},{4,20},{20... | collective-permute-start | bytes 1572872 | tf_op jit(solution)/shard_map/ppermute | solution.py:390
  191.4 37.9 %collective-permute-start.26 = (bf16[512,1024]{1,0:T(8,128)(2,1)S(1)}, bf16[512,1024]{1,0:T(8,128)(2,1)}, u32[]{:S(2)}, u32[]{:S(2)}) collective-permute-start(bf16[512,1024]{1,0:T(8,128)(2,1)S(1)} %slice_dynamic-update-slice_fusion.refs_6_), channel_id=1, source_target_pairs={{0,1},{1,0},{2,3},{3,2},{4,5},{5,4},{6,7},{7,6},{8,9},{9,8},{10,11... | collective-permute-start | bytes 3145736 | tf_op jit(solution)/shard_map/ppermute | solution.py:387
  192.9 34.3 %collective-permute-start.33 = (bf16[1024,256]{1,0:T(8,128)(2,1)S(1)}, bf16[1024,256]{1,0:T(8,128)(2,1)S(1)}, u32[]{:S(2)}, u32[]{:S(2)}) collective-permute-start(bf16[1024,256]{1,0:T(8,128)(2,1)S(1)} %collective-permute-done.29.refs_0_.refs_10_), channel_id=1, source_target_pairs={{0,1},{1,0},{2,3},{3,2},{4,5},{5,4},{6,7},{7,6},{8,9},{9,8},{10,11... | collective-permute-start | bytes 1572872 | tf_op jit(solution)/shard_map/ppermute | solution.py:387
  202.8 10.1 %collective-permute-start.30 = (bf16[512,256]{1,0:T(8,128)(2,1)S(1)}, bf16[512,256]{1,0:T(8,128)(2,1)S(1)}, u32[]{:S(2)}, u32[]{:S(2)}) collective-permute-start(bf16[512,256]{1,0:T(8,128)(2,1)S(1)} %shard_map.91), channel_id=1, source_target_pairs={{0,16},{16,0},{1,17},{17,1},{2,18},{18,2},{3,19},{19,3},{4,20},{20... | collective-permute-start | bytes 786440 | tf_op jit(solution)/shard_map/ppermute | solution.py:390
  207.2 22.0 %collective-permute-start.32 = (bf16[512,256]{1,0:T(8,128)(2,1)S(1)}, bf16[512,256]{1,0:T(8,128)(2,1)S(1)}, u32[]{:S(2)}, u32[]{:S(2)}) collective-permute-start(bf16[512,256]{1,0:T(8,128)(2,1)S(1)} %collective-permute-done.28.refs_9_), channel_id=1, source_target_pairs={{0,1},{1,0},{2,3},{3,2},{4,5},{5,4},{6,7},{7,6},{8,9},{9,8},{10,11... | collective-permute-start | bytes 786440 | tf_op jit(solution)/shard_map/ppermute | solution.py:387
  212.9 16.4 %collective-permute-start.34 = (bf16[512,256]{1,0:T(8,128)(2,1)S(1)}, bf16[512,256]{1,0:T(8,128)(2,1)S(1)}, u32[]{:S(2)}, u32[]{:S(2)}) collective-permute-start(bf16[512,256]{1,0:T(8,128)(2,1)S(1)} %collective-permute-done.30.refs_11_), channel_id=1, source_target_pairs={{0,1},{1,0},{2,3},{3,2},{4,5},{5,4},{6,7},{7,6},{8,9},{9,8},{10,11... | collective-permute-start | bytes 786440 | tf_op jit(solution)/shard_map/ppermute | solution.py:387
  (36 other events, 980.6 us)

commit v4 on v3

--- a/solution.py
+++ b/solution.py
@@ -97,7 +97,7 @@
 
 def norm_in_order(tokens, gain, source, widths):
     rows, width = tokens.shape
-    block = 64
+    block = 128
     return pl.pallas_call(
         norm_kernel,
         out_shape=[jax.ShapeDtypeStruct((rows, w), jnp.bfloat16) for w in widths],
@@ -179,23 +179,25 @@
     for n in range(0, held_ref.shape[1], columns):
         cols = slice(n, n + columns)
         acc = jnp.dot(both, held_ref[:, cols], preferred_element_type=jnp.float32)
-        for side in range(2):
-            term = acc[side * tile : (side + 1) * tile]
-            if has_sum:
-                term += sum_refs[side][:, cols]
-            out_refs[side][:, cols] = term
+        terms = [acc[:tile], acc[tile:]]
+        if has_sum:
+            terms[0] += sum_refs[0][:, cols]
+            terms[1] += sum_refs[1 + n // columns][...]
+        out_refs[0][:, cols] = terms[0]
+        out_refs[1 + n // columns][...] = terms[1]
 
 
 def value_sums(own, far, arrays, plan, width, sums=()):
     rows, depth = own.shape
-    tile = rows_tile(rows)
-    out = jax.ShapeDtypeStruct((rows, width), jnp.float32)
+    tile, columns = rows_tile(rows), 256
+    outs = [jax.ShapeDtypeStruct((rows, width), jnp.float32)]
+    outs += [jax.ShapeDtypeStruct((rows, columns), jnp.float32)] * (width // columns)
     return pl.pallas_call(
-        functools.partial(value_kernel, plan, 256, len(sums), len(arrays)),
-        out_shape=(out, out),
+        functools.partial(value_kernel, plan, columns, len(sums), len(arrays)),
+        out_shape=outs,
         grid=(rows // tile,),
         in_specs=[tiled(b, tile) for b in (own, far, *sums)] + [far_memory()] * len(arrays),
-        out_specs=[tiled(out, tile)] * 2,
+        out_specs=[tiled(o, tile) for o in outs],
         scratch_shapes=[
             pltpu.VMEM((depth, width), jnp.bfloat16),
             pltpu.SemaphoreType.DMA((len(plan),)),
@@ -203,6 +205,31 @@
         compiler_params=pltpu.CompilerParams(vmem_limit_bytes=vmem),
         cost_estimate=light,
     )(own, far, *sums, *arrays)
+
+
+def gather_kernel(plan, *refs):
+    array_refs, out_ref, sem = refs[:-2], refs[-2], refs[-1]
+    copies = [
+        pltpu.make_async_copy(array_refs[i].at[a:b, :], out_ref.at[row : row + b - a, :], sem.at[j])
+        for j, (i, a, b, row) in enumerate(plan)
+    ]
+    for copy in copies:
+        copy.start()
+    for copy in copies:
+        copy.wait()
+
+
+def gather_rows(arrays, plan):
+    rows = sum(b - a for _, a, b, _ in plan)
+    return pl.pallas_call(
+        functools.partial(gather_kernel, plan),
+        out_shape=jax.ShapeDtypeStruct((rows, arrays[0].shape[1]), arrays[0].dtype),
+        in_specs=[far_memory()] * len(arrays),
+        out_specs=pl.BlockSpec(memory_space=pltpu.VMEM),
+        scratch_shapes=[pltpu.SemaphoreType.DMA((len(plan),))],
+        compiler_params=pltpu.CompilerParams(vmem_limit_bytes=12 << 20),
+        cost_estimate=light,
+    )(*arrays)
 
 
 def load_all(array_refs, held_refs, sem, first=0):
@@ -280,8 +307,9 @@
     )(ends, slots, own, far, *arrays)
 
 
-def last_kernel(rank, parts, arrays, slots_ref, ends_ref, at_ref, *refs):
-    sum_refs, mid_refs, token_refs, refs = refs[:2], refs[2:4], refs[4:6], refs[6:]
+def last_kernel(rank, parts, sums, arrays, slots_ref, ends_ref, at_ref, *refs):
+    sum_refs, refs = refs[:sums], refs[sums:]
+    mid_refs, token_refs, refs = refs[:2], refs[2:4], refs[4:]
     up_refs, array_refs, out_ref = refs[:2], refs[2 : 2 + arrays], refs[2 + arrays]
     held_refs, rhs_refs, up_ref, sem = refs[3 + arrays : -4], refs[-4:-2], refs[-2], refs[-1]
     docs = slots_ref.shape[0]
@@ -326,11 +354,11 @@
     adapter = lax.broadcasted_iota(jnp.int32, (tile, flat), 1) // rank
     spread = jnp.where(slot == adapter, jnp.concatenate([mid] * (flat // rank), 1), 0.0)
     spread = spread.astype(jnp.bfloat16)
-    columns = 256
+    columns = sum_refs[1].shape[1]
     for n in range(0, width, columns):
         cols = slice(n, n + columns)
         delta = lax.dot_general(spread, up_ref[cols, :], nt, preferred_element_type=jnp.float32)
-        base = sum_refs[0][:, cols] + sum_refs[1][:, cols]
+        base = sum_refs[0][:, cols] + sum_refs[1 + n // columns][...]
         out_ref[:, cols] = (base + adapter_scale * delta).astype(out_ref.dtype)
 
 
@@ -341,7 +369,7 @@
     tile = rows_tile(rows)
     docs = slots.shape[0]
     return pl.pallas_call(
-        functools.partial(last_kernel, rank, parts, len(arrays)),
+        functools.partial(last_kernel, rank, parts, len(sums), len(arrays)),
         out_shape=jax.ShapeDtypeStruct((rows, width), jnp.bfloat16),
         grid_spec=pltpu.PrefetchScalarGridSpec(
             num_scalar_prefetch=3,
@@ -390,12 +418,12 @@
         return lax.ppermute(value, "groups", [(g, g ^ 1) for g in range(groups)])
 
     class Line:
-        def __init__(self, send):
-            self.send, self.sent = send, []
+        def __init__(self, send, most=2):
+            self.send, self.most, self.sent = send, most, []
 
         def __call__(self, value, *args):
-            if len(self.sent) >= 2:
-                value = after(value, self.sent[-2])
+            if len(self.sent) >= self.most:
+                value = after(value, self.sent[-self.most])
             self.sent.append(self.send(value, *args))
             return self.sent[-1]
 
@@ -462,24 +490,24 @@
         d_miss = {(0, 0): (pick_adapters([d_rest], slots_both, rank), 0)}
         chosen = slots_both.size * rank
 
-        ks = []
+        order = [0]
         for k in range(1, depth // 2 + 1):
-            ks += [k, depth - k] if k != depth - k else [k]
-        last = ks[-1]
-        early = [k for k in ks if k != last]
-        z, y, x = Line(along_z), Line(along_y), Line(along_x)
+            order += [k, depth - k] if k != depth - k else [k]
+        names = [(k, dy) for k in order for dy in range(rows_y)]
+        z, y, x = Line(along_z), Line(along_y, 2), Line(along_x)
 
         def x_values(names, *earlier):
             got = x(after(jnp.concatenate([v_have[name][:cut] for name in names], 0), *earlier))
             for i, name in enumerate(names):
                 v_miss[name] = (got, i * cut)
 
-        def x_down(names):
-            got = x(pick_adapters([d_have[name] for name in names], slots_there, rank))
+        def x_down(names, *earlier):
+            pieces = [d_have[name] for name in names]
+            pieces[0] = after(pieces[0], *earlier)
+            got = x(pick_adapters(pieces, slots_there, rank))
             for i, name in enumerate(names):
-                d_miss[name] = (got, i * chosen)
-
-        names = [(k, dy) for k in [0] + ks for dy in range(rows_y)]
+                d_miss[name] = (got, i * slots_both.size * rank)
+
         source, up_at = [], []
         for lane_at in (mc, 1 - mc):
             for k, dy in names:
@@ -488,17 +516,59 @@
                     piece = c * lane + jnp.where(c * lane < half, 1, -1) * side * half
                     source.append(s * shard + piece)
                 up_at += [(2 * s + side) * bit, (2 * s + 1 - side) * bit]
+        source = jnp.stack(source).astype(jnp.int32)
         up_at = jnp.stack(up_at).astype(jnp.int32).reshape(2, -1)
-        bulk = (len(names) - rows_y) * shard
-        rest = rows_y * shard
+        first, second = names[: len(names) // 2], names[len(names) // 2 :]
+        span = len(first) * shard
+
+        def lay():
+            arrays = []
+
+            def place(array):
+                for i, known in enumerate(arrays):
+                    if known is array:
+                        return i
+                arrays.append(array)
+                return len(arrays) - 1
+
+            return arrays, place
+
+        def values(names):
+            arrays, place = lay()
+            plan = []
+            for i, name in enumerate(names):
+                h, (m, row) = place(v_have[name]), v_miss[name]
+                m, at = place(m), i * shard
+                plan += [
+                    (h, 0, part, at),
+                    (h, cut, cut + half - part, at + part),
+                    (m, row, row + part, at + half),
+                    (h, cut + half - part, cut + 2 * (half - part), at + half + part),
+                ]
+            return arrays, tuple(plan)
+
+        def ups(names):
+            arrays, place = lay()
+            plan = []
+            for i, name in enumerate(names):
+                h, (m, row) = place(v_have[name]), v_miss[name]
+                plan.append((h, part, cut, 2 * i * bit))
+                plan.append((place(m), row + part, row + cut, (2 * i + 1) * bit))
+            return gather_rows(arrays, tuple(plan))
+
+        def slabs(place, names, have, miss):
+            out = []
+            for i, name in enumerate(names):
+                m, row = miss[name]
+                out.append((i * shard, place(have[name]), place(m), row))
+            return tuple(out)
+
+        ks = order[1:]
+        early, last = ks[:-1], ks[-1]
         own, own_rest, other, other_rest = norm_in_order(
-            tokens,
-            input_norm_gain,
-            jnp.stack(source).astype(jnp.int32),
-            [bulk, rest] * 2,
+            tokens, input_norm_gain, source, [span] * 4
         )
         partner, partner_rest = across(other), across(other_rest)
-
         for k in ks:
             v_have[k, 0] = z(v_have[0, 0], k)
         for k in ks:
@@ -515,75 +585,40 @@
         x_down([(0, 1)])
         for k in early:
             d_have[k, 1] = y(d_have[k, 0])
-        x_values([(last, 1)])
+        arrays, plan = values(first)
+        sums = value_sums(after(own, v_have[last, 1]), partner, arrays, plan, width)
+        x_values([(last, 1)], sums[0])
         x_down([(k, 0) for k in early])
         x_down([(k, 1) for k in early])
         d_have[last, 1] = y(d_have[last, 0])
         x_down([(last, 0)])
-        x_down([(last, 1)])
-
-        def lay():
-            arrays = []
-
-            def place(array):
-                for i, known in enumerate(arrays):
-                    if known is array:
-                        return i
-                arrays.append(array)
-                return len(arrays) - 1
-
-            return arrays, place
-
-        def values(names, *args):
-            arrays, place = lay()
-            plan = []
-            for i, name in enumerate(names):
-                h, (m, row) = place(v_have[name]), v_miss[name]
-                m, at = place(m), i * shard
-                plan += [
-                    (h, 0, part, at),
-                    (h, cut, cut + half - part, at + part),
-                    (m, row, row + part, at + half),
-                    (h, cut + half - part, cut + 2 * (half - part), at + half + part),
-                ]
-            return arrays, tuple(plan)
-
-        arrays, plan = values(names[:-rows_y])
-        sums = value_sums(own, partner, arrays, plan, width)
-        arrays, plan = values(names[-rows_y:])
-        sum_own, sum_far = value_sums(own_rest, partner_rest, arrays, plan, width, sums)
-        sums = (sum_own, across(sum_far))
-
-        up_lane = []
-        for name in names:
-            miss, row = v_miss[name]
-            up_lane += [v_have[name][part:cut], miss[row + part : row + cut]]
-        up_lane = jnp.concatenate(up_lane, 0)
-        ups = (up_lane, across(up_lane))
-
-        def slabs(place, names, have, miss):
-            out = []
-            for i, name in enumerate(names):
-                m, row = miss[name]
-                out.append((i * shard, place(have[name]), place(m), row))
-            return tuple(out)
+
+        arrays, plan = values(second)
+        ready = [d_have[k, 0] for k in ks]
+        sum_own, *sum_far = value_sums(
+            after(own_rest, *ready), partner_rest, arrays, plan, width, sums
+        )
+        sums = (sum_own, *[across(part) for part in sum_far])
+        up_lane = ups(names)
+        up_both = (up_lane, across(up_lane))
 
         arrays, place = lay()
-        parts = slabs(place, names[:-rows_y], d_have, d_miss)
+        parts = slabs(place, first, d_have, d_miss)
         mid_own, mid_far = mid_partials(own, partner, arrays, parts, ends_both, slots_both, rank)
         mids = (mid_own, across(mid_far))
-
-        final = names[-rows_y:]
+        x_down([(last, 1)], mids[1], up_both[1])
+
         arrays, place = lay()
-        parts = [(0, slabs(place, final, d_have, d_miss))]
-        far_have = {n: across(d_have[n]) for n in final}
-        far_miss = {n: (across(d_miss[n][0]), d_miss[n][1]) for n in final}
-        parts.append((slots.shape[1], slabs(place, final, far_have, far_miss)))
+        parts = [(0, slabs(place, second, d_have, d_miss))]
+        done = d_have[last, 1]
+        far_have = {n: across(after(d_have[n], done)) for n in second}
+        far_miss = {n: (across(after(d_miss[n][0], done)), d_miss[n][1]) for n in second}
+        parts.append((slots.shape[1], slabs(place, second, far_have, far_miss)))
         return last_values(
             sums,
             mids,
             (own_rest, other_rest),
-            ups,
+            up_both,
             up_at,
             arrays,
             tuple(parts),

time: 246 us -> 256 us (1.041)
  waiting for transfers between devices: 95.3 us -> 114 us
  starting transfers between devices: 47.5 us -> 37.3 us
  Pallas kernels: 70 us -> 74.2 us
  local copies, waits for them, and re-layouts: 26.4 us -> 22.6 us
    ppermute x8, waiting for transfers between devices: 25.7 us -> 48.1 us  [along_y(): return lax.ppermute(value, 'store', pairs(lambda z, y, c: (z, 1 - y, c)))]
    ppermute x6, waiting for transfers between devices: 50.9 us -> 34.4 us  [along_z(): lax.ppermute(value, 'store', pairs(lambda z, y, c: ((z + k) % depth, y, c)))]
    ppermute x6, starting transfers between devices: 17.7 us -> 3.46 us  [along_z(): lax.ppermute(value, 'store', pairs(lambda z, y, c: ((z + k) % depth, y, c)))]
    ppermute x11, waiting for transfers between devices: 16.1 us -> 30.1 us  [along_x(): return lax.ppermute(value, 'groups', [(g, g ^ 1) for g in range(groups)])]
    ppermute x10 -> x17, starting transfers between devices: 12.9 us -> 19.5 us  [across(): return lax.ppermute(value, 'store', pairs(lambda z, y, c: (z, y, 1 - c)))]
    pallas_call x3 -> x4, Pallas kernels: 40 us -> 44.9 us  [the longest x2 26.2 us: value_sums(): pl.pallas_call(functools.partial(value_kernel, plan, columns, len(sums),...]
    pallas_call x6, Pallas kernels: 3.45 us -> 6.56 us  [pick_adapters(): pl.pallas_call(functools.partial(pick_kernel, rank), out_shape=jax.ShapeD...]
    unnamed x83 -> x104, local copies, waits for them, and re-layouts: 13.8 us -> 12 us
  transfers between devices with their start and end apart: 35 -> 42, of which waited for: 12 -> 16; matrix products, arithmetic and copies ran while one was open for 11% -> 6% of each run, Pallas kernels for 17% -> 17%
where the time goes in v4:
time: 256 us; the launch traced here: 253 us
  waiting for transfers between devices  114 us (45%)
  Pallas kernels  74.2 us (29%)
  starting transfers between devices  37.3 us (15%)
  local copies, waits for them, and re-layouts  22.6 us (9%)
  other arithmetic  4.64 us (2%)
    ppermute x8, waiting for transfers between devices, along_y(): return lax.ppermute(value, 'store', pairs(lambda z, y, c: (z, 1 - y, c)))  48.1 us
    ppermute x6, waiting for transfers between devices, along_z(): lax.ppermute(value, 'store', pairs(lambda z, y, c: ((z + k) % depth, y, c)))  34.4 us
    ppermute x11, waiting for transfers between devices, along_x(): return lax.ppermute(value, 'groups', [(g, g ^ 1) for g in range(groups)])  30.1 us
    pallas_call x2, Pallas kernels, value_sums(): pl.pallas_call(functools.partial(value_kernel, plan, columns, len(sums),...  26.2 us
    ppermute x17, starting transfers between devices, across(): return lax.ppermute(value, 'store', pairs(lambda z, y, c: (z, y, 1 - c)))  19.5 us
    pallas_call x1, Pallas kernels, last_values(): pl.pallas_call(functools.partial(last_kernel, rank, parts, len(sums), len...  16.8 us
    pallas_call x1, Pallas kernels, norm_in_order(): pl.pallas_call(norm_kernel, out_shape=[jax.ShapeDtypeStruct((rows, w), jn...  13.7 us
    unnamed x104, local copies, waits for them, and re-layouts  12 us
  transfers between devices with their start and end apart: 42, of which 16 were waited for; matrix products, arithmetic and copies ran while one was open for 6% of the time, Pallas kernels for 17%

profile of v4, /device:TPU:9, one launch (start us, length us, event | category | flops | bytes accessed | tf_op | source)
XLA Modules:
  0.0 253.0 jit_solution(12952478452177887747)
XLA Ops:
  0.0 1.3 reshape.15.gain_ref
  2.1 13.7 %shard_map.82 = (bf16[768,2048]{1,0:T(8,128)(2,1)}, bf16[768,2048]{1,0:T(8,128)(2,1)}, bf16[768,2048]{1,0:T(8,128)(2,1)}, bf16[768,2048]{1,0:T(8,128)(2,1)}) custom-call(s32[64]{0:T(128)} %stack.391.source_ref, bf16[768,8192]{1,0:T(8,128)(2,1)} %tokens_ref.1, bf16[1,8192]{1,0:T(2,128)(2,1)} %reshape.15.gain_ref), custom_call_target="tpu_custom_call" | custom-call | tf_op jit(solution)/shard_map/pallas_call | solution.py:101
  17.8 1.3 collective-permute-start.8
  19.1 1.3 collective-permute-start.2
  22.5 2.3 dynamic-slice_bitcast_fusion
  26.6 1.6 collective-permute-done.10.slots_ref
  28.5 7.2 %collective-permute-done.8.refs_4_.refs_2_ = bf16[352,1024]{1,0:T(8,128)(2,1)S(1)} collective-permute-done((bf16[352,1024]{1,0:T(8,128)(2,1)S(1)}, bf16[352,1024]{1,0:T(8,128)(2,1)S(1)}, u32[]{:S(2)}, u32[]{:S(2)}) %collective-permute-start.8) | collective-permute-done | bytes 720928 | tf_op jit(solution)/shard_map/ppermute | solution.py:412
  36.8 16.6 %collective-permute-done.refs_7_.refs_8_ = bf16[352,1024]{1,0:T(8,128)(2,1)S(1)} collective-permute-done((bf16[352,1024]{1,0:T(8,128)(2,1)S(1)}, bf16[352,1024]{1,0:T(8,128)(2,1)S(1)}, u32[]{:S(2)}, u32[]{:S(2)}) %collective-permute-start) | collective-permute-done | bytes 720928 | tf_op jit(solution)/shard_map/ppermute | solution.py:409
  55.7 9.3 %collective-permute-done.11.refs_5_.refs_3_ = bf16[224,1024]{1,0:T(8,128)(2,1)S(1)} collective-permute-done((bf16[224,1024]{1,0:T(8,128)(2,1)S(1)}, bf16[224,1024]{1,0:T(8,128)(2,1)S(1)}, u32[]{:S(2)}, u32[]{:S(2)}) %collective-permute-start.11) | collective-permute-done | bytes 458784 | tf_op jit(solution)/shard_map/ppermute | solution.py:418
  68.7 13.0 %collective-permute-done.12.refs_8_.refs_6_ = bf16[352,1024]{1,0:T(8,128)(2,1)S(1)} collective-permute-done((bf16[352,1024]{1,0:T(8,128)(2,1)}, bf16[352,1024]{1,0:T(8,128)(2,1)S(1)}, u32[]{:S(2)}, u32[]{:S(2)}) %collective-permute-start.12) | collective-permute-done | bytes 720928 | tf_op jit(solution)/shard_map/ppermute | solution.py:412
  81.7 15.4 %collective-permute-done.16.refs_9_ = bf16[352,1024]{1,0:T(8,128)(2,1)S(1)} collective-permute-done((bf16[352,1024]{1,0:T(8,128)(2,1)S(1)}, bf16[352,1024]{1,0:T(8,128)(2,1)S(1)}, u32[]{:S(2)}, u32[]{:S(2)}) %collective-permute-start.16) | collective-permute-done | bytes 720928 | tf_op jit(solution)/shard_map/ppermute | solution.py:412
  100.3 10.6 %collective-permute-done.3.refs_11_.refs_10_ = bf16[352,1024]{1,0:T(8,128)(2,1)} collective-permute-done((bf16[352,1024]{1,0:T(8,128)(2,1)S(1)}, bf16[352,1024]{1,0:T(8,128)(2,1)}, u32[]{:S(2)}, u32[]{:S(2)}) %collective-permute-start.3) | collective-permute-done | bytes 720928 | tf_op jit(solution)/shard_map/ppermute | solution.py:409
  113.1 1.9 slice.41
  115.0 7.2 %collective-permute-done.5.refs_0_.refs_15_ = bf16[1024,256]{1,0:T(8,128)(2,1)} collective-permute-done((bf16[1024,256]{1,0:T(8,128)(2,1)}, bf16[1024,256]{1,0:T(8,128)(2,1)}, u32[]{:S(2)}, u32[]{:S(2)}) %collective-permute-start.5) | collective-permute-done | bytes 524320 | tf_op jit(solution)/shard_map/ppermute | solution.py:409
  123.7 2.0 collective-permute-start.4
  126.5 11.9 %collective-permute-done.13.refs_13_.refs_12_ = bf16[352,1024]{1,0:T(8,128)(2,1)S(1)} collective-permute-done((bf16[352,1024]{1,0:T(8,128)(2,1)}, bf16[352,1024]{1,0:T(8,128)(2,1)S(1)}, u32[]{:S(2)}, u32[]{:S(2)}) %collective-permute-start.13) | collective-permute-done | bytes 720928 | tf_op jit(solution)/shard_map/ppermute | solution.py:412
  139.2 1.8 pad_maximum_fusion.3.refs_3_.refs_1_
  142.9 12.5 %shard_map.83 = (f32[768,1024]{1,0:T(8,128)}, f32[768,256]{1,0:T(8,128)}, f32[768,256]{1,0:T(8,128)}, f32[768,256]{1,0:T(8,128)}, f32[768,256]{1,0:T(8,128)}) custom-call(bf16[768,2048]{1,0:T(8,128)(2,1)} %get-tuple-element.67.refs_0_, bf16[768,2048]{1,0:T(8,128)(2,1)} %collective-permute-done.7.refs_1_, bf16[352,1024]{1,0:T(8,128)(2,1)} %copy-done.4, ...), custom_call_target="tpu_custom_call" | custom-call | tf_op jit(solution)/shard_map/pallas_call | solution.py:195
  159.3 3.4 %collective-permute-start.34 = (bf16[1024,256]{1,0:T(8,128)(2,1)}, bf16[1024,256]{1,0:T(8,128)(2,1)S(1)}, u32[]{:S(2)}, u32[]{:S(2)}) collective-permute-start(bf16[1024,256]{1,0:T(8,128)(2,1)} %collective-permute-done.4.refs_1_.refs_11_), channel_id=1, source_target_pairs={{0,1},{1,0},{2,3},{3,2},{4,5},{5,4},{6,7},{7,6},{8,9},{9,8},{10,11... | collective-permute-start | bytes 1572872 | tf_op jit(solution)/shard_map/ppermute | solution.py:415
  162.7 2.5 collective-permute-done.19.refs_14_.refs_13_
  169.7 1.9 shard_map.90.refs_9_
  171.7 6.3 %collective-permute-start.30 = (bf16[512,1024]{1,0:T(8,128)(2,1)S(1)}, bf16[512,1024]{1,0:T(8,128)(2,1)S(1)}, u32[]{:S(2)}, u32[]{:S(2)}) collective-permute-start(bf16[512,1024]{1,0:T(8,128)(2,1)S(1)} %shard_map.90.refs_9_), channel_id=1, source_target_pairs={{0,1},{1,0},{2,3},{3,2},{4,5},{5,4},{6,7},{7,6},{8,9},{9,8},{10,11... | collective-permute-start | bytes 3145736 | tf_op jit(solution)/shard_map/ppermute | solution.py:415
  178.0 1.6 shard_map.87
  183.9 13.7 %shard_map.84 = (f32[768,1024]{1,0:T(8,128)}, f32[768,256]{1,0:T(8,128)}, f32[768,256]{1,0:T(8,128)}, f32[768,256]{1,0:T(8,128)}, f32[768,256]{1,0:T(8,128)}) custom-call(bf16[768,2048]{1,0:T(8,128)(2,1)} %get-tuple-element.59.refs_0_.refs_7_, bf16[768,2048]{1,0:T(8,128)(2,1)} %collective-permute-done.6.refs_1_, f32[768,1024]{1,0:T(8,128)} %get-tuple-element.71.refs_2_, ...), custom_call_target="tpu_custom_call" | custom-call | tf_op jit(solution)/shard_map/pallas_call | solution.py:195
  198.1 6.4 %collective-permute-done.28.refs_9_.refs_14_ = bf16[1024,256]{1,0:T(8,128)(2,1)S(1)} collective-permute-done((bf16[1024,256]{1,0:T(8,128)(2,1)S(1)}, bf16[1024,256]{1,0:T(8,128)(2,1)S(1)}, u32[]{:S(2)}, u32[]{:S(2)}) %collective-permute-start.28) | collective-permute-done | bytes 524320 | tf_op jit(solution)/shard_map/ppermute | solution.py:418
  205.9 9.0 %shard_map.89 = (f32[768,64]{1,0:T(8,128)}, f32[768,64]{1,0:T(8,128)}) custom-call(s32[2,4]{1,0:T(2,128)} %pad_add_fusion.ends_ref, s32[2,4]{1,0:T(2,128)} %copy-done.29, bf16[768,2048]{1,0:T(8,128)(2,1)} %get-tuple-element.67.refs_0_, bf16[768,2048]{1,0:T(8,128)(2,1)} %collective-permute-done.7.refs_1_, bf16[1024,256]{1,0:T(8,128)(2,1)} %get-tuple-element.58.refs_2_, ...), custom_call_target="tpu_custom_call" | custom-call | tf_op jit(solution)/shard_map/pallas_call | solution.py:293
  215.2 1.6 shard_map.91
  218.1 1.6 shard_map.92
  219.8 5.1 %collective-permute-done.31.refs_16_ = bf16[512,256]{1,0:T(8,128)(2,1)S(1)} collective-permute-done((bf16[512,256]{1,0:T(8,128)(2,1)S(1)}, bf16[512,256]{1,0:T(8,128)(2,1)S(1)}, u32[]{:S(2)}, u32[]{:S(2)}) %collective-permute-start.31) | collective-permute-done | bytes 262176 | tf_op jit(solution)/shard_map/ppermute | solution.py:418
  226.6 5.2 %collective-permute-done.33.refs_18_ = bf16[512,256]{1,0:T(8,128)(2,1)S(1)} collective-permute-done((bf16[512,256]{1,0:T(8,128)(2,1)S(1)}, bf16[512,256]{1,0:T(8,128)(2,1)S(1)}, u32[]{:S(2)}, u32[]{:S(2)}) %collective-permute-start.33) | collective-permute-done | bytes 262176 | tf_op jit(solution)/shard_map/ppermute | solution.py:418
  231.8 1.9 collective-permute-start.37
  236.1 16.8 %shard_map.93 = bf16[768,1024]{1,0:T(8,128)(2,1)} custom-call(s32[4]{0:T(128)} %copy-done.47, s32[4]{0:T(128)} %bitcast.111, s32[2,16]{1,0:T(2,128)} %reshape.14.at_ref, f32[768,1024]{1,0:T(8,128)} %get-tuple-element.79.refs_0_, f32[768,256]{1,0:T(8,128)} %copy-done.35, f32[768,256]{1,0:T(8,128)} %copy-done.36, f32[768,256]{1,0:T(8,128)} %copy-done.37, ...), custom_call_target="tpu_custom_call" | custom-call | tf_op jit(solution)/shard_map/pallas_call | solution.py:371
  (193 shorter events, 44.4 us)
Async XLA Ops:
  15.8 49.3 %collective-permute-start.7 = (bf16[768,2048]{1,0:T(8,128)(2,1)}, bf16[768,2048]{1,0:T(8,128)(2,1)}, u32[]{:S(2)}, u32[]{:S(2)}) collective-permute-start(bf16[768,2048]{1,0:T(8,128)(2,1)} %get-tuple-element.62), channel_id=1, source_target_pairs={{0,1},{1,0},{2,3},{3,2},{4,5},{5,4},{6,7},{7,6},{8,9},{9,8},{10,11... | collective-permute-start | bytes 9437192 | tf_op jit(solution)/shard_map/ppermute | solution.py:415
  17.8 17.9 %collective-permute-start.8 = (bf16[352,1024]{1,0:T(8,128)(2,1)S(1)}, bf16[352,1024]{1,0:T(8,128)(2,1)S(1)}, u32[]{:S(2)}, u32[]{:S(2)}) collective-permute-start(bf16[352,1024]{1,0:T(8,128)(2,1)S(1)} %pad_maximum_fusion.2.refs_2_.refs_0_), channel_id=1, source_target_pairs={{0,2},{1,3},{2,0},{3,1},{4,6},{5,7},{6,4},{7,5},{8,10},{9,11},{10,... | collective-permute-start | bytes 2162696 | tf_op jit(solution)/shard_map/ppermute | solution.py:412
  19.1 35.5 %collective-permute-start.2 = (bf16[352,1024]{1,0:T(8,128)(2,1)S(1)}, bf16[352,1024]{1,0:T(8,128)(2,1)}, u32[]{:S(2)}, u32[]{:S(2)}) collective-permute-start(bf16[352,1024]{1,0:T(8,128)(2,1)S(1)} %pad_maximum_fusion.2.refs_2_.refs_0_), channel_id=1, source_target_pairs={{0,4},{1,5},{2,6},{3,7},{4,8},{5,9},{6,10},{7,11},{8,12},{9,13},{1... | collective-permute-start | bytes 2162696 | tf_op jit(solution)/shard_map/ppermute | solution.py:409
  20.4 33.1 %collective-permute-start = (bf16[352,1024]{1,0:T(8,128)(2,1)S(1)}, bf16[352,1024]{1,0:T(8,128)(2,1)S(1)}, u32[]{:S(2)}, u32[]{:S(2)}) collective-permute-start(bf16[352,1024]{1,0:T(8,128)(2,1)S(1)} %pad_maximum_fusion.2.refs_2_.refs_0_), channel_id=1, source_target_pairs={{0,12},{1,13},{2,14},{3,15},{4,0},{5,1},{6,2},{7,3},{8,4},{9,5},{1... | collective-permute-start | bytes 2162696 | tf_op jit(solution)/shard_map/ppermute | solution.py:409
  28.3 37.6 %collective-permute-start.15 = (bf16[1024,256]{1,0:T(8,128)(2,1)}, bf16[1024,256]{1,0:T(8,128)(2,1)S(1)}, u32[]{:S(2)}, u32[]{:S(2)}) collective-permute-start(bf16[1024,256]{1,0:T(8,128)(2,1)} %get-tuple-element.58.refs_2_), channel_id=1, source_target_pairs={{0,2},{1,3},{2,0},{3,1},{4,6},{5,7},{6,4},{7,5},{8,10},{9,11},{10,... | collective-permute-start | bytes 1572872 | tf_op jit(solution)/shard_map/ppermute | solution.py:412
  35.7 146.1 %collective-permute-start.6 = (bf16[768,2048]{1,0:T(8,128)(2,1)}, bf16[768,2048]{1,0:T(8,128)(2,1)}, u32[]{:S(2)}, u32[]{:S(2)}) collective-permute-start(bf16[768,2048]{1,0:T(8,128)(2,1)} %get-tuple-element.60.refs_8_), channel_id=1, source_target_pairs={{0,1},{1,0},{2,3},{3,2},{4,5},{5,4},{6,7},{7,6},{8,9},{9,8},{10,11... | collective-permute-start | bytes 9437192 | tf_op jit(solution)/shard_map/ppermute | solution.py:415
  53.5 11.6 %collective-permute-start.11 = (bf16[224,1024]{1,0:T(8,128)(2,1)S(1)}, bf16[224,1024]{1,0:T(8,128)(2,1)S(1)}, u32[]{:S(2)}, u32[]{:S(2)}) collective-permute-start(bf16[224,1024]{1,0:T(8,128)(2,1)S(1)} %slice.36), channel_id=1, source_target_pairs={{0,16},{16,0},{1,17},{17,1},{2,18},{18,2},{3,19},{19,3},{4,20},{20... | collective-permute-start | bytes 1376264 | tf_op jit(solution)/shard_map/ppermute | solution.py:418
  54.6 14.0 %collective-permute-start.1 = (bf16[1024,256]{1,0:T(8,128)(2,1)}, bf16[1024,256]{1,0:T(8,128)(2,1)S(1)}, u32[]{:S(2)}, u32[]{:S(2)}) collective-permute-start(bf16[1024,256]{1,0:T(8,128)(2,1)} %get-tuple-element.58.refs_2_), channel_id=1, source_target_pairs={{0,4},{1,5},{2,6},{3,7},{4,8},{5,9},{6,10},{7,11},{8,12},{9,13},{1... | collective-permute-start | bytes 1572872 | tf_op jit(solution)/shard_map/ppermute | solution.py:409
  65.1 16.6 %collective-permute-start.12 = (bf16[352,1024]{1,0:T(8,128)(2,1)}, bf16[352,1024]{1,0:T(8,128)(2,1)S(1)}, u32[]{:S(2)}, u32[]{:S(2)}) collective-permute-start(bf16[352,1024]{1,0:T(8,128)(2,1)} %collective-permute-done.2.refs_6_.refs_4_), channel_id=1, source_target_pairs={{0,2},{1,3},{2,0},{3,1},{4,6},{5,7},{6,4},{7,5},{8,10},{9,11},{10,... | collective-permute-start | bytes 2162696 | tf_op jit(solution)/shard_map/ppermute | solution.py:412
  66.7 30.5 %collective-permute-start.16 = (bf16[352,1024]{1,0:T(8,128)(2,1)S(1)}, bf16[352,1024]{1,0:T(8,128)(2,1)S(1)}, u32[]{:S(2)}, u32[]{:S(2)}) collective-permute-start(bf16[352,1024]{1,0:T(8,128)(2,1)S(1)} %collective-permute-done.refs_7_.refs_8_), channel_id=1, source_target_pairs={{0,2},{1,3},{2,0},{3,1},{4,6},{5,7},{6,4},{7,5},{8,10},{9,11},{10,... | collective-permute-start | bytes 2162696 | tf_op jit(solution)/shard_map/ppermute | solution.py:412
  67.4 45.0 %collective-permute-start.14 = (bf16[448,1024]{1,0:T(8,128)(2,1)S(1)}, bf16[448,1024]{1,0:T(8,128)(2,1)S(1)}, u32[]{:S(2)}, u32[]{:S(2)}) collective-permute-start(bf16[448,1024]{1,0:T(8,128)(2,1)S(1)} %pad_maximum_fusion), channel_id=1, source_target_pairs={{0,16},{16,0},{1,17},{17,1},{2,18},{18,2},{3,19},{19,3},{4,20},{20... | collective-permute-start | bytes 2752520 | tf_op jit(solution)/shard_map/ppermute | solution.py:418
  68.7 42.2 %collective-permute-start.3 = (bf16[352,1024]{1,0:T(8,128)(2,1)S(1)}, bf16[352,1024]{1,0:T(8,128)(2,1)}, u32[]{:S(2)}, u32[]{:S(2)}) collective-permute-start(bf16[352,1024]{1,0:T(8,128)(2,1)S(1)} %pad_maximum_fusion.2.refs_2_.refs_0_), channel_id=1, source_target_pairs={{0,8},{1,9},{2,10},{3,11},{4,12},{5,13},{6,14},{7,15},{8,0},{9,1},... | collective-permute-start | bytes 2162696 | tf_op jit(solution)/shard_map/ppermute | solution.py:409
  81.7 40.5 %collective-permute-start.5 = (bf16[1024,256]{1,0:T(8,128)(2,1)}, bf16[1024,256]{1,0:T(8,128)(2,1)}, u32[]{:S(2)}, u32[]{:S(2)}) collective-permute-start(bf16[1024,256]{1,0:T(8,128)(2,1)} %get-tuple-element.58.refs_2_), channel_id=1, source_target_pairs={{0,8},{1,9},{2,10},{3,11},{4,12},{5,13},{6,14},{7,15},{8,0},{9,1},... | collective-permute-start | bytes 1572872 | tf_op jit(solution)/shard_map/ppermute | solution.py:409
  99.1 42.7 %collective-permute-start.17 = (bf16[448,1024]{1,0:T(8,128)(2,1)}, bf16[448,1024]{1,0:T(8,128)(2,1)S(1)}, u32[]{:S(2)}, u32[]{:S(2)}) collective-permute-start(bf16[448,1024]{1,0:T(8,128)(2,1)} %pad_maximum_fusion.1), channel_id=1, source_target_pairs={{0,16},{16,0},{1,17},{17,1},{2,18},{18,2},{3,19},{19,3},{4,20},{20... | collective-permute-start | bytes 2752520 | tf_op jit(solution)/shard_map/ppermute | solution.py:418
  110.9 12.1 %collective-permute-start.26 = (bf16[1024,256]{1,0:T(8,128)(2,1)S(1)}, bf16[1024,256]{1,0:T(8,128)(2,1)S(1)}, u32[]{:S(2)}, u32[]{:S(2)}) collective-permute-start(bf16[1024,256]{1,0:T(8,128)(2,1)S(1)} %collective-permute-done.1.refs_0_.refs_6_), channel_id=1, source_target_pairs={{0,2},{1,3},{2,0},{3,1},{4,6},{5,7},{6,4},{7,5},{8,10},{9,11},{10,... | collective-permute-start | bytes 1572872 | tf_op jit(solution)/shard_map/ppermute | solution.py:412
  112.4 26.0 %collective-permute-start.13 = (bf16[352,1024]{1,0:T(8,128)(2,1)}, bf16[352,1024]{1,0:T(8,128)(2,1)S(1)}, u32[]{:S(2)}, u32[]{:S(2)}) collective-permute-start(bf16[352,1024]{1,0:T(8,128)(2,1)} %collective-permute-done.3.refs_11_.refs_10_), channel_id=1, source_target_pairs={{0,2},{1,3},{2,0},{3,1},{4,6},{5,7},{6,4},{7,5},{8,10},{9,11},{10,... | collective-permute-start | bytes 2162696 | tf_op jit(solution)/shard_map/ppermute | solution.py:412
  122.2 33.2 %collective-permute-start.18 = (bf16[224,1024]{1,0:T(8,128)(2,1)}, bf16[224,1024]{1,0:T(8,128)(2,1)}, u32[]{:S(2)}, u32[]{:S(2)}) collective-permute-start(bf16[224,1024]{1,0:T(8,128)(2,1)} %slice.41), channel_id=1, source_target_pairs={{0,16},{16,0},{1,17},{17,1},{2,18},{18,2},{3,19},{19,3},{4,20},{20... | collective-permute-start | bytes 1376264 | tf_op jit(solution)/shard_map/ppermute | solution.py:418
  123.7 32.1 %collective-permute-start.4 = (bf16[1024,256]{1,0:T(8,128)(2,1)}, bf16[1024,256]{1,0:T(8,128)(2,1)}, u32[]{:S(2)}, u32[]{:S(2)}) collective-permute-start(bf16[1024,256]{1,0:T(8,128)(2,1)} %get-tuple-element.58.refs_2_), channel_id=1, source_target_pairs={{0,12},{1,13},{2,14},{3,15},{4,0},{5,1},{6,2},{7,3},{8,4},{9,5},{1... | collective-permute-start | bytes 1572872 | tf_op jit(solution)/shard_map/ppermute | solution.py:409
  138.4 20.9 %collective-permute-start.32 = (bf16[1024,256]{1,0:T(8,128)(2,1)}, bf16[1024,256]{1,0:T(8,128)(2,1)}, u32[]{:S(2)}, u32[]{:S(2)}) collective-permute-start(bf16[1024,256]{1,0:T(8,128)(2,1)} %collective-permute-done.5.refs_0_.refs_15_), channel_id=1, source_target_pairs={{0,2},{1,3},{2,0},{3,1},{4,6},{5,7},{6,4},{7,5},{8,10},{9,11},{10,... | collective-permute-start | bytes 1572872 | tf_op jit(solution)/shard_map/ppermute | solution.py:412
  155.8 24.2 %collective-permute-start.27 = (bf16[1024,256]{1,0:T(8,128)(2,1)}, bf16[1024,256]{1,0:T(8,128)(2,1)S(1)}, u32[]{:S(2)}, u32[]{:S(2)}) collective-permute-start(bf16[1024,256]{1,0:T(8,128)(2,1)} %collective-permute-done.4.refs_1_.refs_11_), channel_id=1, source_target_pairs={{0,2},{1,3},{2,0},{3,1},{4,6},{5,7},{6,4},{7,5},{8,10},{9,11},{10,... | collective-permute-start | bytes 1572872 | tf_op jit(solution)/shard_map/ppermute | solution.py:412
  158.1 21.5 %collective-permute-start.24 = (bf16[512,256]{1,0:T(8,128)(2,1)S(1)}, bf16[512,256]{1,0:T(8,128)(2,1)S(1)}, u32[]{:S(2)}, u32[]{:S(2)}) collective-permute-start(bf16[512,256]{1,0:T(8,128)(2,1)S(1)} %shard_map.86), channel_id=1, source_target_pairs={{0,16},{16,0},{1,17},{17,1},{2,18},{18,2},{3,19},{19,3},{4,20},{20... | collective-permute-start | bytes 786440 | tf_op jit(solution)/shard_map/ppermute | solution.py:418
  159.3 23.1 %collective-permute-start.34 = (bf16[1024,256]{1,0:T(8,128)(2,1)}, bf16[1024,256]{1,0:T(8,128)(2,1)S(1)}, u32[]{:S(2)}, u32[]{:S(2)}) collective-permute-start(bf16[1024,256]{1,0:T(8,128)(2,1)} %collective-permute-done.4.refs_1_.refs_11_), channel_id=1, source_target_pairs={{0,1},{1,0},{2,3},{3,2},{4,5},{5,4},{6,7},{7,6},{8,9},{9,8},{10,11... | collective-permute-start | bytes 1572872 | tf_op jit(solution)/shard_map/ppermute | solution.py:415
  171.7 45.9 %collective-permute-start.30 = (bf16[512,1024]{1,0:T(8,128)(2,1)S(1)}, bf16[512,1024]{1,0:T(8,128)(2,1)S(1)}, u32[]{:S(2)}, u32[]{:S(2)}) collective-permute-start(bf16[512,1024]{1,0:T(8,128)(2,1)S(1)} %shard_map.90.refs_9_), channel_id=1, source_target_pairs={{0,1},{1,0},{2,3},{3,2},{4,5},{5,4},{6,7},{7,6},{8,9},{9,8},{10,11... | collective-permute-start | bytes 3145736 | tf_op jit(solution)/shard_map/ppermute | solution.py:415
  179.6 17.9 %collective-permute-start.25 = (bf16[1024,256]{1,0:T(8,128)(2,1)S(1)}, bf16[1024,256]{1,0:T(8,128)(2,1)S(1)}, u32[]{:S(2)}, u32[]{:S(2)}) collective-permute-start(bf16[1024,256]{1,0:T(8,128)(2,1)S(1)} %shard_map.87), channel_id=1, source_target_pairs={{0,16},{16,0},{1,17},{17,1},{2,18},{18,2},{3,19},{19,3},{4,20},{20... | collective-permute-start | bytes 1572872 | tf_op jit(solution)/shard_map/ppermute | solution.py:418
  180.7 23.8 %collective-permute-start.28 = (bf16[1024,256]{1,0:T(8,128)(2,1)S(1)}, bf16[1024,256]{1,0:T(8,128)(2,1)S(1)}, u32[]{:S(2)}, u32[]{:S(2)}) collective-permute-start(bf16[1024,256]{1,0:T(8,128)(2,1)S(1)} %shard_map.88), channel_id=1, source_target_pairs={{0,16},{16,0},{1,17},{17,1},{2,18},{18,2},{3,19},{19,3},{4,20},{20... | collective-permute-start | bytes 1572872 | tf_op jit(solution)/shard_map/ppermute | solution.py:418
  181.9 33.1 %collective-permute-start.38 = (bf16[1024,256]{1,0:T(8,128)(2,1)}, bf16[1024,256]{1,0:T(8,128)(2,1)S(1)}, u32[]{:S(2)}, u32[]{:S(2)}) collective-permute-start(bf16[1024,256]{1,0:T(8,128)(2,1)} %collective-permute-done.5.refs_0_.refs_15_), channel_id=1, source_target_pairs={{0,1},{1,0},{2,3},{3,2},{4,5},{5,4},{6,7},{7,6},{8,9},{9,8},{10,11... | collective-permute-start | bytes 1572872 | tf_op jit(solution)/shard_map/ppermute | solution.py:415
  182.5 34.4 %collective-permute-start.40 = (bf16[1024,256]{1,0:T(8,128)(2,1)}, bf16[1024,256]{1,0:T(8,128)(2,1)}, u32[]{:S(2)}, u32[]{:S(2)}) collective-permute-start(bf16[1024,256]{1,0:T(8,128)(2,1)} %collective-permute-done.32.refs_0_.refs_17_), channel_id=1, source_target_pairs={{0,1},{1,0},{2,3},{3,2},{4,5},{5,4},{6,7},{7,6},{8,9},{9,8},{10,11... | collective-permute-start | bytes 1572872 | tf_op jit(solution)/shard_map/ppermute | solution.py:415
  197.6 22.2 %collective-permute-start.36 = (bf16[1024,256]{1,0:T(8,128)(2,1)S(1)}, bf16[1024,256]{1,0:T(8,128)(2,1)}, u32[]{:S(2)}, u32[]{:S(2)}) collective-permute-start(bf16[1024,256]{1,0:T(8,128)(2,1)S(1)} %collective-permute-done.27.refs_1_.refs_13_), channel_id=1, source_target_pairs={{0,1},{1,0},{2,3},{3,2},{4,5},{5,4},{6,7},{7,6},{8,9},{9,8},{10,11... | collective-permute-start | bytes 1572872 | tf_op jit(solution)/shard_map/ppermute | solution.py:415
  204.4 20.9 %collective-permute-start.20 = (f32[768,256]{1,0:T(8,128)}, f32[768,256]{1,0:T(8,128)S(1)}, u32[]{:S(2)}, u32[]{:S(2)}) collective-permute-start(f32[768,256]{1,0:T(8,128)} %get-tuple-element.80), channel_id=1, source_target_pairs={{0,1},{1,0},{2,3},{3,2},{4,5},{5,4},{6,7},{7,6},{8,9},{9,8},{10,11... | collective-permute-start | bytes 2359304 | tf_op jit(solution)/shard_map/ppermute | solution.py:415
  216.8 16.8 %collective-permute-start.21 = (f32[768,256]{1,0:T(8,128)}, f32[768,256]{1,0:T(8,128)S(1)}, u32[]{:S(2)}, u32[]{:S(2)}) collective-permute-start(f32[768,256]{1,0:T(8,128)} %get-tuple-element.81), channel_id=1, source_target_pairs={{0,1},{1,0},{2,3},{3,2},{4,5},{5,4},{6,7},{7,6},{8,9},{9,8},{10,11... | collective-permute-start | bytes 2359304 | tf_op jit(solution)/shard_map/ppermute | solution.py:415
  217.6 16.2 %collective-permute-start.22 = (f32[768,256]{1,0:T(8,128)}, f32[768,256]{1,0:T(8,128)S(1)}, u32[]{:S(2)}, u32[]{:S(2)}) collective-permute-start(f32[768,256]{1,0:T(8,128)} %get-tuple-element.82), channel_id=1, source_target_pairs={{0,1},{1,0},{2,3},{3,2},{4,5},{5,4},{6,7},{7,6},{8,9},{9,8},{10,11... | collective-permute-start | bytes 2359304 | tf_op jit(solution)/shard_map/ppermute | solution.py:415
  219.7 15.3 %collective-permute-start.23 = (f32[768,256]{1,0:T(8,128)}, f32[768,256]{1,0:T(8,128)S(1)}, u32[]{:S(2)}, u32[]{:S(2)}) collective-permute-start(f32[768,256]{1,0:T(8,128)} %get-tuple-element.83), channel_id=1, source_target_pairs={{0,1},{1,0},{2,3},{3,2},{4,5},{5,4},{6,7},{7,6},{8,9},{9,8},{10,11... | collective-permute-start | bytes 2359304 | tf_op jit(solution)/shard_map/ppermute | solution.py:415
  (61 other events, 1035.3 us)

commit v5 on v4

--- a/solution.py
+++ b/solution.py
@@ -10,7 +10,6 @@
 adapter_scale = 2.0
 cores, rows_y, lane = 2, 2, 128
 nt = (((1,), (1,)), ((), ()))
-vmem = 58 << 20
 light = pl.CostEstimate(flops=0, bytes_accessed=0, transcendentals=0)
 
 
@@ -110,13 +109,13 @@
             ],
             out_specs=[pl.BlockSpec((block, w), lambda i, *_: (i, 0)) for w in widths],
         ),
-        compiler_params=pltpu.CompilerParams(vmem_limit_bytes=vmem),
+        compiler_params=pltpu.CompilerParams(vmem_limit_bytes=20 << 20),
         cost_estimate=light,
     )(source, tokens, gain.reshape(1, width))
 
 
 def far_memory():
-    return pl.BlockSpec(memory_space=pltpu.HBM)
+    return pl.BlockSpec(memory_space=pl.ANY)
 
 
 def tiled(array, tile):
@@ -202,7 +201,7 @@
             pltpu.VMEM((depth, width), jnp.bfloat16),
             pltpu.SemaphoreType.DMA((len(plan),)),
         ],
-        compiler_params=pltpu.CompilerParams(vmem_limit_bytes=vmem),
+        compiler_params=pltpu.CompilerParams(vmem_limit_bytes=24 << 20),
         cost_estimate=light,
     )(own, far, *sums, *arrays)
 
@@ -302,7 +301,7 @@
             + [pltpu.VMEM((docs * rank, depth), jnp.bfloat16)] * 2
             + [pltpu.SemaphoreType.DMA((len(arrays),))],
         ),
-        compiler_params=pltpu.CompilerParams(vmem_limit_bytes=vmem),
+        compiler_params=pltpu.CompilerParams(vmem_limit_bytes=20 << 20),
         cost_estimate=light,
     )(ends, slots, own, far, *arrays)
 
@@ -382,7 +381,7 @@
             + [pltpu.VMEM((width, flat), jnp.bfloat16)]
             + [pltpu.SemaphoreType.DMA((len(arrays) + up_at.size,))],
         ),
-        compiler_params=pltpu.CompilerParams(vmem_limit_bytes=vmem),
+        compiler_params=pltpu.CompilerParams(vmem_limit_bytes=34 << 20),
         cost_estimate=light,
     )(slots, ends, up_at, *sums, *mids, *tokens, *ups, *arrays)
 
@@ -576,20 +575,24 @@
         v_have[0, 1] = y(v_have[0, 0])
         d_have[0, 1] = y(d_have[0, 0])
         x_values([(0, 1)], slots_there)
+        x_down([(0, 1)])
+        for i, k in enumerate(early):
+            pins = [partner, partner_rest][: i + 1] + [d_miss[0, 1][0]] * i
+            v_have[k, 1] = y(after(v_have[k, 0], *pins))
+            x_values([(k, 0)])
         for k in early:
-            v_have[k, 1] = y(after(v_have[k, 0], partner, v_miss[0, 1][0]))
-        x_values([(k, 0) for k in early])
-        x_values([(k, 1) for k in early])
+            x_values([(k, 1)])
         v_have[last, 1] = y(v_have[last, 0])
         x_values([(last, 0)])
-        x_down([(0, 1)])
         for k in early:
             d_have[k, 1] = y(d_have[k, 0])
         arrays, plan = values(first)
         sums = value_sums(after(own, v_have[last, 1]), partner, arrays, plan, width)
         x_values([(last, 1)], sums[0])
-        x_down([(k, 0) for k in early])
-        x_down([(k, 1) for k in early])
+        for k in early:
+            x_down([(k, 0)])
+        for k in early:
+            x_down([(k, 1)])
         d_have[last, 1] = y(d_have[last, 0])
         x_down([(last, 0)])
 

time: 256 us -> 247 us (0.965)
  waiting for transfers between devices: 114 us -> 59.7 us
  local copies, waits for them, and re-layouts: 22.6 us -> 53.9 us
  starting transfers between devices: 37.3 us -> 65.9 us
  Pallas kernels: 74.2 us -> 61 us
    ppermute x8, waiting for transfers between devices: 48.1 us -> 6.64 us  [along_y(): return lax.ppermute(value, 'store', pairs(lambda z, y, c: (z, 1 - y, c)))]
    unnamed x104 -> x114, local copies, waits for them, and re-layouts: 12 us -> 40.1 us
    ppermute x17, starting transfers between devices: 19.5 us -> 37 us  [across(): return lax.ppermute(value, 'store', pairs(lambda z, y, c: (z, y, 1 - c)))]
    ppermute x11 -> x15, waiting for transfers between devices: 30.1 us -> 14.4 us  [along_x(): return lax.ppermute(value, 'groups', [(g, g ^ 1) for g in range(groups)])]
    pallas_call x1, Pallas kernels: 13.7 us -> 8.55 us  [norm_in_order(): pl.pallas_call(norm_kernel, out_shape=[jax.ShapeDtypeStruct((rows, w), jn...]
    ppermute x11 -> x15, starting transfers between devices: 9.01 us -> 13.5 us  [along_x(): return lax.ppermute(value, 'groups', [(g, g ^ 1) for g in range(groups)])]
    ppermute x6, starting transfers between devices: 3.46 us -> 7.96 us  [along_z(): lax.ppermute(value, 'store', pairs(lambda z, y, c: ((z + k) % depth, y, c)))]
    pallas_call x2, Pallas kernels: 26.2 us -> 22.9 us  [value_sums(): pl.pallas_call(functools.partial(value_kernel, plan, columns, len(sums),...]
  transfers between devices with their start and end apart: 42 -> 46, of which waited for: 16 -> 15; matrix products, arithmetic and copies ran while one was open for 6% -> 8% of each run, Pallas kernels for 17% -> 15%
where the time goes in v5:
time: 247 us; the launch traced here: 245 us
  starting transfers between devices  65.9 us (27%)
  Pallas kernels  61 us (25%)
  waiting for transfers between devices  59.7 us (24%)
  local copies, waits for them, and re-layouts  53.9 us (22%)
  other arithmetic  3.65 us (1%)
    unnamed x114, local copies, waits for them, and re-layouts  40.1 us
    ppermute x17, starting transfers between devices, across(): return lax.ppermute(value, 'store', pairs(lambda z, y, c: (z, y, 1 - c)))  37 us
    ppermute x6, waiting for transfers between devices, along_z(): lax.ppermute(value, 'store', pairs(lambda z, y, c: ((z + k) % depth, y, c)))  35 us
    pallas_call x2, Pallas kernels, value_sums(): pl.pallas_call(functools.partial(value_kernel, plan, columns, len(sums),...  22.9 us
    pallas_call x1, Pallas kernels, last_values(): pl.pallas_call(functools.partial(last_kernel, rank, parts, len(sums), len...  15.4 us
    ppermute x15, waiting for transfers between devices, along_x(): return lax.ppermute(value, 'groups', [(g, g ^ 1) for g in range(groups)])  14.4 us
    ppermute x15, starting transfers between devices, along_x(): return lax.ppermute(value, 'groups', [(g, g ^ 1) for g in range(groups)])  13.5 us
    pallas_call x1, Pallas kernels, norm_in_order(): pl.pallas_call(norm_kernel, out_shape=[jax.ShapeDtypeStruct((rows, w), jn...  8.55 us
  transfers between devices with their start and end apart: 46, of which 15 were waited for; matrix products, arithmetic and copies ran while one was open for 8% of the time, Pallas kernels for 15%

profile of v5, /device:TPU:9, one launch (start us, length us, event | category | flops | bytes accessed | tf_op | source)
XLA Modules:
  0.0 244.8 jit_solution(10460021075891416398)
XLA Ops:
  0.9 4.6 %copy-done = bf16[768,8192]{1,0:T(8,128)(2,1)S(1)} copy-done((bf16[768,8192]{1,0:T(8,128)(2,1)S(1)}, bf16[768,8192]{1,0:T(8,128)(2,1)}, u32[]{:S(2)}) %copy-start) | copy-done | bytes 12582936
  5.5 8.6 %shard_map.82 = (bf16[768,2048]{1,0:T(8,128)(2,1)S(1)}, bf16[768,2048]{1,0:T(8,128)(2,1)S(1)}, bf16[768,2048]{1,0:T(8,128)(2,1)}, bf16[768,2048]{1,0:T(8,128)(2,1)}) custom-call(s32[64]{0:T(128)S(1)} %stack.391.source_ref, bf16[768,8192]{1,0:T(8,128)(2,1)S(1)} %copy-done, bf16[1,8192]{1,0:T(2,128)(2,1)S(1)} %reshape.15.gain_ref), custom_call_target="tpu_custom_call" | custom-call | tf_op jit(solution)/shard_map/pallas_call | solution.py:100
  14.0 1.6 copy-done.1
  16.4 2.0 constant_dynamic-slice_fusion
  21.2 1.7 pad_maximum_fusion.refs_2_.refs_0_
  28.7 2.2 dynamic-slice_bitcast_fusion
  30.9 9.6 %collective-permute-done.2.refs_6_.refs_4_ = bf16[352,1024]{1,0:T(8,128)(2,1)} collective-permute-done((bf16[352,1024]{1,0:T(8,128)(2,1)}, bf16[352,1024]{1,0:T(8,128)(2,1)}, u32[]{:S(2)}, u32[]{:S(2)}) %collective-permute-start.2) | collective-permute-done | bytes 720928 | tf_op jit(solution)/shard_map/ppermute | solution.py:408
  43.6 2.5 %collective-permute-start.3 = (bf16[352,1024]{1,0:T(8,128)(2,1)}, bf16[352,1024]{1,0:T(8,128)(2,1)}, u32[]{:S(2)}, u32[]{:S(2)}) collective-permute-start(bf16[352,1024]{1,0:T(8,128)(2,1)} %pad_maximum_fusion.refs_2_.refs_0_), channel_id=1, source_target_pairs={{0,8},{1,9},{2,10},{3,11},{4,12},{5,13},{6,14},{7,15},{8,0},{9,1},... | collective-permute-start | bytes 2162696 | tf_op jit(solution)/shard_map/ppermute | solution.py:408
  47.4 4.3 %collective-permute-done.16.refs_0_.refs_4_ = bf16[1024,256]{1,0:T(8,128)(2,1)S(1)} collective-permute-done((bf16[1024,256]{1,0:T(8,128)(2,1)}, bf16[1024,256]{1,0:T(8,128)(2,1)S(1)}, u32[]{:S(2)}, u32[]{:S(2)}) %collective-permute-start.16) | collective-permute-done | bytes 524320 | tf_op jit(solution)/shard_map/ppermute | solution.py:411
  53.7 4.4 %collective-permute-done.refs_7_.refs_8_ = bf16[352,1024]{1,0:T(8,128)(2,1)S(1)} collective-permute-done((bf16[352,1024]{1,0:T(8,128)(2,1)}, bf16[352,1024]{1,0:T(8,128)(2,1)S(1)}, u32[]{:S(2)}, u32[]{:S(2)}) %collective-permute-start) | collective-permute-done | bytes 720928 | tf_op jit(solution)/shard_map/ppermute | solution.py:408
  59.7 3.8 %collective-permute-done.17.refs_5_ = bf16[512,256]{1,0:T(8,128)(2,1)S(1)} collective-permute-done((bf16[512,256]{1,0:T(8,128)(2,1)S(1)}, bf16[512,256]{1,0:T(8,128)(2,1)S(1)}, u32[]{:S(2)}, u32[]{:S(2)}) %collective-permute-start.17) | collective-permute-done | bytes 262176 | tf_op jit(solution)/shard_map/ppermute | solution.py:417
  64.1 1.8 collective-permute-start.19
  69.3 17.6 %collective-permute-done.3.refs_11_.refs_12_ = bf16[352,1024]{1,0:T(8,128)(2,1)} collective-permute-done((bf16[352,1024]{1,0:T(8,128)(2,1)}, bf16[352,1024]{1,0:T(8,128)(2,1)}, u32[]{:S(2)}, u32[]{:S(2)}) %collective-permute-start.3) | collective-permute-done | bytes 720928 | tf_op jit(solution)/shard_map/ppermute | solution.py:408
  93.7 1.7 copy.13
  95.4 3.5 %collective-permute-done.1.refs_0_.refs_6_ = bf16[1024,256]{1,0:T(8,128)(2,1)} collective-permute-done((bf16[1024,256]{1,0:T(8,128)(2,1)}, bf16[1024,256]{1,0:T(8,128)(2,1)}, u32[]{:S(2)}, u32[]{:S(2)}) %collective-permute-start.1) | collective-permute-done | bytes 524320 | tf_op jit(solution)/shard_map/ppermute | solution.py:408
  101.0 2.2 collective-permute-start.4
  103.1 2.3 collective-permute-done.10.refs_13_.refs_14_
  110.8 10.8 %shard_map.83 = (f32[768,1024]{1,0:T(8,128)S(1)}, f32[768,256]{1,0:T(8,128)S(1)}, f32[768,256]{1,0:T(8,128)S(1)}, f32[768,256]{1,0:T(8,128)S(1)}, f32[768,256]{1,0:T(8,128)S(1)}) custom-call(bf16[768,2048]{1,0:T(8,128)(2,1)S(1)} %get-tuple-element.70.refs_0_, bf16[768,2048]{1,0:T(8,128)(2,1)} %collective-permute-done.7.refs_1_, ...), custom_call_target="tpu_custom_call" | custom-call | tf_op jit(solution)/shard_map/pallas_call | solution.py:194
  121.7 1.6 shard_map.87
  126.4 2.9 %collective-permute-done.22.refs_14_.refs_15_ = bf16[224,1024]{1,0:T(8,128)(2,1)S(1)} collective-permute-done((bf16[224,1024]{1,0:T(8,128)(2,1)S(1)}, bf16[224,1024]{1,0:T(8,128)(2,1)S(1)}, u32[]{:S(2)}, u32[]{:S(2)}) %collective-permute-start.22) | collective-permute-done | bytes 458784 | tf_op jit(solution)/shard_map/ppermute | solution.py:417
  129.3 1.7 shard_map.90.refs_9_
  131.0 24.3 %collective-permute-start.31 = (bf16[512,1024]{1,0:T(8,128)(2,1)S(1)}, bf16[512,1024]{1,0:T(8,128)(2,1)S(1)}, u32[]{:S(2)}, u32[]{:S(2)}) collective-permute-start(bf16[512,1024]{1,0:T(8,128)(2,1)S(1)} %shard_map.90.refs_9_), channel_id=1, source_target_pairs={{0,1},{1,0},{2,3},{3,2},{4,5},{5,4},{6,7},{7,6},{8,9},{9,8},{10,11... | collective-permute-start | bytes 3145736 | tf_op jit(solution)/shard_map/ppermute | solution.py:414
  159.7 2.4 collective-permute-start.42
  163.5 1.9 collective-permute-start.44
  165.5 6.9 %shard_map.89 = (f32[768,64]{1,0:T(8,128)S(1)}, f32[768,64]{1,0:T(8,128)S(1)}) custom-call(s32[2,4]{1,0:T(2,128)S(1)} %pad_add_fusion.ends_ref, s32[2,4]{1,0:T(2,128)S(1)} %pad_add_fusion.2.slots_ref, bf16[768,2048]{1,0:T(8,128)(2,1)S(1)} %get-tuple-element.70.refs_0_, bf16[768,2048]{1,0:T(8,128)(2,1)} %collective-permute-done.7.refs_1_, ...), custom_call_target="tpu_custom_call" | custom-call | tf_op jit(solution)/shard_map/pallas_call | solution.py:292
  175.0 12.2 %shard_map.85 = (f32[768,1024]{1,0:T(8,128)S(1)}, f32[768,256]{1,0:T(8,128)S(1)}, f32[768,256]{1,0:T(8,128)S(1)}, f32[768,256]{1,0:T(8,128)}, f32[768,256]{1,0:T(8,128)}) custom-call(bf16[768,2048]{1,0:T(8,128)(2,1)S(1)} %copy-done.2, bf16[768,2048]{1,0:T(8,128)(2,1)} %collective-permute-done.6.refs_1_, f32[768,1024]{1,0:T(8,128)S(1)} %get-tuple-element.74.refs_2_, ...), custom_call_target="tpu_custom_call" | custom-call | tf_op jit(solution)/shard_map/pallas_call | solution.py:194
  187.2 1.8 copy-done.12
  196.7 2.8 %collective-permute-done.35.refs_16_ = bf16[512,256]{1,0:T(8,128)(2,1)} collective-permute-done((bf16[512,256]{1,0:T(8,128)(2,1)S(1)}, bf16[512,256]{1,0:T(8,128)(2,1)}, u32[]{:S(2)}, u32[]{:S(2)}) %collective-permute-start.35) | collective-permute-done | bytes 262176 | tf_op jit(solution)/shard_map/ppermute | solution.py:417
  199.5 2.1 collective-permute-start.25
  201.7 3.5 %collective-permute-done.37.refs_18_ = bf16[512,256]{1,0:T(8,128)(2,1)} collective-permute-done((bf16[512,256]{1,0:T(8,128)(2,1)S(1)}, bf16[512,256]{1,0:T(8,128)(2,1)}, u32[]{:S(2)}, u32[]{:S(2)}) %collective-permute-start.37) | collective-permute-done | bytes 262176 | tf_op jit(solution)/shard_map/ppermute | solution.py:417
  212.6 1.9 copy-done.13
  229.2 15.4 %shard_map.95 = bf16[768,1024]{1,0:T(8,128)(2,1)} custom-call(s32[4]{0:T(128)S(1)} %select_reduce_fusion.slots_ref, s32[4]{0:T(128)S(1)} %bitcast.109, s32[2,16]{1,0:T(2,128)S(1)} %reshape.14.at_ref, f32[768,1024]{1,0:T(8,128)S(1)} %copy-done.13, f32[768,256]{1,0:T(8,128)S(1)} %copy-done.34, f32[768,256]{1,0:T(8,128)S(1)} %copy-done.36, ...), custom_call_target="tpu_custom_call" | custom-call | tf_op jit(solution)/shard_map/pallas_call | solution.py:370
  (211 shorter events, 77.8 us)
Async XLA Ops:
  15.7 26.5 %collective-permute-start.7 = (bf16[768,2048]{1,0:T(8,128)(2,1)}, bf16[768,2048]{1,0:T(8,128)(2,1)}, u32[]{:S(2)}, u32[]{:S(2)}) collective-permute-start(bf16[768,2048]{1,0:T(8,128)(2,1)} %get-tuple-element.66), channel_id=1, source_target_pairs={{0,1},{1,0},{2,3},{3,2},{4,5},{5,4},{6,7},{7,6},{8,9},{9,8},{10,11... | collective-permute-start | bytes 9437192 | tf_op jit(solution)/shard_map/ppermute | solution.py:414
  16.4 47.8 %collective-permute-start.6 = (bf16[768,2048]{1,0:T(8,128)(2,1)}, bf16[768,2048]{1,0:T(8,128)(2,1)}, u32[]{:S(2)}, u32[]{:S(2)}) collective-permute-start(bf16[768,2048]{1,0:T(8,128)(2,1)} %get-tuple-element.64.refs_8_), channel_id=1, source_target_pairs={{0,1},{1,0},{2,3},{3,2},{4,5},{5,4},{6,7},{7,6},{8,9},{9,8},{10,11... | collective-permute-start | bytes 9437192 | tf_op jit(solution)/shard_map/ppermute | solution.py:414
  23.0 17.5 %collective-permute-start.2 = (bf16[352,1024]{1,0:T(8,128)(2,1)}, bf16[352,1024]{1,0:T(8,128)(2,1)}, u32[]{:S(2)}, u32[]{:S(2)}) collective-permute-start(bf16[352,1024]{1,0:T(8,128)(2,1)} %pad_maximum_fusion.refs_2_.refs_0_), channel_id=1, source_target_pairs={{0,4},{1,5},{2,6},{3,7},{4,8},{5,9},{6,10},{7,11},{8,12},{9,13},{1... | collective-permute-start | bytes 2162696 | tf_op jit(solution)/shard_map/ppermute | solution.py:408
  24.3 19.3 %collective-permute-start.8 = (bf16[352,1024]{1,0:T(8,128)(2,1)}, bf16[352,1024]{1,0:T(8,128)(2,1)}, u32[]{:S(2)}, u32[]{:S(2)}) collective-permute-start(bf16[352,1024]{1,0:T(8,128)(2,1)} %pad_maximum_fusion.refs_2_.refs_0_), channel_id=1, source_target_pairs={{0,2},{1,3},{2,0},{3,1},{4,6},{5,7},{6,4},{7,5},{8,10},{9,11},{10,... | collective-permute-start | bytes 2162696 | tf_op jit(solution)/shard_map/ppermute | solution.py:411
  28.5 29.6 %collective-permute-start = (bf16[352,1024]{1,0:T(8,128)(2,1)}, bf16[352,1024]{1,0:T(8,128)(2,1)S(1)}, u32[]{:S(2)}, u32[]{:S(2)}) collective-permute-start(bf16[352,1024]{1,0:T(8,128)(2,1)} %pad_maximum_fusion.refs_2_.refs_0_), channel_id=1, source_target_pairs={{0,12},{1,13},{2,14},{3,15},{4,0},{5,1},{6,2},{7,3},{8,4},{9,5},{1... | collective-permute-start | bytes 2162696 | tf_op jit(solution)/shard_map/ppermute | solution.py:408
  40.5 11.3 %collective-permute-start.16 = (bf16[1024,256]{1,0:T(8,128)(2,1)}, bf16[1024,256]{1,0:T(8,128)(2,1)S(1)}, u32[]{:S(2)}, u32[]{:S(2)}) collective-permute-start(bf16[1024,256]{1,0:T(8,128)(2,1)} %get-tuple-element.62.refs_2_), channel_id=1, source_target_pairs={{0,2},{1,3},{2,0},{3,1},{4,6},{5,7},{6,4},{7,5},{8,10},{9,11},{10,... | collective-permute-start | bytes 1572872 | tf_op jit(solution)/shard_map/ppermute | solution.py:411
  43.6 43.2 %collective-permute-start.3 = (bf16[352,1024]{1,0:T(8,128)(2,1)}, bf16[352,1024]{1,0:T(8,128)(2,1)}, u32[]{:S(2)}, u32[]{:S(2)}) collective-permute-start(bf16[352,1024]{1,0:T(8,128)(2,1)} %pad_maximum_fusion.refs_2_.refs_0_), channel_id=1, source_target_pairs={{0,8},{1,9},{2,10},{3,11},{4,12},{5,13},{6,14},{7,15},{8,0},{9,1},... | collective-permute-start | bytes 2162696 | tf_op jit(solution)/shard_map/ppermute | solution.py:408
  46.1 40.7 %collective-permute-start.9 = (bf16[352,1024]{1,0:T(8,128)(2,1)}, bf16[352,1024]{1,0:T(8,128)(2,1)S(1)}, u32[]{:S(2)}, u32[]{:S(2)}) collective-permute-start(bf16[352,1024]{1,0:T(8,128)(2,1)} %collective-permute-done.2.refs_6_.refs_4_), channel_id=1, source_target_pairs={{0,2},{1,3},{2,0},{3,1},{4,6},{5,7},{6,4},{7,5},{8,10},{9,11},{10,... | collective-permute-start | bytes 2162696 | tf_op jit(solution)/shard_map/ppermute | solution.py:411
  51.8 15.2 %collective-permute-start.13 = (bf16[224,1024]{1,0:T(8,128)(2,1)S(1)}, bf16[224,1024]{1,0:T(8,128)(2,1)S(1)}, u32[]{:S(2)}, u32[]{:S(2)}) collective-permute-start(bf16[224,1024]{1,0:T(8,128)(2,1)S(1)} %slice.36), channel_id=1, source_target_pairs={{0,16},{16,0},{1,17},{17,1},{2,18},{18,2},{3,19},{19,3},{4,20},{20... | collective-permute-start | bytes 1376264 | tf_op jit(solution)/shard_map/ppermute | solution.py:417
  64.1 27.0 %collective-permute-start.19 = (bf16[352,1024]{1,0:T(8,128)(2,1)S(1)}, bf16[352,1024]{1,0:T(8,128)(2,1)S(1)}, u32[]{:S(2)}, u32[]{:S(2)}) collective-permute-start(bf16[352,1024]{1,0:T(8,128)(2,1)S(1)} %collective-permute-done.refs_7_.refs_8_), channel_id=1, source_target_pairs={{0,2},{1,3},{2,0},{3,1},{4,6},{5,7},{6,4},{7,5},{8,10},{9,11},{10,... | collective-permute-start | bytes 2162696 | tf_op jit(solution)/shard_map/ppermute | solution.py:411
  67.7 22.1 %collective-permute-start.14 = (bf16[224,1024]{1,0:T(8,128)(2,1)S(1)}, bf16[224,1024]{1,0:T(8,128)(2,1)S(1)}, u32[]{:S(2)}, u32[]{:S(2)}) collective-permute-start(bf16[224,1024]{1,0:T(8,128)(2,1)S(1)} %slice.37), channel_id=1, source_target_pairs={{0,16},{16,0},{1,17},{17,1},{2,18},{18,2},{3,19},{19,3},{4,20},{20... | collective-permute-start | bytes 1376264 | tf_op jit(solution)/shard_map/ppermute | solution.py:417
  69.1 23.7 %collective-permute-start.18 = (bf16[224,1024]{1,0:T(8,128)(2,1)S(1)}, bf16[224,1024]{1,0:T(8,128)(2,1)S(1)}, u32[]{:S(2)}, u32[]{:S(2)}) collective-permute-start(bf16[224,1024]{1,0:T(8,128)(2,1)S(1)} %slice.39), channel_id=1, source_target_pairs={{0,16},{16,0},{1,17},{17,1},{2,18},{18,2},{3,19},{19,3},{4,20},{20... | collective-permute-start | bytes 1376264 | tf_op jit(solution)/shard_map/ppermute | solution.py:417
  86.9 18.5 %collective-permute-start.10 = (bf16[352,1024]{1,0:T(8,128)(2,1)}, bf16[352,1024]{1,0:T(8,128)(2,1)}, u32[]{:S(2)}, u32[]{:S(2)}) collective-permute-start(bf16[352,1024]{1,0:T(8,128)(2,1)} %collective-permute-done.3.refs_11_.refs_12_), channel_id=1, source_target_pairs={{0,2},{1,3},{2,0},{3,1},{4,6},{5,7},{6,4},{7,5},{8,10},{9,11},{10,... | collective-permute-start | bytes 2162696 | tf_op jit(solution)/shard_map/ppermute | solution.py:411
  88.2 10.7 %collective-permute-start.1 = (bf16[1024,256]{1,0:T(8,128)(2,1)}, bf16[1024,256]{1,0:T(8,128)(2,1)}, u32[]{:S(2)}, u32[]{:S(2)}) collective-permute-start(bf16[1024,256]{1,0:T(8,128)(2,1)} %get-tuple-element.62.refs_2_), channel_id=1, source_target_pairs={{0,4},{1,5},{2,6},{3,7},{4,8},{5,9},{6,10},{7,11},{8,12},{9,13},{1... | collective-permute-start | bytes 1572872 | tf_op jit(solution)/shard_map/ppermute | solution.py:408
  89.8 13.4 %collective-permute-start.15 = (bf16[224,1024]{1,0:T(8,128)(2,1)}, bf16[224,1024]{1,0:T(8,128)(2,1)}, u32[]{:S(2)}, u32[]{:S(2)}) collective-permute-start(bf16[224,1024]{1,0:T(8,128)(2,1)} %slice.38), channel_id=1, source_target_pairs={{0,16},{16,0},{1,17},{17,1},{2,18},{18,2},{3,19},{19,3},{4,20},{20... | collective-permute-start | bytes 1376264 | tf_op jit(solution)/shard_map/ppermute | solution.py:417
  93.6 28.0 %collective-permute-start.20 = (bf16[224,1024]{1,0:T(8,128)(2,1)}, bf16[224,1024]{1,0:T(8,128)(2,1)}, u32[]{:S(2)}, u32[]{:S(2)}) collective-permute-start(bf16[224,1024]{1,0:T(8,128)(2,1)} %slice.40), channel_id=1, source_target_pairs={{0,16},{16,0},{1,17},{17,1},{2,18},{18,2},{3,19},{19,3},{4,20},{20... | collective-permute-start | bytes 1376264 | tf_op jit(solution)/shard_map/ppermute | solution.py:417
  98.9 24.5 %collective-permute-start.5 = (bf16[1024,256]{1,0:T(8,128)(2,1)}, bf16[1024,256]{1,0:T(8,128)(2,1)S(1)}, u32[]{:S(2)}, u32[]{:S(2)}) collective-permute-start(bf16[1024,256]{1,0:T(8,128)(2,1)} %get-tuple-element.62.refs_2_), channel_id=1, source_target_pairs={{0,8},{1,9},{2,10},{3,11},{4,12},{5,13},{6,14},{7,15},{8,0},{9,1},... | collective-permute-start | bytes 1572872 | tf_op jit(solution)/shard_map/ppermute | solution.py:408
  101.0 23.8 %collective-permute-start.4 = (bf16[1024,256]{1,0:T(8,128)(2,1)}, bf16[1024,256]{1,0:T(8,128)(2,1)S(1)}, u32[]{:S(2)}, u32[]{:S(2)}) collective-permute-start(bf16[1024,256]{1,0:T(8,128)(2,1)} %get-tuple-element.62.refs_2_), channel_id=1, source_target_pairs={{0,12},{1,13},{2,14},{3,15},{4,0},{5,1},{6,2},{7,3},{8,4},{9,5},{1... | collective-permute-start | bytes 1572872 | tf_op jit(solution)/shard_map/ppermute | solution.py:408
  103.1 20.2 %collective-permute-start.28 = (bf16[1024,256]{1,0:T(8,128)(2,1)}, bf16[1024,256]{1,0:T(8,128)(2,1)S(1)}, u32[]{:S(2)}, u32[]{:S(2)}) collective-permute-start(bf16[1024,256]{1,0:T(8,128)(2,1)} %collective-permute-done.1.refs_0_.refs_6_), channel_id=1, source_target_pairs={{0,2},{1,3},{2,0},{3,1},{4,6},{5,7},{6,4},{7,5},{8,10},{9,11},{10,... | collective-permute-start | bytes 1572872 | tf_op jit(solution)/shard_map/ppermute | solution.py:411
  105.4 19.3 %collective-permute-start.21 = (bf16[224,1024]{1,0:T(8,128)(2,1)S(1)}, bf16[224,1024]{1,0:T(8,128)(2,1)S(1)}, u32[]{:S(2)}, u32[]{:S(2)}) collective-permute-start(bf16[224,1024]{1,0:T(8,128)(2,1)S(1)} %slice.41), channel_id=1, source_target_pairs={{0,16},{16,0},{1,17},{17,1},{2,18},{18,2},{3,19},{19,3},{4,20},{20... | collective-permute-start | bytes 1376264 | tf_op jit(solution)/shard_map/ppermute | solution.py:417
  123.4 35.3 %collective-permute-start.36 = (bf16[1024,256]{1,0:T(8,128)(2,1)S(1)}, bf16[1024,256]{1,0:T(8,128)(2,1)S(1)}, u32[]{:S(2)}, u32[]{:S(2)}) collective-permute-start(bf16[1024,256]{1,0:T(8,128)(2,1)S(1)} %collective-permute-done.5.refs_0_.refs_15_), channel_id=1, source_target_pairs={{0,2},{1,3},{2,0},{3,1},{4,6},{5,7},{6,4},{7,5},{8,10},{9,11},{10,... | collective-permute-start | bytes 1572872 | tf_op jit(solution)/shard_map/ppermute | solution.py:411
  124.8 31.1 %collective-permute-start.27 = (bf16[512,256]{1,0:T(8,128)(2,1)S(1)}, bf16[512,256]{1,0:T(8,128)(2,1)S(1)}, u32[]{:S(2)}, u32[]{:S(2)}) collective-permute-start(bf16[512,256]{1,0:T(8,128)(2,1)S(1)} %shard_map.87), channel_id=1, source_target_pairs={{0,16},{16,0},{1,17},{17,1},{2,18},{18,2},{3,19},{19,3},{4,20},{20... | collective-permute-start | bytes 786440 | tf_op jit(solution)/shard_map/ppermute | solution.py:417
  126.2 33.5 %collective-permute-start.33 = (bf16[1024,256]{1,0:T(8,128)(2,1)S(1)}, bf16[1024,256]{1,0:T(8,128)(2,1)S(1)}, u32[]{:S(2)}, u32[]{:S(2)}) collective-permute-start(bf16[1024,256]{1,0:T(8,128)(2,1)S(1)} %collective-permute-done.4.refs_0_.refs_11_), channel_id=1, source_target_pairs={{0,2},{1,3},{2,0},{3,1},{4,6},{5,7},{6,4},{7,5},{8,10},{9,11},{10,... | collective-permute-start | bytes 1572872 | tf_op jit(solution)/shard_map/ppermute | solution.py:411
  131.0 58.0 %collective-permute-start.31 = (bf16[512,1024]{1,0:T(8,128)(2,1)S(1)}, bf16[512,1024]{1,0:T(8,128)(2,1)S(1)}, u32[]{:S(2)}, u32[]{:S(2)}) collective-permute-start(bf16[512,1024]{1,0:T(8,128)(2,1)S(1)} %shard_map.90.refs_9_), channel_id=1, source_target_pairs={{0,1},{1,0},{2,3},{3,2},{4,5},{5,4},{6,7},{7,6},{8,9},{9,8},{10,11... | collective-permute-start | bytes 3145736 | tf_op jit(solution)/shard_map/ppermute | solution.py:414
  156.8 15.6 %collective-permute-start.32 = (bf16[512,256]{1,0:T(8,128)(2,1)S(1)}, bf16[512,256]{1,0:T(8,128)(2,1)S(1)}, u32[]{:S(2)}, u32[]{:S(2)}) collective-permute-start(bf16[512,256]{1,0:T(8,128)(2,1)S(1)} %shard_map.91), channel_id=1, source_target_pairs={{0,16},{16,0},{1,17},{17,1},{2,18},{18,2},{3,19},{19,3},{4,20},{20... | collective-permute-start | bytes 786440 | tf_op jit(solution)/shard_map/ppermute | solution.py:417
  158.7 32.5 %collective-permute-start.38 = (bf16[1024,256]{1,0:T(8,128)(2,1)S(1)}, bf16[1024,256]{1,0:T(8,128)(2,1)S(1)}, u32[]{:S(2)}, u32[]{:S(2)}) collective-permute-start(bf16[1024,256]{1,0:T(8,128)(2,1)S(1)} %collective-permute-done.4.refs_0_.refs_11_), channel_id=1, source_target_pairs={{0,1},{1,0},{2,3},{3,2},{4,5},{5,4},{6,7},{7,6},{8,9},{9,8},{10,11... | collective-permute-start | bytes 1572872 | tf_op jit(solution)/shard_map/ppermute | solution.py:414
  159.7 33.6 %collective-permute-start.42 = (bf16[1024,256]{1,0:T(8,128)(2,1)S(1)}, bf16[1024,256]{1,0:T(8,128)(2,1)S(1)}, u32[]{:S(2)}, u32[]{:S(2)}) collective-permute-start(bf16[1024,256]{1,0:T(8,128)(2,1)S(1)} %collective-permute-done.5.refs_0_.refs_15_), channel_id=1, source_target_pairs={{0,1},{1,0},{2,3},{3,2},{4,5},{5,4},{6,7},{7,6},{8,9},{9,8},{10,11... | collective-permute-start | bytes 1572872 | tf_op jit(solution)/shard_map/ppermute | solution.py:414
  163.5 30.7 %collective-permute-start.44 = (bf16[1024,256]{1,0:T(8,128)(2,1)S(1)}, bf16[1024,256]{1,0:T(8,128)(2,1)S(1)}, u32[]{:S(2)}, u32[]{:S(2)}) collective-permute-start(bf16[1024,256]{1,0:T(8,128)(2,1)S(1)} %collective-permute-done.36.refs_0_.refs_17_), channel_id=1, source_target_pairs={{0,1},{1,0},{2,3},{3,2},{4,5},{5,4},{6,7},{7,6},{8,9},{9,8},{10,11... | collective-permute-start | bytes 1572872 | tf_op jit(solution)/shard_map/ppermute | solution.py:414
  174.2 16.8 %collective-permute-start.34 = (bf16[512,256]{1,0:T(8,128)(2,1)S(1)}, bf16[512,256]{1,0:T(8,128)(2,1)}, u32[]{:S(2)}, u32[]{:S(2)}) collective-permute-start(bf16[512,256]{1,0:T(8,128)(2,1)S(1)} %shard_map.92), channel_id=1, source_target_pairs={{0,16},{16,0},{1,17},{17,1},{2,18},{18,2},{3,19},{19,3},{4,20},{20... | collective-permute-start | bytes 786440 | tf_op jit(solution)/shard_map/ppermute | solution.py:417
  190.0 17.2 %collective-permute-start.23 = (f32[768,256]{1,0:T(8,128)S(1)}, f32[768,256]{1,0:T(8,128)S(1)}, u32[]{:S(2)}, u32[]{:S(2)}) collective-permute-start(f32[768,256]{1,0:T(8,128)S(1)} %get-tuple-element.87), channel_id=1, source_target_pairs={{0,1},{1,0},{2,3},{3,2},{4,5},{5,4},{6,7},{7,6},{8,9},{9,8},{10,11... | collective-permute-start | bytes 2359304 | tf_op jit(solution)/shard_map/ppermute | solution.py:414
  194.0 11.1 %collective-permute-start.37 = (bf16[512,256]{1,0:T(8,128)(2,1)S(1)}, bf16[512,256]{1,0:T(8,128)(2,1)}, u32[]{:S(2)}, u32[]{:S(2)}) collective-permute-start(bf16[512,256]{1,0:T(8,128)(2,1)S(1)} %shard_map.94), channel_id=1, source_target_pairs={{0,16},{16,0},{1,17},{17,1},{2,18},{18,2},{3,19},{19,3},{4,20},{20... | collective-permute-start | bytes 786440 | tf_op jit(solution)/shard_map/ppermute | solution.py:417
  195.0 13.6 %collective-permute-start.24 = (f32[768,256]{1,0:T(8,128)S(1)}, f32[768,256]{1,0:T(8,128)S(1)}, u32[]{:S(2)}, u32[]{:S(2)}) collective-permute-start(f32[768,256]{1,0:T(8,128)S(1)} %get-tuple-element.88), channel_id=1, source_target_pairs={{0,1},{1,0},{2,3},{3,2},{4,5},{5,4},{6,7},{7,6},{8,9},{9,8},{10,11... | collective-permute-start | bytes 2359304 | tf_op jit(solution)/shard_map/ppermute | solution.py:414
  (70 other events, 679.7 us)

commit v6 on v5

--- a/solution.py
+++ b/solution.py
@@ -183,14 +183,14 @@
             terms[0] += sum_refs[0][:, cols]
             terms[1] += sum_refs[1 + n // columns][...]
         out_refs[0][:, cols] = terms[0]
-        out_refs[1 + n // columns][...] = terms[1]
-
-
-def value_sums(own, far, arrays, plan, width, sums=()):
+        out_refs[1 + n // columns][...] = terms[1].astype(out_refs[1].dtype)
+
+
+def value_sums(own, far, arrays, plan, width, sums=(), far_type=jnp.float32):
     rows, depth = own.shape
     tile, columns = rows_tile(rows), 256
     outs = [jax.ShapeDtypeStruct((rows, width), jnp.float32)]
-    outs += [jax.ShapeDtypeStruct((rows, columns), jnp.float32)] * (width // columns)
+    outs += [jax.ShapeDtypeStruct((rows, columns), far_type)] * (width // columns)
     return pl.pallas_call(
         functools.partial(value_kernel, plan, columns, len(sums), len(arrays)),
         out_shape=outs,
@@ -204,6 +204,39 @@
         compiler_params=pltpu.CompilerParams(vmem_limit_bytes=24 << 20),
         cost_estimate=light,
     )(own, far, *sums, *arrays)
+
+
+def cut_kernel(plan, side_ref, *refs):
+    arrays = 1 + max(p[0] for p in plan)
+    array_refs, out_refs, sem = refs[:arrays], refs[arrays:-1], refs[-1]
+    copies = []
+    for j, (i, o, axis, length, even, odd, at) in enumerate(plan):
+        start = pl.multiple_of(even + side_ref[0] * (odd - even), 16 if axis == 0 else lane)
+        src, dst = [slice(None)] * 2, [slice(None)] * 2
+        src[axis], dst[axis] = pl.ds(start, length), slice(at, at + length)
+        copies.append(
+            pltpu.make_async_copy(
+                array_refs[i].at[tuple(src)], out_refs[o].at[tuple(dst)], sem.at[j]
+            )
+        )
+        copies[-1].start()
+    for copy in copies:
+        copy.wait()
+
+
+def cut_shards(arrays, shapes, plan, side):
+    return pl.pallas_call(
+        functools.partial(cut_kernel, plan),
+        out_shape=[jax.ShapeDtypeStruct(s, jnp.bfloat16) for s in shapes],
+        grid_spec=pltpu.PrefetchScalarGridSpec(
+            num_scalar_prefetch=1,
+            in_specs=[far_memory()] * len(arrays),
+            out_specs=[pl.BlockSpec(memory_space=pltpu.VMEM)] * len(shapes),
+            scratch_shapes=[pltpu.SemaphoreType.DMA((len(plan),))],
+        ),
+        compiler_params=pltpu.CompilerParams(vmem_limit_bytes=12 << 20),
+        cost_estimate=light,
+    )(side.reshape(1).astype(jnp.int32), *arrays)
 
 
 def gather_kernel(plan, *refs):
@@ -374,7 +407,7 @@
             num_scalar_prefetch=3,
             grid=(rows // tile,),
             in_specs=[tiled(a, tile) for a in (*sums, *mids, *tokens)]
-            + [far_memory()] * (2 + len(arrays)),
+            + [pl.BlockSpec(memory_space=pltpu.HBM)] * (2 + len(arrays)),
             out_specs=pl.BlockSpec((tile, width), lambda i, *_: (i, 0)),
             scratch_shapes=[pltpu.VMEM(a.shape, a.dtype) for a in arrays]
             + [pltpu.VMEM((docs * rank, tokens[0].shape[1]), jnp.bfloat16)] * 2
@@ -449,31 +482,22 @@
         up = adapter_up_factors.reshape(flat, -1).T
         bit = up.shape[0] // 2
         cut = part + bit
-        v_have = {
-            (0, 0): jnp.concatenate(
-                [
-                    take(value_matrix, side * half, part, 0),
-                    take(up, side * bit, bit, 0),
-                    take(value_matrix, side * half + part, half - part, 0),
-                    take(value_matrix, half + part - side * half, half - part, 0),
-                ],
-                0,
-            )
-        }
-        v_miss = {
-            (0, 0): (
-                jnp.concatenate(
-                    [
-                        take(value_matrix, half - side * half, part, 0),
-                        take(up, bit - side * bit, bit, 0),
-                    ],
-                    0,
-                ),
-                0,
-            )
-        }
-        d_have = {(0, 0): take(down, side * half, half, 1)}
-        d_rest = take(down, half - side * half, half, 1)
+        rest = half - part
+        plan = (
+            (0, 0, 0, part, 0, half, 0),
+            (1, 0, 0, bit, 0, bit, part),
+            (0, 0, 0, rest, part, half + part, cut),
+            (0, 0, 0, rest, half + part, part, cut + rest),
+            (0, 1, 0, part, half, 0, 0),
+            (1, 1, 0, bit, bit, 0, part),
+            (2, 2, 1, half, 0, half, 0),
+            (2, 3, 1, half, half, 0, 0),
+        )
+        shapes = [(cut + 2 * rest, width), (cut, width), (flat, half), (flat, half)]
+        v_first, v_second, d_first, d_rest = cut_shards(
+            [value_matrix, up, down], shapes, plan, side
+        )
+        v_have, v_miss, d_have = {(0, 0): v_first}, {(0, 0): (v_second, 0)}, {(0, 0): d_first}
 
         ends = jnp.cumsum(document_lengths, axis=1).astype(jnp.int32)
         slots = jnp.sum(
@@ -489,11 +513,9 @@
         d_miss = {(0, 0): (pick_adapters([d_rest], slots_both, rank), 0)}
         chosen = slots_both.size * rank
 
-        order = [0]
-        for k in range(1, depth // 2 + 1):
-            order += [k, depth - k] if k != depth - k else [k]
+        order = list(range(depth))
         names = [(k, dy) for k in order for dy in range(rows_y)]
-        z, y, x = Line(along_z), Line(along_y, 2), Line(along_x)
+        z, y, x = Line(along_z, 3), Line(along_y, 3), Line(along_x, 3)
 
         def x_values(names, *earlier):
             got = x(after(jnp.concatenate([v_have[name][:cut] for name in names], 0), *earlier))
@@ -587,7 +609,9 @@
         for k in early:
             d_have[k, 1] = y(d_have[k, 0])
         arrays, plan = values(first)
-        sums = value_sums(after(own, v_have[last, 1]), partner, arrays, plan, width)
+        sums = value_sums(
+            after(own, v_have[last, 1], *[d_have[k, 0] for k in early], d_have[early[0], 1]), partner, arrays, plan, width
+        )
         x_values([(last, 1)], sums[0])
         for k in early:
             x_down([(k, 0)])
@@ -597,9 +621,9 @@
         x_down([(last, 0)])
 
         arrays, plan = values(second)
-        ready = [d_have[k, 0] for k in ks]
+        ready = [d_have[last, 1], d_miss[last, 0][0]]
         sum_own, *sum_far = value_sums(
-            after(own_rest, *ready), partner_rest, arrays, plan, width, sums
+            after(own_rest, *ready), partner_rest, arrays, plan, width, sums, jnp.bfloat16
         )
         sums = (sum_own, *[across(part) for part in sum_far])
         up_lane = ups(names)

time: 247 us -> 264 us (1.069)
  waiting for transfers between devices: 59.7 us -> 113 us
  starting transfers between devices: 65.9 us -> 45.3 us
  local copies, waits for them, and re-layouts: 53.9 us -> 42.6 us
  other arithmetic: 3.65 us -> 0.39 us
    ppermute x6, waiting for transfers between devices: 35 us -> 68 us  [along_z(): lax.ppermute(value, 'store', pairs(lambda z, y, c: ((z + k) % depth, y, c)))]
    ppermute x17, starting transfers between devices: 37 us -> 12.3 us  [across(): return lax.ppermute(value, 'store', pairs(lambda z, y, c: (z, y, 1 - c)))]
    ppermute x15, waiting for transfers between devices: 14.4 us -> 30.5 us  [along_x(): return lax.ppermute(value, 'groups', [(g, g ^ 1) for g in range(groups)])]
    dynamic_slice x3 -> x0, local copies, waits for them, and re-layouts: 4.4 us -> none  [the longest x1 2.24 us: per_device(): d_rest = take(down, half - side * half, half, 1)]
    ppermute x8, waiting for transfers between devices: 6.64 us -> 10.9 us  [along_y(): return lax.ppermute(value, 'store', pairs(lambda z, y, c: (z, 1 - y, c)))]
    slice x7, local copies, waits for them, and re-layouts: 5.83 us -> 2.25 us  [x_values(): v_have[name][:cut]]
    unnamed x114 -> x104, local copies, waits for them, and re-layouts: 40.1 us -> 39.2 us
  transfers between devices with their start and end apart: 46 -> 46, of which waited for: 15 -> 20; matrix products, arithmetic and copies ran while one was open for 8% -> 1% of each run, Pallas kernels for 15% -> 14%
where the time goes in v6:
time: 264 us; the launch traced here: 262 us
  waiting for transfers between devices  113 us (43%)
  Pallas kernels  60.2 us (23%)
  starting transfers between devices  45.3 us (17%)
  local copies, waits for them, and re-layouts  42.6 us (16%)
    ppermute x6, waiting for transfers between devices, along_z(): lax.ppermute(value, 'store', pairs(lambda z, y, c: ((z + k) % depth, y, c)))  68 us
    unnamed x104, local copies, waits for them, and re-layouts  39.2 us
    ppermute x15, waiting for transfers between devices, along_x(): return lax.ppermute(value, 'groups', [(g, g ^ 1) for g in range(groups)])  30.5 us
    pallas_call x2, Pallas kernels, value_sums(): pl.pallas_call(functools.partial(value_kernel, plan, columns, len(sums),...  22.6 us
    pallas_call x1, Pallas kernels, last_values(): pl.pallas_call(functools.partial(last_kernel, rank, parts, len(sums), len...  15.5 us
    ppermute x15, starting transfers between devices, along_x(): return lax.ppermute(value, 'groups', [(g, g ^ 1) for g in range(groups)])  15.5 us
    ppermute x17, starting transfers between devices, across(): return lax.ppermute(value, 'store', pairs(lambda z, y, c: (z, y, 1 - c)))  12.3 us
    ppermute x8, waiting for transfers between devices, along_y(): return lax.ppermute(value, 'store', pairs(lambda z, y, c: (z, 1 - y, c)))  10.9 us
  transfers between devices with their start and end apart: 46, of which 20 were waited for; matrix products, arithmetic and copies ran while one was open for 1% of the time, Pallas kernels for 14%

profile of v6, /device:TPU:9, one launch (start us, length us, event | category | flops | bytes accessed | tf_op | source)
XLA Modules:
  0.0 261.7 jit_solution(2597735098600985614)
XLA Ops:
  0.9 4.6 %copy-done = bf16[768,8192]{1,0:T(8,128)(2,1)S(1)} copy-done((bf16[768,8192]{1,0:T(8,128)(2,1)S(1)}, bf16[768,8192]{1,0:T(8,128)(2,1)}, u32[]{:S(2)}) %copy-start) | copy-done | bytes 12582936
  5.5 8.5 %shard_map.82 = (bf16[768,2048]{1,0:T(8,128)(2,1)S(1)}, bf16[768,2048]{1,0:T(8,128)(2,1)S(1)}, bf16[768,2048]{1,0:T(8,128)(2,1)}, bf16[768,2048]{1,0:T(8,128)(2,1)}) custom-call(s32[64]{0:T(128)S(1)} %stack.391.source_ref, bf16[768,8192]{1,0:T(8,128)(2,1)S(1)} %copy-done, bf16[1,8192]{1,0:T(2,128)(2,1)S(1)} %reshape.18.gain_ref), custom_call_target="tpu_custom_call" | custom-call | tf_op jit(solution)/shard_map/pallas_call | solution.py:100
  14.0 1.7 copy-done.1
  19.0 1.9 shard_map.83
  29.5 1.5 collective-permute-done.6.slots_ref
  31.2 9.6 %collective-permute-done.16.refs_6_.refs_4_ = bf16[352,1024]{1,0:T(8,128)(2,1)} collective-permute-done((bf16[352,1024]{1,0:T(8,128)(2,1)}, bf16[352,1024]{1,0:T(8,128)(2,1)}, u32[]{:S(2)}, u32[]{:S(2)}) %collective-permute-start.16) | collective-permute-done | bytes 720928 | tf_op jit(solution)/shard_map/ppermute | solution.py:441
  40.8 2.5 collective-permute-start.7
  47.0 4.8 %collective-permute-done.2.refs_0_.refs_4_ = bf16[1024,256]{1,0:T(8,128)(2,1)S(1)} collective-permute-done((bf16[1024,256]{1,0:T(8,128)(2,1)}, bf16[1024,256]{1,0:T(8,128)(2,1)S(1)}, u32[]{:S(2)}, u32[]{:S(2)}) %collective-permute-start.2) | collective-permute-done | bytes 524320 | tf_op jit(solution)/shard_map/ppermute | solution.py:444
  53.1 5.2 %collective-permute-done.refs_11_.refs_12_ = bf16[352,1024]{1,0:T(8,128)(2,1)S(1)} collective-permute-done((bf16[352,1024]{1,0:T(8,128)(2,1)}, bf16[352,1024]{1,0:T(8,128)(2,1)S(1)}, u32[]{:S(2)}, u32[]{:S(2)}) %collective-permute-start) | collective-permute-done | bytes 720928 | tf_op jit(solution)/shard_map/ppermute | solution.py:441
  58.3 1.5 collective-permute-start.3
  60.4 26.8 %collective-permute-done.7.refs_7_.refs_8_ = bf16[352,1024]{1,0:T(8,128)(2,1)S(1)} collective-permute-done((bf16[352,1024]{1,0:T(8,128)(2,1)}, bf16[352,1024]{1,0:T(8,128)(2,1)S(1)}, u32[]{:S(2)}, u32[]{:S(2)}) %collective-permute-start.7) | collective-permute-done | bytes 720928 | tf_op jit(solution)/shard_map/ppermute | solution.py:441
  89.3 5.5 %collective-permute-done.22.refs_5_ = bf16[512,256]{1,0:T(8,128)(2,1)S(1)} collective-permute-done((bf16[512,256]{1,0:T(8,128)(2,1)S(1)}, bf16[512,256]{1,0:T(8,128)(2,1)S(1)}, u32[]{:S(2)}, u32[]{:S(2)}) %collective-permute-start.22) | collective-permute-done | bytes 262176 | tf_op jit(solution)/shard_map/ppermute | solution.py:450
  97.4 5.3 %collective-permute-done.17.refs_0_.refs_6_ = bf16[1024,256]{1,0:T(8,128)(2,1)S(1)} collective-permute-done((bf16[1024,256]{1,0:T(8,128)(2,1)}, bf16[1024,256]{1,0:T(8,128)(2,1)S(1)}, u32[]{:S(2)}, u32[]{:S(2)}) %collective-permute-start.17) | collective-permute-done | bytes 524320 | tf_op jit(solution)/shard_map/ppermute | solution.py:441
  102.7 1.7 collective-permute-start.8
  108.5 3.9 %collective-permute-done.24.refs_9_.refs_10_ = bf16[352,1024]{1,0:T(8,128)(2,1)S(1)} collective-permute-done((bf16[352,1024]{1,0:T(8,128)(2,1)S(1)}, bf16[352,1024]{1,0:T(8,128)(2,1)S(1)}, u32[]{:S(2)}, u32[]{:S(2)}) %collective-permute-start.24) | collective-permute-done | bytes 720928 | tf_op jit(solution)/shard_map/ppermute | solution.py:444
  112.4 1.9 collective-permute-start.1
  114.3 2.4 collective-permute-done.21.refs_7_.refs_5_
  116.9 21.0 %collective-permute-done.8.refs_0_.refs_11_ = bf16[1024,256]{1,0:T(8,128)(2,1)S(1)} collective-permute-done((bf16[1024,256]{1,0:T(8,128)(2,1)}, bf16[1024,256]{1,0:T(8,128)(2,1)S(1)}, u32[]{:S(2)}, u32[]{:S(2)}) %collective-permute-start.8) | collective-permute-done | bytes 524320 | tf_op jit(solution)/shard_map/ppermute | solution.py:441
  138.0 10.1 %shard_map.87 = (f32[768,1024]{1,0:T(8,128)S(1)}, f32[768,256]{1,0:T(8,128)S(1)}, f32[768,256]{1,0:T(8,128)S(1)}, f32[768,256]{1,0:T(8,128)S(1)}, f32[768,256]{1,0:T(8,128)S(1)}) custom-call(bf16[768,2048]{1,0:T(8,128)(2,1)S(1)} %get-tuple-element.78.refs_0_, bf16[768,2048]{1,0:T(8,128)(2,1)} %collective-permute-done.18.refs_1_, ...), custom_call_target="tpu_custom_call" | custom-call | tf_op jit(solution)/shard_map/pallas_call | solution.py:194
  149.5 8.9 %collective-permute-done.26.refs_14_.refs_15_ = bf16[224,1024]{1,0:T(8,128)(2,1)S(1)} collective-permute-done((bf16[224,1024]{1,0:T(8,128)(2,1)S(1)}, bf16[224,1024]{1,0:T(8,128)(2,1)S(1)}, u32[]{:S(2)}, u32[]{:S(2)}) %collective-permute-start.26) | collective-permute-done | bytes 458784 | tf_op jit(solution)/shard_map/ppermute | solution.py:450
  159.7 2.8 %collective-permute-start.34 = (bf16[512,1024]{1,0:T(8,128)(2,1)S(1)}, bf16[512,1024]{1,0:T(8,128)(2,1)S(1)}, u32[]{:S(2)}, u32[]{:S(2)}) collective-permute-start(bf16[512,1024]{1,0:T(8,128)(2,1)S(1)} %shard_map.93.refs_9_), channel_id=1, source_target_pairs={{0,1},{1,0},{2,3},{3,2},{4,5},{5,4},{6,7},{7,6},{8,9},{9,8},{10,11... | collective-permute-start | bytes 3145736 | tf_op jit(solution)/shard_map/ppermute | solution.py:447
  167.3 4.6 %collective-permute-done.13.refs_12_ = bf16[512,256]{1,0:T(8,128)(2,1)S(1)} collective-permute-done((bf16[512,256]{1,0:T(8,128)(2,1)S(1)}, bf16[512,256]{1,0:T(8,128)(2,1)S(1)}, u32[]{:S(2)}, u32[]{:S(2)}) %collective-permute-start.13) | collective-permute-done | bytes 262176 | tf_op jit(solution)/shard_map/ppermute | solution.py:450
  173.8 2.1 collective-permute-done.4.refs_0_.refs_17_
  177.9 1.7 collective-permute-start.38
  179.6 3.6 %collective-permute-done.32.refs_9_ = bf16[512,256]{1,0:T(8,128)(2,1)S(1)} collective-permute-done((bf16[512,256]{1,0:T(8,128)(2,1)S(1)}, bf16[512,256]{1,0:T(8,128)(2,1)S(1)}, u32[]{:S(2)}, u32[]{:S(2)}) %collective-permute-start.32) | collective-permute-done | bytes 262176 | tf_op jit(solution)/shard_map/ppermute | solution.py:450
  183.2 2.0 collective-permute-start.42
  185.2 5.8 %shard_map.92 = (f32[768,64]{1,0:T(8,128)S(1)}, f32[768,64]{1,0:T(8,128)S(1)}) custom-call(s32[2,4]{1,0:T(2,128)S(1)} %pad_add_fusion.ends_ref, s32[2,4]{1,0:T(2,128)S(1)} %pad_add_fusion.2.slots_ref, bf16[768,2048]{1,0:T(8,128)(2,1)S(1)} %get-tuple-element.78.refs_0_, bf16[768,2048]{1,0:T(8,128)(2,1)} %collective-permute-done.18.refs_1_, ...), custom_call_target="tpu_custom_call" | custom-call | tf_op jit(solution)/shard_map/pallas_call | solution.py:325
  198.3 3.9 %collective-permute-done.36.refs_14_ = bf16[512,256]{1,0:T(8,128)(2,1)S(1)} collective-permute-done((bf16[512,256]{1,0:T(8,128)(2,1)S(1)}, bf16[512,256]{1,0:T(8,128)(2,1)S(1)}, u32[]{:S(2)}, u32[]{:S(2)}) %collective-permute-start.36) | collective-permute-done | bytes 262176 | tf_op jit(solution)/shard_map/ppermute | solution.py:450
  206.5 12.5 %shard_map.88 = (f32[768,1024]{1,0:T(8,128)S(1)}, bf16[768,256]{1,0:T(8,128)(2,1)}, bf16[768,256]{1,0:T(8,128)(2,1)}, bf16[768,256]{1,0:T(8,128)(2,1)}, bf16[768,256]{1,0:T(8,128)(2,1)}) custom-call(bf16[768,2048]{1,0:T(8,128)(2,1)S(1)} %copy-done.2, bf16[768,2048]{1,0:T(8,128)(2,1)} %collective-permute-done.15.refs_1_, ...), custom_call_target="tpu_custom_call" | custom-call | tf_op jit(solution)/shard_map/pallas_call | solution.py:194
  219.0 1.7 copy-done.6
  227.8 1.9 copy-done.7
  246.0 15.5 %shard_map.96 = bf16[768,1024]{1,0:T(8,128)(2,1)} custom-call(s32[4]{0:T(128)S(1)} %select_reduce_fusion.slots_ref, s32[4]{0:T(128)S(1)} %bitcast.107, s32[2,16]{1,0:T(2,128)S(1)} %reshape.17.at_ref, f32[768,1024]{1,0:T(8,128)S(1)} %copy-done.7, bf16[768,256]{1,0:T(8,128)(2,1)} %collective-permute-done.27.refs_1_, ...), custom_call_target="tpu_custom_call" | custom-call | tf_op jit(solution)/shard_map/pallas_call | solution.py:403
  (197 shorter events, 73.4 us)
Async XLA Ops:
  15.7 29.9 %collective-permute-start.18 = (bf16[768,2048]{1,0:T(8,128)(2,1)}, bf16[768,2048]{1,0:T(8,128)(2,1)}, u32[]{:S(2)}, u32[]{:S(2)}) collective-permute-start(bf16[768,2048]{1,0:T(8,128)(2,1)} %get-tuple-element.75), channel_id=1, source_target_pairs={{0,1},{1,0},{2,3},{3,2},{4,5},{5,4},{6,7},{7,6},{8,9},{9,8},{10,11... | collective-permute-start | bytes 9437192 | tf_op jit(solution)/shard_map/ppermute | solution.py:447
  16.4 79.8 %collective-permute-start.15 = (bf16[768,2048]{1,0:T(8,128)(2,1)}, bf16[768,2048]{1,0:T(8,128)(2,1)}, u32[]{:S(2)}, u32[]{:S(2)}) collective-permute-start(bf16[768,2048]{1,0:T(8,128)(2,1)} %get-tuple-element.72.refs_8_), channel_id=1, source_target_pairs={{0,1},{1,0},{2,3},{3,2},{4,5},{5,4},{6,7},{7,6},{8,9},{9,8},{10,11... | collective-permute-start | bytes 9437192 | tf_op jit(solution)/shard_map/ppermute | solution.py:447
  23.3 17.5 %collective-permute-start.16 = (bf16[352,1024]{1,0:T(8,128)(2,1)}, bf16[352,1024]{1,0:T(8,128)(2,1)}, u32[]{:S(2)}, u32[]{:S(2)}) collective-permute-start(bf16[352,1024]{1,0:T(8,128)(2,1)} %get-tuple-element.61.refs_2_.refs_0_), channel_id=1, source_target_pairs={{0,4},{1,5},{2,6},{3,7},{4,8},{5,9},{6,10},{7,11},{8,12},{9,13},{1... | collective-permute-start | bytes 2162696 | tf_op jit(solution)/shard_map/ppermute | solution.py:441
  24.6 18.7 %collective-permute-start.9 = (bf16[352,1024]{1,0:T(8,128)(2,1)}, bf16[352,1024]{1,0:T(8,128)(2,1)}, u32[]{:S(2)}, u32[]{:S(2)}) collective-permute-start(bf16[352,1024]{1,0:T(8,128)(2,1)} %get-tuple-element.61.refs_2_.refs_0_), channel_id=1, source_target_pairs={{0,2},{1,3},{2,0},{3,1},{4,6},{5,7},{6,4},{7,5},{8,10},{9,11},{10,... | collective-permute-start | bytes 2162696 | tf_op jit(solution)/shard_map/ppermute | solution.py:444
  31.0 27.3 %collective-permute-start = (bf16[352,1024]{1,0:T(8,128)(2,1)}, bf16[352,1024]{1,0:T(8,128)(2,1)S(1)}, u32[]{:S(2)}, u32[]{:S(2)}) collective-permute-start(bf16[352,1024]{1,0:T(8,128)(2,1)} %get-tuple-element.61.refs_2_.refs_0_), channel_id=1, source_target_pairs={{0,12},{1,13},{2,14},{3,15},{4,0},{5,1},{6,2},{7,3},{8,4},{9,5},{1... | collective-permute-start | bytes 2162696 | tf_op jit(solution)/shard_map/ppermute | solution.py:441
  40.8 46.5 %collective-permute-start.7 = (bf16[352,1024]{1,0:T(8,128)(2,1)}, bf16[352,1024]{1,0:T(8,128)(2,1)S(1)}, u32[]{:S(2)}, u32[]{:S(2)}) collective-permute-start(bf16[352,1024]{1,0:T(8,128)(2,1)} %get-tuple-element.61.refs_2_.refs_0_), channel_id=1, source_target_pairs={{0,8},{1,9},{2,10},{3,11},{4,12},{5,13},{6,14},{7,15},{8,0},{9,1},... | collective-permute-start | bytes 2162696 | tf_op jit(solution)/shard_map/ppermute | solution.py:441
  45.6 42.9 %collective-permute-start.10 = (bf16[224,1024]{1,0:T(8,128)(2,1)S(1)}, bf16[224,1024]{1,0:T(8,128)(2,1)S(1)}, u32[]{:S(2)}, u32[]{:S(2)}) collective-permute-start(bf16[224,1024]{1,0:T(8,128)(2,1)S(1)} %slice.38), channel_id=1, source_target_pairs={{0,16},{16,0},{1,17},{17,1},{2,18},{18,2},{3,19},{19,3},{4,20},{20... | collective-permute-start | bytes 1376264 | tf_op jit(solution)/shard_map/ppermute | solution.py:450
  51.8 52.6 %collective-permute-start.19 = (bf16[352,1024]{1,0:T(8,128)(2,1)}, bf16[352,1024]{1,0:T(8,128)(2,1)S(1)}, u32[]{:S(2)}, u32[]{:S(2)}) collective-permute-start(bf16[352,1024]{1,0:T(8,128)(2,1)} %collective-permute-done.16.refs_6_.refs_4_), channel_id=1, source_target_pairs={{0,2},{1,3},{2,0},{3,1},{4,6},{5,7},{6,4},{7,5},{8,10},{9,11},{10,... | collective-permute-start | bytes 2162696 | tf_op jit(solution)/shard_map/ppermute | solution.py:444
  58.3 48.4 %collective-permute-start.3 = (bf16[352,1024]{1,0:T(8,128)(2,1)S(1)}, bf16[352,1024]{1,0:T(8,128)(2,1)S(1)}, u32[]{:S(2)}, u32[]{:S(2)}) collective-permute-start(bf16[352,1024]{1,0:T(8,128)(2,1)S(1)} %collective-permute-done.refs_11_.refs_12_), channel_id=1, source_target_pairs={{0,2},{1,3},{2,0},{3,1},{4,6},{5,7},{6,4},{7,5},{8,10},{9,11},{10,... | collective-permute-start | bytes 2162696 | tf_op jit(solution)/shard_map/ppermute | solution.py:444
  88.6 14.2 %collective-permute-start.17 = (bf16[1024,256]{1,0:T(8,128)(2,1)}, bf16[1024,256]{1,0:T(8,128)(2,1)S(1)}, u32[]{:S(2)}, u32[]{:S(2)}) collective-permute-start(bf16[1024,256]{1,0:T(8,128)(2,1)} %copy-done.30), channel_id=1, source_target_pairs={{0,4},{1,5},{2,6},{3,7},{4,8},{5,9},{6,10},{7,11},{8,12},{9,13},{1... | collective-permute-start | bytes 1572872 | tf_op jit(solution)/shard_map/ppermute | solution.py:441
  94.8 12.2 %collective-permute-start.11 = (bf16[224,1024]{1,0:T(8,128)(2,1)S(1)}, bf16[224,1024]{1,0:T(8,128)(2,1)S(1)}, u32[]{:S(2)}, u32[]{:S(2)}) collective-permute-start(bf16[224,1024]{1,0:T(8,128)(2,1)S(1)} %slice.37), channel_id=1, source_target_pairs={{0,16},{16,0},{1,17},{17,1},{2,18},{18,2},{3,19},{19,3},{4,20},{20... | collective-permute-start | bytes 1376264 | tf_op jit(solution)/shard_map/ppermute | solution.py:450
  96.2 16.2 %collective-permute-start.24 = (bf16[352,1024]{1,0:T(8,128)(2,1)S(1)}, bf16[352,1024]{1,0:T(8,128)(2,1)S(1)}, u32[]{:S(2)}, u32[]{:S(2)}) collective-permute-start(bf16[352,1024]{1,0:T(8,128)(2,1)S(1)} %collective-permute-done.7.refs_7_.refs_8_), channel_id=1, source_target_pairs={{0,2},{1,3},{2,0},{3,1},{4,6},{5,7},{6,4},{7,5},{8,10},{9,11},{10,... | collective-permute-start | bytes 2162696 | tf_op jit(solution)/shard_map/ppermute | solution.py:444
  102.7 35.1 %collective-permute-start.8 = (bf16[1024,256]{1,0:T(8,128)(2,1)}, bf16[1024,256]{1,0:T(8,128)(2,1)S(1)}, u32[]{:S(2)}, u32[]{:S(2)}) collective-permute-start(bf16[1024,256]{1,0:T(8,128)(2,1)} %copy-done.30), channel_id=1, source_target_pairs={{0,8},{1,9},{2,10},{3,11},{4,12},{5,13},{6,14},{7,15},{8,0},{9,1},... | collective-permute-start | bytes 1572872 | tf_op jit(solution)/shard_map/ppermute | solution.py:441
  104.4 33.5 %collective-permute-start.20 = (bf16[1024,256]{1,0:T(8,128)(2,1)S(1)}, bf16[1024,256]{1,0:T(8,128)(2,1)S(1)}, u32[]{:S(2)}, u32[]{:S(2)}) collective-permute-start(bf16[1024,256]{1,0:T(8,128)(2,1)S(1)} %collective-permute-done.17.refs_0_.refs_6_), channel_id=1, source_target_pairs={{0,2},{1,3},{2,0},{3,1},{4,6},{5,7},{6,4},{7,5},{8,10},{9,11},{10,... | collective-permute-start | bytes 1572872 | tf_op jit(solution)/shard_map/ppermute | solution.py:444
  107.0 31.0 %collective-permute-start.23 = (bf16[224,1024]{1,0:T(8,128)(2,1)S(1)}, bf16[224,1024]{1,0:T(8,128)(2,1)S(1)}, u32[]{:S(2)}, u32[]{:S(2)}) collective-permute-start(bf16[224,1024]{1,0:T(8,128)(2,1)S(1)} %slice.40), channel_id=1, source_target_pairs={{0,16},{16,0},{1,17},{17,1},{2,18},{18,2},{3,19},{19,3},{4,20},{20... | collective-permute-start | bytes 1376264 | tf_op jit(solution)/shard_map/ppermute | solution.py:450
  112.4 50.1 %collective-permute-start.1 = (bf16[1024,256]{1,0:T(8,128)(2,1)S(1)}, bf16[1024,256]{1,0:T(8,128)(2,1)S(1)}, u32[]{:S(2)}, u32[]{:S(2)}) collective-permute-start(bf16[1024,256]{1,0:T(8,128)(2,1)S(1)} %copy-done.31), channel_id=1, source_target_pairs={{0,12},{1,13},{2,14},{3,15},{4,0},{5,1},{6,2},{7,3},{8,4},{9,5},{1... | collective-permute-start | bytes 1572872 | tf_op jit(solution)/shard_map/ppermute | solution.py:441
  116.7 32.8 %collective-permute-start.12 = (bf16[224,1024]{1,0:T(8,128)(2,1)S(1)}, bf16[224,1024]{1,0:T(8,128)(2,1)S(1)}, u32[]{:S(2)}, u32[]{:S(2)}) collective-permute-start(bf16[224,1024]{1,0:T(8,128)(2,1)S(1)} %slice.36), channel_id=1, source_target_pairs={{0,16},{16,0},{1,17},{17,1},{2,18},{18,2},{3,19},{19,3},{4,20},{20... | collective-permute-start | bytes 1376264 | tf_op jit(solution)/shard_map/ppermute | solution.py:450
  137.8 11.6 %collective-permute-start.25 = (bf16[224,1024]{1,0:T(8,128)(2,1)S(1)}, bf16[224,1024]{1,0:T(8,128)(2,1)S(1)}, u32[]{:S(2)}, u32[]{:S(2)}) collective-permute-start(bf16[224,1024]{1,0:T(8,128)(2,1)S(1)} %slice.41), channel_id=1, source_target_pairs={{0,16},{16,0},{1,17},{17,1},{2,18},{18,2},{3,19},{19,3},{4,20},{20... | collective-permute-start | bytes 1376264 | tf_op jit(solution)/shard_map/ppermute | solution.py:450
  159.7 34.0 %collective-permute-start.34 = (bf16[512,1024]{1,0:T(8,128)(2,1)S(1)}, bf16[512,1024]{1,0:T(8,128)(2,1)S(1)}, u32[]{:S(2)}, u32[]{:S(2)}) collective-permute-start(bf16[512,1024]{1,0:T(8,128)(2,1)S(1)} %shard_map.93.refs_9_), channel_id=1, source_target_pairs={{0,1},{1,0},{2,3},{3,2},{4,5},{5,4},{6,7},{7,6},{8,9},{9,8},{10,11... | collective-permute-start | bytes 3145736 | tf_op jit(solution)/shard_map/ppermute | solution.py:447
  162.5 13.5 %collective-permute-start.4 = (bf16[1024,256]{1,0:T(8,128)(2,1)S(1)}, bf16[1024,256]{1,0:T(8,128)(2,1)S(1)}, u32[]{:S(2)}, u32[]{:S(2)}) collective-permute-start(bf16[1024,256]{1,0:T(8,128)(2,1)S(1)} %collective-permute-done.1.refs_0_.refs_15_), channel_id=1, source_target_pairs={{0,2},{1,3},{2,0},{3,1},{4,6},{5,7},{6,4},{7,5},{8,10},{9,11},{10,... | collective-permute-start | bytes 1572872 | tf_op jit(solution)/shard_map/ppermute | solution.py:444
  165.7 25.4 %collective-permute-start.35 = (bf16[1024,256]{1,0:T(8,128)(2,1)S(1)}, bf16[1024,256]{1,0:T(8,128)(2,1)S(1)}, u32[]{:S(2)}, u32[]{:S(2)}) collective-permute-start(bf16[1024,256]{1,0:T(8,128)(2,1)S(1)} %collective-permute-done.8.refs_0_.refs_11_), channel_id=1, source_target_pairs={{0,2},{1,3},{2,0},{3,1},{4,6},{5,7},{6,4},{7,5},{8,10},{9,11},{10,... | collective-permute-start | bytes 1572872 | tf_op jit(solution)/shard_map/ppermute | solution.py:444
  166.5 11.4 %collective-permute-start.31 = (bf16[512,256]{1,0:T(8,128)(2,1)S(1)}, bf16[512,256]{1,0:T(8,128)(2,1)S(1)}, u32[]{:S(2)}, u32[]{:S(2)}) collective-permute-start(bf16[512,256]{1,0:T(8,128)(2,1)S(1)} %shard_map.90), channel_id=1, source_target_pairs={{0,16},{16,0},{1,17},{17,1},{2,18},{18,2},{3,19},{19,3},{4,20},{20... | collective-permute-start | bytes 786440 | tf_op jit(solution)/shard_map/ppermute | solution.py:450
  172.0 11.2 %collective-permute-start.32 = (bf16[512,256]{1,0:T(8,128)(2,1)S(1)}, bf16[512,256]{1,0:T(8,128)(2,1)S(1)}, u32[]{:S(2)}, u32[]{:S(2)}) collective-permute-start(bf16[512,256]{1,0:T(8,128)(2,1)S(1)} %shard_map.91), channel_id=1, source_target_pairs={{0,16},{16,0},{1,17},{17,1},{2,18},{18,2},{3,19},{19,3},{4,20},{20... | collective-permute-start | bytes 786440 | tf_op jit(solution)/shard_map/ppermute | solution.py:450
  176.0 15.1 %collective-permute-start.14 = (bf16[512,256]{1,0:T(8,128)(2,1)S(1)}, bf16[512,256]{1,0:T(8,128)(2,1)S(1)}, u32[]{:S(2)}, u32[]{:S(2)}) collective-permute-start(bf16[512,256]{1,0:T(8,128)(2,1)S(1)} %shard_map.84), channel_id=1, source_target_pairs={{0,16},{16,0},{1,17},{17,1},{2,18},{18,2},{3,19},{19,3},{4,20},{20... | collective-permute-start | bytes 786440 | tf_op jit(solution)/shard_map/ppermute | solution.py:450
  177.9 18.1 %collective-permute-start.38 = (bf16[1024,256]{1,0:T(8,128)(2,1)S(1)}, bf16[1024,256]{1,0:T(8,128)(2,1)S(1)}, u32[]{:S(2)}, u32[]{:S(2)}) collective-permute-start(bf16[1024,256]{1,0:T(8,128)(2,1)S(1)} %collective-permute-done.8.refs_0_.refs_11_), channel_id=1, source_target_pairs={{0,1},{1,0},{2,3},{3,2},{4,5},{5,4},{6,7},{7,6},{8,9},{9,8},{10,11... | collective-permute-start | bytes 1572872 | tf_op jit(solution)/shard_map/ppermute | solution.py:447
  183.2 13.6 %collective-permute-start.42 = (bf16[1024,256]{1,0:T(8,128)(2,1)S(1)}, bf16[1024,256]{1,0:T(8,128)(2,1)S(1)}, u32[]{:S(2)}, u32[]{:S(2)}) collective-permute-start(bf16[1024,256]{1,0:T(8,128)(2,1)S(1)} %collective-permute-done.1.refs_0_.refs_15_), channel_id=1, source_target_pairs={{0,1},{1,0},{2,3},{3,2},{4,5},{5,4},{6,7},{7,6},{8,9},{9,8},{10,11... | collective-permute-start | bytes 1572872 | tf_op jit(solution)/shard_map/ppermute | solution.py:447
  191.2 12.4 %collective-permute-start.44 = (bf16[1024,256]{1,0:T(8,128)(2,1)S(1)}, bf16[1024,256]{1,0:T(8,128)(2,1)S(1)}, u32[]{:S(2)}, u32[]{:S(2)}) collective-permute-start(bf16[1024,256]{1,0:T(8,128)(2,1)S(1)} %collective-permute-done.4.refs_0_.refs_17_), channel_id=1, source_target_pairs={{0,1},{1,0},{2,3},{3,2},{4,5},{5,4},{6,7},{7,6},{8,9},{9,8},{10,11... | collective-permute-start | bytes 1572872 | tf_op jit(solution)/shard_map/ppermute | solution.py:447
  193.6 29.1 %collective-permute-start.40 = (bf16[1024,256]{1,0:T(8,128)(2,1)S(1)}, bf16[1024,256]{1,0:T(8,128)(2,1)S(1)}, u32[]{:S(2)}, u32[]{:S(2)}) collective-permute-start(bf16[1024,256]{1,0:T(8,128)(2,1)S(1)} %collective-permute-done.35.refs_0_.refs_13_), channel_id=1, source_target_pairs={{0,1},{1,0},{2,3},{3,2},{4,5},{5,4},{6,7},{7,6},{8,9},{9,8},{10,11... | collective-permute-start | bytes 1572872 | tf_op jit(solution)/shard_map/ppermute | solution.py:447
  196.0 24.7 %collective-permute-start.39 = (bf16[512,256]{1,0:T(8,128)(2,1)S(1)}, bf16[512,256]{1,0:T(8,128)(2,1)S(1)}, u32[]{:S(2)}, u32[]{:S(2)}) collective-permute-start(bf16[512,256]{1,0:T(8,128)(2,1)S(1)} %collective-permute-done.13.refs_12_), channel_id=1, source_target_pairs={{0,1},{1,0},{2,3},{3,2},{4,5},{5,4},{6,7},{7,6},{8,9},{9,8},{10,11... | collective-permute-start | bytes 786440 | tf_op jit(solution)/shard_map/ppermute | solution.py:447
  197.6 23.9 %collective-permute-start.43 = (bf16[512,256]{1,0:T(8,128)(2,1)S(1)}, bf16[512,256]{1,0:T(8,128)(2,1)S(1)}, u32[]{:S(2)}, u32[]{:S(2)}) collective-permute-start(bf16[512,256]{1,0:T(8,128)(2,1)S(1)} %collective-permute-done.14.refs_16_), channel_id=1, source_target_pairs={{0,1},{1,0},{2,3},{3,2},{4,5},{5,4},{6,7},{7,6},{8,9},{9,8},{10,11... | collective-permute-start | bytes 786440 | tf_op jit(solution)/shard_map/ppermute | solution.py:447
  202.2 21.3 %collective-permute-start.37 = (bf16[512,256]{1,0:T(8,128)(2,1)S(1)}, bf16[512,256]{1,0:T(8,128)(2,1)}, u32[]{:S(2)}, u32[]{:S(2)}) collective-permute-start(bf16[512,256]{1,0:T(8,128)(2,1)S(1)} %shard_map.95), channel_id=1, source_target_pairs={{0,16},{16,0},{1,17},{17,1},{2,18},{18,2},{3,19},{19,3},{4,20},{20... | collective-permute-start | bytes 786440 | tf_op jit(solution)/shard_map/ppermute | solution.py:450
  204.3 19.7 %collective-permute-start.41 = (bf16[512,256]{1,0:T(8,128)(2,1)S(1)}, bf16[512,256]{1,0:T(8,128)(2,1)S(1)}, u32[]{:S(2)}, u32[]{:S(2)}) collective-permute-start(bf16[512,256]{1,0:T(8,128)(2,1)S(1)} %collective-permute-done.36.refs_14_), channel_id=1, source_target_pairs={{0,1},{1,0},{2,3},{3,2},{4,5},{5,4},{6,7},{7,6},{8,9},{9,8},{10,11... | collective-permute-start | bytes 786440 | tf_op jit(solution)/shard_map/ppermute | solution.py:447
  (66 other events, 614.8 us)

commit v7 on v6

--- a/solution.py
+++ b/solution.py
@@ -109,7 +109,7 @@
             ],
             out_specs=[pl.BlockSpec((block, w), lambda i, *_: (i, 0)) for w in widths],
         ),
-        compiler_params=pltpu.CompilerParams(vmem_limit_bytes=20 << 20),
+        compiler_params=pltpu.CompilerParams(vmem_limit_bytes=12 << 20),
         cost_estimate=light,
     )(source, tokens, gain.reshape(1, width))
 
@@ -201,7 +201,7 @@
             pltpu.VMEM((depth, width), jnp.bfloat16),
             pltpu.SemaphoreType.DMA((len(plan),)),
         ],
-        compiler_params=pltpu.CompilerParams(vmem_limit_bytes=24 << 20),
+        compiler_params=pltpu.CompilerParams(vmem_limit_bytes=14 << 20),
         cost_estimate=light,
     )(own, far, *sums, *arrays)
 
@@ -334,7 +334,7 @@
             + [pltpu.VMEM((docs * rank, depth), jnp.bfloat16)] * 2
             + [pltpu.SemaphoreType.DMA((len(arrays),))],
         ),
-        compiler_params=pltpu.CompilerParams(vmem_limit_bytes=20 << 20),
+        compiler_params=pltpu.CompilerParams(vmem_limit_bytes=12 << 20),
         cost_estimate=light,
     )(ends, slots, own, far, *arrays)
 
@@ -407,14 +407,14 @@
             num_scalar_prefetch=3,
             grid=(rows // tile,),
             in_specs=[tiled(a, tile) for a in (*sums, *mids, *tokens)]
-            + [pl.BlockSpec(memory_space=pltpu.HBM)] * (2 + len(arrays)),
+            + [far_memory()] * (2 + len(arrays)),
             out_specs=pl.BlockSpec((tile, width), lambda i, *_: (i, 0)),
             scratch_shapes=[pltpu.VMEM(a.shape, a.dtype) for a in arrays]
             + [pltpu.VMEM((docs * rank, tokens[0].shape[1]), jnp.bfloat16)] * 2
             + [pltpu.VMEM((width, flat), jnp.bfloat16)]
             + [pltpu.SemaphoreType.DMA((len(arrays) + up_at.size,))],
         ),
-        compiler_params=pltpu.CompilerParams(vmem_limit_bytes=34 << 20),
+        compiler_params=pltpu.CompilerParams(vmem_limit_bytes=20 << 20),
         cost_estimate=light,
     )(slots, ends, up_at, *sums, *mids, *tokens, *ups, *arrays)
 
@@ -589,7 +589,7 @@
         own, own_rest, other, other_rest = norm_in_order(
             tokens, input_norm_gain, source, [span] * 4
         )
-        partner, partner_rest = across(other), across(other_rest)
+        partner = across(other)
         for k in ks:
             v_have[k, 0] = z(v_have[0, 0], k)
         for k in ks:
@@ -599,7 +599,7 @@
         x_values([(0, 1)], slots_there)
         x_down([(0, 1)])
         for i, k in enumerate(early):
-            pins = [partner, partner_rest][: i + 1] + [d_miss[0, 1][0]] * i
+            pins = [partner] + [d_miss[0, 1][0]] * i
             v_have[k, 1] = y(after(v_have[k, 0], *pins))
             x_values([(k, 0)])
         for k in early:
@@ -610,22 +610,24 @@
             d_have[k, 1] = y(d_have[k, 0])
         arrays, plan = values(first)
         sums = value_sums(
-            after(own, v_have[last, 1], *[d_have[k, 0] for k in early], d_have[early[0], 1]), partner, arrays, plan, width
-        )
-        x_values([(last, 1)], sums[0])
+            after(own, v_have[last, 1], d_have[last, 0], d_have[early[0], 1]), partner, arrays, plan, width
+        )
+        x_values([(last, 1)])
         for k in early:
             x_down([(k, 0)])
         for k in early:
             x_down([(k, 1)])
         d_have[last, 1] = y(d_have[last, 0])
-        x_down([(last, 0)])
-
+        x_down([(last, 0)], sums[0])
+
+        partner_rest = across(after(other_rest, v_have[last, 1]))
         arrays, plan = values(second)
-        ready = [d_have[last, 1], d_miss[last, 0][0]]
+        ready = [d_have[last, 1], d_miss[early[-1], 1][0]]
         sum_own, *sum_far = value_sums(
             after(own_rest, *ready), partner_rest, arrays, plan, width, sums, jnp.bfloat16
         )
         sums = (sum_own, *[across(part) for part in sum_far])
+        v_have[0, 0] = after(v_have[0, 0], d_miss[early[-1], 1][0])
         up_lane = ups(names)
         up_both = (up_lane, across(up_lane))
 
@@ -633,7 +635,7 @@
         parts = slabs(place, first, d_have, d_miss)
         mid_own, mid_far = mid_partials(own, partner, arrays, parts, ends_both, slots_both, rank)
         mids = (mid_own, across(mid_far))
-        x_down([(last, 1)], mids[1], up_both[1])
+        x_down([(last, 1)], mids[1])
 
         arrays, place = lay()
         parts = [(0, slabs(place, second, d_have, d_miss))]

time: 264 us -> 268 us (1.015)
  local copies, waits for them, and re-layouts: 42.6 us -> 48.2 us
  starting transfers between devices: 45.3 us -> 41.9 us
    ppermute x8, waiting for transfers between devices: 10.9 us -> 33.3 us  [along_y(): return lax.ppermute(value, 'store', pairs(lambda z, y, c: (z, 1 - y, c)))]
    ppermute x6, waiting for transfers between devices: 68 us -> 52.6 us  [along_z(): lax.ppermute(value, 'store', pairs(lambda z, y, c: ((z + k) % depth, y, c)))]
    unnamed x104 -> x108, local copies, waits for them, and re-layouts: 39.2 us -> 42.7 us
    ppermute x15, waiting for transfers between devices: 30.5 us -> 27 us  [along_x(): return lax.ppermute(value, 'groups', [(g, g ^ 1) for g in range(groups)])]
  transfers between devices with their start and end apart: 46 -> 46, of which waited for: 20 -> 20; matrix products, arithmetic and copies ran while one was open for 1% -> 2% of each run, Pallas kernels for 14% -> 14%
where the time goes in v7:
time: 268 us; the launch traced here: 264 us
  waiting for transfers between devices  115 us (43%)
  Pallas kernels  57.7 us (22%)
  local copies, waits for them, and re-layouts  48.2 us (18%)
  starting transfers between devices  41.9 us (16%)
    ppermute x6, waiting for transfers between devices, along_z(): lax.ppermute(value, 'store', pairs(lambda z, y, c: ((z + k) % depth, y, c)))  52.6 us
    unnamed x108, local copies, waits for them, and re-layouts  42.7 us
    ppermute x8, waiting for transfers between devices, along_y(): return lax.ppermute(value, 'store', pairs(lambda z, y, c: (z, 1 - y, c)))  33.3 us
    ppermute x15, waiting for transfers between devices, along_x(): return lax.ppermute(value, 'groups', [(g, g ^ 1) for g in range(groups)])  27 us
    pallas_call x2, Pallas kernels, value_sums(): pl.pallas_call(functools.partial(value_kernel, plan, columns, len(sums),...  21.1 us
    ppermute x17, starting transfers between devices, across(): return lax.ppermute(value, 'store', pairs(lambda z, y, c: (z, y, 1 - c)))  14.3 us
    pallas_call x1, Pallas kernels, last_values(): pl.pallas_call(functools.partial(last_kernel, rank, parts, len(sums), len...  13.2 us
    ppermute x15, starting transfers between devices, along_x(): return lax.ppermute(value, 'groups', [(g, g ^ 1) for g in range(groups)])  12.9 us
  transfers between devices with their start and end apart: 46, of which 20 were waited for; matrix products, arithmetic and copies ran while one was open for 2% of the time, Pallas kernels for 14%

profile of v7, /device:TPU:9, one launch (start us, length us, event | category | flops | bytes accessed | tf_op | source)
XLA Modules:
  0.0 264.3 jit_solution(5389900751791597293)
XLA Ops:
  0.9 4.6 %copy-done = bf16[768,8192]{1,0:T(8,128)(2,1)S(1)} copy-done((bf16[768,8192]{1,0:T(8,128)(2,1)S(1)}, bf16[768,8192]{1,0:T(8,128)(2,1)}, u32[]{:S(2)}) %copy-start) | copy-done | bytes 12582936
  5.5 8.4 %shard_map.82 = (bf16[768,2048]{1,0:T(8,128)(2,1)S(1)}, bf16[768,2048]{1,0:T(8,128)(2,1)S(1)}, bf16[768,2048]{1,0:T(8,128)(2,1)}, bf16[768,2048]{1,0:T(8,128)(2,1)S(1)}) custom-call(s32[64]{0:T(128)S(1)} %stack.391.source_ref, bf16[768,8192]{1,0:T(8,128)(2,1)S(1)} %copy-done, bf16[1,8192]{1,0:T(2,128)(2,1)S(1)} %reshape.18.gain_ref), custom_call_target="tpu_custom_call" | custom-call | tf_op jit(solution)/shard_map/pallas_call | solution.py:100
  13.8 1.7 copy-done.1
  20.4 1.9 shard_map.83
  25.3 12.3 %collective-permute-done.2.refs_0_.refs_4_ = bf16[1024,256]{1,0:T(8,128)(2,1)S(1)} collective-permute-done((bf16[1024,256]{1,0:T(8,128)(2,1)S(1)}, bf16[1024,256]{1,0:T(8,128)(2,1)S(1)}, u32[]{:S(2)}, u32[]{:S(2)}) %collective-permute-start.2) | collective-permute-done | bytes 524320 | tf_op jit(solution)/shard_map/ppermute | solution.py:444
  38.4 3.6 %collective-permute-done.refs_11_.refs_12_ = bf16[352,1024]{1,0:T(8,128)(2,1)} collective-permute-done((bf16[352,1024]{1,0:T(8,128)(2,1)}, bf16[352,1024]{1,0:T(8,128)(2,1)}, u32[]{:S(2)}, u32[]{:S(2)}) %collective-permute-start) | collective-permute-done | bytes 720928 | tf_op jit(solution)/shard_map/ppermute | solution.py:441
  45.2 1.7 collective-permute-start.5
  47.7 11.5 %collective-permute-done.3.refs_13_.refs_14_ = bf16[352,1024]{1,0:T(8,128)(2,1)} collective-permute-done((bf16[352,1024]{1,0:T(8,128)(2,1)}, bf16[352,1024]{1,0:T(8,128)(2,1)}, u32[]{:S(2)}, u32[]{:S(2)}) %collective-permute-start.3) | collective-permute-done | bytes 720928 | tf_op jit(solution)/shard_map/ppermute | solution.py:444
  59.2 2.9 %collective-permute-start.20 = (bf16[768,2048]{1,0:T(8,128)(2,1)}, bf16[768,2048]{1,0:T(8,128)(2,1)S(1)}, u32[]{:S(2)}, u32[]{:S(2)}) collective-permute-start(bf16[768,2048]{1,0:T(8,128)(2,1)} %copy-done.3), channel_id=1, source_target_pairs={{0,1},{1,0},{2,3},{3,2},{4,5},{5,4},{6,7},{7,6},{8,9},{9,8},{10,11... | collective-permute-start | bytes 9437192 | tf_op jit(solution)/shard_map/ppermute | solution.py:447
  65.0 4.1 %collective-permute-start.7 = (bf16[352,1024]{1,0:T(8,128)(2,1)}, bf16[352,1024]{1,0:T(8,128)(2,1)S(1)}, u32[]{:S(2)}, u32[]{:S(2)}) collective-permute-start(bf16[352,1024]{1,0:T(8,128)(2,1)} %get-tuple-element.103.refs_2_.refs_0_), channel_id=1, source_target_pairs={{0,8},{1,9},{2,10},{3,11},{4,12},{5,13},{6,14},{7,15},{8,0},{9,1},... | collective-permute-start | bytes 2162696 | tf_op jit(solution)/shard_map/ppermute | solution.py:441
  77.0 21.8 %collective-permute-done.7.refs_7_.refs_8_ = bf16[352,1024]{1,0:T(8,128)(2,1)S(1)} collective-permute-done((bf16[352,1024]{1,0:T(8,128)(2,1)}, bf16[352,1024]{1,0:T(8,128)(2,1)S(1)}, u32[]{:S(2)}, u32[]{:S(2)}) %collective-permute-start.7) | collective-permute-done | bytes 720928 | tf_op jit(solution)/shard_map/ppermute | solution.py:441
  101.7 8.7 %collective-permute-done.23.refs_5_.refs_3_ = bf16[224,1024]{1,0:T(8,128)(2,1)S(1)} collective-permute-done((bf16[224,1024]{1,0:T(8,128)(2,1)S(1)}, bf16[224,1024]{1,0:T(8,128)(2,1)S(1)}, u32[]{:S(2)}, u32[]{:S(2)}) %collective-permute-start.23) | collective-permute-done | bytes 458784 | tf_op jit(solution)/shard_map/ppermute | solution.py:450
  110.4 2.2 collective-permute-done.15.refs_0_.refs_6_
  112.8 4.0 %collective-permute-done.21.refs_8_.refs_6_ = bf16[352,1024]{1,0:T(8,128)(2,1)S(1)} collective-permute-done((bf16[352,1024]{1,0:T(8,128)(2,1)}, bf16[352,1024]{1,0:T(8,128)(2,1)S(1)}, u32[]{:S(2)}, u32[]{:S(2)}) %collective-permute-start.21) | collective-permute-done | bytes 720928 | tf_op jit(solution)/shard_map/ppermute | solution.py:444
  116.8 2.1 collective-permute-start.8
  118.9 8.8 %collective-permute-done.1.refs_0_.refs_15_ = bf16[1024,256]{1,0:T(8,128)(2,1)S(1)} collective-permute-done((bf16[1024,256]{1,0:T(8,128)(2,1)}, bf16[1024,256]{1,0:T(8,128)(2,1)S(1)}, u32[]{:S(2)}, u32[]{:S(2)}) %collective-permute-start.1) | collective-permute-done | bytes 524320 | tf_op jit(solution)/shard_map/ppermute | solution.py:441
  130.1 2.1 collective-permute-done.12.refs_9_.refs_10_
  132.4 16.2 %collective-permute-done.8.refs_0_.refs_11_ = bf16[1024,256]{1,0:T(8,128)(2,1)S(1)} collective-permute-done((bf16[1024,256]{1,0:T(8,128)(2,1)S(1)}, bf16[1024,256]{1,0:T(8,128)(2,1)S(1)}, u32[]{:S(2)}, u32[]{:S(2)}) %collective-permute-start.8) | collective-permute-done | bytes 524320 | tf_op jit(solution)/shard_map/ppermute | solution.py:441
  152.7 7.5 %collective-permute-done.17.refs_10_.refs_11_ = bf16[224,1024]{1,0:T(8,128)(2,1)S(1)} collective-permute-done((bf16[224,1024]{1,0:T(8,128)(2,1)S(1)}, bf16[224,1024]{1,0:T(8,128)(2,1)S(1)}, u32[]{:S(2)}, u32[]{:S(2)}) %collective-permute-start.17) | collective-permute-done | bytes 458784 | tf_op jit(solution)/shard_map/ppermute | solution.py:450
  160.2 2.3 collective-permute-start.38
  165.0 5.0 %collective-permute-done.27.refs_14_.refs_15_ = bf16[224,1024]{1,0:T(8,128)(2,1)S(1)} collective-permute-done((bf16[224,1024]{1,0:T(8,128)(2,1)S(1)}, bf16[224,1024]{1,0:T(8,128)(2,1)S(1)}, u32[]{:S(2)}, u32[]{:S(2)}) %collective-permute-start.27) | collective-permute-done | bytes 458784 | tf_op jit(solution)/shard_map/ppermute | solution.py:450
  171.9 1.9 collective-permute-done.13.refs_0_.refs_13_
  177.0 10.2 %shard_map.87 = (f32[768,1024]{1,0:T(8,128)S(1)}, f32[768,256]{1,0:T(8,128)S(1)}, f32[768,256]{1,0:T(8,128)S(1)}, f32[768,256]{1,0:T(8,128)S(1)}, f32[768,256]{1,0:T(8,128)S(1)}) custom-call(bf16[768,2048]{1,0:T(8,128)(2,1)S(1)} %get-tuple-element.82.refs_0_, bf16[768,2048]{1,0:T(8,128)(2,1)} %collective-permute-done.9.refs_1_, ...), custom_call_target="tpu_custom_call" | custom-call | tf_op jit(solution)/shard_map/pallas_call | solution.py:194
  189.4 2.8 %collective-permute-start.42 = (bf16[1024,256]{1,0:T(8,128)(2,1)S(1)}, bf16[1024,256]{1,0:T(8,128)(2,1)S(1)}, u32[]{:S(2)}, u32[]{:S(2)}) collective-permute-start(bf16[1024,256]{1,0:T(8,128)(2,1)S(1)} %collective-permute-done.1.refs_0_.refs_15_), channel_id=1, source_target_pairs={{0,1},{1,0},{2,3},{3,2},{4,5},{5,4},{6,7},{7,6},{8,9},{9,8},{10,11... | collective-permute-start | bytes 1572872 | tf_op jit(solution)/shard_map/ppermute | solution.py:447
  192.8 5.6 %shard_map.91 = (f32[768,64]{1,0:T(8,128)S(1)}, f32[768,64]{1,0:T(8,128)S(1)}) custom-call(s32[2,4]{1,0:T(2,128)S(1)} %pad_add_fusion.ends_ref, s32[2,4]{1,0:T(2,128)S(1)} %pad_add_fusion.2.slots_ref, bf16[768,2048]{1,0:T(8,128)(2,1)S(1)} %get-tuple-element.82.refs_0_, bf16[768,2048]{1,0:T(8,128)(2,1)} %collective-permute-done.9.refs_1_, ...), custom_call_target="tpu_custom_call" | custom-call | tf_op jit(solution)/shard_map/pallas_call | solution.py:325
  198.5 3.1 %shard_map.92.refs_9_ = bf16[512,1024]{1,0:T(8,128)(2,1)} custom-call(bf16[352,1024]{1,0:T(8,128)(2,1)} %get-tuple-element.103.refs_2_.refs_0_, bf16[224,1024]{1,0:T(8,128)(2,1)S(1)} %copy-done.19, bf16[352,1024]{1,0:T(8,128)(2,1)} %collective-permute-done.11.refs_4_.refs_2_, bf16[224,1024]{1,0:T(8,128)(2,1)S(1)} %collective-permute-done.23.refs_5_.refs_3_, ...), custom_call_target="tpu_custom_call" | custom-call | tf_op jit(solution)/shard_map/pallas_call | solution.py:256
  203.0 10.9 %shard_map.88 = (f32[768,1024]{1,0:T(8,128)S(1)}, bf16[768,256]{1,0:T(8,128)(2,1)S(1)}, bf16[768,256]{1,0:T(8,128)(2,1)}, bf16[768,256]{1,0:T(8,128)(2,1)}, bf16[768,256]{1,0:T(8,128)(2,1)}) custom-call(bf16[768,2048]{1,0:T(8,128)(2,1)S(1)} %copy-done.2, bf16[768,2048]{1,0:T(8,128)(2,1)S(1)} %collective-permute-done.20.refs_1_, ...), custom_call_target="tpu_custom_call" | custom-call | tf_op jit(solution)/shard_map/pallas_call | solution.py:194
  213.9 1.6 copy-done.5
  224.3 3.2 %collective-permute-done.37.refs_18_ = bf16[512,256]{1,0:T(8,128)(2,1)} collective-permute-done((bf16[512,256]{1,0:T(8,128)(2,1)S(1)}, bf16[512,256]{1,0:T(8,128)(2,1)}, u32[]{:S(2)}, u32[]{:S(2)}) %collective-permute-start.37) | collective-permute-done | bytes 262176 | tf_op jit(solution)/shard_map/ppermute | solution.py:450
  231.2 1.9 copy-done.4
  233.0 1.9 copy-done.6
  251.0 13.2 %shard_map.96 = bf16[768,1024]{1,0:T(8,128)(2,1)} custom-call(s32[4]{0:T(128)S(1)} %select_reduce_fusion.slots_ref, s32[4]{0:T(128)S(1)} %bitcast.107, s32[2,16]{1,0:T(2,128)S(1)} %reshape.17.at_ref, f32[768,1024]{1,0:T(8,128)S(1)} %copy-done.6, bf16[768,256]{1,0:T(8,128)(2,1)S(1)} %copy-done.37, bf16[768,256]{1,0:T(8,128)(2,1)} %collective-permute-done.29.refs_2_, ...), custom_call_target="tpu_custom_call" | custom-call | tf_op jit(solution)/shard_map/pallas_call | solution.py:403
  (201 shorter events, 74.1 us)
Async XLA Ops:
  17.1 83.0 %collective-permute-start.9 = (bf16[768,2048]{1,0:T(8,128)(2,1)}, bf16[768,2048]{1,0:T(8,128)(2,1)}, u32[]{:S(2)}, u32[]{:S(2)}) collective-permute-start(bf16[768,2048]{1,0:T(8,128)(2,1)} %get-tuple-element.68), channel_id=1, source_target_pairs={{0,1},{1,0},{2,3},{3,2},{4,5},{5,4},{6,7},{7,6},{8,9},{9,8},{10,11... | collective-permute-start | bytes 9437192 | tf_op jit(solution)/shard_map/ppermute | solution.py:447
  23.9 18.1 %collective-permute-start = (bf16[352,1024]{1,0:T(8,128)(2,1)}, bf16[352,1024]{1,0:T(8,128)(2,1)}, u32[]{:S(2)}, u32[]{:S(2)}) collective-permute-start(bf16[352,1024]{1,0:T(8,128)(2,1)} %get-tuple-element.103.refs_2_.refs_0_), channel_id=1, source_target_pairs={{0,12},{1,13},{2,14},{3,15},{4,0},{5,1},{6,2},{7,3},{8,4},{9,5},{1... | collective-permute-start | bytes 2162696 | tf_op jit(solution)/shard_map/ppermute | solution.py:441
  23.9 13.7 %collective-permute-start.2 = (bf16[1024,256]{1,0:T(8,128)(2,1)S(1)}, bf16[1024,256]{1,0:T(8,128)(2,1)S(1)}, u32[]{:S(2)}, u32[]{:S(2)}) collective-permute-start(bf16[1024,256]{1,0:T(8,128)(2,1)S(1)} %get-tuple-element.72.refs_2_), channel_id=1, source_target_pairs={{0,2},{1,3},{2,0},{3,1},{4,6},{5,7},{6,4},{7,5},{8,10},{9,11},{10,... | collective-permute-start | bytes 1572872 | tf_op jit(solution)/shard_map/ppermute | solution.py:444
  42.0 17.2 %collective-permute-start.3 = (bf16[352,1024]{1,0:T(8,128)(2,1)}, bf16[352,1024]{1,0:T(8,128)(2,1)}, u32[]{:S(2)}, u32[]{:S(2)}) collective-permute-start(bf16[352,1024]{1,0:T(8,128)(2,1)} %collective-permute-done.refs_11_.refs_12_), channel_id=1, source_target_pairs={{0,2},{1,3},{2,0},{3,1},{4,6},{5,7},{6,4},{7,5},{8,10},{9,11},{10,... | collective-permute-start | bytes 2162696 | tf_op jit(solution)/shard_map/ppermute | solution.py:444
  43.3 27.5 %collective-permute-start.14 = (bf16[352,1024]{1,0:T(8,128)(2,1)}, bf16[352,1024]{1,0:T(8,128)(2,1)}, u32[]{:S(2)}, u32[]{:S(2)}) collective-permute-start(bf16[352,1024]{1,0:T(8,128)(2,1)} %get-tuple-element.103.refs_2_.refs_0_), channel_id=1, source_target_pairs={{0,4},{1,5},{2,6},{3,7},{4,8},{5,9},{6,10},{7,11},{8,12},{9,13},{1... | collective-permute-start | bytes 2162696 | tf_op jit(solution)/shard_map/ppermute | solution.py:441
  44.6 30.1 %collective-permute-start.11 = (bf16[352,1024]{1,0:T(8,128)(2,1)}, bf16[352,1024]{1,0:T(8,128)(2,1)}, u32[]{:S(2)}, u32[]{:S(2)}) collective-permute-start(bf16[352,1024]{1,0:T(8,128)(2,1)} %get-tuple-element.103.refs_2_.refs_0_), channel_id=1, source_target_pairs={{0,2},{1,3},{2,0},{3,1},{4,6},{5,7},{6,4},{7,5},{8,10},{9,11},{10,... | collective-permute-start | bytes 2162696 | tf_op jit(solution)/shard_map/ppermute | solution.py:444
  59.2 133.0 %collective-permute-start.20 = (bf16[768,2048]{1,0:T(8,128)(2,1)}, bf16[768,2048]{1,0:T(8,128)(2,1)S(1)}, u32[]{:S(2)}, u32[]{:S(2)}) collective-permute-start(bf16[768,2048]{1,0:T(8,128)(2,1)} %copy-done.3), channel_id=1, source_target_pairs={{0,1},{1,0},{2,3},{3,2},{4,5},{5,4},{6,7},{7,6},{8,9},{9,8},{10,11... | collective-permute-start | bytes 9437192 | tf_op jit(solution)/shard_map/ppermute | solution.py:447
  65.0 33.8 %collective-permute-start.7 = (bf16[352,1024]{1,0:T(8,128)(2,1)}, bf16[352,1024]{1,0:T(8,128)(2,1)S(1)}, u32[]{:S(2)}, u32[]{:S(2)}) collective-permute-start(bf16[352,1024]{1,0:T(8,128)(2,1)} %get-tuple-element.103.refs_2_.refs_0_), channel_id=1, source_target_pairs={{0,8},{1,9},{2,10},{3,11},{4,12},{5,13},{6,14},{7,15},{8,0},{9,1},... | collective-permute-start | bytes 2162696 | tf_op jit(solution)/shard_map/ppermute | solution.py:441
  70.7 29.4 %collective-permute-start.10 = (bf16[512,256]{1,0:T(8,128)(2,1)S(1)}, bf16[512,256]{1,0:T(8,128)(2,1)S(1)}, u32[]{:S(2)}, u32[]{:S(2)}) collective-permute-start(bf16[512,256]{1,0:T(8,128)(2,1)S(1)} %shard_map.84), channel_id=1, source_target_pairs={{0,16},{16,0},{1,17},{17,1},{2,18},{18,2},{3,19},{19,3},{4,20},{20... | collective-permute-start | bytes 786440 | tf_op jit(solution)/shard_map/ppermute | solution.py:450
  74.7 26.8 %collective-permute-start.16 = (bf16[224,1024]{1,0:T(8,128)(2,1)S(1)}, bf16[224,1024]{1,0:T(8,128)(2,1)S(1)}, u32[]{:S(2)}, u32[]{:S(2)}) collective-permute-start(bf16[224,1024]{1,0:T(8,128)(2,1)S(1)} %slice.37), channel_id=1, source_target_pairs={{0,16},{16,0},{1,17},{17,1},{2,18},{18,2},{3,19},{19,3},{4,20},{20... | collective-permute-start | bytes 1376264 | tf_op jit(solution)/shard_map/ppermute | solution.py:450
  100.1 16.6 %collective-permute-start.21 = (bf16[352,1024]{1,0:T(8,128)(2,1)}, bf16[352,1024]{1,0:T(8,128)(2,1)S(1)}, u32[]{:S(2)}, u32[]{:S(2)}) collective-permute-start(bf16[352,1024]{1,0:T(8,128)(2,1)} %collective-permute-done.14.refs_6_.refs_4_), channel_id=1, source_target_pairs={{0,2},{1,3},{2,0},{3,1},{4,6},{5,7},{6,4},{7,5},{8,10},{9,11},{10,... | collective-permute-start | bytes 2162696 | tf_op jit(solution)/shard_map/ppermute | solution.py:444
  101.5 30.8 %collective-permute-start.12 = (bf16[352,1024]{1,0:T(8,128)(2,1)S(1)}, bf16[352,1024]{1,0:T(8,128)(2,1)S(1)}, u32[]{:S(2)}, u32[]{:S(2)}) collective-permute-start(bf16[352,1024]{1,0:T(8,128)(2,1)S(1)} %collective-permute-done.7.refs_7_.refs_8_), channel_id=1, source_target_pairs={{0,2},{1,3},{2,0},{3,1},{4,6},{5,7},{6,4},{7,5},{8,10},{9,11},{10,... | collective-permute-start | bytes 2162696 | tf_op jit(solution)/shard_map/ppermute | solution.py:444
  110.4 17.3 %collective-permute-start.1 = (bf16[1024,256]{1,0:T(8,128)(2,1)}, bf16[1024,256]{1,0:T(8,128)(2,1)S(1)}, u32[]{:S(2)}, u32[]{:S(2)}) collective-permute-start(bf16[1024,256]{1,0:T(8,128)(2,1)} %copy-done.30), channel_id=1, source_target_pairs={{0,12},{1,13},{2,14},{3,15},{4,0},{5,1},{6,2},{7,3},{8,4},{9,5},{1... | collective-permute-start | bytes 1572872 | tf_op jit(solution)/shard_map/ppermute | solution.py:441
  112.6 15.1 %collective-permute-start.25 = (bf16[224,1024]{1,0:T(8,128)(2,1)S(1)}, bf16[224,1024]{1,0:T(8,128)(2,1)S(1)}, u32[]{:S(2)}, u32[]{:S(2)}) collective-permute-start(bf16[224,1024]{1,0:T(8,128)(2,1)S(1)} %slice.40), channel_id=1, source_target_pairs={{0,16},{16,0},{1,17},{17,1},{2,18},{18,2},{3,19},{19,3},{4,20},{20... | collective-permute-start | bytes 1376264 | tf_op jit(solution)/shard_map/ppermute | solution.py:450
  116.8 31.8 %collective-permute-start.8 = (bf16[1024,256]{1,0:T(8,128)(2,1)S(1)}, bf16[1024,256]{1,0:T(8,128)(2,1)S(1)}, u32[]{:S(2)}, u32[]{:S(2)}) collective-permute-start(bf16[1024,256]{1,0:T(8,128)(2,1)S(1)} %copy-done.31), channel_id=1, source_target_pairs={{0,8},{1,9},{2,10},{3,11},{4,12},{5,13},{6,14},{7,15},{8,0},{9,1},... | collective-permute-start | bytes 1572872 | tf_op jit(solution)/shard_map/ppermute | solution.py:441
  127.7 22.2 %collective-permute-start.24 = (bf16[224,1024]{1,0:T(8,128)(2,1)S(1)}, bf16[224,1024]{1,0:T(8,128)(2,1)S(1)}, u32[]{:S(2)}, u32[]{:S(2)}) collective-permute-start(bf16[224,1024]{1,0:T(8,128)(2,1)S(1)} %slice.39), channel_id=1, source_target_pairs={{0,16},{16,0},{1,17},{17,1},{2,18},{18,2},{3,19},{19,3},{4,20},{20... | collective-permute-start | bytes 1376264 | tf_op jit(solution)/shard_map/ppermute | solution.py:450
  127.7 24.5 %collective-permute-start.4 = (bf16[1024,256]{1,0:T(8,128)(2,1)S(1)}, bf16[1024,256]{1,0:T(8,128)(2,1)S(1)}, u32[]{:S(2)}, u32[]{:S(2)}) collective-permute-start(bf16[1024,256]{1,0:T(8,128)(2,1)S(1)} %collective-permute-done.1.refs_0_.refs_15_), channel_id=1, source_target_pairs={{0,2},{1,3},{2,0},{3,1},{4,6},{5,7},{6,4},{7,5},{8,10},{9,11},{10,... | collective-permute-start | bytes 1572872 | tf_op jit(solution)/shard_map/ppermute | solution.py:444
  132.2 20.3 %collective-permute-start.26 = (bf16[224,1024]{1,0:T(8,128)(2,1)S(1)}, bf16[224,1024]{1,0:T(8,128)(2,1)S(1)}, u32[]{:S(2)}, u32[]{:S(2)}) collective-permute-start(bf16[224,1024]{1,0:T(8,128)(2,1)S(1)} %slice.41), channel_id=1, source_target_pairs={{0,16},{16,0},{1,17},{17,1},{2,18},{18,2},{3,19},{19,3},{4,20},{20... | collective-permute-start | bytes 1376264 | tf_op jit(solution)/shard_map/ppermute | solution.py:450
  149.9 13.1 %collective-permute-start.22 = (bf16[1024,256]{1,0:T(8,128)(2,1)S(1)}, bf16[1024,256]{1,0:T(8,128)(2,1)S(1)}, u32[]{:S(2)}, u32[]{:S(2)}) collective-permute-start(bf16[1024,256]{1,0:T(8,128)(2,1)S(1)} %collective-permute-done.15.refs_0_.refs_6_), channel_id=1, source_target_pairs={{0,2},{1,3},{2,0},{3,1},{4,6},{5,7},{6,4},{7,5},{8,10},{9,11},{10,... | collective-permute-start | bytes 1572872 | tf_op jit(solution)/shard_map/ppermute | solution.py:444
  152.3 17.8 %collective-permute-start.27 = (bf16[224,1024]{1,0:T(8,128)(2,1)S(1)}, bf16[224,1024]{1,0:T(8,128)(2,1)S(1)}, u32[]{:S(2)}, u32[]{:S(2)}) collective-permute-start(bf16[224,1024]{1,0:T(8,128)(2,1)S(1)} %slice.42), channel_id=1, source_target_pairs={{0,16},{16,0},{1,17},{17,1},{2,18},{18,2},{3,19},{19,3},{4,20},{20... | collective-permute-start | bytes 1376264 | tf_op jit(solution)/shard_map/ppermute | solution.py:450
  152.5 21.4 %collective-permute-start.13 = (bf16[1024,256]{1,0:T(8,128)(2,1)S(1)}, bf16[1024,256]{1,0:T(8,128)(2,1)S(1)}, u32[]{:S(2)}, u32[]{:S(2)}) collective-permute-start(bf16[1024,256]{1,0:T(8,128)(2,1)S(1)} %collective-permute-done.8.refs_0_.refs_11_), channel_id=1, source_target_pairs={{0,2},{1,3},{2,0},{3,1},{4,6},{5,7},{6,4},{7,5},{8,10},{9,11},{10,... | collective-permute-start | bytes 1572872 | tf_op jit(solution)/shard_map/ppermute | solution.py:444
  160.2 28.4 %collective-permute-start.38 = (bf16[1024,256]{1,0:T(8,128)(2,1)S(1)}, bf16[1024,256]{1,0:T(8,128)(2,1)S(1)}, u32[]{:S(2)}, u32[]{:S(2)}) collective-permute-start(bf16[1024,256]{1,0:T(8,128)(2,1)S(1)} %collective-permute-done.8.refs_0_.refs_11_), channel_id=1, source_target_pairs={{0,1},{1,0},{2,3},{3,2},{4,5},{5,4},{6,7},{7,6},{8,9},{9,8},{10,11... | collective-permute-start | bytes 1572872 | tf_op jit(solution)/shard_map/ppermute | solution.py:447
  163.1 12.6 %collective-permute-start.18 = (bf16[512,256]{1,0:T(8,128)(2,1)S(1)}, bf16[512,256]{1,0:T(8,128)(2,1)S(1)}, u32[]{:S(2)}, u32[]{:S(2)}) collective-permute-start(bf16[512,256]{1,0:T(8,128)(2,1)S(1)} %shard_map.86), channel_id=1, source_target_pairs={{0,16},{16,0},{1,17},{17,1},{2,18},{18,2},{3,19},{19,3},{4,20},{20... | collective-permute-start | bytes 786440 | tf_op jit(solution)/shard_map/ppermute | solution.py:450
  170.0 17.7 %collective-permute-start.35 = (bf16[512,256]{1,0:T(8,128)(2,1)S(1)}, bf16[512,256]{1,0:T(8,128)(2,1)S(1)}, u32[]{:S(2)}, u32[]{:S(2)}) collective-permute-start(bf16[512,256]{1,0:T(8,128)(2,1)S(1)} %shard_map.93), channel_id=1, source_target_pairs={{0,16},{16,0},{1,17},{17,1},{2,18},{18,2},{3,19},{19,3},{4,20},{20... | collective-permute-start | bytes 786440 | tf_op jit(solution)/shard_map/ppermute | solution.py:450
  173.9 18.4 %collective-permute-start.32 = (bf16[512,256]{1,0:T(8,128)(2,1)S(1)}, bf16[512,256]{1,0:T(8,128)(2,1)S(1)}, u32[]{:S(2)}, u32[]{:S(2)}) collective-permute-start(bf16[512,256]{1,0:T(8,128)(2,1)S(1)} %shard_map.90), channel_id=1, source_target_pairs={{0,16},{16,0},{1,17},{17,1},{2,18},{18,2},{3,19},{19,3},{4,20},{20... | collective-permute-start | bytes 786440 | tf_op jit(solution)/shard_map/ppermute | solution.py:450
  175.7 22.7 %collective-permute-start.19 = (bf16[512,256]{1,0:T(8,128)(2,1)S(1)}, bf16[512,256]{1,0:T(8,128)(2,1)S(1)}, u32[]{:S(2)}, u32[]{:S(2)}) collective-permute-start(bf16[512,256]{1,0:T(8,128)(2,1)S(1)} %shard_map.85), channel_id=1, source_target_pairs={{0,16},{16,0},{1,17},{17,1},{2,18},{18,2},{3,19},{19,3},{4,20},{20... | collective-permute-start | bytes 786440 | tf_op jit(solution)/shard_map/ppermute | solution.py:450
  187.8 13.9 %collective-permute-start.36 = (bf16[512,256]{1,0:T(8,128)(2,1)S(1)}, bf16[512,256]{1,0:T(8,128)(2,1)S(1)}, u32[]{:S(2)}, u32[]{:S(2)}) collective-permute-start(bf16[512,256]{1,0:T(8,128)(2,1)S(1)} %shard_map.94), channel_id=1, source_target_pairs={{0,16},{16,0},{1,17},{17,1},{2,18},{18,2},{3,19},{19,3},{4,20},{20... | collective-permute-start | bytes 786440 | tf_op jit(solution)/shard_map/ppermute | solution.py:450
  189.4 26.7 %collective-permute-start.42 = (bf16[1024,256]{1,0:T(8,128)(2,1)S(1)}, bf16[1024,256]{1,0:T(8,128)(2,1)S(1)}, u32[]{:S(2)}, u32[]{:S(2)}) collective-permute-start(bf16[1024,256]{1,0:T(8,128)(2,1)S(1)} %collective-permute-done.1.refs_0_.refs_15_), channel_id=1, source_target_pairs={{0,1},{1,0},{2,3},{3,2},{4,5},{5,4},{6,7},{7,6},{8,9},{9,8},{10,11... | collective-permute-start | bytes 1572872 | tf_op jit(solution)/shard_map/ppermute | solution.py:447
  192.3 25.7 %collective-permute-start.44 = (bf16[1024,256]{1,0:T(8,128)(2,1)S(1)}, bf16[1024,256]{1,0:T(8,128)(2,1)S(1)}, u32[]{:S(2)}, u32[]{:S(2)}) collective-permute-start(bf16[1024,256]{1,0:T(8,128)(2,1)S(1)} %collective-permute-done.4.refs_0_.refs_17_), channel_id=1, source_target_pairs={{0,1},{1,0},{2,3},{3,2},{4,5},{5,4},{6,7},{7,6},{8,9},{9,8},{10,11... | collective-permute-start | bytes 1572872 | tf_op jit(solution)/shard_map/ppermute | solution.py:447
  192.3 28.7 %collective-permute-start.40 = (bf16[1024,256]{1,0:T(8,128)(2,1)S(1)}, bf16[1024,256]{1,0:T(8,128)(2,1)S(1)}, u32[]{:S(2)}, u32[]{:S(2)}) collective-permute-start(bf16[1024,256]{1,0:T(8,128)(2,1)S(1)} %collective-permute-done.13.refs_0_.refs_13_), channel_id=1, source_target_pairs={{0,1},{1,0},{2,3},{3,2},{4,5},{5,4},{6,7},{7,6},{8,9},{9,8},{10,11... | collective-permute-start | bytes 1572872 | tf_op jit(solution)/shard_map/ppermute | solution.py:447
  201.7 29.5 %collective-permute-start.34 = (bf16[512,1024]{1,0:T(8,128)(2,1)}, bf16[512,1024]{1,0:T(8,128)(2,1)}, u32[]{:S(2)}, u32[]{:S(2)}) collective-permute-start(bf16[512,1024]{1,0:T(8,128)(2,1)} %shard_map.92.refs_9_), channel_id=1, source_target_pairs={{0,1},{1,0},{2,3},{3,2},{4,5},{5,4},{6,7},{7,6},{8,9},{9,8},{10,11... | collective-permute-start | bytes 3145736 | tf_op jit(solution)/shard_map/ppermute | solution.py:447
  202.7 16.2 %collective-permute-start.39 = (bf16[512,256]{1,0:T(8,128)(2,1)S(1)}, bf16[512,256]{1,0:T(8,128)(2,1)S(1)}, u32[]{:S(2)}, u32[]{:S(2)}) collective-permute-start(bf16[512,256]{1,0:T(8,128)(2,1)S(1)} %collective-permute-done.35.refs_12_), channel_id=1, source_target_pairs={{0,1},{1,0},{2,3},{3,2},{4,5},{5,4},{6,7},{7,6},{8,9},{9,8},{10,11... | collective-permute-start | bytes 786440 | tf_op jit(solution)/shard_map/ppermute | solution.py:447
  (68 other events, 622.0 us)

commit v8 on v7

--- a/solution.py
+++ b/solution.py
@@ -109,7 +109,7 @@
             ],
             out_specs=[pl.BlockSpec((block, w), lambda i, *_: (i, 0)) for w in widths],
         ),
-        compiler_params=pltpu.CompilerParams(vmem_limit_bytes=12 << 20),
+        compiler_params=pltpu.CompilerParams(vmem_limit_bytes=58 << 20),
         cost_estimate=light,
     )(source, tokens, gain.reshape(1, width))
 
@@ -234,7 +234,7 @@
             out_specs=[pl.BlockSpec(memory_space=pltpu.VMEM)] * len(shapes),
             scratch_shapes=[pltpu.SemaphoreType.DMA((len(plan),))],
         ),
-        compiler_params=pltpu.CompilerParams(vmem_limit_bytes=12 << 20),
+        compiler_params=pltpu.CompilerParams(vmem_limit_bytes=58 << 20),
         cost_estimate=light,
     )(side.reshape(1).astype(jnp.int32), *arrays)
 
@@ -414,7 +414,7 @@
             + [pltpu.VMEM((width, flat), jnp.bfloat16)]
             + [pltpu.SemaphoreType.DMA((len(arrays) + up_at.size,))],
         ),
-        compiler_params=pltpu.CompilerParams(vmem_limit_bytes=20 << 20),
+        compiler_params=pltpu.CompilerParams(vmem_limit_bytes=58 << 20),
         cost_estimate=light,
     )(slots, ends, up_at, *sums, *mids, *tokens, *ups, *arrays)
 
@@ -515,7 +515,7 @@
 
         order = list(range(depth))
         names = [(k, dy) for k in order for dy in range(rows_y)]
-        z, y, x = Line(along_z, 3), Line(along_y, 3), Line(along_x, 3)
+        z, y, x = Line(along_z), Line(along_y, 3), Line(along_x, 3)
 
         def x_values(names, *earlier):
             got = x(after(jnp.concatenate([v_have[name][:cut] for name in names], 0), *earlier))
@@ -595,7 +595,7 @@
         for k in ks:
             d_have[k, 0] = z(d_have[0, 0], k)
         v_have[0, 1] = y(v_have[0, 0])
-        d_have[0, 1] = y(d_have[0, 0])
+        d_have[0, 1] = y(after(d_have[0, 0], v_have[0, 1]))
         x_values([(0, 1)], slots_there)
         x_down([(0, 1)])
         for i, k in enumerate(early):
@@ -610,19 +610,19 @@
             d_have[k, 1] = y(d_have[k, 0])
         arrays, plan = values(first)
         sums = value_sums(
-            after(own, v_have[last, 1], d_have[last, 0], d_have[early[0], 1]), partner, arrays, plan, width
-        )
-        x_values([(last, 1)])
+            after(own, v_have[last, 1], *[d_have[k, 0] for k in early], d_have[early[0], 1]), partner, arrays, plan, width
+        )
+        x_values([(last, 1)], sums[0])
         for k in early:
             x_down([(k, 0)])
         for k in early:
             x_down([(k, 1)])
         d_have[last, 1] = y(d_have[last, 0])
-        x_down([(last, 0)], sums[0])
+        x_down([(last, 0)])
 
         partner_rest = across(after(other_rest, v_have[last, 1]))
         arrays, plan = values(second)
-        ready = [d_have[last, 1], d_miss[early[-1], 1][0]]
+        ready = [d_have[last, 1], d_miss[last, 0][0]]
         sum_own, *sum_far = value_sums(
             after(own_rest, *ready), partner_rest, arrays, plan, width, sums, jnp.bfloat16
         )
@@ -635,7 +635,7 @@
         parts = slabs(place, first, d_have, d_miss)
         mid_own, mid_far = mid_partials(own, partner, arrays, parts, ends_both, slots_both, rank)
         mids = (mid_own, across(mid_far))
-        x_down([(last, 1)], mids[1])
+        x_down([(last, 1)])
 
         arrays, place = lay()
         parts = [(0, slabs(place, second, d_have, d_miss))]

time: 268 us -> 250 us (0.933)
  local copies, waits for them, and re-layouts: 48.2 us -> 11.1 us
  starting transfers between devices: 41.9 us -> 67.2 us
  waiting for transfers between devices: 115 us -> 104 us
  Pallas kernels: 57.7 us -> 65.5 us
    unnamed x108 -> x70, local copies, waits for them, and re-layouts: 42.7 us -> 3.23 us
    ppermute x17, starting transfers between devices: 14.3 us -> 39.2 us  [across(): return lax.ppermute(value, 'store', pairs(lambda z, y, c: (z, y, 1 - c)))]
    ppermute x8, waiting for transfers between devices: 33.3 us -> 21.9 us  [along_y(): return lax.ppermute(value, 'store', pairs(lambda z, y, c: (z, 1 - y, c)))]
    ppermute x15, waiting for transfers between devices: 27 us -> 32.4 us  [along_x(): return lax.ppermute(value, 'groups', [(g, g ^ 1) for g in range(groups)])]
    pallas_call x1, Pallas kernels: 8.35 us -> 13.7 us  [norm_in_order(): pl.pallas_call(norm_kernel, out_shape=[jax.ShapeDtypeStruct((rows, w), jn...]
    ppermute x6, waiting for transfers between devices: 52.6 us -> 48.8 us  [along_z(): lax.ppermute(value, 'store', pairs(lambda z, y, c: ((z + k) % depth, y, c)))]
    pallas_call x1, Pallas kernels: 13.2 us -> 16.2 us  [last_values(): pl.pallas_call(functools.partial(last_kernel, rank, parts, len(sums), len...]
  transfers between devices with their start and end apart: 46 -> 46, of which waited for: 20 -> 14; matrix products, arithmetic and copies ran while one was open for 2% -> 3% of each run, Pallas kernels for 14% -> 14%
where the time goes in v8:
time: 250 us; the launch traced here: 249 us
  waiting for transfers between devices  104 us (42%)
  starting transfers between devices  67.2 us (27%)
  Pallas kernels  65.5 us (26%)
  local copies, waits for them, and re-layouts  11.1 us (4%)
    ppermute x6, waiting for transfers between devices, along_z(): lax.ppermute(value, 'store', pairs(lambda z, y, c: ((z + k) % depth, y, c)))  48.8 us
    ppermute x17, starting transfers between devices, across(): return lax.ppermute(value, 'store', pairs(lambda z, y, c: (z, y, 1 - c)))  39.2 us
    ppermute x15, waiting for transfers between devices, along_x(): return lax.ppermute(value, 'groups', [(g, g ^ 1) for g in range(groups)])  32.4 us
    ppermute x8, waiting for transfers between devices, along_y(): return lax.ppermute(value, 'store', pairs(lambda z, y, c: (z, 1 - y, c)))  21.9 us
    pallas_call x2, Pallas kernels, value_sums(): pl.pallas_call(functools.partial(value_kernel, plan, columns, len(sums),...  18.9 us
    pallas_call x1, Pallas kernels, last_values(): pl.pallas_call(functools.partial(last_kernel, rank, parts, len(sums), len...  16.2 us
    ppermute x15, starting transfers between devices, along_x(): return lax.ppermute(value, 'groups', [(g, g ^ 1) for g in range(groups)])  14.7 us
    pallas_call x1, Pallas kernels, norm_in_order(): pl.pallas_call(norm_kernel, out_shape=[jax.ShapeDtypeStruct((rows, w), jn...  13.7 us
  transfers between devices with their start and end apart: 46, of which 14 were waited for; matrix products, arithmetic and copies ran while one was open for 3% of the time, Pallas kernels for 14%

profile of v8, /device:TPU:9, one launch (start us, length us, event | category | flops | bytes accessed | tf_op | source)
XLA Modules:
  0.0 248.8 jit_solution(17241305597755717630)
XLA Ops:
  0.0 1.3 reshape.18.gain_ref
  2.0 13.7 %shard_map.82 = (bf16[768,2048]{1,0:T(8,128)(2,1)}, bf16[768,2048]{1,0:T(8,128)(2,1)}, bf16[768,2048]{1,0:T(8,128)(2,1)}, bf16[768,2048]{1,0:T(8,128)(2,1)}) custom-call(s32[64]{0:T(128)} %stack.391.source_ref, bf16[768,8192]{1,0:T(8,128)(2,1)} %tokens_ref.1, bf16[1,8192]{1,0:T(2,128)(2,1)} %reshape.18.gain_ref), custom_call_target="tpu_custom_call" | custom-call | tf_op jit(solution)/shard_map/pallas_call | solution.py:100
  17.2 3.0 %shard_map.83 = (bf16[352,1024]{1,0:T(8,128)(2,1)}, bf16[224,1024]{1,0:T(8,128)(2,1)}, bf16[1024,256]{1,0:T(8,128)(2,1)}, bf16[1024,256]{1,0:T(8,128)(2,1)}) custom-call(s32[1]{0:T(128)} %bitcast.98.side_ref, bf16[512,1024]{1,0:T(8,128)(2,1)} %refs_0_.1, bf16[64,1024]{1,0:T(8,128)(2,1)} %bitcast.106, bf16[1024,512]{1,0:T(8,128)(2,1)} %bitcast.105), custom_call_target="tpu_custom_call" | custom-call | tf_op jit(solution)/shard_map/pallas_call | solution.py:228
  20.2 1.3 collective-permute-start.3
  22.8 15.5 %collective-permute-done.3.refs_6_.refs_4_ = bf16[352,1024]{1,0:T(8,128)(2,1)} collective-permute-done((bf16[352,1024]{1,0:T(8,128)(2,1)}, bf16[352,1024]{1,0:T(8,128)(2,1)}, u32[]{:S(2)}, u32[]{:S(2)}) %collective-permute-start.3) | collective-permute-done | bytes 720928 | tf_op jit(solution)/shard_map/ppermute | solution.py:441
  38.3 2.2 collective-permute-start.4
  42.5 1.7 collective-permute-start.9
  44.1 9.3 %collective-permute-done.6.refs_0_.refs_4_ = bf16[1024,256]{1,0:T(8,128)(2,1)} collective-permute-done((bf16[1024,256]{1,0:T(8,128)(2,1)}, bf16[1024,256]{1,0:T(8,128)(2,1)}, u32[]{:S(2)}, u32[]{:S(2)}) %collective-permute-start.6) | collective-permute-done | bytes 524320 | tf_op jit(solution)/shard_map/ppermute | solution.py:444
  53.5 2.8 %collective-permute-done.4.refs_11_.refs_12_ = bf16[352,1024]{1,0:T(8,128)(2,1)} collective-permute-done((bf16[352,1024]{1,0:T(8,128)(2,1)}, bf16[352,1024]{1,0:T(8,128)(2,1)}, u32[]{:S(2)}, u32[]{:S(2)}) %collective-permute-start.4) | collective-permute-done | bytes 720928 | tf_op jit(solution)/shard_map/ppermute | solution.py:441
  62.7 4.4 %collective-permute-done.7.refs_13_.refs_14_ = bf16[352,1024]{1,0:T(8,128)(2,1)S(1)} collective-permute-done((bf16[352,1024]{1,0:T(8,128)(2,1)}, bf16[352,1024]{1,0:T(8,128)(2,1)S(1)}, u32[]{:S(2)}, u32[]{:S(2)}) %collective-permute-start.7) | collective-permute-done | bytes 720928 | tf_op jit(solution)/shard_map/ppermute | solution.py:444
  67.1 18.4 %collective-permute-start.17 = (bf16[768,2048]{1,0:T(8,128)(2,1)}, bf16[768,2048]{1,0:T(8,128)(2,1)S(1)}, u32[]{:S(2)}, u32[]{:S(2)}) collective-permute-start(bf16[768,2048]{1,0:T(8,128)(2,1)} %get-tuple-element.79.refs_8_), channel_id=1, source_target_pairs={{0,1},{1,0},{2,3},{3,2},{4,5},{5,4},{6,7},{7,6},{8,9},{9,8},{10,11... | collective-permute-start | bytes 9437192 | tf_op jit(solution)/shard_map/ppermute | solution.py:447
  85.4 3.2 %collective-permute-done.refs_7_.refs_8_ = bf16[352,1024]{1,0:T(8,128)(2,1)} collective-permute-done((bf16[352,1024]{1,0:T(8,128)(2,1)}, bf16[352,1024]{1,0:T(8,128)(2,1)}, u32[]{:S(2)}, u32[]{:S(2)}) %collective-permute-start) | collective-permute-done | bytes 720928 | tf_op jit(solution)/shard_map/ppermute | solution.py:441
  90.9 1.6 shard_map.86
  93.1 13.9 %collective-permute-done.22.refs_5_ = bf16[512,256]{1,0:T(8,128)(2,1)S(1)} collective-permute-done((bf16[512,256]{1,0:T(8,128)(2,1)S(1)}, bf16[512,256]{1,0:T(8,128)(2,1)S(1)}, u32[]{:S(2)}, u32[]{:S(2)}) %collective-permute-start.22) | collective-permute-done | bytes 262176 | tf_op jit(solution)/shard_map/ppermute | solution.py:450
  107.0 3.1 %collective-permute-start.11 = (bf16[1024,256]{1,0:T(8,128)(2,1)S(1)}, bf16[1024,256]{1,0:T(8,128)(2,1)S(1)}, u32[]{:S(2)}, u32[]{:S(2)}) collective-permute-start(bf16[1024,256]{1,0:T(8,128)(2,1)S(1)} %copy-done.9), channel_id=1, source_target_pairs={{0,8},{1,9},{2,10},{3,11},{4,12},{5,13},{6,14},{7,15},{8,0},{9,1},... | collective-permute-start | bytes 1572872 | tf_op jit(solution)/shard_map/ppermute | solution.py:441
  112.4 27.2 %collective-permute-done.11.refs_0_.refs_11_ = bf16[1024,256]{1,0:T(8,128)(2,1)S(1)} collective-permute-done((bf16[1024,256]{1,0:T(8,128)(2,1)S(1)}, bf16[1024,256]{1,0:T(8,128)(2,1)S(1)}, u32[]{:S(2)}, u32[]{:S(2)}) %collective-permute-start.11) | collective-permute-done | bytes 524320 | tf_op jit(solution)/shard_map/ppermute | solution.py:441
  139.6 1.3 collective-permute-start.20
  144.4 8.2 %collective-permute-done.20.refs_0_.refs_8_ = bf16[1024,256]{1,0:T(8,128)(2,1)S(1)} collective-permute-done((bf16[1024,256]{1,0:T(8,128)(2,1)S(1)}, bf16[1024,256]{1,0:T(8,128)(2,1)S(1)}, u32[]{:S(2)}, u32[]{:S(2)}) %collective-permute-start.20) | collective-permute-done | bytes 524320 | tf_op jit(solution)/shard_map/ppermute | solution.py:444
  154.0 9.4 %shard_map.87 = (f32[768,1024]{1,0:T(8,128)S(1)}, f32[768,256]{1,0:T(8,128)S(1)}, f32[768,256]{1,0:T(8,128)S(1)}, f32[768,256]{1,0:T(8,128)S(1)}, f32[768,256]{1,0:T(8,128)S(1)}) custom-call(bf16[768,2048]{1,0:T(8,128)(2,1)S(1)} %copy-done, bf16[768,2048]{1,0:T(8,128)(2,1)S(1)} %collective-permute-done.18.refs_1_, bf16[352,1024]{1,0:T(8,128)(2,1)S(1)} %copy-done.3, ...), custom_call_target="tpu_custom_call" | custom-call | tf_op jit(solution)/shard_map/pallas_call | solution.py:194
  165.2 2.5 %collective-permute-done.15.refs_12_ = bf16[512,256]{1,0:T(8,128)(2,1)S(1)} collective-permute-done((bf16[512,256]{1,0:T(8,128)(2,1)S(1)}, bf16[512,256]{1,0:T(8,128)(2,1)S(1)}, u32[]{:S(2)}, u32[]{:S(2)}) %collective-permute-start.15) | collective-permute-done | bytes 262176 | tf_op jit(solution)/shard_map/ppermute | solution.py:450
  169.6 13.5 %collective-permute-done.16.refs_16_ = bf16[512,256]{1,0:T(8,128)(2,1)S(1)} collective-permute-done((bf16[512,256]{1,0:T(8,128)(2,1)S(1)}, bf16[512,256]{1,0:T(8,128)(2,1)S(1)}, u32[]{:S(2)}, u32[]{:S(2)}) %collective-permute-start.16) | collective-permute-done | bytes 262176 | tf_op jit(solution)/shard_map/ppermute | solution.py:450
  184.3 1.9 collective-permute-start.43
  187.5 1.8 collective-permute-done.31.refs_7_
  191.5 3.2 %collective-permute-start.42 = (bf16[1024,256]{1,0:T(8,128)(2,1)S(1)}, bf16[1024,256]{1,0:T(8,128)(2,1)S(1)}, u32[]{:S(2)}, u32[]{:S(2)}) collective-permute-start(bf16[1024,256]{1,0:T(8,128)(2,1)S(1)} %collective-permute-done.2.refs_0_.refs_15_), channel_id=1, source_target_pairs={{0,1},{1,0},{2,3},{3,2},{4,5},{5,4},{6,7},{7,6},{8,9},{9,8},{10,11... | collective-permute-start | bytes 1572872 | tf_op jit(solution)/shard_map/ppermute | solution.py:447
  194.7 6.2 %collective-permute-start.44 = (bf16[1024,256]{1,0:T(8,128)(2,1)S(1)}, bf16[1024,256]{1,0:T(8,128)(2,1)S(1)}, u32[]{:S(2)}, u32[]{:S(2)}) collective-permute-start(bf16[1024,256]{1,0:T(8,128)(2,1)S(1)} %collective-permute-done.8.refs_0_.refs_17_), channel_id=1, source_target_pairs={{0,1},{1,0},{2,3},{3,2},{4,5},{5,4},{6,7},{7,6},{8,9},{9,8},{10,11... | collective-permute-start | bytes 1572872 | tf_op jit(solution)/shard_map/ppermute | solution.py:447
  202.7 2.8 %shard_map.94.refs_9_ = bf16[512,1024]{1,0:T(8,128)(2,1)} custom-call(bf16[352,1024]{1,0:T(8,128)(2,1)S(1)} %copy-done.3, bf16[224,1024]{1,0:T(8,128)(2,1)S(1)} %copy-done.8, bf16[352,1024]{1,0:T(8,128)(2,1)} %collective-permute-done.5.refs_4_.refs_2_, bf16[224,1024]{1,0:T(8,128)(2,1)S(1)} %collective-permute-done.12.refs_5_.refs_3_, ...), custom_call_target="tpu_custom_call" | custom-call | tf_op jit(solution)/shard_map/pallas_call | solution.py:256
  205.6 2.5 %collective-permute-start.36 = (bf16[512,1024]{1,0:T(8,128)(2,1)}, bf16[512,1024]{1,0:T(8,128)(2,1)}, u32[]{:S(2)}, u32[]{:S(2)}) collective-permute-start(bf16[512,1024]{1,0:T(8,128)(2,1)} %shard_map.94.refs_9_), channel_id=1, source_target_pairs={{0,1},{1,0},{2,3},{3,2},{4,5},{5,4},{6,7},{7,6},{8,9},{9,8},{10,11... | collective-permute-start | bytes 3145736 | tf_op jit(solution)/shard_map/ppermute | solution.py:447
  208.1 2.1 collective-permute-start.40
  211.5 5.3 %shard_map.92 = (f32[768,64]{1,0:T(8,128)S(1)}, f32[768,64]{1,0:T(8,128)S(1)}) custom-call(s32[2,4]{1,0:T(2,128)S(1)} %pad_add_fusion.ends_ref, s32[2,4]{1,0:T(2,128)S(1)} %pad_add_fusion.2.slots_ref, bf16[768,2048]{1,0:T(8,128)(2,1)S(1)} %copy-done, bf16[768,2048]{1,0:T(8,128)(2,1)S(1)} %collective-permute-done.18.refs_1_, bf16[1024,256]{1,0:T(8,128)(2,1)S(1)} %copy-done.9, ...), custom_call_target="tpu_custom_call" | custom-call | tf_op jit(solution)/shard_map/pallas_call | solution.py:325
  217.1 9.5 %shard_map.88 = (f32[768,1024]{1,0:T(8,128)S(1)}, bf16[768,256]{1,0:T(8,128)(2,1)S(1)}, bf16[768,256]{1,0:T(8,128)(2,1)S(1)}, bf16[768,256]{1,0:T(8,128)(2,1)S(1)}, bf16[768,256]{1,0:T(8,128)(2,1)S(1)}) custom-call(bf16[768,2048]{1,0:T(8,128)(2,1)S(1)} %copy-done.1, bf16[768,2048]{1,0:T(8,128)(2,1)S(1)} %collective-permute-done.17.refs_1_, ...), custom_call_target="tpu_custom_call" | custom-call | tf_op jit(solution)/shard_map/pallas_call | solution.py:194
  226.6 1.6 copy-done.2
  232.5 16.2 %shard_map.96 = bf16[768,1024]{1,0:T(8,128)(2,1)} custom-call(s32[4]{0:T(128)} %copy-done.31, s32[4]{0:T(128)} %bitcast.108, s32[2,16]{1,0:T(2,128)} %reshape.17.at_ref, f32[768,1024]{1,0:T(8,128)} %copy-done.2, bf16[768,256]{1,0:T(8,128)(2,1)} %copy-done.17, bf16[768,256]{1,0:T(8,128)(2,1)} %copy-done.18, bf16[768,256]{1,0:T(8,128)(2,1)} %copy-done.19, ...), custom_call_target="tpu_custom_call" | custom-call | tf_op jit(solution)/shard_map/pallas_call | solution.py:403
  (163 shorter events, 37.0 us)
Async XLA Ops:
  15.7 77.2 %collective-permute-start.18 = (bf16[768,2048]{1,0:T(8,128)(2,1)}, bf16[768,2048]{1,0:T(8,128)(2,1)S(1)}, u32[]{:S(2)}, u32[]{:S(2)}) collective-permute-start(bf16[768,2048]{1,0:T(8,128)(2,1)} %get-tuple-element.81), channel_id=1, source_target_pairs={{0,1},{1,0},{2,3},{3,2},{4,5},{5,4},{6,7},{7,6},{8,9},{9,8},{10,11... | collective-permute-start | bytes 9437192 | tf_op jit(solution)/shard_map/ppermute | solution.py:447
  20.2 18.1 %collective-permute-start.3 = (bf16[352,1024]{1,0:T(8,128)(2,1)}, bf16[352,1024]{1,0:T(8,128)(2,1)}, u32[]{:S(2)}, u32[]{:S(2)}) collective-permute-start(bf16[352,1024]{1,0:T(8,128)(2,1)} %get-tuple-element.109.refs_2_.refs_0_), channel_id=1, source_target_pairs={{0,4},{1,5},{2,6},{3,7},{4,8},{5,9},{6,10},{7,11},{8,12},{9,13},{1... | collective-permute-start | bytes 2162696 | tf_op jit(solution)/shard_map/ppermute | solution.py:441
  21.6 19.0 %collective-permute-start.5 = (bf16[352,1024]{1,0:T(8,128)(2,1)}, bf16[352,1024]{1,0:T(8,128)(2,1)}, u32[]{:S(2)}, u32[]{:S(2)}) collective-permute-start(bf16[352,1024]{1,0:T(8,128)(2,1)} %get-tuple-element.109.refs_2_.refs_0_), channel_id=1, source_target_pairs={{0,2},{1,3},{2,0},{3,1},{4,6},{5,7},{6,4},{7,5},{8,10},{9,11},{10,... | collective-permute-start | bytes 2162696 | tf_op jit(solution)/shard_map/ppermute | solution.py:444
  38.3 18.0 %collective-permute-start.4 = (bf16[352,1024]{1,0:T(8,128)(2,1)}, bf16[352,1024]{1,0:T(8,128)(2,1)}, u32[]{:S(2)}, u32[]{:S(2)}) collective-permute-start(bf16[352,1024]{1,0:T(8,128)(2,1)} %get-tuple-element.109.refs_2_.refs_0_), channel_id=1, source_target_pairs={{0,12},{1,13},{2,14},{3,15},{4,0},{5,1},{6,2},{7,3},{8,4},{9,5},{1... | collective-permute-start | bytes 2162696 | tf_op jit(solution)/shard_map/ppermute | solution.py:441
  41.7 46.9 %collective-permute-start = (bf16[352,1024]{1,0:T(8,128)(2,1)}, bf16[352,1024]{1,0:T(8,128)(2,1)}, u32[]{:S(2)}, u32[]{:S(2)}) collective-permute-start(bf16[352,1024]{1,0:T(8,128)(2,1)} %get-tuple-element.109.refs_2_.refs_0_), channel_id=1, source_target_pairs={{0,8},{1,9},{2,10},{3,11},{4,12},{5,13},{6,14},{7,15},{8,0},{9,1},... | collective-permute-start | bytes 2162696 | tf_op jit(solution)/shard_map/ppermute | solution.py:441
  42.5 14.7 %collective-permute-start.9 = (s32[2,4]{1,0:T(2,128)S(1)}, s32[2,4]{1,0:T(2,128)S(1)}, u32[]{:S(2)}, u32[]{:S(2)}) collective-permute-start(s32[2,4]{1,0:T(2,128)S(1)} %pad_add_fusion.1), channel_id=1, source_target_pairs={{0,1},{1,0},{2,3},{3,2},{4,5},{5,4},{6,7},{7,6},{8,9},{9,8},{10,11... | collective-permute-start | bytes 104 | tf_op jit(solution)/shard_map/ppermute | solution.py:447
  60.1 29.6 %collective-permute-start.12 = (bf16[224,1024]{1,0:T(8,128)(2,1)S(1)}, bf16[224,1024]{1,0:T(8,128)(2,1)S(1)}, u32[]{:S(2)}, u32[]{:S(2)}) collective-permute-start(bf16[224,1024]{1,0:T(8,128)(2,1)S(1)} %slice.38), channel_id=1, source_target_pairs={{0,16},{16,0},{1,17},{17,1},{2,18},{18,2},{3,19},{19,3},{4,20},{20... | collective-permute-start | bytes 1376264 | tf_op jit(solution)/shard_map/ppermute | solution.py:450
  62.3 30.7 %collective-permute-start.21 = (bf16[224,1024]{1,0:T(8,128)(2,1)S(1)}, bf16[224,1024]{1,0:T(8,128)(2,1)S(1)}, u32[]{:S(2)}, u32[]{:S(2)}) collective-permute-start(bf16[224,1024]{1,0:T(8,128)(2,1)S(1)} %slice.39), channel_id=1, source_target_pairs={{0,16},{16,0},{1,17},{17,1},{2,18},{18,2},{3,19},{19,3},{4,20},{20... | collective-permute-start | bytes 1376264 | tf_op jit(solution)/shard_map/ppermute | solution.py:450
  67.1 149.8 %collective-permute-start.17 = (bf16[768,2048]{1,0:T(8,128)(2,1)}, bf16[768,2048]{1,0:T(8,128)(2,1)S(1)}, u32[]{:S(2)}, u32[]{:S(2)}) collective-permute-start(bf16[768,2048]{1,0:T(8,128)(2,1)} %get-tuple-element.79.refs_8_), channel_id=1, source_target_pairs={{0,1},{1,0},{2,3},{3,2},{4,5},{5,4},{6,7},{7,6},{8,9},{9,8},{10,11... | collective-permute-start | bytes 9437192 | tf_op jit(solution)/shard_map/ppermute | solution.py:447
  89.7 20.4 %collective-permute-start.13 = (bf16[224,1024]{1,0:T(8,128)(2,1)S(1)}, bf16[224,1024]{1,0:T(8,128)(2,1)S(1)}, u32[]{:S(2)}, u32[]{:S(2)}) collective-permute-start(bf16[224,1024]{1,0:T(8,128)(2,1)S(1)} %slice.37), channel_id=1, source_target_pairs={{0,16},{16,0},{1,17},{17,1},{2,18},{18,2},{3,19},{19,3},{4,20},{20... | collective-permute-start | bytes 1376264 | tf_op jit(solution)/shard_map/ppermute | solution.py:450
  92.5 14.4 %collective-permute-start.22 = (bf16[512,256]{1,0:T(8,128)(2,1)S(1)}, bf16[512,256]{1,0:T(8,128)(2,1)S(1)}, u32[]{:S(2)}, u32[]{:S(2)}) collective-permute-start(bf16[512,256]{1,0:T(8,128)(2,1)S(1)} %shard_map.86), channel_id=1, source_target_pairs={{0,16},{16,0},{1,17},{17,1},{2,18},{18,2},{3,19},{19,3},{4,20},{20... | collective-permute-start | bytes 786440 | tf_op jit(solution)/shard_map/ppermute | solution.py:450
  92.9 19.5 %collective-permute-start.19 = (bf16[352,1024]{1,0:T(8,128)(2,1)}, bf16[352,1024]{1,0:T(8,128)(2,1)S(1)}, u32[]{:S(2)}, u32[]{:S(2)}) collective-permute-start(bf16[352,1024]{1,0:T(8,128)(2,1)} %collective-permute-done.3.refs_6_.refs_4_), channel_id=1, source_target_pairs={{0,2},{1,3},{2,0},{3,1},{4,6},{5,7},{6,4},{7,5},{8,10},{9,11},{10,... | collective-permute-start | bytes 2162696 | tf_op jit(solution)/shard_map/ppermute | solution.py:444
  93.1 18.1 %collective-permute-start.1 = (bf16[1024,256]{1,0:T(8,128)(2,1)S(1)}, bf16[1024,256]{1,0:T(8,128)(2,1)S(1)}, u32[]{:S(2)}, u32[]{:S(2)}) collective-permute-start(bf16[1024,256]{1,0:T(8,128)(2,1)S(1)} %copy-done.9), channel_id=1, source_target_pairs={{0,4},{1,5},{2,6},{3,7},{4,8},{5,9},{6,10},{7,11},{8,12},{9,13},{1... | collective-permute-start | bytes 1572872 | tf_op jit(solution)/shard_map/ppermute | solution.py:441
  107.0 32.6 %collective-permute-start.11 = (bf16[1024,256]{1,0:T(8,128)(2,1)S(1)}, bf16[1024,256]{1,0:T(8,128)(2,1)S(1)}, u32[]{:S(2)}, u32[]{:S(2)}) collective-permute-start(bf16[1024,256]{1,0:T(8,128)(2,1)S(1)} %copy-done.9), channel_id=1, source_target_pairs={{0,8},{1,9},{2,10},{3,11},{4,12},{5,13},{6,14},{7,15},{8,0},{9,1},... | collective-permute-start | bytes 1572872 | tf_op jit(solution)/shard_map/ppermute | solution.py:441
  110.1 30.9 %collective-permute-start.24 = (bf16[352,1024]{1,0:T(8,128)(2,1)}, bf16[352,1024]{1,0:T(8,128)(2,1)S(1)}, u32[]{:S(2)}, u32[]{:S(2)}) collective-permute-start(bf16[352,1024]{1,0:T(8,128)(2,1)} %collective-permute-done.refs_7_.refs_8_), channel_id=1, source_target_pairs={{0,2},{1,3},{2,0},{3,1},{4,6},{5,7},{6,4},{7,5},{8,10},{9,11},{10,... | collective-permute-start | bytes 2162696 | tf_op jit(solution)/shard_map/ppermute | solution.py:444
  111.1 31.1 %collective-permute-start.14 = (bf16[224,1024]{1,0:T(8,128)(2,1)S(1)}, bf16[224,1024]{1,0:T(8,128)(2,1)S(1)}, u32[]{:S(2)}, u32[]{:S(2)}) collective-permute-start(bf16[224,1024]{1,0:T(8,128)(2,1)S(1)} %slice.36), channel_id=1, source_target_pairs={{0,16},{16,0},{1,17},{17,1},{2,18},{18,2},{3,19},{19,3},{4,20},{20... | collective-permute-start | bytes 1376264 | tf_op jit(solution)/shard_map/ppermute | solution.py:450
  112.4 30.8 %collective-permute-start.2 = (bf16[1024,256]{1,0:T(8,128)(2,1)S(1)}, bf16[1024,256]{1,0:T(8,128)(2,1)S(1)}, u32[]{:S(2)}, u32[]{:S(2)}) collective-permute-start(bf16[1024,256]{1,0:T(8,128)(2,1)S(1)} %copy-done.9), channel_id=1, source_target_pairs={{0,12},{1,13},{2,14},{3,15},{4,0},{5,1},{6,2},{7,3},{8,4},{9,5},{1... | collective-permute-start | bytes 1572872 | tf_op jit(solution)/shard_map/ppermute | solution.py:441
  139.6 13.0 %collective-permute-start.20 = (bf16[1024,256]{1,0:T(8,128)(2,1)S(1)}, bf16[1024,256]{1,0:T(8,128)(2,1)S(1)}, u32[]{:S(2)}, u32[]{:S(2)}) collective-permute-start(bf16[1024,256]{1,0:T(8,128)(2,1)S(1)} %collective-permute-done.1.refs_0_.refs_6_), channel_id=1, source_target_pairs={{0,2},{1,3},{2,0},{3,1},{4,6},{5,7},{6,4},{7,5},{8,10},{9,11},{10,... | collective-permute-start | bytes 1572872 | tf_op jit(solution)/shard_map/ppermute | solution.py:444
  140.9 13.0 %collective-permute-start.23 = (bf16[224,1024]{1,0:T(8,128)(2,1)S(1)}, bf16[224,1024]{1,0:T(8,128)(2,1)S(1)}, u32[]{:S(2)}, u32[]{:S(2)}) collective-permute-start(bf16[224,1024]{1,0:T(8,128)(2,1)S(1)} %slice.40), channel_id=1, source_target_pairs={{0,16},{16,0},{1,17},{17,1},{2,18},{18,2},{3,19},{19,3},{4,20},{20... | collective-permute-start | bytes 1376264 | tf_op jit(solution)/shard_map/ppermute | solution.py:450
  142.2 25.7 %collective-permute-start.25 = (bf16[224,1024]{1,0:T(8,128)(2,1)S(1)}, bf16[224,1024]{1,0:T(8,128)(2,1)S(1)}, u32[]{:S(2)}, u32[]{:S(2)}) collective-permute-start(bf16[224,1024]{1,0:T(8,128)(2,1)S(1)} %slice.41), channel_id=1, source_target_pairs={{0,16},{16,0},{1,17},{17,1},{2,18},{18,2},{3,19},{19,3},{4,20},{20... | collective-permute-start | bytes 1376264 | tf_op jit(solution)/shard_map/ppermute | solution.py:450
  143.2 24.5 %collective-permute-start.15 = (bf16[512,256]{1,0:T(8,128)(2,1)S(1)}, bf16[512,256]{1,0:T(8,128)(2,1)S(1)}, u32[]{:S(2)}, u32[]{:S(2)}) collective-permute-start(bf16[512,256]{1,0:T(8,128)(2,1)S(1)} %shard_map.85), channel_id=1, source_target_pairs={{0,16},{16,0},{1,17},{17,1},{2,18},{18,2},{3,19},{19,3},{4,20},{20... | collective-permute-start | bytes 786440 | tf_op jit(solution)/shard_map/ppermute | solution.py:450
  152.6 31.7 %collective-permute-start.8 = (bf16[1024,256]{1,0:T(8,128)(2,1)S(1)}, bf16[1024,256]{1,0:T(8,128)(2,1)S(1)}, u32[]{:S(2)}, u32[]{:S(2)}) collective-permute-start(bf16[1024,256]{1,0:T(8,128)(2,1)S(1)} %collective-permute-done.2.refs_0_.refs_15_), channel_id=1, source_target_pairs={{0,2},{1,3},{2,0},{3,1},{4,6},{5,7},{6,4},{7,5},{8,10},{9,11},{10,... | collective-permute-start | bytes 1572872 | tf_op jit(solution)/shard_map/ppermute | solution.py:444
  163.4 22.9 %collective-permute-start.26 = (bf16[224,1024]{1,0:T(8,128)(2,1)S(1)}, bf16[224,1024]{1,0:T(8,128)(2,1)S(1)}, u32[]{:S(2)}, u32[]{:S(2)}) collective-permute-start(bf16[224,1024]{1,0:T(8,128)(2,1)S(1)} %slice.42), channel_id=1, source_target_pairs={{0,16},{16,0},{1,17},{17,1},{2,18},{18,2},{3,19},{19,3},{4,20},{20... | collective-permute-start | bytes 1376264 | tf_op jit(solution)/shard_map/ppermute | solution.py:450
  167.7 19.2 %collective-permute-start.34 = (bf16[1024,256]{1,0:T(8,128)(2,1)S(1)}, bf16[1024,256]{1,0:T(8,128)(2,1)S(1)}, u32[]{:S(2)}, u32[]{:S(2)}) collective-permute-start(bf16[1024,256]{1,0:T(8,128)(2,1)S(1)} %collective-permute-done.11.refs_0_.refs_11_), channel_id=1, source_target_pairs={{0,2},{1,3},{2,0},{3,1},{4,6},{5,7},{6,4},{7,5},{8,10},{9,11},{10,... | collective-permute-start | bytes 1572872 | tf_op jit(solution)/shard_map/ppermute | solution.py:444
  167.9 15.3 %collective-permute-start.16 = (bf16[512,256]{1,0:T(8,128)(2,1)S(1)}, bf16[512,256]{1,0:T(8,128)(2,1)S(1)}, u32[]{:S(2)}, u32[]{:S(2)}) collective-permute-start(bf16[512,256]{1,0:T(8,128)(2,1)S(1)} %shard_map.84), channel_id=1, source_target_pairs={{0,16},{16,0},{1,17},{17,1},{2,18},{18,2},{3,19},{19,3},{4,20},{20... | collective-permute-start | bytes 786440 | tf_op jit(solution)/shard_map/ppermute | solution.py:450
  186.3 19.3 %collective-permute-start.38 = (bf16[1024,256]{1,0:T(8,128)(2,1)S(1)}, bf16[1024,256]{1,0:T(8,128)(2,1)S(1)}, u32[]{:S(2)}, u32[]{:S(2)}) collective-permute-start(bf16[1024,256]{1,0:T(8,128)(2,1)S(1)} %collective-permute-done.11.refs_0_.refs_11_), channel_id=1, source_target_pairs={{0,1},{1,0},{2,3},{3,2},{4,5},{5,4},{6,7},{7,6},{8,9},{9,8},{10,11... | collective-permute-start | bytes 1572872 | tf_op jit(solution)/shard_map/ppermute | solution.py:447
  191.5 19.4 %collective-permute-start.42 = (bf16[1024,256]{1,0:T(8,128)(2,1)S(1)}, bf16[1024,256]{1,0:T(8,128)(2,1)S(1)}, u32[]{:S(2)}, u32[]{:S(2)}) collective-permute-start(bf16[1024,256]{1,0:T(8,128)(2,1)S(1)} %collective-permute-done.2.refs_0_.refs_15_), channel_id=1, source_target_pairs={{0,1},{1,0},{2,3},{3,2},{4,5},{5,4},{6,7},{7,6},{8,9},{9,8},{10,11... | collective-permute-start | bytes 1572872 | tf_op jit(solution)/shard_map/ppermute | solution.py:447
  194.7 16.3 %collective-permute-start.44 = (bf16[1024,256]{1,0:T(8,128)(2,1)S(1)}, bf16[1024,256]{1,0:T(8,128)(2,1)S(1)}, u32[]{:S(2)}, u32[]{:S(2)}) collective-permute-start(bf16[1024,256]{1,0:T(8,128)(2,1)S(1)} %collective-permute-done.8.refs_0_.refs_17_), channel_id=1, source_target_pairs={{0,1},{1,0},{2,3},{3,2},{4,5},{5,4},{6,7},{7,6},{8,9},{9,8},{10,11... | collective-permute-start | bytes 1572872 | tf_op jit(solution)/shard_map/ppermute | solution.py:447
  205.6 26.1 %collective-permute-start.36 = (bf16[512,1024]{1,0:T(8,128)(2,1)}, bf16[512,1024]{1,0:T(8,128)(2,1)}, u32[]{:S(2)}, u32[]{:S(2)}) collective-permute-start(bf16[512,1024]{1,0:T(8,128)(2,1)} %shard_map.94.refs_9_), channel_id=1, source_target_pairs={{0,1},{1,0},{2,3},{3,2},{4,5},{5,4},{6,7},{7,6},{8,9},{9,8},{10,11... | collective-permute-start | bytes 3145736 | tf_op jit(solution)/shard_map/ppermute | solution.py:447
  208.1 20.2 %collective-permute-start.40 = (bf16[1024,256]{1,0:T(8,128)(2,1)S(1)}, bf16[1024,256]{1,0:T(8,128)(2,1)S(1)}, u32[]{:S(2)}, u32[]{:S(2)}) collective-permute-start(bf16[1024,256]{1,0:T(8,128)(2,1)S(1)} %collective-permute-done.34.refs_0_.refs_13_), channel_id=1, source_target_pairs={{0,1},{1,0},{2,3},{3,2},{4,5},{5,4},{6,7},{7,6},{8,9},{9,8},{10,11... | collective-permute-start | bytes 1572872 | tf_op jit(solution)/shard_map/ppermute | solution.py:447
  210.9 17.7 %collective-permute-start.41 = (bf16[512,256]{1,0:T(8,128)(2,1)S(1)}, bf16[512,256]{1,0:T(8,128)(2,1)S(1)}, u32[]{:S(2)}, u32[]{:S(2)}) collective-permute-start(bf16[512,256]{1,0:T(8,128)(2,1)S(1)} %collective-permute-done.35.refs_14_), channel_id=1, source_target_pairs={{0,1},{1,0},{2,3},{3,2},{4,5},{5,4},{6,7},{7,6},{8,9},{9,8},{10,11... | collective-permute-start | bytes 786440 | tf_op jit(solution)/shard_map/ppermute | solution.py:447
  211.0 18.2 %collective-permute-start.45 = (bf16[512,256]{1,0:T(8,128)(2,1)S(1)}, bf16[512,256]{1,0:T(8,128)(2,1)S(1)}, u32[]{:S(2)}, u32[]{:S(2)}) collective-permute-start(bf16[512,256]{1,0:T(8,128)(2,1)S(1)} %collective-permute-done.37.refs_18_), channel_id=1, source_target_pairs={{0,1},{1,0},{2,3},{3,2},{4,5},{5,4},{6,7},{7,6},{8,9},{9,8},{10,11... | collective-permute-start | bytes 786440 | tf_op jit(solution)/shard_map/ppermute | solution.py:447
  (49 other events, 1094.6 us)

commit v9 on v8

--- a/solution.py
+++ b/solution.py
@@ -472,7 +472,7 @@
         shard, adapters, rank = adapter_down_factors.shape
         flat = adapters * rank
         width = value_matrix.shape[1]
-        half, part = shard // 2, 3 * shard // 8
+        half, part = shard // 2, shard // 4
         me = lax.axis_index("store")
         side = lax.axis_index("groups") % 2
         mz, my, mc = me // (rows_y * cores), (me // cores) % rows_y, me % cores
@@ -596,7 +596,7 @@
             d_have[k, 0] = z(d_have[0, 0], k)
         v_have[0, 1] = y(v_have[0, 0])
         d_have[0, 1] = y(after(d_have[0, 0], v_have[0, 1]))
-        x_values([(0, 1)], slots_there)
+        x_values([(0, 1)], partner)
         x_down([(0, 1)])
         for i, k in enumerate(early):
             pins = [partner] + [d_miss[0, 1][0]] * i
@@ -615,17 +615,18 @@
         x_values([(last, 1)], sums[0])
         for k in early:
             x_down([(k, 0)])
-        for k in early:
+        for k in early[:-1]:
             x_down([(k, 1)])
+        partner_rest = across(after(other_rest, v_have[last, 1]))
+        arrays, plan = values(second)
+        ready = [d_have[last, 0], d_have[early[0], 1]]
+        sum_own, *sum_far = value_sums(
+            after(own_rest, *ready), partner_rest, arrays, plan, width, sums, jnp.bfloat16
+        )
+        x_down([(early[-1], 1)], sum_own)
         d_have[last, 1] = y(d_have[last, 0])
         x_down([(last, 0)])
 
-        partner_rest = across(after(other_rest, v_have[last, 1]))
-        arrays, plan = values(second)
-        ready = [d_have[last, 1], d_miss[last, 0][0]]
-        sum_own, *sum_far = value_sums(
-            after(own_rest, *ready), partner_rest, arrays, plan, width, sums, jnp.bfloat16
-        )
         sums = (sum_own, *[across(part) for part in sum_far])
         v_have[0, 0] = after(v_have[0, 0], d_miss[early[-1], 1][0])
         up_lane = ups(names)
@@ -635,7 +636,7 @@
         parts = slabs(place, first, d_have, d_miss)
         mid_own, mid_far = mid_partials(own, partner, arrays, parts, ends_both, slots_both, rank)
         mids = (mid_own, across(mid_far))
-        x_down([(last, 1)])
+        x_down([(last, 1)], mid_own)
 
         arrays, place = lay()
         parts = [(0, slabs(place, second, d_have, d_miss))]

time: 250 us -> 259 us (1.036)
  waiting for transfers between devices: 104 us -> 123 us
  starting transfers between devices: 67.2 us -> 53.4 us
  local copies, waits for them, and re-layouts: 11.1 us -> 14.1 us
    ppermute x6, waiting for transfers between devices: 48.8 us -> 67.9 us  [along_z(): lax.ppermute(value, 'store', pairs(lambda z, y, c: ((z + k) % depth, y, c)))]
    ppermute x17, starting transfers between devices: 39.2 us -> 20.4 us  [across(): return lax.ppermute(value, 'store', pairs(lambda z, y, c: (z, y, 1 - c)))]
    ppermute x15, waiting for transfers between devices: 32.4 us -> 23.1 us  [along_x(): return lax.ppermute(value, 'groups', [(g, g ^ 1) for g in range(groups)])]
    ppermute x6, starting transfers between devices: 7.06 us -> 15.3 us  [along_z(): lax.ppermute(value, 'store', pairs(lambda z, y, c: ((z + k) % depth, y, c)))]
    ppermute x8, waiting for transfers between devices: 21.9 us -> 28.5 us  [along_y(): return lax.ppermute(value, 'store', pairs(lambda z, y, c: (z, 1 - y, c)))]
    ppermute x15, starting transfers between devices: 14.7 us -> 9.84 us  [along_x(): return lax.ppermute(value, 'groups', [(g, g ^ 1) for g in range(groups)])]
    ppermute x17, waiting for transfers between devices: 0.81 us -> 3.85 us  [across(): return lax.ppermute(value, 'store', pairs(lambda z, y, c: (z, y, 1 - c)))]
    unnamed x70 -> x76, local copies, waits for them, and re-layouts: 3.23 us -> 5.46 us
  transfers between devices with their start and end apart: 46 -> 46, of which waited for: 14 -> 19; matrix products, arithmetic and copies ran while one was open for 3% -> 3% of each run, Pallas kernels for 14% -> 18%
where the time goes in v9:
time: 259 us; the launch traced here: 257 us
  waiting for transfers between devices  123 us (47%)
  Pallas kernels  65.5 us (25%)
  starting transfers between devices  53.4 us (21%)
  local copies, waits for them, and re-layouts  14.1 us (5%)
    ppermute x6, waiting for transfers between devices, along_z(): lax.ppermute(value, 'store', pairs(lambda z, y, c: ((z + k) % depth, y, c)))  67.9 us
    ppermute x8, waiting for transfers between devices, along_y(): return lax.ppermute(value, 'store', pairs(lambda z, y, c: (z, 1 - y, c)))  28.5 us
    ppermute x15, waiting for transfers between devices, along_x(): return lax.ppermute(value, 'groups', [(g, g ^ 1) for g in range(groups)])  23.1 us
    pallas_call x2, Pallas kernels, value_sums(): pl.pallas_call(functools.partial(value_kernel, plan, columns, len(sums),...  21.1 us
    ppermute x17, starting transfers between devices, across(): return lax.ppermute(value, 'store', pairs(lambda z, y, c: (z, y, 1 - c)))  20.4 us
    pallas_call x1, Pallas kernels, last_values(): pl.pallas_call(functools.partial(last_kernel, rank, parts, len(sums), len...  16.2 us
    ppermute x6, starting transfers between devices, along_z(): lax.ppermute(value, 'store', pairs(lambda z, y, c: ((z + k) % depth, y, c)))  15.3 us
    pallas_call x1, Pallas kernels, norm_in_order(): pl.pallas_call(norm_kernel, out_shape=[jax.ShapeDtypeStruct((rows, w), jn...  13.7 us
  transfers between devices with their start and end apart: 46, of which 19 were waited for; matrix products, arithmetic and copies ran while one was open for 3% of the time, Pallas kernels for 18%

profile of v9, /device:TPU:9, one launch (start us, length us, event | category | flops | bytes accessed | tf_op | source)
XLA Modules:
  0.0 257.4 jit_solution(15841535025865765008)
XLA Ops:
  0.0 1.7 copy.11
  1.7 3.0 %shard_map.83 = (bf16[416,1024]{1,0:T(8,128)(2,1)}, bf16[160,1024]{1,0:T(8,128)(2,1)}, bf16[1024,256]{1,0:T(8,128)(2,1)}, bf16[1024,256]{1,0:T(8,128)(2,1)}) custom-call(s32[1]{0:T(128)} %bitcast.98.side_ref, bf16[512,1024]{1,0:T(8,128)(2,1)} %refs_0_.1, bf16[64,1024]{1,0:T(8,128)(2,1)} %bitcast.106, bf16[1024,512]{1,0:T(8,128)(2,1)} %bitcast.105), custom_call_target="tpu_custom_call" | custom-call | tf_op jit(solution)/shard_map/pallas_call | solution.py:228
  4.8 1.3 collective-permute-start.3
  7.4 1.3 reshape.18.gain_ref
  9.5 13.7 %shard_map.82 = (bf16[768,2048]{1,0:T(8,128)(2,1)}, bf16[768,2048]{1,0:T(8,128)(2,1)}, bf16[768,2048]{1,0:T(8,128)(2,1)}, bf16[768,2048]{1,0:T(8,128)(2,1)}) custom-call(s32[64]{0:T(128)} %stack.391.source_ref, bf16[768,8192]{1,0:T(8,128)(2,1)} %tokens_ref.1, bf16[1,8192]{1,0:T(2,128)(2,1)} %reshape.18.gain_ref), custom_call_target="tpu_custom_call" | custom-call | tf_op jit(solution)/shard_map/pallas_call | solution.py:100
  25.0 2.4 collective-permute-start.7
  28.3 10.9 %collective-permute-done.9.refs_0_.refs_4_ = bf16[1024,256]{1,0:T(8,128)(2,1)S(1)} collective-permute-done((bf16[1024,256]{1,0:T(8,128)(2,1)S(1)}, bf16[1024,256]{1,0:T(8,128)(2,1)S(1)}, u32[]{:S(2)}, u32[]{:S(2)}) %collective-permute-start.9) | collective-permute-done | bytes 524320 | tf_op jit(solution)/shard_map/ppermute | solution.py:444
  40.1 4.5 %collective-permute-done.7.refs_11_.refs_12_ = bf16[416,1024]{1,0:T(8,128)(2,1)S(1)} collective-permute-done((bf16[416,1024]{1,0:T(8,128)(2,1)}, bf16[416,1024]{1,0:T(8,128)(2,1)S(1)}, u32[]{:S(2)}, u32[]{:S(2)}) %collective-permute-start.7) | collective-permute-done | bytes 852000 | tf_op jit(solution)/shard_map/ppermute | solution.py:441
  46.3 17.5 %collective-permute-done.10.refs_13_.refs_14_ = bf16[416,1024]{1,0:T(8,128)(2,1)S(1)} collective-permute-done((bf16[416,1024]{1,0:T(8,128)(2,1)S(1)}, bf16[416,1024]{1,0:T(8,128)(2,1)S(1)}, u32[]{:S(2)}, u32[]{:S(2)}) %collective-permute-start.10) | collective-permute-done | bytes 852000 | tf_op jit(solution)/shard_map/ppermute | solution.py:444
  64.8 3.1 %collective-permute-start.11 = (bf16[768,2048]{1,0:T(8,128)(2,1)}, bf16[768,2048]{1,0:T(8,128)(2,1)}, u32[]{:S(2)}, u32[]{:S(2)}) collective-permute-start(bf16[768,2048]{1,0:T(8,128)(2,1)} %get-tuple-element.77.refs_8_), channel_id=1, source_target_pairs={{0,1},{1,0},{2,3},{3,2},{4,5},{5,4},{6,7},{7,6},{8,9},{9,8},{10,11... | collective-permute-start | bytes 9437192 | tf_op jit(solution)/shard_map/ppermute | solution.py:447
  67.8 3.5 %collective-permute-start = (bf16[416,1024]{1,0:T(8,128)(2,1)}, bf16[416,1024]{1,0:T(8,128)(2,1)}, u32[]{:S(2)}, u32[]{:S(2)}) collective-permute-start(bf16[416,1024]{1,0:T(8,128)(2,1)} %get-tuple-element.109.refs_2_.refs_0_), channel_id=1, source_target_pairs={{0,8},{1,9},{2,10},{3,11},{4,12},{5,13},{6,14},{7,15},{8,0},{9,1},... | collective-permute-start | bytes 2555912 | tf_op jit(solution)/shard_map/ppermute | solution.py:441
  73.1 33.8 %collective-permute-done.refs_7_.refs_8_ = bf16[416,1024]{1,0:T(8,128)(2,1)} collective-permute-done((bf16[416,1024]{1,0:T(8,128)(2,1)}, bf16[416,1024]{1,0:T(8,128)(2,1)}, u32[]{:S(2)}, u32[]{:S(2)}) %collective-permute-start) | collective-permute-done | bytes 852000 | tf_op jit(solution)/shard_map/ppermute | solution.py:441
  108.8 1.8 collective-permute-done.16.slots_ref
  116.5 1.5 collective-permute-done.17.refs_5_
  118.5 3.5 %collective-permute-done.1.refs_0_.refs_6_ = bf16[1024,256]{1,0:T(8,128)(2,1)S(1)} collective-permute-done((bf16[1024,256]{1,0:T(8,128)(2,1)}, bf16[1024,256]{1,0:T(8,128)(2,1)S(1)}, u32[]{:S(2)}, u32[]{:S(2)}) %collective-permute-start.1) | collective-permute-done | bytes 524320 | tf_op jit(solution)/shard_map/ppermute | solution.py:441
  122.4 2.5 collective-permute-done.14.refs_7_.refs_5_
  125.0 2.3 collective-permute-start.2
  127.2 4.8 %collective-permute-done.13.refs_5_.refs_3_ = bf16[160,1024]{1,0:T(8,128)(2,1)S(1)} collective-permute-done((bf16[160,1024]{1,0:T(8,128)(2,1)S(1)}, bf16[160,1024]{1,0:T(8,128)(2,1)S(1)}, u32[]{:S(2)}, u32[]{:S(2)}) %collective-permute-start.13) | collective-permute-done | bytes 327712 | tf_op jit(solution)/shard_map/ppermute | solution.py:450
  132.0 4.6 %collective-permute-start.12 = (bf16[1024,256]{1,0:T(8,128)(2,1)}, bf16[1024,256]{1,0:T(8,128)(2,1)S(1)}, u32[]{:S(2)}, u32[]{:S(2)}) collective-permute-start(bf16[1024,256]{1,0:T(8,128)(2,1)} %get-tuple-element.79.refs_2_), channel_id=1, source_target_pairs={{0,8},{1,9},{2,10},{3,11},{4,12},{5,13},{6,14},{7,15},{8,0},{9,1},... | collective-permute-start | bytes 1572872 | tf_op jit(solution)/shard_map/ppermute | solution.py:441
  139.4 25.5 %collective-permute-done.12.refs_0_.refs_11_ = bf16[1024,256]{1,0:T(8,128)(2,1)S(1)} collective-permute-done((bf16[1024,256]{1,0:T(8,128)(2,1)}, bf16[1024,256]{1,0:T(8,128)(2,1)S(1)}, u32[]{:S(2)}, u32[]{:S(2)}) %collective-permute-start.12) | collective-permute-done | bytes 524320 | tf_op jit(solution)/shard_map/ppermute | solution.py:441
  167.1 6.6 %collective-permute-done.18.refs_9_.refs_7_ = bf16[160,1024]{1,0:T(8,128)(2,1)S(1)} collective-permute-done((bf16[160,1024]{1,0:T(8,128)(2,1)S(1)}, bf16[160,1024]{1,0:T(8,128)(2,1)S(1)}, u32[]{:S(2)}, u32[]{:S(2)}) %collective-permute-start.18) | collective-permute-done | bytes 327712 | tf_op jit(solution)/shard_map/ppermute | solution.py:450
  174.4 1.3 collective-permute-start.22
  176.7 10.6 %shard_map.85 = (f32[768,1024]{1,0:T(8,128)S(1)}, f32[768,256]{1,0:T(8,128)S(1)}, f32[768,256]{1,0:T(8,128)S(1)}, f32[768,256]{1,0:T(8,128)S(1)}, f32[768,256]{1,0:T(8,128)S(1)}) custom-call(bf16[768,2048]{1,0:T(8,128)(2,1)S(1)} %copy-done, bf16[768,2048]{1,0:T(8,128)(2,1)} %collective-permute-done.4.refs_1_, ...), custom_call_target="tpu_custom_call" | custom-call | tf_op jit(solution)/shard_map/pallas_call | solution.py:194
  188.3 1.3 collective-permute-start.28
  189.6 3.4 %collective-permute-start.38 = (bf16[1024,256]{1,0:T(8,128)(2,1)S(1)}, bf16[1024,256]{1,0:T(8,128)(2,1)S(1)}, u32[]{:S(2)}, u32[]{:S(2)}) collective-permute-start(bf16[1024,256]{1,0:T(8,128)(2,1)S(1)} %collective-permute-done.12.refs_0_.refs_11_), channel_id=1, source_target_pairs={{0,1},{1,0},{2,3},{3,2},{4,5},{5,4},{6,7},{7,6},{8,9},{9,8},{10,11... | collective-permute-start | bytes 1572872 | tf_op jit(solution)/shard_map/ppermute | solution.py:447
  195.7 7.3 %collective-permute-start.42 = (bf16[1024,256]{1,0:T(8,128)(2,1)S(1)}, bf16[1024,256]{1,0:T(8,128)(2,1)S(1)}, u32[]{:S(2)}, u32[]{:S(2)}) collective-permute-start(bf16[1024,256]{1,0:T(8,128)(2,1)S(1)} %collective-permute-done.2.refs_0_.refs_15_), channel_id=1, source_target_pairs={{0,1},{1,0},{2,3},{3,2},{4,5},{5,4},{6,7},{7,6},{8,9},{9,8},{10,11... | collective-permute-start | bytes 1572872 | tf_op jit(solution)/shard_map/ppermute | solution.py:447
  203.0 10.5 %shard_map.86 = (f32[768,1024]{1,0:T(8,128)S(1)}, bf16[768,256]{1,0:T(8,128)(2,1)S(1)}, bf16[768,256]{1,0:T(8,128)(2,1)}, bf16[768,256]{1,0:T(8,128)(2,1)}, bf16[768,256]{1,0:T(8,128)(2,1)}) custom-call(bf16[768,2048]{1,0:T(8,128)(2,1)S(1)} %copy-done.1, bf16[768,2048]{1,0:T(8,128)(2,1)} %collective-permute-done.11.refs_1_, ...), custom_call_target="tpu_custom_call" | custom-call | tf_op jit(solution)/shard_map/pallas_call | solution.py:194
  217.2 5.6 %shard_map.90 = (f32[768,64]{1,0:T(8,128)S(1)}, f32[768,64]{1,0:T(8,128)S(1)}) custom-call(s32[2,4]{1,0:T(2,128)S(1)} %pad_add_fusion.ends_ref, s32[2,4]{1,0:T(2,128)S(1)} %pad_add_fusion.2.slots_ref, bf16[768,2048]{1,0:T(8,128)(2,1)S(1)} %copy-done, bf16[768,2048]{1,0:T(8,128)(2,1)} %collective-permute-done.4.refs_1_, bf16[1024,256]{1,0:T(8,128)(2,1)S(1)} %copy-done.17, ...), custom_call_target="tpu_custom_call" | custom-call | tf_op jit(solution)/shard_map/pallas_call | solution.py:325
  223.8 1.4 shard_map.92.refs_9_
  226.2 1.5 collective-permute-done.35.refs_16_
  228.9 4.4 %collective-permute-done.37.refs_18_ = bf16[512,256]{1,0:T(8,128)(2,1)S(1)} collective-permute-done((bf16[512,256]{1,0:T(8,128)(2,1)S(1)}, bf16[512,256]{1,0:T(8,128)(2,1)S(1)}, u32[]{:S(2)}, u32[]{:S(2)}) %collective-permute-start.37) | collective-permute-done | bytes 262176 | tf_op jit(solution)/shard_map/ppermute | solution.py:450
  241.0 16.2 %shard_map.96 = bf16[768,1024]{1,0:T(8,128)(2,1)} custom-call(s32[4]{0:T(128)} %copy-done.34, s32[4]{0:T(128)} %bitcast.108, s32[2,16]{1,0:T(2,128)} %reshape.17.at_ref, f32[768,1024]{1,0:T(8,128)} %copy-done.7, bf16[768,256]{1,0:T(8,128)(2,1)} %copy-done.25, bf16[768,256]{1,0:T(8,128)(2,1)} %collective-permute-done.25.refs_2_, ...), custom_call_target="tpu_custom_call" | custom-call | tf_op jit(solution)/shard_map/pallas_call | solution.py:403
  (169 shorter events, 43.5 us)
Async XLA Ops:
  4.8 20.2 %collective-permute-start.3 = (bf16[416,1024]{1,0:T(8,128)(2,1)}, bf16[416,1024]{1,0:T(8,128)(2,1)}, u32[]{:S(2)}, u32[]{:S(2)}) collective-permute-start(bf16[416,1024]{1,0:T(8,128)(2,1)} %get-tuple-element.109.refs_2_.refs_0_), channel_id=1, source_target_pairs={{0,4},{1,5},{2,6},{3,7},{4,8},{5,9},{6,10},{7,11},{8,12},{9,13},{1... | collective-permute-start | bytes 2555912 | tf_op jit(solution)/shard_map/ppermute | solution.py:441
  6.1 21.2 %collective-permute-start.8 = (bf16[416,1024]{1,0:T(8,128)(2,1)}, bf16[416,1024]{1,0:T(8,128)(2,1)}, u32[]{:S(2)}, u32[]{:S(2)}) collective-permute-start(bf16[416,1024]{1,0:T(8,128)(2,1)} %get-tuple-element.109.refs_2_.refs_0_), channel_id=1, source_target_pairs={{0,2},{1,3},{2,0},{3,1},{4,6},{5,7},{6,4},{7,5},{8,10},{9,11},{10,... | collective-permute-start | bytes 2555912 | tf_op jit(solution)/shard_map/ppermute | solution.py:444
  23.1 89.8 %collective-permute-start.4 = (bf16[768,2048]{1,0:T(8,128)(2,1)}, bf16[768,2048]{1,0:T(8,128)(2,1)}, u32[]{:S(2)}, u32[]{:S(2)}) collective-permute-start(bf16[768,2048]{1,0:T(8,128)(2,1)} %get-tuple-element.69), channel_id=1, source_target_pairs={{0,1},{1,0},{2,3},{3,2},{4,5},{5,4},{6,7},{7,6},{8,9},{9,8},{10,11... | collective-permute-start | bytes 9437192 | tf_op jit(solution)/shard_map/ppermute | solution.py:447
  25.0 19.7 %collective-permute-start.7 = (bf16[416,1024]{1,0:T(8,128)(2,1)}, bf16[416,1024]{1,0:T(8,128)(2,1)S(1)}, u32[]{:S(2)}, u32[]{:S(2)}) collective-permute-start(bf16[416,1024]{1,0:T(8,128)(2,1)} %get-tuple-element.109.refs_2_.refs_0_), channel_id=1, source_target_pairs={{0,12},{1,13},{2,14},{3,15},{4,0},{5,1},{6,2},{7,3},{8,4},{9,5},{1... | collective-permute-start | bytes 2555912 | tf_op jit(solution)/shard_map/ppermute | solution.py:441
  27.3 11.9 %collective-permute-start.9 = (bf16[1024,256]{1,0:T(8,128)(2,1)S(1)}, bf16[1024,256]{1,0:T(8,128)(2,1)S(1)}, u32[]{:S(2)}, u32[]{:S(2)}) collective-permute-start(bf16[1024,256]{1,0:T(8,128)(2,1)S(1)} %copy-done.16), channel_id=1, source_target_pairs={{0,2},{1,3},{2,0},{3,1},{4,6},{5,7},{6,4},{7,5},{8,10},{9,11},{10,... | collective-permute-start | bytes 1572872 | tf_op jit(solution)/shard_map/ppermute | solution.py:444
  45.5 18.3 %collective-permute-start.10 = (bf16[416,1024]{1,0:T(8,128)(2,1)S(1)}, bf16[416,1024]{1,0:T(8,128)(2,1)S(1)}, u32[]{:S(2)}, u32[]{:S(2)}) collective-permute-start(bf16[416,1024]{1,0:T(8,128)(2,1)S(1)} %collective-permute-done.7.refs_11_.refs_12_), channel_id=1, source_target_pairs={{0,2},{1,3},{2,0},{3,1},{4,6},{5,7},{6,4},{7,5},{8,10},{9,11},{10,... | collective-permute-start | bytes 2555912 | tf_op jit(solution)/shard_map/ppermute | solution.py:444
  64.8 130.9 %collective-permute-start.11 = (bf16[768,2048]{1,0:T(8,128)(2,1)}, bf16[768,2048]{1,0:T(8,128)(2,1)}, u32[]{:S(2)}, u32[]{:S(2)}) collective-permute-start(bf16[768,2048]{1,0:T(8,128)(2,1)} %get-tuple-element.77.refs_8_), channel_id=1, source_target_pairs={{0,1},{1,0},{2,3},{3,2},{4,5},{5,4},{6,7},{7,6},{8,9},{9,8},{10,11... | collective-permute-start | bytes 9437192 | tf_op jit(solution)/shard_map/ppermute | solution.py:447
  67.8 39.1 %collective-permute-start = (bf16[416,1024]{1,0:T(8,128)(2,1)}, bf16[416,1024]{1,0:T(8,128)(2,1)}, u32[]{:S(2)}, u32[]{:S(2)}) collective-permute-start(bf16[416,1024]{1,0:T(8,128)(2,1)} %get-tuple-element.109.refs_2_.refs_0_), channel_id=1, source_target_pairs={{0,8},{1,9},{2,10},{3,11},{4,12},{5,13},{6,14},{7,15},{8,0},{9,1},... | collective-permute-start | bytes 2555912 | tf_op jit(solution)/shard_map/ppermute | solution.py:441
  106.9 15.0 %collective-permute-start.1 = (bf16[1024,256]{1,0:T(8,128)(2,1)}, bf16[1024,256]{1,0:T(8,128)(2,1)S(1)}, u32[]{:S(2)}, u32[]{:S(2)}) collective-permute-start(bf16[1024,256]{1,0:T(8,128)(2,1)} %get-tuple-element.79.refs_2_), channel_id=1, source_target_pairs={{0,4},{1,5},{2,6},{3,7},{4,8},{5,9},{6,10},{7,11},{8,12},{9,13},{1... | collective-permute-start | bytes 1572872 | tf_op jit(solution)/shard_map/ppermute | solution.py:441
  112.9 24.7 %collective-permute-start.5 = (bf16[416,1024]{1,0:T(8,128)(2,1)}, bf16[416,1024]{1,0:T(8,128)(2,1)S(1)}, u32[]{:S(2)}, u32[]{:S(2)}) collective-permute-start(bf16[416,1024]{1,0:T(8,128)(2,1)} %collective-permute-done.3.refs_6_.refs_4_), channel_id=1, source_target_pairs={{0,2},{1,3},{2,0},{3,1},{4,6},{5,7},{6,4},{7,5},{8,10},{9,11},{10,... | collective-permute-start | bytes 2555912 | tf_op jit(solution)/shard_map/ppermute | solution.py:444
  115.2 9.8 %collective-permute-start.14 = (bf16[160,1024]{1,0:T(8,128)(2,1)S(1)}, bf16[160,1024]{1,0:T(8,128)(2,1)S(1)}, u32[]{:S(2)}, u32[]{:S(2)}) collective-permute-start(bf16[160,1024]{1,0:T(8,128)(2,1)S(1)} %slice.37), channel_id=1, source_target_pairs={{0,16},{16,0},{1,17},{17,1},{2,18},{18,2},{3,19},{19,3},{4,20},{20... | collective-permute-start | bytes 983048 | tf_op jit(solution)/shard_map/ppermute | solution.py:450
  118.0 14.0 %collective-permute-start.13 = (bf16[160,1024]{1,0:T(8,128)(2,1)S(1)}, bf16[160,1024]{1,0:T(8,128)(2,1)S(1)}, u32[]{:S(2)}, u32[]{:S(2)}) collective-permute-start(bf16[160,1024]{1,0:T(8,128)(2,1)S(1)} %slice.36), channel_id=1, source_target_pairs={{0,16},{16,0},{1,17},{17,1},{2,18},{18,2},{3,19},{19,3},{4,20},{20... | collective-permute-start | bytes 983048 | tf_op jit(solution)/shard_map/ppermute | solution.py:450
  121.9 43.6 %collective-permute-start.20 = (bf16[416,1024]{1,0:T(8,128)(2,1)}, bf16[416,1024]{1,0:T(8,128)(2,1)S(1)}, u32[]{:S(2)}, u32[]{:S(2)}) collective-permute-start(bf16[416,1024]{1,0:T(8,128)(2,1)} %collective-permute-done.refs_7_.refs_8_), channel_id=1, source_target_pairs={{0,2},{1,3},{2,0},{3,1},{4,6},{5,7},{6,4},{7,5},{8,10},{9,11},{10,... | collective-permute-start | bytes 2555912 | tf_op jit(solution)/shard_map/ppermute | solution.py:444
  125.0 13.2 %collective-permute-start.2 = (bf16[1024,256]{1,0:T(8,128)(2,1)}, bf16[1024,256]{1,0:T(8,128)(2,1)S(1)}, u32[]{:S(2)}, u32[]{:S(2)}) collective-permute-start(bf16[1024,256]{1,0:T(8,128)(2,1)} %get-tuple-element.79.refs_2_), channel_id=1, source_target_pairs={{0,12},{1,13},{2,14},{3,15},{4,0},{5,1},{6,2},{7,3},{8,4},{9,5},{1... | collective-permute-start | bytes 1572872 | tf_op jit(solution)/shard_map/ppermute | solution.py:441
  132.0 32.9 %collective-permute-start.12 = (bf16[1024,256]{1,0:T(8,128)(2,1)}, bf16[1024,256]{1,0:T(8,128)(2,1)S(1)}, u32[]{:S(2)}, u32[]{:S(2)}) collective-permute-start(bf16[1024,256]{1,0:T(8,128)(2,1)} %get-tuple-element.79.refs_2_), channel_id=1, source_target_pairs={{0,8},{1,9},{2,10},{3,11},{4,12},{5,13},{6,14},{7,15},{8,0},{9,1},... | collective-permute-start | bytes 1572872 | tf_op jit(solution)/shard_map/ppermute | solution.py:441
  137.6 29.2 %collective-permute-start.19 = (bf16[160,1024]{1,0:T(8,128)(2,1)S(1)}, bf16[160,1024]{1,0:T(8,128)(2,1)S(1)}, u32[]{:S(2)}, u32[]{:S(2)}) collective-permute-start(bf16[160,1024]{1,0:T(8,128)(2,1)S(1)} %slice.39), channel_id=1, source_target_pairs={{0,16},{16,0},{1,17},{17,1},{2,18},{18,2},{3,19},{19,3},{4,20},{20... | collective-permute-start | bytes 983048 | tf_op jit(solution)/shard_map/ppermute | solution.py:450
  138.2 36.2 %collective-permute-start.6 = (bf16[1024,256]{1,0:T(8,128)(2,1)S(1)}, bf16[1024,256]{1,0:T(8,128)(2,1)S(1)}, u32[]{:S(2)}, u32[]{:S(2)}) collective-permute-start(bf16[1024,256]{1,0:T(8,128)(2,1)S(1)} %collective-permute-done.1.refs_0_.refs_6_), channel_id=1, source_target_pairs={{0,2},{1,3},{2,0},{3,1},{4,6},{5,7},{6,4},{7,5},{8,10},{9,11},{10,... | collective-permute-start | bytes 1572872 | tf_op jit(solution)/shard_map/ppermute | solution.py:444
  165.5 22.7 %collective-permute-start.36 = (bf16[1024,256]{1,0:T(8,128)(2,1)S(1)}, bf16[1024,256]{1,0:T(8,128)(2,1)S(1)}, u32[]{:S(2)}, u32[]{:S(2)}) collective-permute-start(bf16[1024,256]{1,0:T(8,128)(2,1)S(1)} %collective-permute-done.2.refs_0_.refs_15_), channel_id=1, source_target_pairs={{0,2},{1,3},{2,0},{3,1},{4,6},{5,7},{6,4},{7,5},{8,10},{9,11},{10,... | collective-permute-start | bytes 1572872 | tf_op jit(solution)/shard_map/ppermute | solution.py:444
  166.8 20.6 %collective-permute-start.21 = (bf16[160,1024]{1,0:T(8,128)(2,1)S(1)}, bf16[160,1024]{1,0:T(8,128)(2,1)S(1)}, u32[]{:S(2)}, u32[]{:S(2)}) collective-permute-start(bf16[160,1024]{1,0:T(8,128)(2,1)S(1)} %slice.40), channel_id=1, source_target_pairs={{0,16},{16,0},{1,17},{17,1},{2,18},{18,2},{3,19},{19,3},{4,20},{20... | collective-permute-start | bytes 983048 | tf_op jit(solution)/shard_map/ppermute | solution.py:450
  173.7 20.8 %collective-permute-start.31 = (bf16[1024,256]{1,0:T(8,128)(2,1)S(1)}, bf16[1024,256]{1,0:T(8,128)(2,1)S(1)}, u32[]{:S(2)}, u32[]{:S(2)}) collective-permute-start(bf16[1024,256]{1,0:T(8,128)(2,1)S(1)} %collective-permute-done.12.refs_0_.refs_11_), channel_id=1, source_target_pairs={{0,2},{1,3},{2,0},{3,1},{4,6},{5,7},{6,4},{7,5},{8,10},{9,11},{10,... | collective-permute-start | bytes 1572872 | tf_op jit(solution)/shard_map/ppermute | solution.py:444
  174.4 15.2 %collective-permute-start.22 = (bf16[160,1024]{1,0:T(8,128)(2,1)S(1)}, bf16[160,1024]{1,0:T(8,128)(2,1)S(1)}, u32[]{:S(2)}, u32[]{:S(2)}) collective-permute-start(bf16[160,1024]{1,0:T(8,128)(2,1)S(1)} %slice.41), channel_id=1, source_target_pairs={{0,16},{16,0},{1,17},{17,1},{2,18},{18,2},{3,19},{19,3},{4,20},{20... | collective-permute-start | bytes 983048 | tf_op jit(solution)/shard_map/ppermute | solution.py:450
  188.3 25.8 %collective-permute-start.28 = (bf16[512,256]{1,0:T(8,128)(2,1)S(1)}, bf16[512,256]{1,0:T(8,128)(2,1)S(1)}, u32[]{:S(2)}, u32[]{:S(2)}) collective-permute-start(bf16[512,256]{1,0:T(8,128)(2,1)S(1)} %shard_map.88), channel_id=1, source_target_pairs={{0,16},{16,0},{1,17},{17,1},{2,18},{18,2},{3,19},{19,3},{4,20},{20... | collective-permute-start | bytes 786440 | tf_op jit(solution)/shard_map/ppermute | solution.py:450
  189.6 35.6 %collective-permute-start.38 = (bf16[1024,256]{1,0:T(8,128)(2,1)S(1)}, bf16[1024,256]{1,0:T(8,128)(2,1)S(1)}, u32[]{:S(2)}, u32[]{:S(2)}) collective-permute-start(bf16[1024,256]{1,0:T(8,128)(2,1)S(1)} %collective-permute-done.12.refs_0_.refs_11_), channel_id=1, source_target_pairs={{0,1},{1,0},{2,3},{3,2},{4,5},{5,4},{6,7},{7,6},{8,9},{9,8},{10,11... | collective-permute-start | bytes 1572872 | tf_op jit(solution)/shard_map/ppermute | solution.py:447
  194.1 21.4 %collective-permute-start.34 = (bf16[512,256]{1,0:T(8,128)(2,1)S(1)}, bf16[512,256]{1,0:T(8,128)(2,1)S(1)}, u32[]{:S(2)}, u32[]{:S(2)}) collective-permute-start(bf16[512,256]{1,0:T(8,128)(2,1)S(1)} %shard_map.93), channel_id=1, source_target_pairs={{0,16},{16,0},{1,17},{17,1},{2,18},{18,2},{3,19},{19,3},{4,20},{20... | collective-permute-start | bytes 786440 | tf_op jit(solution)/shard_map/ppermute | solution.py:450
  194.5 21.5 %collective-permute-start.29 = (bf16[512,256]{1,0:T(8,128)(2,1)S(1)}, bf16[512,256]{1,0:T(8,128)(2,1)S(1)}, u32[]{:S(2)}, u32[]{:S(2)}) collective-permute-start(bf16[512,256]{1,0:T(8,128)(2,1)S(1)} %shard_map.89), channel_id=1, source_target_pairs={{0,16},{16,0},{1,17},{17,1},{2,18},{18,2},{3,19},{19,3},{4,20},{20... | collective-permute-start | bytes 786440 | tf_op jit(solution)/shard_map/ppermute | solution.py:450
  195.7 30.4 %collective-permute-start.42 = (bf16[1024,256]{1,0:T(8,128)(2,1)S(1)}, bf16[1024,256]{1,0:T(8,128)(2,1)S(1)}, u32[]{:S(2)}, u32[]{:S(2)}) collective-permute-start(bf16[1024,256]{1,0:T(8,128)(2,1)S(1)} %collective-permute-done.2.refs_0_.refs_15_), channel_id=1, source_target_pairs={{0,1},{1,0},{2,3},{3,2},{4,5},{5,4},{6,7},{7,6},{8,9},{9,8},{10,11... | collective-permute-start | bytes 1572872 | tf_op jit(solution)/shard_map/ppermute | solution.py:447
  214.1 9.3 %collective-permute-start.32 = (bf16[512,256]{1,0:T(8,128)(2,1)S(1)}, bf16[512,256]{1,0:T(8,128)(2,1)}, u32[]{:S(2)}, u32[]{:S(2)}) collective-permute-start(bf16[512,256]{1,0:T(8,128)(2,1)S(1)} %shard_map.91), channel_id=1, source_target_pairs={{0,16},{16,0},{1,17},{17,1},{2,18},{18,2},{3,19},{19,3},{4,20},{20... | collective-permute-start | bytes 786440 | tf_op jit(solution)/shard_map/ppermute | solution.py:450
  215.6 18.5 %collective-permute-start.44 = (bf16[1024,256]{1,0:T(8,128)(2,1)S(1)}, bf16[1024,256]{1,0:T(8,128)(2,1)S(1)}, u32[]{:S(2)}, u32[]{:S(2)}) collective-permute-start(bf16[1024,256]{1,0:T(8,128)(2,1)S(1)} %collective-permute-done.36.refs_0_.refs_17_), channel_id=1, source_target_pairs={{0,1},{1,0},{2,3},{3,2},{4,5},{5,4},{6,7},{7,6},{8,9},{9,8},{10,11... | collective-permute-start | bytes 1572872 | tf_op jit(solution)/shard_map/ppermute | solution.py:447
  216.0 11.7 %collective-permute-start.35 = (bf16[512,256]{1,0:T(8,128)(2,1)S(1)}, bf16[512,256]{1,0:T(8,128)(2,1)S(1)}, u32[]{:S(2)}, u32[]{:S(2)}) collective-permute-start(bf16[512,256]{1,0:T(8,128)(2,1)S(1)} %shard_map.94), channel_id=1, source_target_pairs={{0,16},{16,0},{1,17},{17,1},{2,18},{18,2},{3,19},{19,3},{4,20},{20... | collective-permute-start | bytes 786440 | tf_op jit(solution)/shard_map/ppermute | solution.py:450
  223.5 9.8 %collective-permute-start.37 = (bf16[512,256]{1,0:T(8,128)(2,1)S(1)}, bf16[512,256]{1,0:T(8,128)(2,1)S(1)}, u32[]{:S(2)}, u32[]{:S(2)}) collective-permute-start(bf16[512,256]{1,0:T(8,128)(2,1)S(1)} %shard_map.95), channel_id=1, source_target_pairs={{0,16},{16,0},{1,17},{17,1},{2,18},{18,2},{3,19},{19,3},{4,20},{20... | collective-permute-start | bytes 786440 | tf_op jit(solution)/shard_map/ppermute | solution.py:450
  225.2 14.8 %collective-permute-start.33 = (bf16[512,1024]{1,0:T(8,128)(2,1)S(1)}, bf16[512,1024]{1,0:T(8,128)(2,1)S(1)}, u32[]{:S(2)}, u32[]{:S(2)}) collective-permute-start(bf16[512,1024]{1,0:T(8,128)(2,1)S(1)} %shard_map.92.refs_9_), channel_id=1, source_target_pairs={{0,1},{1,0},{2,3},{3,2},{4,5},{5,4},{6,7},{7,6},{8,9},{9,8},{10,11... | collective-permute-start | bytes 3145736 | tf_op jit(solution)/shard_map/ppermute | solution.py:447
  226.1 9.6 %collective-permute-start.40 = (bf16[1024,256]{1,0:T(8,128)(2,1)S(1)}, bf16[1024,256]{1,0:T(8,128)(2,1)S(1)}, u32[]{:S(2)}, u32[]{:S(2)}) collective-permute-start(bf16[1024,256]{1,0:T(8,128)(2,1)S(1)} %collective-permute-done.31.refs_0_.refs_13_), channel_id=1, source_target_pairs={{0,1},{1,0},{2,3},{3,2},{4,5},{5,4},{6,7},{7,6},{8,9},{9,8},{10,11... | collective-permute-start | bytes 1572872 | tf_op jit(solution)/shard_map/ppermute | solution.py:447
  (52 other events, 1302.4 us)

commit v10 on v6

--- a/solution.py
+++ b/solution.py
@@ -407,14 +407,14 @@
             num_scalar_prefetch=3,
             grid=(rows // tile,),
             in_specs=[tiled(a, tile) for a in (*sums, *mids, *tokens)]
-            + [pl.BlockSpec(memory_space=pltpu.HBM)] * (2 + len(arrays)),
+            + [far_memory()] * (2 + len(arrays)),
             out_specs=pl.BlockSpec((tile, width), lambda i, *_: (i, 0)),
             scratch_shapes=[pltpu.VMEM(a.shape, a.dtype) for a in arrays]
             + [pltpu.VMEM((docs * rank, tokens[0].shape[1]), jnp.bfloat16)] * 2
             + [pltpu.VMEM((width, flat), jnp.bfloat16)]
             + [pltpu.SemaphoreType.DMA((len(arrays) + up_at.size,))],
         ),
-        compiler_params=pltpu.CompilerParams(vmem_limit_bytes=34 << 20),
+        compiler_params=pltpu.CompilerParams(vmem_limit_bytes=58 << 20),
         cost_estimate=light,
     )(slots, ends, up_at, *sums, *mids, *tokens, *ups, *arrays)
 
@@ -515,7 +515,7 @@
 
         order = list(range(depth))
         names = [(k, dy) for k in order for dy in range(rows_y)]
-        z, y, x = Line(along_z, 3), Line(along_y, 3), Line(along_x, 3)
+        z, y, x = Line(along_z, 2), Line(along_y, 2), Line(along_x, 2)
 
         def x_values(names, *earlier):
             got = x(after(jnp.concatenate([v_have[name][:cut] for name in names], 0), *earlier))
@@ -610,7 +610,7 @@
             d_have[k, 1] = y(d_have[k, 0])
         arrays, plan = values(first)
         sums = value_sums(
-            after(own, v_have[last, 1], *[d_have[k, 0] for k in early], d_have[early[0], 1]), partner, arrays, plan, width
+            after(own, v_have[last, 1], d_have[early[0], 1]), partner, arrays, plan, width
         )
         x_values([(last, 1)], sums[0])
         for k in early:
@@ -621,7 +621,7 @@
         x_down([(last, 0)])
 
         arrays, plan = values(second)
-        ready = [d_have[last, 1], d_miss[last, 0][0]]
+        ready = [d_have[last, 0], *[d_have[k, 1] for k in early]]
         sum_own, *sum_far = value_sums(
             after(own_rest, *ready), partner_rest, arrays, plan, width, sums, jnp.bfloat16
         )
@@ -633,7 +633,7 @@
         parts = slabs(place, first, d_have, d_miss)
         mid_own, mid_far = mid_partials(own, partner, arrays, parts, ends_both, slots_both, rank)
         mids = (mid_own, across(mid_far))
-        x_down([(last, 1)], mids[1], up_both[1])
+        x_down([(last, 1)])
 
         arrays, place = lay()
         parts = [(0, slabs(place, second, d_have, d_miss))]

time: 264 us -> 222 us (0.84)
  local copies, waits for them, and re-layouts: 42.6 us -> 17.3 us
  waiting for transfers between devices: 113 us -> 87.7 us
  starting transfers between devices: 45.3 us -> 53.6 us
    unnamed x104 -> x70, local copies, waits for them, and re-layouts: 39.2 us -> 13.3 us
    ppermute x15, waiting for transfers between devices: 30.5 us -> 13.4 us  [along_x(): return lax.ppermute(value, 'groups', [(g, g ^ 1) for g in range(groups)])]
    ppermute x6, waiting for transfers between devices: 68 us -> 54.4 us  [along_z(): lax.ppermute(value, 'store', pairs(lambda z, y, c: ((z + k) % depth, y, c)))]
    ppermute x17, starting transfers between devices: 12.3 us -> 22.8 us  [across(): return lax.ppermute(value, 'store', pairs(lambda z, y, c: (z, y, 1 - c)))]
    ppermute x8, waiting for transfers between devices: 10.9 us -> 17.3 us  [along_y(): return lax.ppermute(value, 'store', pairs(lambda z, y, c: (z, 1 - y, c)))]
  transfers between devices with their start and end apart: 46 -> 46, of which waited for: 20 -> 14; matrix products, arithmetic and copies ran while one was open for 1% -> 2% of each run, Pallas kernels for 14% -> 17%
where the time goes in v10:
time: 222 us
  waiting for transfers between devices  87.7 us (40%)
  Pallas kernels  62.2 us (28%)
  starting transfers between devices  53.6 us (24%)
  local copies, waits for them, and re-layouts  17.3 us (8%)
    ppermute x6, waiting for transfers between devices, along_z(): lax.ppermute(value, 'store', pairs(lambda z, y, c: ((z + k) % depth, y, c)))  54.4 us
    ppermute x17, starting transfers between devices, across(): return lax.ppermute(value, 'store', pairs(lambda z, y, c: (z, y, 1 - c)))  22.8 us
    pallas_call x2, Pallas kernels, value_sums(): pl.pallas_call(functools.partial(value_kernel, plan, columns, len(sums),...  22.1 us
    ppermute x8, waiting for transfers between devices, along_y(): return lax.ppermute(value, 'store', pairs(lambda z, y, c: (z, 1 - y, c)))  17.3 us
    pallas_call x1, Pallas kernels, last_values(): pl.pallas_call(functools.partial(last_kernel, rank, parts, len(sums), len...  16.2 us
    ppermute x15, starting transfers between devices, along_x(): return lax.ppermute(value, 'groups', [(g, g ^ 1) for g in range(groups)])  14.6 us
    ppermute x15, waiting for transfers between devices, along_x(): return lax.ppermute(value, 'groups', [(g, g ^ 1) for g in range(groups)])  13.4 us
    unnamed x70, local copies, waits for them, and re-layouts  13.3 us
  transfers between devices with their start and end apart: 46, of which 14 were waited for; matrix products, arithmetic and copies ran while one was open for 2% of the time, Pallas kernels for 17%

profile of v10, /device:TPU:9, one launch (start us, length us, event | category | flops | bytes accessed | tf_op | source)
XLA Modules:
  0.0 221.8 jit_solution(2161939841638470628)
XLA Ops:
  0.9 4.6 %copy-done = bf16[768,8192]{1,0:T(8,128)(2,1)S(1)} copy-done((bf16[768,8192]{1,0:T(8,128)(2,1)S(1)}, bf16[768,8192]{1,0:T(8,128)(2,1)}, u32[]{:S(2)}) %copy-start) | copy-done | bytes 12582936
  5.5 8.6 %shard_map.82 = (bf16[768,2048]{1,0:T(8,128)(2,1)S(1)}, bf16[768,2048]{1,0:T(8,128)(2,1)S(1)}, bf16[768,2048]{1,0:T(8,128)(2,1)}, bf16[768,2048]{1,0:T(8,128)(2,1)}) custom-call(s32[64]{0:T(128)S(1)} %stack.391.source_ref, bf16[768,8192]{1,0:T(8,128)(2,1)S(1)} %copy-done, bf16[1,8192]{1,0:T(2,128)(2,1)S(1)} %reshape.18.gain_ref), custom_call_target="tpu_custom_call" | custom-call | tf_op jit(solution)/shard_map/pallas_call | solution.py:100
  14.1 1.7 copy-done.1
  19.0 1.9 shard_map.83
  29.6 1.5 collective-permute-done.6.slots_ref
  31.3 9.5 %collective-permute-done.14.refs_4_.refs_2_ = bf16[352,1024]{1,0:T(8,128)(2,1)} collective-permute-done((bf16[352,1024]{1,0:T(8,128)(2,1)}, bf16[352,1024]{1,0:T(8,128)(2,1)}, u32[]{:S(2)}, u32[]{:S(2)}) %collective-permute-start.14) | collective-permute-done | bytes 720928 | tf_op jit(solution)/shard_map/ppermute | solution.py:444
  40.8 2.3 %collective-permute-start = (bf16[352,1024]{1,0:T(8,128)(2,1)}, bf16[352,1024]{1,0:T(8,128)(2,1)S(1)}, u32[]{:S(2)}, u32[]{:S(2)}) collective-permute-start(bf16[352,1024]{1,0:T(8,128)(2,1)} %get-tuple-element.71.refs_2_.refs_0_), channel_id=1, source_target_pairs={{0,8},{1,9},{2,10},{3,11},{4,12},{5,13},{6,14},{7,15},{8,0},{9,1},... | collective-permute-start | bytes 2162696 | tf_op jit(solution)/shard_map/ppermute | solution.py:441
  44.2 7.8 %collective-permute-done.7.refs_0_.refs_4_ = bf16[1024,256]{1,0:T(8,128)(2,1)S(1)} collective-permute-done((bf16[1024,256]{1,0:T(8,128)(2,1)}, bf16[1024,256]{1,0:T(8,128)(2,1)S(1)}, u32[]{:S(2)}, u32[]{:S(2)}) %collective-permute-start.7) | collective-permute-done | bytes 524320 | tf_op jit(solution)/shard_map/ppermute | solution.py:444
  55.3 19.3 %collective-permute-done.refs_7_.refs_8_ = bf16[352,1024]{1,0:T(8,128)(2,1)S(1)} collective-permute-done((bf16[352,1024]{1,0:T(8,128)(2,1)}, bf16[352,1024]{1,0:T(8,128)(2,1)S(1)}, u32[]{:S(2)}, u32[]{:S(2)}) %collective-permute-start) | collective-permute-done | bytes 720928 | tf_op jit(solution)/shard_map/ppermute | solution.py:441
  77.0 1.4 collective-permute-start.19
  78.4 1.4 collective-permute-start.1
  80.1 7.1 %collective-permute-done.19.refs_7_.refs_5_ = bf16[224,1024]{1,0:T(8,128)(2,1)S(1)} collective-permute-done((bf16[224,1024]{1,0:T(8,128)(2,1)S(1)}, bf16[224,1024]{1,0:T(8,128)(2,1)S(1)}, u32[]{:S(2)}, u32[]{:S(2)}) %collective-permute-start.19) | collective-permute-done | bytes 458784 | tf_op jit(solution)/shard_map/ppermute | solution.py:450
  88.5 3.6 %collective-permute-done.12.refs_11_.refs_12_ = bf16[352,1024]{1,0:T(8,128)(2,1)S(1)} collective-permute-done((bf16[352,1024]{1,0:T(8,128)(2,1)}, bf16[352,1024]{1,0:T(8,128)(2,1)S(1)}, u32[]{:S(2)}, u32[]{:S(2)}) %collective-permute-start.12) | collective-permute-done | bytes 720928 | tf_op jit(solution)/shard_map/ppermute | solution.py:441
  93.3 12.8 %collective-permute-done.1.refs_0_.refs_6_ = bf16[1024,256]{1,0:T(8,128)(2,1)S(1)} collective-permute-done((bf16[1024,256]{1,0:T(8,128)(2,1)}, bf16[1024,256]{1,0:T(8,128)(2,1)S(1)}, u32[]{:S(2)}, u32[]{:S(2)}) %collective-permute-start.1) | collective-permute-done | bytes 524320 | tf_op jit(solution)/shard_map/ppermute | solution.py:441
  107.6 1.4 collective-permute-start.22
  109.0 2.1 collective-permute-start.13
  111.2 8.0 %collective-permute-done.2.refs_0_.refs_15_ = bf16[1024,256]{1,0:T(8,128)(2,1)S(1)} collective-permute-done((bf16[1024,256]{1,0:T(8,128)(2,1)S(1)}, bf16[1024,256]{1,0:T(8,128)(2,1)S(1)}, u32[]{:S(2)}, u32[]{:S(2)}) %collective-permute-start.2) | collective-permute-done | bytes 524320 | tf_op jit(solution)/shard_map/ppermute | solution.py:441
  121.7 10.3 %shard_map.85 = (f32[768,1024]{1,0:T(8,128)S(1)}, f32[768,256]{1,0:T(8,128)S(1)}, f32[768,256]{1,0:T(8,128)S(1)}, f32[768,256]{1,0:T(8,128)S(1)}, f32[768,256]{1,0:T(8,128)S(1)}) custom-call(bf16[768,2048]{1,0:T(8,128)(2,1)S(1)} %get-tuple-element.79.refs_0_, bf16[768,2048]{1,0:T(8,128)(2,1)} %collective-permute-done.3.refs_1_, ...), custom_call_target="tpu_custom_call" | custom-call | tf_op jit(solution)/shard_map/pallas_call | solution.py:194
  132.0 1.4 collective-permute-start.24
  133.4 10.7 %collective-permute-done.13.refs_0_.refs_11_ = bf16[1024,256]{1,0:T(8,128)(2,1)S(1)} collective-permute-done((bf16[1024,256]{1,0:T(8,128)(2,1)S(1)}, bf16[1024,256]{1,0:T(8,128)(2,1)S(1)}, u32[]{:S(2)}, u32[]{:S(2)}) %collective-permute-start.13) | collective-permute-done | bytes 524320 | tf_op jit(solution)/shard_map/ppermute | solution.py:441
  146.6 3.6 %collective-permute-start.38 = (bf16[1024,256]{1,0:T(8,128)(2,1)S(1)}, bf16[1024,256]{1,0:T(8,128)(2,1)S(1)}, u32[]{:S(2)}, u32[]{:S(2)}) collective-permute-start(bf16[1024,256]{1,0:T(8,128)(2,1)S(1)} %collective-permute-done.13.refs_0_.refs_11_), channel_id=1, source_target_pairs={{0,1},{1,0},{2,3},{3,2},{4,5},{5,4},{6,7},{7,6},{8,9},{9,8},{10,11... | collective-permute-start | bytes 1572872 | tf_op jit(solution)/shard_map/ppermute | solution.py:447
  150.3 6.4 %collective-permute-start.44 = (bf16[1024,256]{1,0:T(8,128)(2,1)S(1)}, bf16[1024,256]{1,0:T(8,128)(2,1)S(1)}, u32[]{:S(2)}, u32[]{:S(2)}) collective-permute-start(bf16[1024,256]{1,0:T(8,128)(2,1)S(1)} %collective-permute-done.36.refs_0_.refs_17_), channel_id=1, source_target_pairs={{0,1},{1,0},{2,3},{3,2},{4,5},{5,4},{6,7},{7,6},{8,9},{9,8},{10,11... | collective-permute-start | bytes 1572872 | tf_op jit(solution)/shard_map/ppermute | solution.py:447
  159.5 11.8 %shard_map.86 = (f32[768,1024]{1,0:T(8,128)S(1)}, bf16[768,256]{1,0:T(8,128)(2,1)S(1)}, bf16[768,256]{1,0:T(8,128)(2,1)S(1)}, bf16[768,256]{1,0:T(8,128)(2,1)S(1)}, bf16[768,256]{1,0:T(8,128)(2,1)S(1)}) custom-call(bf16[768,2048]{1,0:T(8,128)(2,1)S(1)} %copy-done.2, bf16[768,2048]{1,0:T(8,128)(2,1)} %collective-permute-done.4.refs_1_, ...), custom_call_target="tpu_custom_call" | custom-call | tf_op jit(solution)/shard_map/pallas_call | solution.py:194
  171.4 2.8 %collective-permute-start.25 = (bf16[768,256]{1,0:T(8,128)(2,1)S(1)}, bf16[768,256]{1,0:T(8,128)(2,1)S(1)}, u32[]{:S(2)}, u32[]{:S(2)}) collective-permute-start(bf16[768,256]{1,0:T(8,128)(2,1)S(1)} %get-tuple-element.95), channel_id=1, source_target_pairs={{0,1},{1,0},{2,3},{3,2},{4,5},{5,4},{6,7},{7,6},{8,9},{9,8},{10,11... | collective-permute-start | bytes 1179656 | tf_op jit(solution)/shard_map/ppermute | solution.py:447
  174.2 1.6 shard_map.93
  177.3 2.2 shard_map.91.refs_9_
  180.7 2.8 %collective-permute-done.34.refs_14_ = bf16[512,256]{1,0:T(8,128)(2,1)} collective-permute-done((bf16[512,256]{1,0:T(8,128)(2,1)S(1)}, bf16[512,256]{1,0:T(8,128)(2,1)}, u32[]{:S(2)}, u32[]{:S(2)}) %collective-permute-start.34) | collective-permute-done | bytes 262176 | tf_op jit(solution)/shard_map/ppermute | solution.py:450
  185.6 1.8 collective-permute-start.28
  188.1 2.0 collective-permute-done.35.refs_16_
  190.1 3.9 %collective-permute-start.39 = (bf16[512,256]{1,0:T(8,128)(2,1)S(1)}, bf16[512,256]{1,0:T(8,128)(2,1)S(1)}, u32[]{:S(2)}, u32[]{:S(2)}) collective-permute-start(bf16[512,256]{1,0:T(8,128)(2,1)S(1)} %collective-permute-done.33.refs_12_), channel_id=1, source_target_pairs={{0,1},{1,0},{2,3},{3,2},{4,5},{5,4},{6,7},{7,6},{8,9},{9,8},{10,11... | collective-permute-start | bytes 786440 | tf_op jit(solution)/shard_map/ppermute | solution.py:447
  194.1 5.6 %shard_map.90 = (f32[768,64]{1,0:T(8,128)S(1)}, f32[768,64]{1,0:T(8,128)S(1)}) custom-call(s32[2,4]{1,0:T(2,128)S(1)} %pad_add_fusion.ends_ref, s32[2,4]{1,0:T(2,128)S(1)} %pad_add_fusion.2.slots_ref, bf16[768,2048]{1,0:T(8,128)(2,1)S(1)} %get-tuple-element.79.refs_0_, bf16[768,2048]{1,0:T(8,128)(2,1)} %collective-permute-done.3.refs_1_, ...), custom_call_target="tpu_custom_call" | custom-call | tf_op jit(solution)/shard_map/pallas_call | solution.py:325
  205.4 16.2 %shard_map.96 = bf16[768,1024]{1,0:T(8,128)(2,1)} custom-call(s32[4]{0:T(128)} %copy-done.31, s32[4]{0:T(128)} %bitcast.108, s32[2,16]{1,0:T(2,128)} %reshape.17.at_ref, f32[768,1024]{1,0:T(8,128)} %copy-done.3, bf16[768,256]{1,0:T(8,128)(2,1)} %copy-done.19, bf16[768,256]{1,0:T(8,128)(2,1)} %copy-done.20, bf16[768,256]{1,0:T(8,128)(2,1)} %copy-done.21, ...), custom_call_target="tpu_custom_call" | custom-call | tf_op jit(solution)/shard_map/pallas_call | solution.py:403
  (163 shorter events, 43.1 us)
Async XLA Ops:
  15.8 38.3 %collective-permute-start.3 = (bf16[768,2048]{1,0:T(8,128)(2,1)}, bf16[768,2048]{1,0:T(8,128)(2,1)}, u32[]{:S(2)}, u32[]{:S(2)}) collective-permute-start(bf16[768,2048]{1,0:T(8,128)(2,1)} %get-tuple-element.66), channel_id=1, source_target_pairs={{0,1},{1,0},{2,3},{3,2},{4,5},{5,4},{6,7},{7,6},{8,9},{9,8},{10,11... | collective-permute-start | bytes 9437192 | tf_op jit(solution)/shard_map/ppermute | solution.py:447
  16.4 58.4 %collective-permute-start.4 = (bf16[768,2048]{1,0:T(8,128)(2,1)}, bf16[768,2048]{1,0:T(8,128)(2,1)}, u32[]{:S(2)}, u32[]{:S(2)}) collective-permute-start(bf16[768,2048]{1,0:T(8,128)(2,1)} %get-tuple-element.67.refs_8_), channel_id=1, source_target_pairs={{0,1},{1,0},{2,3},{3,2},{4,5},{5,4},{6,7},{7,6},{8,9},{9,8},{10,11... | collective-permute-start | bytes 9437192 | tf_op jit(solution)/shard_map/ppermute | solution.py:447
  23.3 17.5 %collective-permute-start.14 = (bf16[352,1024]{1,0:T(8,128)(2,1)}, bf16[352,1024]{1,0:T(8,128)(2,1)}, u32[]{:S(2)}, u32[]{:S(2)}) collective-permute-start(bf16[352,1024]{1,0:T(8,128)(2,1)} %get-tuple-element.71.refs_2_.refs_0_), channel_id=1, source_target_pairs={{0,2},{1,3},{2,0},{3,1},{4,6},{5,7},{6,4},{7,5},{8,10},{9,11},{10,... | collective-permute-start | bytes 2162696 | tf_op jit(solution)/shard_map/ppermute | solution.py:444
  24.6 29.3 %collective-permute-start.11 = (bf16[352,1024]{1,0:T(8,128)(2,1)}, bf16[352,1024]{1,0:T(8,128)(2,1)}, u32[]{:S(2)}, u32[]{:S(2)}) collective-permute-start(bf16[352,1024]{1,0:T(8,128)(2,1)} %get-tuple-element.71.refs_2_.refs_0_), channel_id=1, source_target_pairs={{0,4},{1,5},{2,6},{3,7},{4,8},{5,9},{6,10},{7,11},{8,12},{9,13},{1... | collective-permute-start | bytes 2162696 | tf_op jit(solution)/shard_map/ppermute | solution.py:441
  31.1 20.9 %collective-permute-start.7 = (bf16[1024,256]{1,0:T(8,128)(2,1)}, bf16[1024,256]{1,0:T(8,128)(2,1)S(1)}, u32[]{:S(2)}, u32[]{:S(2)}) collective-permute-start(bf16[1024,256]{1,0:T(8,128)(2,1)} %copy-done.11), channel_id=1, source_target_pairs={{0,2},{1,3},{2,0},{3,1},{4,6},{5,7},{6,4},{7,5},{8,10},{9,11},{10,... | collective-permute-start | bytes 1572872 | tf_op jit(solution)/shard_map/ppermute | solution.py:444
  40.8 33.8 %collective-permute-start = (bf16[352,1024]{1,0:T(8,128)(2,1)}, bf16[352,1024]{1,0:T(8,128)(2,1)S(1)}, u32[]{:S(2)}, u32[]{:S(2)}) collective-permute-start(bf16[352,1024]{1,0:T(8,128)(2,1)} %get-tuple-element.71.refs_2_.refs_0_), channel_id=1, source_target_pairs={{0,8},{1,9},{2,10},{3,11},{4,12},{5,13},{6,14},{7,15},{8,0},{9,1},... | collective-permute-start | bytes 2162696 | tf_op jit(solution)/shard_map/ppermute | solution.py:441
  52.0 25.1 %collective-permute-start.18 = (bf16[224,1024]{1,0:T(8,128)(2,1)S(1)}, bf16[224,1024]{1,0:T(8,128)(2,1)S(1)}, u32[]{:S(2)}, u32[]{:S(2)}) collective-permute-start(bf16[224,1024]{1,0:T(8,128)(2,1)S(1)} %slice.36), channel_id=1, source_target_pairs={{0,16},{16,0},{1,17},{17,1},{2,18},{18,2},{3,19},{19,3},{4,20},{20... | collective-permute-start | bytes 1376264 | tf_op jit(solution)/shard_map/ppermute | solution.py:450
  53.9 21.0 %collective-permute-start.8 = (bf16[512,256]{1,0:T(8,128)(2,1)S(1)}, bf16[512,256]{1,0:T(8,128)(2,1)S(1)}, u32[]{:S(2)}, u32[]{:S(2)}) collective-permute-start(bf16[512,256]{1,0:T(8,128)(2,1)S(1)} %shard_map.84), channel_id=1, source_target_pairs={{0,16},{16,0},{1,17},{17,1},{2,18},{18,2},{3,19},{19,3},{4,20},{20... | collective-permute-start | bytes 786440 | tf_op jit(solution)/shard_map/ppermute | solution.py:450
  54.1 25.8 %collective-permute-start.15 = (bf16[352,1024]{1,0:T(8,128)(2,1)}, bf16[352,1024]{1,0:T(8,128)(2,1)S(1)}, u32[]{:S(2)}, u32[]{:S(2)}) collective-permute-start(bf16[352,1024]{1,0:T(8,128)(2,1)} %collective-permute-done.11.refs_6_.refs_4_), channel_id=1, source_target_pairs={{0,2},{1,3},{2,0},{3,1},{4,6},{5,7},{6,4},{7,5},{8,10},{9,11},{10,... | collective-permute-start | bytes 2162696 | tf_op jit(solution)/shard_map/ppermute | solution.py:444
  74.6 17.4 %collective-permute-start.12 = (bf16[352,1024]{1,0:T(8,128)(2,1)}, bf16[352,1024]{1,0:T(8,128)(2,1)S(1)}, u32[]{:S(2)}, u32[]{:S(2)}) collective-permute-start(bf16[352,1024]{1,0:T(8,128)(2,1)} %get-tuple-element.71.refs_2_.refs_0_), channel_id=1, source_target_pairs={{0,12},{1,13},{2,14},{3,15},{4,0},{5,1},{6,2},{7,3},{8,4},{9,5},{1... | collective-permute-start | bytes 2162696 | tf_op jit(solution)/shard_map/ppermute | solution.py:441
  74.9 31.5 %collective-permute-start.9 = (bf16[352,1024]{1,0:T(8,128)(2,1)S(1)}, bf16[352,1024]{1,0:T(8,128)(2,1)S(1)}, u32[]{:S(2)}, u32[]{:S(2)}) collective-permute-start(bf16[352,1024]{1,0:T(8,128)(2,1)S(1)} %collective-permute-done.refs_7_.refs_8_), channel_id=1, source_target_pairs={{0,2},{1,3},{2,0},{3,1},{4,6},{5,7},{6,4},{7,5},{8,10},{9,11},{10,... | collective-permute-start | bytes 2162696 | tf_op jit(solution)/shard_map/ppermute | solution.py:444
  78.4 27.6 %collective-permute-start.1 = (bf16[1024,256]{1,0:T(8,128)(2,1)}, bf16[1024,256]{1,0:T(8,128)(2,1)S(1)}, u32[]{:S(2)}, u32[]{:S(2)}) collective-permute-start(bf16[1024,256]{1,0:T(8,128)(2,1)} %copy-done.11), channel_id=1, source_target_pairs={{0,4},{1,5},{2,6},{3,7},{4,8},{5,9},{6,10},{7,11},{8,12},{9,13},{1... | collective-permute-start | bytes 1572872 | tf_op jit(solution)/shard_map/ppermute | solution.py:441
  79.9 27.8 %collective-permute-start.21 = (bf16[224,1024]{1,0:T(8,128)(2,1)S(1)}, bf16[224,1024]{1,0:T(8,128)(2,1)S(1)}, u32[]{:S(2)}, u32[]{:S(2)}) collective-permute-start(bf16[224,1024]{1,0:T(8,128)(2,1)S(1)} %slice.39), channel_id=1, source_target_pairs={{0,16},{16,0},{1,17},{17,1},{2,18},{18,2},{3,19},{19,3},{4,20},{20... | collective-permute-start | bytes 1376264 | tf_op jit(solution)/shard_map/ppermute | solution.py:450
  87.1 21.9 %collective-permute-start.20 = (bf16[224,1024]{1,0:T(8,128)(2,1)S(1)}, bf16[224,1024]{1,0:T(8,128)(2,1)S(1)}, u32[]{:S(2)}, u32[]{:S(2)}) collective-permute-start(bf16[224,1024]{1,0:T(8,128)(2,1)S(1)} %slice.38), channel_id=1, source_target_pairs={{0,16},{16,0},{1,17},{17,1},{2,18},{18,2},{3,19},{19,3},{4,20},{20... | collective-permute-start | bytes 1376264 | tf_op jit(solution)/shard_map/ppermute | solution.py:450
  92.1 29.5 %collective-permute-start.16 = (bf16[352,1024]{1,0:T(8,128)(2,1)S(1)}, bf16[352,1024]{1,0:T(8,128)(2,1)S(1)}, u32[]{:S(2)}, u32[]{:S(2)}) collective-permute-start(bf16[352,1024]{1,0:T(8,128)(2,1)S(1)} %collective-permute-done.12.refs_11_.refs_12_), channel_id=1, source_target_pairs={{0,2},{1,3},{2,0},{3,1},{4,6},{5,7},{6,4},{7,5},{8,10},{9,11},{10,... | collective-permute-start | bytes 2162696 | tf_op jit(solution)/shard_map/ppermute | solution.py:444
  106.3 14.2 %collective-permute-start.10 = (bf16[1024,256]{1,0:T(8,128)(2,1)S(1)}, bf16[1024,256]{1,0:T(8,128)(2,1)S(1)}, u32[]{:S(2)}, u32[]{:S(2)}) collective-permute-start(bf16[1024,256]{1,0:T(8,128)(2,1)S(1)} %collective-permute-done.1.refs_0_.refs_6_), channel_id=1, source_target_pairs={{0,2},{1,3},{2,0},{3,1},{4,6},{5,7},{6,4},{7,5},{8,10},{9,11},{10,... | collective-permute-start | bytes 1572872 | tf_op jit(solution)/shard_map/ppermute | solution.py:444
  107.6 24.3 %collective-permute-start.22 = (bf16[224,1024]{1,0:T(8,128)(2,1)S(1)}, bf16[224,1024]{1,0:T(8,128)(2,1)S(1)}, u32[]{:S(2)}, u32[]{:S(2)}) collective-permute-start(bf16[224,1024]{1,0:T(8,128)(2,1)S(1)} %slice.40), channel_id=1, source_target_pairs={{0,16},{16,0},{1,17},{17,1},{2,18},{18,2},{3,19},{19,3},{4,20},{20... | collective-permute-start | bytes 1376264 | tf_op jit(solution)/shard_map/ppermute | solution.py:450
  109.0 35.0 %collective-permute-start.13 = (bf16[1024,256]{1,0:T(8,128)(2,1)S(1)}, bf16[1024,256]{1,0:T(8,128)(2,1)S(1)}, u32[]{:S(2)}, u32[]{:S(2)}) collective-permute-start(bf16[1024,256]{1,0:T(8,128)(2,1)S(1)} %copy-done.12), channel_id=1, source_target_pairs={{0,8},{1,9},{2,10},{3,11},{4,12},{5,13},{6,14},{7,15},{8,0},{9,1},... | collective-permute-start | bytes 1572872 | tf_op jit(solution)/shard_map/ppermute | solution.py:441
  119.2 26.6 %collective-permute-start.23 = (bf16[224,1024]{1,0:T(8,128)(2,1)S(1)}, bf16[224,1024]{1,0:T(8,128)(2,1)S(1)}, u32[]{:S(2)}, u32[]{:S(2)}) collective-permute-start(bf16[224,1024]{1,0:T(8,128)(2,1)S(1)} %slice.41), channel_id=1, source_target_pairs={{0,16},{16,0},{1,17},{17,1},{2,18},{18,2},{3,19},{19,3},{4,20},{20... | collective-permute-start | bytes 1376264 | tf_op jit(solution)/shard_map/ppermute | solution.py:450
  120.5 26.1 %collective-permute-start.36 = (bf16[1024,256]{1,0:T(8,128)(2,1)S(1)}, bf16[1024,256]{1,0:T(8,128)(2,1)S(1)}, u32[]{:S(2)}, u32[]{:S(2)}) collective-permute-start(bf16[1024,256]{1,0:T(8,128)(2,1)S(1)} %collective-permute-done.2.refs_0_.refs_15_), channel_id=1, source_target_pairs={{0,2},{1,3},{2,0},{3,1},{4,6},{5,7},{6,4},{7,5},{8,10},{9,11},{10,... | collective-permute-start | bytes 1572872 | tf_op jit(solution)/shard_map/ppermute | solution.py:444
  132.0 18.4 %collective-permute-start.24 = (bf16[224,1024]{1,0:T(8,128)(2,1)S(1)}, bf16[224,1024]{1,0:T(8,128)(2,1)S(1)}, u32[]{:S(2)}, u32[]{:S(2)}) collective-permute-start(bf16[224,1024]{1,0:T(8,128)(2,1)S(1)} %slice.42), channel_id=1, source_target_pairs={{0,16},{16,0},{1,17},{17,1},{2,18},{18,2},{3,19},{19,3},{4,20},{20... | collective-permute-start | bytes 1376264 | tf_op jit(solution)/shard_map/ppermute | solution.py:450
  144.0 14.6 %collective-permute-start.17 = (bf16[1024,256]{1,0:T(8,128)(2,1)S(1)}, bf16[1024,256]{1,0:T(8,128)(2,1)}, u32[]{:S(2)}, u32[]{:S(2)}) collective-permute-start(bf16[1024,256]{1,0:T(8,128)(2,1)S(1)} %collective-permute-done.13.refs_0_.refs_11_), channel_id=1, source_target_pairs={{0,2},{1,3},{2,0},{3,1},{4,6},{5,7},{6,4},{7,5},{8,10},{9,11},{10,... | collective-permute-start | bytes 1572872 | tf_op jit(solution)/shard_map/ppermute | solution.py:444
  146.6 30.0 %collective-permute-start.38 = (bf16[1024,256]{1,0:T(8,128)(2,1)S(1)}, bf16[1024,256]{1,0:T(8,128)(2,1)S(1)}, u32[]{:S(2)}, u32[]{:S(2)}) collective-permute-start(bf16[1024,256]{1,0:T(8,128)(2,1)S(1)} %collective-permute-done.13.refs_0_.refs_11_), channel_id=1, source_target_pairs={{0,1},{1,0},{2,3},{3,2},{4,5},{5,4},{6,7},{7,6},{8,9},{9,8},{10,11... | collective-permute-start | bytes 1572872 | tf_op jit(solution)/shard_map/ppermute | solution.py:447
  150.2 29.3 %collective-permute-start.42 = (bf16[1024,256]{1,0:T(8,128)(2,1)S(1)}, bf16[1024,256]{1,0:T(8,128)(2,1)S(1)}, u32[]{:S(2)}, u32[]{:S(2)}) collective-permute-start(bf16[1024,256]{1,0:T(8,128)(2,1)S(1)} %collective-permute-done.2.refs_0_.refs_15_), channel_id=1, source_target_pairs={{0,1},{1,0},{2,3},{3,2},{4,5},{5,4},{6,7},{7,6},{8,9},{9,8},{10,11... | collective-permute-start | bytes 1572872 | tf_op jit(solution)/shard_map/ppermute | solution.py:447
  150.3 29.3 %collective-permute-start.44 = (bf16[1024,256]{1,0:T(8,128)(2,1)S(1)}, bf16[1024,256]{1,0:T(8,128)(2,1)S(1)}, u32[]{:S(2)}, u32[]{:S(2)}) collective-permute-start(bf16[1024,256]{1,0:T(8,128)(2,1)S(1)} %collective-permute-done.36.refs_0_.refs_17_), channel_id=1, source_target_pairs={{0,1},{1,0},{2,3},{3,2},{4,5},{5,4},{6,7},{7,6},{8,9},{9,8},{10,11... | collective-permute-start | bytes 1572872 | tf_op jit(solution)/shard_map/ppermute | solution.py:447
  157.3 14.1 %collective-permute-start.33 = (bf16[512,256]{1,0:T(8,128)(2,1)S(1)}, bf16[512,256]{1,0:T(8,128)(2,1)S(1)}, u32[]{:S(2)}, u32[]{:S(2)}) collective-permute-start(bf16[512,256]{1,0:T(8,128)(2,1)S(1)} %shard_map.92), channel_id=1, source_target_pairs={{0,16},{16,0},{1,17},{17,1},{2,18},{18,2},{3,19},{19,3},{4,20},{20... | collective-permute-start | bytes 786440 | tf_op jit(solution)/shard_map/ppermute | solution.py:450
  158.7 17.1 %collective-permute-start.30 = (bf16[512,256]{1,0:T(8,128)(2,1)S(1)}, bf16[512,256]{1,0:T(8,128)(2,1)S(1)}, u32[]{:S(2)}, u32[]{:S(2)}) collective-permute-start(bf16[512,256]{1,0:T(8,128)(2,1)S(1)} %shard_map.89), channel_id=1, source_target_pairs={{0,16},{16,0},{1,17},{17,1},{2,18},{18,2},{3,19},{19,3},{4,20},{20... | collective-permute-start | bytes 786440 | tf_op jit(solution)/shard_map/ppermute | solution.py:450
  171.4 13.3 %collective-permute-start.25 = (bf16[768,256]{1,0:T(8,128)(2,1)S(1)}, bf16[768,256]{1,0:T(8,128)(2,1)S(1)}, u32[]{:S(2)}, u32[]{:S(2)}) collective-permute-start(bf16[768,256]{1,0:T(8,128)(2,1)S(1)} %get-tuple-element.95), channel_id=1, source_target_pairs={{0,1},{1,0},{2,3},{3,2},{4,5},{5,4},{6,7},{7,6},{8,9},{9,8},{10,11... | collective-permute-start | bytes 1179656 | tf_op jit(solution)/shard_map/ppermute | solution.py:447
  179.5 24.6 %collective-permute-start.32 = (bf16[512,1024]{1,0:T(8,128)(2,1)}, bf16[512,1024]{1,0:T(8,128)(2,1)}, u32[]{:S(2)}, u32[]{:S(2)}) collective-permute-start(bf16[512,1024]{1,0:T(8,128)(2,1)} %shard_map.91.refs_9_), channel_id=1, source_target_pairs={{0,1},{1,0},{2,3},{3,2},{4,5},{5,4},{6,7},{7,6},{8,9},{9,8},{10,11... | collective-permute-start | bytes 3145736 | tf_op jit(solution)/shard_map/ppermute | solution.py:447
  184.8 15.7 %collective-permute-start.37 = (bf16[512,256]{1,0:T(8,128)(2,1)S(1)}, bf16[512,256]{1,0:T(8,128)(2,1)}, u32[]{:S(2)}, u32[]{:S(2)}) collective-permute-start(bf16[512,256]{1,0:T(8,128)(2,1)S(1)} %shard_map.95), channel_id=1, source_target_pairs={{0,16},{16,0},{1,17},{17,1},{2,18},{18,2},{3,19},{19,3},{4,20},{20... | collective-permute-start | bytes 786440 | tf_op jit(solution)/shard_map/ppermute | solution.py:450
  185.6 14.8 %collective-permute-start.28 = (bf16[768,256]{1,0:T(8,128)(2,1)S(1)}, bf16[768,256]{1,0:T(8,128)(2,1)S(1)}, u32[]{:S(2)}, u32[]{:S(2)}) collective-permute-start(bf16[768,256]{1,0:T(8,128)(2,1)S(1)} %get-tuple-element.98), channel_id=1, source_target_pairs={{0,1},{1,0},{2,3},{3,2},{4,5},{5,4},{6,7},{7,6},{8,9},{9,8},{10,11... | collective-permute-start | bytes 1179656 | tf_op jit(solution)/shard_map/ppermute | solution.py:447
  188.0 16.1 %collective-permute-start.40 = (bf16[1024,256]{1,0:T(8,128)(2,1)}, bf16[1024,256]{1,0:T(8,128)(2,1)}, u32[]{:S(2)}, u32[]{:S(2)}) collective-permute-start(bf16[1024,256]{1,0:T(8,128)(2,1)} %collective-permute-done.17.refs_0_.refs_13_), channel_id=1, source_target_pairs={{0,1},{1,0},{2,3},{3,2},{4,5},{5,4},{6,7},{7,6},{8,9},{9,8},{10,11... | collective-permute-start | bytes 1572872 | tf_op jit(solution)/shard_map/ppermute | solution.py:447
  (49 other events, 873.9 us)
